TPU v7x, 32 devices: a whole 2x2x4 slice. The times are simulated.
32 devices in a mesh: row: 2 (over x), col: 16 (over z, y, core).
Axes of the slice: x: 2, y: 2, z: 4, core: 2. Of those that a mesh axis runs over, the one named last changes fastest.
Arguments:
- image: bfloat16 [32, 1024, 96], P('row', 'col'), may hold values from -6 to 6
- kernels: float32 [2, 7, 7, 96], replicated, may hold values from -0.875 to 0.875
- gains: float32 [2, 96], replicated, may hold values from 0.5 to 1.5
- up_weights: bfloat16 [2, 96, 384], replicated, may hold values from -0.625 to 0.625
- down_weights: bfloat16 [2, 384, 96], replicated, may hold values from -0.3125 to 0.3125
- cotangent: bfloat16 [32, 1024, 96], P('row', 'col'), may hold values from -6 to 6
Outputs:
- output: bfloat16 [32, 1024, 96], P('row', 'col')
- grad_image: bfloat16 [32, 1024, 96], P('row', 'col')
- grad_kernels: float32 [2, 7, 7, 96], replicated
- grad_gains: float32 [2, 96], replicated
- grad_up: float32 [2, 96, 384], P(None, 'row', 'col')
- grad_down: float32 [2, 384, 96], P(None, 'col', 'row')
All inputs are finite; a program needn't handle non-finite values.
Results may differ from a plain program's by a relative error of at most 0.029.
Values may be sent and summed in bfloat16 or wider, within the bound.
No kernel may reach another device: no remote copies, remote signals or barrier semaphores. Data moves between devices by JAX's collectives and lax.ppermute only.
A program may use at most 64 MiB of HBM per device.

v0:
```python
import math

import jax
import jax.numpy as jnp
from jax import lax
from jax.sharding import PartitionSpec as P

epsilon = 1e-06
inv_sqrt_two = 0.7071067811865476
inv_sqrt_two_pi = 0.3989422804014327


def extended(array, sides, width):
    for axis, dim in sides:
        count, length = (lax.axis_size(axis), array.shape[dim])
        up = [(i, (i + 1) % count) for i in range(count - 1)]
        down = [(j, i) for i, j in up]
        last = lax.slice_in_dim(array, length - width, length, axis=dim)
        first = lax.slice_in_dim(array, 0, width, axis=dim)
        before = lax.ppermute(last, axis, up)
        after = lax.ppermute(first, axis, down)
        array = jnp.concatenate([before, array, after], axis=dim)
    return array


def contract_leading(left, right):
    return lax.dot_general(
        left, right, (((0,), (0,)), ((), ())), preferred_element_type=jnp.float32
    )


def contract_trailing(left, right):
    return lax.dot_general(
        left, right, (((1,), (1,)), ((), ())), preferred_element_type=jnp.float32
    )


def depthwise(padded, kernel, tile_rows, tile_cols):
    padded_f = padded.astype(jnp.float32)
    tap_count = kernel.shape[0]
    accumulated = jnp.zeros((tile_rows, tile_cols, padded.shape[2]), jnp.float32)
    for tap_row in range(tap_count):
        for tap_col in range(tap_count):
            accumulated = (
                accumulated
                + padded_f[tap_row : tap_row + tile_rows, tap_col : tap_col + tile_cols]
                * kernel[tap_row, tap_col]
            )
    return accumulated


def flipped_conv(padded, kernel, tile_rows, tile_cols):
    padded_f = padded.astype(jnp.float32)
    tap_count = kernel.shape[0]
    last_tap = tap_count - 1
    accumulated = jnp.zeros((tile_rows, tile_cols, padded.shape[2]), jnp.float32)
    for tap_row in range(tap_count):
        for tap_col in range(tap_count):
            start_row = last_tap - tap_row
            start_col = last_tap - tap_col
            accumulated = (
                accumulated
                + padded_f[start_row : start_row + tile_rows, start_col : start_col + tile_cols]
                * kernel[tap_row, tap_col]
            )
    return accumulated


def kernel_grad(padded, conv_grad, tile_rows, tile_cols, tap_count):
    padded_f = padded.astype(jnp.float32)
    grad_f = conv_grad.astype(jnp.float32)
    rows_out = []
    for tap_row in range(tap_count):
        entries = []
        for tap_col in range(tap_count):
            entries.append(
                jnp.sum(
                    padded_f[tap_row : tap_row + tile_rows, tap_col : tap_col + tile_cols] * grad_f,
                    axis=(0, 1),
                )
            )
        rows_out.append(jnp.stack(entries))
    return jnp.stack(rows_out)


def normalize(conv_out):
    centred = conv_out - jnp.mean(conv_out, axis=-1, keepdims=True)
    variance = jnp.mean(centred * centred, axis=-1, keepdims=True)
    inverse_std = lax.rsqrt(variance + epsilon)
    return (centred * inverse_std, inverse_std)


def gelu_parts(pre):
    normal_cdf = 0.5 * (1.0 + lax.erf(pre * inv_sqrt_two))
    density = jnp.exp(-0.5 * pre * pre) * inv_sqrt_two_pi
    return (pre * normal_cdf, normal_cdf + pre * density)


def mixing(padded, kernel, gain, up_weight, tile_rows, tile_cols):
    conv_out = depthwise(padded, kernel, tile_rows, tile_cols)
    unit_vals, inverse_std = normalize(conv_out)
    normed = (unit_vals * gain).astype(jnp.bfloat16).reshape(tile_rows * tile_cols, -1)
    pre = jnp.dot(normed, up_weight, preferred_element_type=jnp.float32)
    gelu_value, gelu_slope = gelu_parts(pre)
    return (unit_vals, inverse_std, normed, gelu_value.astype(jnp.bfloat16), gelu_slope)


def backward_rows(
    padded, upstream, saved, kernel, gain, up_weight, down_weight, tile_rows, tile_cols
):
    unit_vals, inverse_std, normed, hidden, gelu_slope = saved
    channels = upstream.shape[2]
    flat_grad = upstream.reshape(tile_rows * tile_cols, channels)
    down_term = contract_leading(hidden, flat_grad)
    hidden_grad = contract_trailing(flat_grad, down_weight)
    pre_grad = (hidden_grad * gelu_slope).astype(jnp.bfloat16)
    up_term = contract_leading(normed, pre_grad)
    normed_grad = contract_trailing(pre_grad, up_weight).reshape(tile_rows, tile_cols, channels)
    gain_term = jnp.sum(normed_grad * unit_vals, axis=(0, 1))
    unit_grad = normed_grad * gain
    conv_grad = inverse_std * (
        unit_grad
        - jnp.mean(unit_grad, axis=-1, keepdims=True)
        - unit_vals * jnp.mean(unit_grad * unit_vals, axis=-1, keepdims=True)
    )
    conv_grad = conv_grad.astype(jnp.bfloat16)
    kernel_term = kernel_grad(padded, conv_grad, tile_rows, tile_cols, kernel.shape[0])
    return (conv_grad, kernel_term, gain_term, up_term, down_term)


def deliver(up_term, down_term):
    up_part, down_part = (
        lax.psum_scatter(
            up_term.astype(jnp.bfloat16), "row", scatter_dimension=0, tiled=True
        ).astype(jnp.float32),
        lax.psum_scatter(
            down_term.astype(jnp.bfloat16), "row", scatter_dimension=1, tiled=True
        ).astype(jnp.float32),
    )
    up_part, down_part = (
        lax.psum_scatter(
            up_part.astype(jnp.bfloat16), "col", scatter_dimension=1, tiled=True
        ).astype(jnp.float32),
        lax.psum_scatter(
            down_part.astype(jnp.bfloat16), "col", scatter_dimension=0, tiled=True
        ).astype(jnp.float32),
    )
    return (up_part, down_part)


def per_device(image, kernels, gains, up_weights, down_weights, cotangent):
    tile_rows, tile_cols, channels = image.shape
    layer_count = kernels.shape[0]
    halo_width = kernels.shape[1] // 2
    pixel_total = tile_rows * tile_cols * lax.axis_size("row") * lax.axis_size("col")
    factor = 1.0 / math.sqrt(pixel_total)
    current = image
    stored = []
    saved_list = []
    for layer_index in range(layer_count):
        padded = extended(current, (("row", 0), ("col", 1)), halo_width)
        stored.append(padded)
        saved = mixing(
            padded,
            kernels[layer_index],
            gains[layer_index],
            up_weights[layer_index],
            tile_rows,
            tile_cols,
        )
        saved_list.append(saved)
        branch = jnp.dot(
            saved[3], down_weights[layer_index], preferred_element_type=jnp.float32
        ).reshape(tile_rows, tile_cols, channels)
        current = (current.astype(jnp.float32) + branch).astype(jnp.bfloat16)
    gradient = cotangent
    kernel_list = [None] * layer_count
    gain_list = [None] * layer_count
    up_list = [None] * layer_count
    down_list = [None] * layer_count
    for layer_index in reversed(range(layer_count)):
        padded = stored[layer_index]
        saved = saved_list[layer_index]
        conv_grad, kernel_term, gain_term, up_term, down_term = backward_rows(
            padded,
            gradient,
            saved,
            kernels[layer_index],
            gains[layer_index],
            up_weights[layer_index],
            down_weights[layer_index],
            tile_rows,
            tile_cols,
        )
        kernel_list[layer_index] = kernel_term * factor
        gain_list[layer_index] = gain_term * factor
        up_list[layer_index], down_list[layer_index] = deliver(up_term * factor, down_term * factor)
        padded_grad = extended(conv_grad, (("row", 0), ("col", 1)), halo_width)
        gradient = (
            gradient.astype(jnp.float32)
            + flipped_conv(padded_grad, kernels[layer_index], tile_rows, tile_cols)
        ).astype(jnp.bfloat16)
    kernel_total, gain_total = lax.psum(
        (jnp.stack(kernel_list), jnp.stack(gain_list)), ("row", "col")
    )
    return (current, gradient, kernel_total, gain_total, jnp.stack(up_list), jnp.stack(down_list))


def solution(mesh):
    placed = (P("row", "col", None), P(), P(), P(), P(), P("row", "col", None))
    return jax.shard_map(
        per_device,
        mesh=mesh,
        in_specs=placed,
        out_specs=(
            P("row", "col", None),
            P("row", "col", None),
            P(),
            P(),
            P(None, "row", "col"),
            P(None, "col", "row"),
        ),
        check_vma=False,
    )
```

profile of v0, /device:TPU:0, one launch (start us, length us, event | category | flops | bytes accessed | tf_op | source)
XLA Modules:
  0.0 257.1 jit_solution(14199202965456487302)
XLA Ops:
  8.0 4.8 %collective-permute-start = (bf16[3,64,96]{2,1,0:T(8,128)(2,1)S(1)}, bf16[3,64,96]{2,1,0:T(8,128)(2,1)S(1)}, u32[]{:S(2)}, u32[]{:S(2)}) collective-permute-start(bf16[3,64,96]{2,1,0:T(8,128)(2,1)S(1)} %get-tuple-element.155), channel_id=1, source_target_pairs={{0,16},{1,17},{2,18},{3,19},{4,20},{5,21},{6,22},{7,23},{8,24},{9,... | collective-permute-start | bytes 110600 | tf_op jit(solution)/shard_map/ppermute | solution.py:20
  20.2 3.0 %collective-permute-start.2 = (bf16[22,3,96]{2,1,0:T(4,128)(2,1)S(1)}, bf16[22,3,96]{2,1,0:T(4,128)(2,1)S(1)}, u32[]{:S(2)}, u32[]{:S(2)}) collective-permute-start(bf16[22,3,96]{2,1,0:T(4,128)(2,1)S(1)} %get-tuple-element.146), channel_id=1, source_target_pairs={{0,1},{1,2},{2,3},{3,4},{4,5},{5,6},{6,7},{7,8},{8,9},{9,10},{10,1... | collective-permute-start | bytes 38024 | tf_op jit(solution)/shard_map/ppermute | solution.py:20
  24.2 4.3 %fusion.237 = (f32[16,64]{1,0:T(8,128)S(1)}, f32[16,64,96]{2,1,0:T(8,128)S(1)}) fusion(f32[96]{0:T(128)S(1)} %get-tuple-element.208, f32[22,70,96]{2,1,0:T(8,128)S(1)} %maximum_convert_fusion, f32[96]{0:T(128)S(1)} %get-tuple-element.209, f32[96]{0:T(128)S(1)} %get-tuple-element.210, f32[96]{0:T(128)S(1)} %get-tuple-element.211, ...), kind=kLoop, calls=%fused_computation.613 | loop fusion | flops 9632768 | bytes 19683712 | tf_op jit(solution)/shard_map/reduce_sum | solution.py:87
  29.8 1.5 multiply_convert_fusion.1
  31.7 1.3 collective-permute-start.5
  33.0 4.5 %collective-permute-start.4 = (bf16[3,64,96]{2,1,0:T(8,128)(2,1)S(1)}, bf16[3,64,96]{2,1,0:T(8,128)(2,1)S(1)}, u32[]{:S(2)}, u32[]{:S(2)}) collective-permute-start(bf16[3,64,96]{2,1,0:T(8,128)(2,1)S(1)} %get-tuple-element.152), channel_id=1, source_target_pairs={{0,16},{1,17},{2,18},{3,19},{4,20},{5,21},{6,22},{7,23},{8,24},{9,... | collective-permute-start | bytes 110600 | tf_op jit(solution)/shard_map/ppermute | solution.py:20
  38.0 1.7 collective-permute-done.4
  41.0 3.2 %collective-permute-start.6 = (bf16[22,3,96]{2,1,0:T(4,128)(2,1)S(1)}, bf16[22,3,96]{2,1,0:T(4,128)(2,1)S(1)}, u32[]{:S(2)}, u32[]{:S(2)}) collective-permute-start(bf16[22,3,96]{2,1,0:T(4,128)(2,1)S(1)} %get-tuple-element.144), channel_id=1, source_target_pairs={{0,1},{1,2},{2,3},{3,4},{4,5},{5,6},{6,7},{7,8},{8,9},{9,10},{10,1... | collective-permute-start | bytes 38024 | tf_op jit(solution)/shard_map/ppermute | solution.py:20
  45.8 4.3 %fusion.236 = (f32[16,64]{1,0:T(8,128)S(1)}, f32[16,64,96]{2,1,0:T(8,128)S(1)}) fusion(f32[96]{0:T(128)} %get-tuple-element.159, f32[22,70,96]{2,1,0:T(8,128)S(1)} %maximum_convert_fusion.1, f32[96]{0:T(128)} %get-tuple-element.160, f32[96]{0:T(128)} %get-tuple-element.161, f32[96]{0:T(128)} %get-tuple-element.162, f32[96]{0:T(128)} %get-tuple-element.163, ...), kind=kLoop, calls=%fused_computation.612 | loop fusion | flops 9632768 | bytes 19683712 | tf_op jit(solution)/shard_map/reduce_sum | solution.py:87
  53.6 2.5 fusion.114
  56.7 1.5 fusion.113
  58.2 1.9 fusion.115
  61.1 1.9 fusion.17
  63.0 1.9 fusion.13
  66.5 4.5 %collective-permute-start.8 = (bf16[3,64,96]{2,1,0:T(8,128)(2,1)}, bf16[3,64,96]{2,1,0:T(8,128)(2,1)S(1)}, u32[]{:S(2)}, u32[]{:S(2)}) collective-permute-start(bf16[3,64,96]{2,1,0:T(8,128)(2,1)} %get-tuple-element.150), channel_id=1, source_target_pairs={{0,16},{1,17},{2,18},{3,19},{4,20},{5,21},{6,22},{7,23},{8,24},{9,... | collective-permute-start | bytes 110600 | tf_op jit(solution)/shard_map/ppermute | solution.py:20
  77.6 4.6 %collective-permute-start.10 = (bf16[22,3,96]{2,1,0:T(4,128)(2,1)S(1)}, bf16[22,3,96]{2,1,0:T(4,128)(2,1)S(1)}, u32[]{:S(2)}, u32[]{:S(2)}) collective-permute-start(bf16[22,3,96]{2,1,0:T(4,128)(2,1)S(1)} %get-tuple-element.142), channel_id=1, source_target_pairs={{0,1},{1,2},{2,3},{3,4},{4,5},{5,6},{6,7},{7,8},{8,9},{9,10},{10,1... | collective-permute-start | bytes 38024 | tf_op jit(solution)/shard_map/ppermute | solution.py:20
  83.6 4.5 %fusion.168 = bf16[16,64,96]{2,1,0:T(8,128)(2,1)S(1)} fusion(f32[22,70,96]{2,1,0:T(8,128)S(1)} %maximum_convert_fusion.2, bf16[16,64,96]{2,1,0:T(8,128)(2,1)S(1)} %copy-done.5, f32[96]{0:T(128)} %get-tuple-element.159, f32[96]{0:T(128)} %get-tuple-element.160, f32[96]{0:T(128)} %get-tuple-element.161, f32[96]{0:T(128)} %get-tuple-element.162, ...), kind=kLoop, calls=%fused_computation.328 | loop fusion | flops 9830400 | bytes 19679616 | tf_op jit(solution)/shard_map/convert_element_type | solution.py:202
  89.8 1.8 fusion.65
  97.5 4.5 %collective-permute-start.12 = (bf16[3,64,96]{2,1,0:T(8,128)(2,1)S(1)}, bf16[3,64,96]{2,1,0:T(8,128)(2,1)S(1)}, u32[]{:S(2)}, u32[]{:S(2)}) collective-permute-start(bf16[3,64,96]{2,1,0:T(8,128)(2,1)S(1)} %get-tuple-element.148), channel_id=1, source_target_pairs={{0,16},{1,17},{2,18},{3,19},{4,20},{5,21},{6,22},{7,23},{8,24},{9,... | collective-permute-start | bytes 110600 | tf_op jit(solution)/shard_map/ppermute | solution.py:20
  103.8 1.3 collective-permute-start.15
  105.1 3.6 %collective-permute-start.14 = (bf16[22,3,96]{2,1,0:T(4,128)(2,1)S(1)}, bf16[22,3,96]{2,1,0:T(4,128)(2,1)S(1)}, u32[]{:S(2)}, u32[]{:S(2)}) collective-permute-start(bf16[22,3,96]{2,1,0:T(4,128)(2,1)S(1)} %get-tuple-element.140), channel_id=1, source_target_pairs={{0,1},{1,2},{2,3},{3,4},{4,5},{5,6},{6,7},{7,8},{8,9},{9,10},{10,1... | collective-permute-start | bytes 38024 | tf_op jit(solution)/shard_map/ppermute | solution.py:20
  108.7 46.4 %all-reduce.4 = (f32[2,7,7,96]{3,2,1,0:T(8,128)S(1)}, f32[2,96]{1,0:T(2,128)}) all-reduce(f32[2,7,7,96]{3,2,1,0:T(8,128)S(1)} %pad_maximum_fusion, f32[2,96]{1,0:T(2,128)S(1)} %pad_maximum_fusion.10), channel_id=1, replica_groups=mesh['row'=2,'col'=16] {'row','col'}, use_global_device_ids=true, to_apply=%region_106.0 | all-reduce | flops 9600 | bytes 76800 | tf_op jit(solution)/shard_map/psum | solution.py:203
  156.4 5.0 %fusion.118 = bf16[16,64,96]{2,1,0:T(8,128)(2,1)} fusion(f32[22,70,96]{2,1,0:T(8,128)S(1)} %maximum_convert_fusion.3, bf16[16,64,96]{2,1,0:T(8,128)(2,1)S(1)} %fusion.168, f32[96]{0:T(128)S(1)} %copy-done.15, f32[96]{0:T(128)S(1)} %copy-done.17, f32[96]{0:T(128)S(1)} %copy-done.19, f32[96]{0:T(128)S(1)} %copy-done.21, f32[96]{0:T(128)S(1)} %copy-done.23, ...), kind=kLoop, calls=%fused_computation.229 | loop fusion | flops 9830400 | bytes 19679616 | tf_op jit(solution)/shard_map/convert_element_type | solution.py:202
  161.4 84.6 %all-reduce.8.cloned.1.call-done = (bf16[48,384]{1,0:T(8,128)(2,1)}, bf16[48,384]{1,0:T(8,128)(2,1)}, bf16[384,48]{0,1:T(8,128)(2,1)}, bf16[384,48]{0,1:T(8,128)(2,1)}) async-done(((bf16[48,384]{1,0:T(8,128)(2,1)}, bf16[48,384]{1,0:T(8,128)(2,1)}, bf16[384,48]{0,1:T(8,128)(2,1)}, bf16[384,48]{0,1:T(8,128)(2,1)}), (bf16[48,384]{1,0:T(8,128)(2,1)}, bf16[48,384]{1,0:T(8,128)(2,1)}, bf16[384,48]{0,1:T(8,128)(2,1)}, ...) | async-done | bytes 147472
  (428 shorter events, 40.4 us)
Async XLA Ops:
  7.2 148.7 %reduce-scatter.11.cloned.1.call-start = ((), (), s32[]{:S(2)}) async-start(), calls=%async_computation.5 | async-start | bytes 110592 | tf_op jit(solution)/shard_map/reduce_scatter | solution.py:133
  8.0 8.8 %collective-permute-start = (bf16[3,64,96]{2,1,0:T(8,128)(2,1)S(1)}, bf16[3,64,96]{2,1,0:T(8,128)(2,1)S(1)}, u32[]{:S(2)}, u32[]{:S(2)}) collective-permute-start(bf16[3,64,96]{2,1,0:T(8,128)(2,1)S(1)} %get-tuple-element.155), channel_id=1, source_target_pairs={{0,16},{1,17},{2,18},{3,19},{4,20},{5,21},{6,22},{7,23},{8,24},{9,... | collective-permute-start | bytes 110600 | tf_op jit(solution)/shard_map/ppermute | solution.py:20
  12.9 6.0 %collective-permute-start.1 = (bf16[3,64,96]{2,1,0:T(8,128)(2,1)S(1)}, bf16[3,64,96]{2,1,0:T(8,128)(2,1)S(1)}, u32[]{:S(2)}, u32[]{:S(2)}) collective-permute-start(bf16[3,64,96]{2,1,0:T(8,128)(2,1)S(1)} %get-tuple-element.154), channel_id=1, source_target_pairs={{16,0},{17,1},{18,2},{19,3},{20,4},{21,5},{22,6},{23,7},{24,8},{25... | collective-permute-start | bytes 110600 | tf_op jit(solution)/shard_map/ppermute | solution.py:21
  18.9 5.1 %collective-permute-start.3 = (bf16[22,3,96]{2,1,0:T(4,128)(2,1)S(1)}, bf16[22,3,96]{2,1,0:T(4,128)(2,1)S(1)}, u32[]{:S(2)}, u32[]{:S(2)}) collective-permute-start(bf16[22,3,96]{2,1,0:T(4,128)(2,1)S(1)} %get-tuple-element.147), channel_id=1, source_target_pairs={{1,0},{2,1},{3,2},{4,3},{5,4},{6,5},{7,6},{8,7},{9,8},{10,9},{11,1... | collective-permute-start | bytes 38024 | tf_op jit(solution)/shard_map/ppermute | solution.py:21
  20.2 3.9 %collective-permute-start.2 = (bf16[22,3,96]{2,1,0:T(4,128)(2,1)S(1)}, bf16[22,3,96]{2,1,0:T(4,128)(2,1)S(1)}, u32[]{:S(2)}, u32[]{:S(2)}) collective-permute-start(bf16[22,3,96]{2,1,0:T(4,128)(2,1)S(1)} %get-tuple-element.146), channel_id=1, source_target_pairs={{0,1},{1,2},{2,3},{3,4},{4,5},{5,6},{6,7},{7,8},{8,9},{9,10},{10,1... | collective-permute-start | bytes 38024 | tf_op jit(solution)/shard_map/ppermute | solution.py:20
  31.7 6.3 %collective-permute-start.5 = (bf16[3,64,96]{2,1,0:T(8,128)(2,1)S(1)}, bf16[3,64,96]{2,1,0:T(8,128)(2,1)S(1)}, u32[]{:S(2)}, u32[]{:S(2)}) collective-permute-start(bf16[3,64,96]{2,1,0:T(8,128)(2,1)S(1)} %get-tuple-element.153), channel_id=1, source_target_pairs={{16,0},{17,1},{18,2},{19,3},{20,4},{21,5},{22,6},{23,7},{24,8},{25... | collective-permute-start | bytes 110600 | tf_op jit(solution)/shard_map/ppermute | solution.py:21
  33.0 6.7 %collective-permute-start.4 = (bf16[3,64,96]{2,1,0:T(8,128)(2,1)S(1)}, bf16[3,64,96]{2,1,0:T(8,128)(2,1)S(1)}, u32[]{:S(2)}, u32[]{:S(2)}) collective-permute-start(bf16[3,64,96]{2,1,0:T(8,128)(2,1)S(1)} %get-tuple-element.152), channel_id=1, source_target_pairs={{0,16},{1,17},{2,18},{3,19},{4,20},{5,21},{6,22},{7,23},{8,24},{9,... | collective-permute-start | bytes 110600 | tf_op jit(solution)/shard_map/ppermute | solution.py:20
  39.7 5.9 %collective-permute-start.7 = (bf16[22,3,96]{2,1,0:T(4,128)(2,1)S(1)}, bf16[22,3,96]{2,1,0:T(4,128)(2,1)S(1)}, u32[]{:S(2)}, u32[]{:S(2)}) collective-permute-start(bf16[22,3,96]{2,1,0:T(4,128)(2,1)S(1)} %get-tuple-element.145), channel_id=1, source_target_pairs={{1,0},{2,1},{3,2},{4,3},{5,4},{6,5},{7,6},{8,7},{9,8},{10,9},{11,1... | collective-permute-start | bytes 38024 | tf_op jit(solution)/shard_map/ppermute | solution.py:21
  41.0 4.6 %collective-permute-start.6 = (bf16[22,3,96]{2,1,0:T(4,128)(2,1)S(1)}, bf16[22,3,96]{2,1,0:T(4,128)(2,1)S(1)}, u32[]{:S(2)}, u32[]{:S(2)}) collective-permute-start(bf16[22,3,96]{2,1,0:T(4,128)(2,1)S(1)} %get-tuple-element.144), channel_id=1, source_target_pairs={{0,1},{1,2},{2,3},{3,4},{4,5},{5,6},{6,7},{7,8},{8,9},{9,10},{10,1... | collective-permute-start | bytes 38024 | tf_op jit(solution)/shard_map/ppermute | solution.py:20
  65.2 11.0 %collective-permute-start.9 = (bf16[3,64,96]{2,1,0:T(8,128)(2,1)}, bf16[3,64,96]{2,1,0:T(8,128)(2,1)S(1)}, u32[]{:S(2)}, u32[]{:S(2)}) collective-permute-start(bf16[3,64,96]{2,1,0:T(8,128)(2,1)} %get-tuple-element.151), channel_id=1, source_target_pairs={{16,0},{17,1},{18,2},{19,3},{20,4},{21,5},{22,6},{23,7},{24,8},{25... | collective-permute-start | bytes 110600 | tf_op jit(solution)/shard_map/ppermute | solution.py:21
  66.5 9.7 %collective-permute-start.8 = (bf16[3,64,96]{2,1,0:T(8,128)(2,1)}, bf16[3,64,96]{2,1,0:T(8,128)(2,1)S(1)}, u32[]{:S(2)}, u32[]{:S(2)}) collective-permute-start(bf16[3,64,96]{2,1,0:T(8,128)(2,1)} %get-tuple-element.150), channel_id=1, source_target_pairs={{0,16},{1,17},{2,18},{3,19},{4,20},{5,21},{6,22},{7,23},{8,24},{9,... | collective-permute-start | bytes 110600 | tf_op jit(solution)/shard_map/ppermute | solution.py:20
  76.2 79.8 %reduce-scatter.15.cloned.1.call-start = ((), (), s32[]{:S(2)}) async-start(), calls=%async_computation.7 | async-start | bytes 110592 | tf_op jit(solution)/shard_map/reduce_scatter | solution.py:136
  76.3 6.9 %collective-permute-start.11 = (bf16[22,3,96]{2,1,0:T(4,128)(2,1)S(1)}, bf16[22,3,96]{2,1,0:T(4,128)(2,1)S(1)}, u32[]{:S(2)}, u32[]{:S(2)}) collective-permute-start(bf16[22,3,96]{2,1,0:T(4,128)(2,1)S(1)} %get-tuple-element.143), channel_id=1, source_target_pairs={{1,0},{2,1},{3,2},{4,3},{5,4},{6,5},{7,6},{8,7},{9,8},{10,9},{11,1... | collective-permute-start | bytes 38024 | tf_op jit(solution)/shard_map/ppermute | solution.py:21
  77.6 5.6 %collective-permute-start.10 = (bf16[22,3,96]{2,1,0:T(4,128)(2,1)S(1)}, bf16[22,3,96]{2,1,0:T(4,128)(2,1)S(1)}, u32[]{:S(2)}, u32[]{:S(2)}) collective-permute-start(bf16[22,3,96]{2,1,0:T(4,128)(2,1)S(1)} %get-tuple-element.142), channel_id=1, source_target_pairs={{0,1},{1,2},{2,3},{3,4},{4,5},{5,6},{6,7},{7,8},{8,9},{9,10},{10,1... | collective-permute-start | bytes 38024 | tf_op jit(solution)/shard_map/ppermute | solution.py:20
  82.9 73.1 %reduce-scatter.9.cloned.1.call-start = ((), (), s32[]{:S(2)}) async-start(), calls=%async_computation.4 | async-start | bytes 110592 | tf_op jit(solution)/shard_map/reduce_scatter | solution.py:133
  95.8 60.2 %copy-start.21 = (f32[96]{0:T(128)S(1)}, f32[96]{0:T(128)}, u32[]{:S(2)}) copy-start(f32[96]{0:T(128)} %copy-done.20) | copy-start | bytes 1156
  95.9 60.2 %copy-start.23 = (f32[96]{0:T(128)S(1)}, f32[96]{0:T(128)}, u32[]{:S(2)}) copy-start(f32[96]{0:T(128)} %copy-done.22) | copy-start | bytes 1156
  95.9 60.2 %copy-start.25 = (f32[96]{0:T(128)S(1)}, f32[96]{0:T(128)}, u32[]{:S(2)}) copy-start(f32[96]{0:T(128)} %copy-done.24) | copy-start | bytes 1156
  96.2 6.8 %collective-permute-start.13 = (bf16[3,64,96]{2,1,0:T(8,128)(2,1)S(1)}, bf16[3,64,96]{2,1,0:T(8,128)(2,1)S(1)}, u32[]{:S(2)}, u32[]{:S(2)}) collective-permute-start(bf16[3,64,96]{2,1,0:T(8,128)(2,1)S(1)} %get-tuple-element.149), channel_id=1, source_target_pairs={{16,0},{17,1},{18,2},{19,3},{20,4},{21,5},{22,6},{23,7},{24,8},{25... | collective-permute-start | bytes 110600 | tf_op jit(solution)/shard_map/ppermute | solution.py:21
  97.5 6.3 %collective-permute-start.12 = (bf16[3,64,96]{2,1,0:T(8,128)(2,1)S(1)}, bf16[3,64,96]{2,1,0:T(8,128)(2,1)S(1)}, u32[]{:S(2)}, u32[]{:S(2)}) collective-permute-start(bf16[3,64,96]{2,1,0:T(8,128)(2,1)S(1)} %get-tuple-element.148), channel_id=1, source_target_pairs={{0,16},{1,17},{2,18},{3,19},{4,20},{5,21},{6,22},{7,23},{8,24},{9,... | collective-permute-start | bytes 110600 | tf_op jit(solution)/shard_map/ppermute | solution.py:20
  102.4 53.6 %reduce-scatter.13.cloned.1.call-start = ((), (), s32[]{:S(2)}) async-start(), calls=%async_computation.6 | async-start | bytes 110592 | tf_op jit(solution)/shard_map/reduce_scatter | solution.py:136
  102.9 143.0 %all-reduce.8.cloned.1.call-start = ((), (), s32[]{:S(2)}) async-start(), calls=%async_computation.8 | async-start | bytes 294912
  103.8 51.9 %collective-permute-start.15 = (bf16[22,3,96]{2,1,0:T(4,128)(2,1)S(1)}, bf16[22,3,96]{2,1,0:T(4,128)(2,1)S(1)}, u32[]{:S(2)}, u32[]{:S(2)}) collective-permute-start(bf16[22,3,96]{2,1,0:T(4,128)(2,1)S(1)} %get-tuple-element.141), channel_id=1, source_target_pairs={{1,0},{2,1},{3,2},{4,3},{5,4},{6,5},{7,6},{8,7},{9,8},{10,9},{11,1... | collective-permute-start | bytes 38024 | tf_op jit(solution)/shard_map/ppermute | solution.py:21
  105.1 50.6 %collective-permute-start.14 = (bf16[22,3,96]{2,1,0:T(4,128)(2,1)S(1)}, bf16[22,3,96]{2,1,0:T(4,128)(2,1)S(1)}, u32[]{:S(2)}, u32[]{:S(2)}) collective-permute-start(bf16[22,3,96]{2,1,0:T(4,128)(2,1)S(1)} %get-tuple-element.140), channel_id=1, source_target_pairs={{0,1},{1,2},{2,3},{3,4},{4,5},{5,6},{6,7},{7,8},{8,9},{9,10},{10,1... | collective-permute-start | bytes 38024 | tf_op jit(solution)/shard_map/ppermute | solution.py:20
  (148 other events, 3611.0 us)
Sparse Core Ops, SparseCore 0:
  76.3 13.7 reduce-scatter.10
  92.2 9.9 reduce-scatter.14
  105.0 12.2 reduce-scatter.8
  119.4 9.8 reduce-scatter.12
  156.1 89.7 all-reduce.7
where the time goes:
time: 259 us; the launch traced here: 257 us
  waiting for transfers between devices  89 us (34%)
  blocking collectives  46.4 us (18%)
  starting transfers between devices  43.7 us (17%)
  other arithmetic  30.9 us (12%)
  local copies, waits for them, and re-layouts  17.6 us (7%)
  between operations  17.3 us (7%)
  matrix products  12.3 us (5%)
    unnamed x6, waiting for transfers between devices  85.1 us
    psum x1, blocking collectives, per_device(): lax.psum((jnp.stack(kernel_list), jnp.stack(gain_list)), ('row', 'col'))  46.4 us
    ppermute x8, starting transfers between devices, extended(): before = lax.ppermute(last, axis, up)  32.9 us
    ppermute x8, starting transfers between devices, extended(): after = lax.ppermute(first, axis, down)  10.3 us
    reduce_sum x6, other arithmetic, kernel_grad(): jnp.sum(padded_f[tap_row:tap_row + tile_rows, tap_col:tap_col + tile_cols...  9.92 us
    convert_element_type x2, other arithmetic, per_device(): gradient = (gradient.astype(jnp.float32) + flipped_conv(padded_grad, kern...  9.48 us
    reduce_sum x2, other arithmetic, normalize(): centred = conv_out - jnp.mean(conv_out, axis=-1, keepdims=True)  8.69 us
    another operation x14, local copies, waits for them, and re-layouts, kernel_grad(): rows_out.append(jnp.stack(entries))  5.21 us
  transfers between devices with their start and end apart: 21, of which 6 were waited for; matrix products, arithmetic and copies ran while one was open for 11% of the time, Pallas kernels for 0%

commit v1 on v0

--- a/solution.py
+++ b/solution.py
@@ -10,17 +10,51 @@
 inv_sqrt_two_pi = 0.3989422804014327
 
 
+def swap_pairs(row_count, col_count, row_start, col_start):
+    def partner(index, start, count):
+        if start is None:
+            return index
+        other = index + 1 if (index - start) % 2 == 0 else index - 1
+        return other if 0 <= other < count else None
+
+    pairs = []
+    for r in range(row_count):
+        for c in range(col_count):
+            pr, pc = (partner(r, row_start, row_count), partner(c, col_start, col_count))
+            if pr is not None and pc is not None:
+                pairs.append((r * col_count + c, pr * col_count + pc))
+    return pairs
+
+
 def extended(array, sides, width):
-    for axis, dim in sides:
-        count, length = (lax.axis_size(axis), array.shape[dim])
-        up = [(i, (i + 1) % count) for i in range(count - 1)]
-        down = [(j, i) for i, j in up]
-        last = lax.slice_in_dim(array, length - width, length, axis=dim)
-        first = lax.slice_in_dim(array, 0, width, axis=dim)
-        before = lax.ppermute(last, axis, up)
-        after = lax.ppermute(first, axis, down)
-        array = jnp.concatenate([before, array, after], axis=dim)
-    return array
+    row_count, col_count = (lax.axis_size("row"), lax.axis_size("col"))
+    rows, cols, _ = array.shape
+    even_row, even_col = (lax.axis_index("row") % 2 == 0, lax.axis_index("col") % 2 == 0)
+    first_cols, last_cols = (array[:, :width], array[:, cols - width :])
+    facing_cols = {
+        0: jnp.where(even_col, last_cols, first_cols),
+        1: jnp.where(even_col, first_cols, last_cols),
+        None: array,
+    }
+
+    def swapped(row_start, col_start):
+        strip = facing_cols[col_start]
+        if row_start is not None:
+            low, high = (strip[:width], strip[rows - width :])
+            strip = jnp.where(even_row == (row_start == 0), high, low)
+        pairs = swap_pairs(row_count, col_count, row_start, col_start)
+        return lax.ppermute(strip, ("row", "col"), pairs)
+
+    def band(row_start):
+        middle = array if row_start is None else swapped(row_start, None)
+        near, far = (swapped(row_start, 0), swapped(row_start, 1))
+        left, right = (jnp.where(even_col, far, near), jnp.where(even_col, near, far))
+        return jnp.concatenate([left, middle, right], axis=1)
+
+    near = band(0)
+    far = band(1) if row_count > 2 else jnp.zeros_like(near)
+    above, below = (jnp.where(even_row, far, near), jnp.where(even_row, near, far))
+    return jnp.concatenate([above, band(None), below], axis=0)
 
 
 def contract_leading(left, right):
@@ -128,24 +162,33 @@
     return (conv_grad, kernel_term, gain_term, up_term, down_term)
 
 
-def deliver(up_term, down_term):
-    up_part, down_part = (
-        lax.psum_scatter(
-            up_term.astype(jnp.bfloat16), "row", scatter_dimension=0, tiled=True
-        ).astype(jnp.float32),
-        lax.psum_scatter(
-            down_term.astype(jnp.bfloat16), "row", scatter_dimension=1, tiled=True
-        ).astype(jnp.float32),
-    )
-    up_part, down_part = (
-        lax.psum_scatter(
-            up_part.astype(jnp.bfloat16), "col", scatter_dimension=1, tiled=True
-        ).astype(jnp.float32),
-        lax.psum_scatter(
-            down_part.astype(jnp.bfloat16), "col", scatter_dimension=0, tiled=True
-        ).astype(jnp.float32),
-    )
-    return (up_part, down_part)
+def deliver(kernel_total, gain_total, up_total, down_total):
+    axes = ("row", "col")
+    row_count, col_count = (lax.axis_size("row"), lax.axis_size("col"))
+    count = row_count * col_count
+    layers, channels, units = up_total.shape
+    half, part = (channels // row_count, units // col_count)
+    up = up_total.reshape(layers, row_count, half, col_count, part).transpose(1, 3, 0, 2, 4)
+    down = down_total.reshape(layers, col_count, part, row_count, half).transpose(3, 1, 0, 2, 4)
+    size = layers * half * part
+    small = jnp.concatenate([kernel_total.reshape(-1), gain_total.reshape(-1)])
+    share = -(-small.shape[0] // (count * 128)) * 128
+    small = jnp.pad(small, (0, share * count - small.shape[0])).reshape(count, share)
+    packed = jnp.concatenate([up.reshape(count, size), down.reshape(count, size), small], axis=1)
+    width = packed.shape[1]
+    packed = jnp.pad(packed, ((0, 0), (0, -width % 128)))
+    packed = packed.astype(jnp.bfloat16).reshape(count, -1, 128)
+    got = lax.all_to_all(packed, axes, 0, 0, tiled=True)
+    total = jnp.sum(got.astype(jnp.float32), axis=0).reshape(-1)
+    up_part = total[:size].reshape(layers, half, part)
+    down_part = total[size : 2 * size].reshape(layers, part, half)
+    mine = total[2 * size : width]
+    copies = jnp.broadcast_to(mine.reshape(1, -1, 128), (count, share // 128, 128))
+    every = lax.all_to_all(copies, axes, 0, 0, tiled=True).reshape(-1)
+    kernel_size = kernel_total.size
+    kernel_out = every[:kernel_size].reshape(kernel_total.shape)
+    gain_out = every[kernel_size : kernel_size + gain_total.size].reshape(gain_total.shape)
+    return (kernel_out, gain_out, up_part, down_part)
 
 
 def per_device(image, kernels, gains, up_weights, down_weights, cotangent):
@@ -194,16 +237,16 @@
         )
         kernel_list[layer_index] = kernel_term * factor
         gain_list[layer_index] = gain_term * factor
-        up_list[layer_index], down_list[layer_index] = deliver(up_term * factor, down_term * factor)
+        up_list[layer_index], down_list[layer_index] = (up_term * factor, down_term * factor)
         padded_grad = extended(conv_grad, (("row", 0), ("col", 1)), halo_width)
         gradient = (
             gradient.astype(jnp.float32)
             + flipped_conv(padded_grad, kernels[layer_index], tile_rows, tile_cols)
         ).astype(jnp.bfloat16)
-    kernel_total, gain_total = lax.psum(
-        (jnp.stack(kernel_list), jnp.stack(gain_list)), ("row", "col")
-    )
-    return (current, gradient, kernel_total, gain_total, jnp.stack(up_list), jnp.stack(down_list))
+    sums = deliver(
+        jnp.stack(kernel_list), jnp.stack(gain_list), jnp.stack(up_list), jnp.stack(down_list)
+    )
+    return (current, gradient) + sums
 
 
 def solution(mesh):

time: 259 us -> 129 us (0.50)
  waiting for transfers between devices: 89 us -> 16.3 us
  blocking collectives: 46.4 us -> 0 us
  between operations: 17.3 us -> 2.75 us
  other arithmetic: 30.9 us -> 41.4 us
  matrix products: 12.3 us -> 7.91 us
  local copies, waits for them, and re-layouts: 17.6 us -> 13.7 us
  starting transfers between devices: 43.7 us -> 46.4 us
    unnamed x6 -> x0, waiting for transfers between devices: 85.1 us -> none
    psum x1 -> x0, blocking collectives: 46.4 us -> none  [per_device(): lax.psum((jnp.stack(kernel_list), jnp.stack(gain_list)), ('row', 'col'))]
    all_to_all x0 -> x2, starting transfers between devices: none -> 12.3 us  [the longest x1 9.7 us: deliver(): got = lax.all_to_all(packed, axes, 0, 0, tiled=True)]
    all_to_all x0 -> x2, waiting for transfers between devices: none -> 12 us  [the longest x1 6.01 us: deliver(): got = lax.all_to_all(packed, axes, 0, 0, tiled=True)]
    ppermute x16 -> x20, starting transfers between devices: 43.3 us -> 34.2 us  [swapped(): return lax.ppermute(strip, ('row', 'col'), pairs)]
    select_n x0 -> x28, other arithmetic: none -> 8.08 us  [the longest x12 4.11 us: swapped(): strip = jnp.where(even_row == (row_start == 0), high, low)]
    another operation x14, local copies, waits for them, and re-layouts: 5.21 us -> 1.01 us  [kernel_grad(): rows_out.append(jnp.stack(entries))]
    dot_general x4, matrix products: 4.78 us -> 1.31 us  [contract_leading(): lax.dot_general(left, right, (((0,), (0,)), ((), ())), preferred_element_...]
  transfers between devices with their start and end apart: 21 -> 22, of which waited for: 6 -> 5; matrix products, arithmetic and copies ran while one was open for 11% -> 20% of each run, Pallas kernels for 0% -> 0%
where the time goes in v1:
time: 129 us
  starting transfers between devices  46.4 us (36%)
  other arithmetic  41.4 us (32%)
  waiting for transfers between devices  16.3 us (13%)
  local copies, waits for them, and re-layouts  13.7 us (11%)
  matrix products  7.91 us (6%)
  between operations  2.75 us (2%)
    ppermute x20, starting transfers between devices, swapped(): return lax.ppermute(strip, ('row', 'col'), pairs)  34.2 us
    all_to_all x1, starting transfers between devices, deliver(): got = lax.all_to_all(packed, axes, 0, 0, tiled=True)  9.7 us
    convert_element_type x2, other arithmetic, per_device(): gradient = (gradient.astype(jnp.float32) + flipped_conv(padded_grad, kern...  9.64 us
    reduce_sum x2, other arithmetic, normalize(): centred = conv_out - jnp.mean(conv_out, axis=-1, keepdims=True)  8.92 us
    reduce_sum x6, other arithmetic, kernel_grad(): jnp.sum(padded_f[tap_row:tap_row + tile_rows, tap_col:tap_col + tile_cols...  8.56 us
    all_to_all x1, waiting for transfers between devices, deliver(): got = lax.all_to_all(packed, axes, 0, 0, tiled=True)  6.01 us
    all_to_all x1, waiting for transfers between devices, deliver(): every = lax.all_to_all(copies, axes, 0, 0, tiled=True).reshape(-1)  5.94 us
    ppermute x20, waiting for transfers between devices, swapped(): return lax.ppermute(strip, ('row', 'col'), pairs)  4.33 us
  transfers between devices with their start and end apart: 22, of which 5 were waited for; matrix products, arithmetic and copies ran while one was open for 20% of the time, Pallas kernels for 0%

profile of v1, /device:TPU:0, one launch (start us, length us, event | category | flops | bytes accessed | tf_op | source)
XLA Modules:
  0.0 128.5 jit_solution(4729558821830855138)
XLA Ops:
  2.0 2.6 %collective-permute-start.1 = (bf16[3,3,96]{2,1,0:T(4,128)(2,1)S(1)}, bf16[3,3,96]{2,1,0:T(4,128)(2,1)S(1)}, u32[]{:S(2)}, u32[]{:S(2)}) collective-permute-start(bf16[3,3,96]{2,1,0:T(4,128)(2,1)S(1)} %slice_select_fusion.10), channel_id=1, source_target_pairs={{0,17},{1,16},{2,19},{3,18},{4,21},{5,20},{6,23},{7,22},{8,25},{9,... | collective-permute-start | bytes 5192 | tf_op jit(solution)/shard_map/ppermute | solution.py:46
  12.7 4.4 %fusion.240 = (f32[16,64]{1,0:T(8,128)S(1)}, f32[16,64,96]{2,1,0:T(8,128)S(1)}) fusion(f32[96]{0:T(128)S(1)} %get-tuple-element.198, f32[22,70,96]{2,1,0:T(8,128)S(1)} %maximum_convert_fusion, f32[96]{0:T(128)S(1)} %get-tuple-element.199, f32[96]{0:T(128)S(1)} %get-tuple-element.200, f32[96]{0:T(128)S(1)} %get-tuple-element.201, ...), kind=kLoop, calls=%fused_computation.651 | loop fusion | flops 9632768 | bytes 19683712 | tf_op jit(solution)/shard_map/reduce_sum | solution.py:121
  18.3 1.5 %multiply_convert_fusion.1 = (bf16[1024,384]{1,0:T(8,128)(2,1)S(1)}, f32[1024,384]{1,0:T(8,128)}) fusion(bf16[1024,96]{1,0:T(8,128)(2,1)S(1)} %bitcast.408, bf16[2,96,384]{2,1,0:T(8,128)(2,1)S(1)} %copy-done.3), kind=kOutput, calls=%fused_computation.114 | convolution fusion | flops 77463552 | bytes 2695168 | tf_op jit(solution)/shard_map/dot_general | solution.py:137
  21.0 8.6 %collective-permute-start.9 = (bf16[16,3,96]{2,1,0:T(4,128)(2,1)S(1)}, bf16[16,3,96]{2,1,0:T(4,128)(2,1)S(1)}, u32[]{:S(2)}, u32[]{:S(2)}) collective-permute-start(bf16[16,3,96]{2,1,0:T(4,128)(2,1)S(1)} %get-tuple-element.127), channel_id=1, source_target_pairs={{0,1},{1,0},{2,3},{3,2},{4,5},{5,4},{6,7},{7,6},{8,9},{9,8},{10,11... | collective-permute-start | bytes 27656 | tf_op jit(solution)/shard_map/ppermute | solution.py:46
  30.7 1.5 %collective-permute-start.7 = (bf16[3,64,96]{2,1,0:T(8,128)(2,1)S(1)}, bf16[3,64,96]{2,1,0:T(8,128)(2,1)S(1)}, u32[]{:S(2)}, u32[]{:S(2)}) collective-permute-start(bf16[3,64,96]{2,1,0:T(8,128)(2,1)S(1)} %slice_select_fusion.2), channel_id=1, source_target_pairs={{0,16},{1,17},{2,18},{3,19},{4,20},{5,21},{6,22},{7,23},{8,24},{9,... | collective-permute-start | bytes 110600 | tf_op jit(solution)/shard_map/ppermute | solution.py:46
  32.7 2.2 %collective-permute-done.7 = bf16[3,64,96]{2,1,0:T(8,128)(2,1)S(1)} collective-permute-done((bf16[3,64,96]{2,1,0:T(8,128)(2,1)S(1)}, bf16[3,64,96]{2,1,0:T(8,128)(2,1)S(1)}, u32[]{:S(2)}, u32[]{:S(2)}) %collective-permute-start.7) | collective-permute-done | bytes 36896 | tf_op jit(solution)/shard_map/ppermute | solution.py:46
  35.0 4.5 %fusion.239 = (f32[16,64]{1,0:T(8,128)S(1)}, f32[16,64,96]{2,1,0:T(8,128)S(1)}) fusion(f32[96]{0:T(128)} %get-tuple-element.149, f32[22,70,96]{2,1,0:T(8,128)S(1)} %maximum_convert_fusion.1, f32[96]{0:T(128)} %get-tuple-element.150, f32[96]{0:T(128)} %get-tuple-element.151, f32[96]{0:T(128)} %get-tuple-element.152, f32[96]{0:T(128)} %get-tuple-element.153, ...), kind=kLoop, calls=%fused_computation.650 | loop fusion | flops 9632768 | bytes 19683712 | tf_op jit(solution)/shard_map/reduce_sum | solution.py:121
  43.0 1.8 %fusion.114 = (f32[96]{0:T(128)S(1)}, f32[96]{0:T(128)S(1)}, f32[96]{0:T(128)S(1)}, f32[96]{0:T(128)S(1)}, f32[96]{0:T(128)S(1)}, /*index=5*/f32[96]{0:T(128)S(1...) fusion(f32[22,70,96]{2,1,0:T(8,128)S(1)} %maximum_convert_fusio, ...), kind=kLoop, calls=%fused_computation.225 | loop fusion | flops 4421952 | bytes 8084608 | tf_op jit(solution)/shard_map/reduce_sum | solution.py:111
  44.8 1.4 %fusion.113 = (f32[96]{0:T(128)S(1)}, f32[96]{0:T(128)S(1)}, f32[96]{0:T(128)S(1)}, f32[96]{0:T(128)S(1)}, f32[96]{0:T(128)S(1)}, /*index=5*/f32[96]{0:T(128)S(1...) fusion(bf16[16,64,96]{2,1,0:T(8,128)(2,1)S(1)} %get-tuple-eleme, ...), kind=kLoop, calls=%fused_computation.224 | loop fusion | flops 2652960 | bytes 5313408 | tf_op jit(solution)/shard_map/reduce_sum | solution.py:111
  46.2 1.3 %fusion.115 = (f32[96]{0:T(128)S(1)}, f32[96]{0:T(128)S(1)}, f32[96]{0:T(128)S(1)}, f32[96]{0:T(128)S(1)}, f32[96]{0:T(128)S(1)}, /*index=5*/f32[96]{0:T(128)S(1...) fusion(bf16[16,64,96]{2,1,0:T(8,128)(2,1)S(1)} %get-tuple-eleme, ...), kind=kLoop, calls=%fused_computation.226 | loop fusion | flops 3635520 | bytes 7281408 | tf_op jit(solution)/shard_map/reduce_sum | solution.py:111
  48.1 1.3 %slice_select_fusion.7 = bf16[3,3,96]{2,1,0:T(4,128)(2,1)} fusion(bf16[16,3,96]{2,1,0:T(4,128)(2,1)} %get-tuple-element.124, pred[]{:T(512)S(6)} %eq.21), kind=kLoop, calls=%fused_computation.534 | loop fusion | flops 864 | bytes 5185 | tf_op jit(solution)/shard_map/jit(_where)/select_n | solution.py:44
  50.7 1.3 %slice_select_fusion.6 = bf16[3,3,96]{2,1,0:T(4,128)(2,1)} fusion(bf16[16,3,96]{2,1,0:T(4,128)(2,1)} %get-tuple-element.125, pred[]{:T(512)S(6)} %eq.21), kind=kLoop, calls=%fused_computation.533 | loop fusion | flops 864 | bytes 5185 | tf_op jit(solution)/shard_map/jit(_where)/select_n | solution.py:44
  52.0 5.0 %collective-permute-start.14 = (bf16[16,3,96]{2,1,0:T(4,128)(2,1)}, bf16[16,3,96]{2,1,0:T(4,128)(2,1)}, u32[]{:S(2)}, u32[]{:S(2)}) collective-permute-start(bf16[16,3,96]{2,1,0:T(4,128)(2,1)} %get-tuple-element.125), channel_id=1, source_target_pairs={{0,1},{1,0},{2,3},{3,2},{4,5},{5,4},{6,7},{7,6},{8,9},{9,8},{10,11... | collective-permute-start | bytes 27656 | tf_op jit(solution)/shard_map/ppermute | solution.py:46
  66.6 1.7 %collective-permute-done.12 = bf16[3,64,96]{2,1,0:T(8,128)(2,1)} collective-permute-done((bf16[3,64,96]{2,1,0:T(8,128)(2,1)}, bf16[3,64,96]{2,1,0:T(8,128)(2,1)}, u32[]{:S(2)}, u32[]{:S(2)}) %collective-permute-start.12) | collective-permute-done | bytes 36896 | tf_op jit(solution)/shard_map/ppermute | solution.py:46
  69.4 4.6 %fusion.168 = bf16[16,64,96]{2,1,0:T(8,128)(2,1)S(1)} fusion(f32[22,70,96]{2,1,0:T(8,128)S(1)} %maximum_convert_fusion.2, bf16[16,64,96]{2,1,0:T(8,128)(2,1)S(1)} %copy-done.2, f32[96]{0:T(128)} %get-tuple-element.149, f32[96]{0:T(128)} %get-tuple-element.150, f32[96]{0:T(128)} %get-tuple-element.151, f32[96]{0:T(128)} %get-tuple-element.152, ...), kind=kLoop, calls=%fused_computation.329 | loop fusion | flops 9830400 | bytes 19679616 | tf_op jit(solution)/shard_map/convert_element_type | solution.py:245
  76.2 1.8 %fusion.65 = (f32[96]{0:T(128)S(1)}, f32[96]{0:T(128)S(1)}, f32[96]{0:T(128)S(1)}, f32[96]{0:T(128)S(1)}, f32[96]{0:T(128)S(1)}, /*index=5*/f32[96]{0:T(128)S(1)...) fusion(f32[22,70,96]{2,1,0:T(8,128)S(1)} %maximum_convert_fusio, ...), kind=kLoop, calls=%fused_computation.176 | loop fusion | flops 4421952 | bytes 8084608 | tf_op jit(solution)/shard_map/reduce_sum | solution.py:111
  78.9 1.3 %fusion.66 = (f32[96]{0:T(128)S(1)}, f32[96]{0:T(128)S(1)}, f32[96]{0:T(128)S(1)}, f32[96]{0:T(128)S(1)}, f32[96]{0:T(128)S(1)}, /*index=5*/f32[96]{0:T(128)S(1)...) fusion(bf16[16,64,96]{2,1,0:T(8,128)(2,1)S(1)} %get-tuple-eleme, ...), kind=kLoop, calls=%fused_computation.177 | loop fusion | flops 3635520 | bytes 7281408 | tf_op jit(solution)/shard_map/reduce_sum | solution.py:111
  81.0 5.2 %collective-permute-start.19 = (bf16[16,3,96]{2,1,0:T(4,128)(2,1)S(1)}, bf16[16,3,96]{2,1,0:T(4,128)(2,1)S(1)}, u32[]{:S(2)}, u32[]{:S(2)}) collective-permute-start(bf16[16,3,96]{2,1,0:T(4,128)(2,1)S(1)} %get-tuple-element.123), channel_id=1, source_target_pairs={{0,1},{1,0},{2,3},{3,2},{4,5},{5,4},{6,7},{7,6},{8,9},{9,8},{10,11... | collective-permute-start | bytes 27656 | tf_op jit(solution)/shard_map/ppermute | solution.py:46
  87.1 1.4 %collective-permute-start.16 = (bf16[3,3,96]{2,1,0:T(4,128)(2,1)S(1)}, bf16[3,3,96]{2,1,0:T(4,128)(2,1)S(1)}, u32[]{:S(2)}, u32[]{:S(2)}) collective-permute-start(bf16[3,3,96]{2,1,0:T(4,128)(2,1)S(1)} %slice_select_fusion.4), channel_id=1, source_target_pairs={{0,17},{1,16},{2,19},{3,18},{4,21},{5,20},{6,23},{7,22},{8,25},{9,... | collective-permute-start | bytes 5192 | tf_op jit(solution)/shard_map/ppermute | solution.py:46
  95.0 9.7 %all-to-all-start = ((bf16[32,39,128]{2,1,0:T(8,128)(2,1)}), bf16[32,39,128]{2,1,0:T(8,128)(2,1)S(1)}, u32[]{:S(2)}, u32[]{:S(2)}) async-start(bf16[32,39,128]{2,1,0:T(8,128)(2,1)} %convert_element_type.100), calls=%async_computation | async-start | bytes 655360 | tf_op jit(solution)/shard_map/all_to_all | solution.py:181
  105.3 5.0 %fusion.118 = bf16[16,64,96]{2,1,0:T(8,128)(2,1)} fusion(f32[22,70,96]{2,1,0:T(8,128)S(1)} %maximum_convert_fusion.3, bf16[16,64,96]{2,1,0:T(8,128)(2,1)S(1)} %fusion.168, f32[96]{0:T(128)S(1)} %copy-done.74, f32[96]{0:T(128)S(1)} %copy-done.76, f32[96]{0:T(128)S(1)} %copy-done.78, f32[96]{0:T(128)S(1)} %copy-done.80, f32[96]{0:T(128)S(1)} %copy-done.82, ...), kind=kLoop, calls=%fused_computation.230 | loop fusion | flops 9830400 | bytes 19679616 | tf_op jit(solution)/shard_map/convert_element_type | solution.py:245
  110.4 6.0 %all-to-all-done = bf16[32,39,128]{2,1,0:T(8,128)(2,1)S(1)} async-done(((bf16[32,39,128]{2,1,0:T(8,128)(2,1)}), bf16[32,39,128]{2,1,0:T(8,128)(2,1)S(1)}, u32[]{:S(2)}, u32[]{:S(2)}) %all-to-all-start) | async-done | bytes 319520 | tf_op jit(solution)/shard_map/all_to_all | solution.py:181
  117.1 2.6 %all-to-all-start.1 = ((f32[32,3,128]{2,1,0:T(4,128)}), f32[32,3,128]{2,1,0:T(4,128)S(1)}, u32[]{:S(2)}, u32[]{:S(2)}) async-start(f32[32,3,128]{2,1,0:T(4,128)} %broadcast_in_dim.2), calls=%async_computation.1 | async-start | bytes 131072 | tf_op jit(solution)/shard_map/all_to_all | solution.py:187
  121.1 5.9 %all-to-all-done.1 = f32[32,3,128]{2,1,0:T(4,128)S(1)} async-done(((f32[32,3,128]{2,1,0:T(4,128)}), f32[32,3,128]{2,1,0:T(4,128)S(1)}, u32[]{:S(2)}, u32[]{:S(2)}) %all-to-all-start.1) | async-done | bytes 49184 | tf_op jit(solution)/shard_map/all_to_all | solution.py:187
  (338 shorter events, 42.9 us)
Async XLA Ops:
  1.4 10.1 %collective-permute-start.4 = (bf16[16,3,96]{2,1,0:T(4,128)(2,1)S(1)}, bf16[16,3,96]{2,1,0:T(4,128)(2,1)S(1)}, u32[]{:S(2)}, u32[]{:S(2)}) collective-permute-start(bf16[16,3,96]{2,1,0:T(4,128)(2,1)S(1)} %get-tuple-element.129), channel_id=1, source_target_pairs={{0,1},{1,0},{2,3},{3,2},{4,5},{5,4},{6,7},{7,6},{8,9},{9,8},{10,11... | collective-permute-start | bytes 27656 | tf_op jit(solution)/shard_map/ppermute | solution.py:46
  2.0 9.5 %collective-permute-start.1 = (bf16[3,3,96]{2,1,0:T(4,128)(2,1)S(1)}, bf16[3,3,96]{2,1,0:T(4,128)(2,1)S(1)}, u32[]{:S(2)}, u32[]{:S(2)}) collective-permute-start(bf16[3,3,96]{2,1,0:T(4,128)(2,1)S(1)} %slice_select_fusion.10), channel_id=1, source_target_pairs={{0,17},{1,16},{2,19},{3,18},{4,21},{5,20},{6,23},{7,22},{8,25},{9,... | collective-permute-start | bytes 5192 | tf_op jit(solution)/shard_map/ppermute | solution.py:46
  4.6 6.9 %collective-permute-start.3 = (bf16[16,3,96]{2,1,0:T(4,128)(2,1)S(1)}, bf16[16,3,96]{2,1,0:T(4,128)(2,1)S(1)}, u32[]{:S(2)}, u32[]{:S(2)}) collective-permute-start(bf16[16,3,96]{2,1,0:T(4,128)(2,1)S(1)} %get-tuple-element.128), channel_id=1, source_target_pairs={{1,2},{2,1},{3,4},{4,3},{5,6},{6,5},{7,8},{8,7},{9,10},{10,9},{11,... | collective-permute-start | bytes 27656 | tf_op jit(solution)/shard_map/ppermute | solution.py:46
  5.3 6.2 %collective-permute-start = (bf16[3,3,96]{2,1,0:T(4,128)(2,1)S(1)}, bf16[3,3,96]{2,1,0:T(4,128)(2,1)S(1)}, u32[]{:S(2)}, u32[]{:S(2)}) collective-permute-start(bf16[3,3,96]{2,1,0:T(4,128)(2,1)S(1)} %slice_select_fusion.11), channel_id=1, source_target_pairs={{1,18},{2,17},{3,20},{4,19},{5,22},{6,21},{7,24},{8,23},{9,26},{10... | collective-permute-start | bytes 5192 | tf_op jit(solution)/shard_map/ppermute | solution.py:46
  6.8 4.8 %collective-permute-start.2 = (bf16[3,64,96]{2,1,0:T(8,128)(2,1)S(1)}, bf16[3,64,96]{2,1,0:T(8,128)(2,1)S(1)}, u32[]{:S(2)}, u32[]{:S(2)}) collective-permute-start(bf16[3,64,96]{2,1,0:T(8,128)(2,1)S(1)} %slice_select_fusion.3), channel_id=1, source_target_pairs={{0,16},{1,17},{2,18},{3,19},{4,20},{5,21},{6,22},{7,23},{8,24},{9,... | collective-permute-start | bytes 110600 | tf_op jit(solution)/shard_map/ppermute | solution.py:46
  20.3 12.3 %collective-permute-start.8 = (bf16[16,3,96]{2,1,0:T(4,128)(2,1)S(1)}, bf16[16,3,96]{2,1,0:T(4,128)(2,1)S(1)}, u32[]{:S(2)}, u32[]{:S(2)}) collective-permute-start(bf16[16,3,96]{2,1,0:T(4,128)(2,1)S(1)} %get-tuple-element.126), channel_id=1, source_target_pairs={{1,2},{2,1},{3,4},{4,3},{5,6},{6,5},{7,8},{8,7},{9,10},{10,9},{11,... | collective-permute-start | bytes 27656 | tf_op jit(solution)/shard_map/ppermute | solution.py:46
  21.0 11.7 %collective-permute-start.9 = (bf16[16,3,96]{2,1,0:T(4,128)(2,1)S(1)}, bf16[16,3,96]{2,1,0:T(4,128)(2,1)S(1)}, u32[]{:S(2)}, u32[]{:S(2)}) collective-permute-start(bf16[16,3,96]{2,1,0:T(4,128)(2,1)S(1)} %get-tuple-element.127), channel_id=1, source_target_pairs={{0,1},{1,0},{2,3},{3,2},{4,5},{5,4},{6,7},{7,6},{8,9},{9,8},{10,11... | collective-permute-start | bytes 27656 | tf_op jit(solution)/shard_map/ppermute | solution.py:46
  29.6 3.0 %collective-permute-start.6 = (bf16[3,3,96]{2,1,0:T(4,128)(2,1)S(1)}, bf16[3,3,96]{2,1,0:T(4,128)(2,1)S(1)}, u32[]{:S(2)}, u32[]{:S(2)}) collective-permute-start(bf16[3,3,96]{2,1,0:T(4,128)(2,1)S(1)} %slice_select_fusion.8), channel_id=1, source_target_pairs={{0,17},{1,16},{2,19},{3,18},{4,21},{5,20},{6,23},{7,22},{8,25},{9,... | collective-permute-start | bytes 5192 | tf_op jit(solution)/shard_map/ppermute | solution.py:46
  29.8 2.8 %collective-permute-start.5 = (bf16[3,3,96]{2,1,0:T(4,128)(2,1)S(1)}, bf16[3,3,96]{2,1,0:T(4,128)(2,1)S(1)}, u32[]{:S(2)}, u32[]{:S(2)}) collective-permute-start(bf16[3,3,96]{2,1,0:T(4,128)(2,1)S(1)} %slice_select_fusion.9), channel_id=1, source_target_pairs={{1,18},{2,17},{3,20},{4,19},{5,22},{6,21},{7,24},{8,23},{9,26},{10... | collective-permute-start | bytes 5192 | tf_op jit(solution)/shard_map/ppermute | solution.py:46
  30.7 4.2 %collective-permute-start.7 = (bf16[3,64,96]{2,1,0:T(8,128)(2,1)S(1)}, bf16[3,64,96]{2,1,0:T(8,128)(2,1)S(1)}, u32[]{:S(2)}, u32[]{:S(2)}) collective-permute-start(bf16[3,64,96]{2,1,0:T(8,128)(2,1)S(1)} %slice_select_fusion.2), channel_id=1, source_target_pairs={{0,16},{1,17},{2,18},{3,19},{4,20},{5,21},{6,22},{7,23},{8,24},{9,... | collective-permute-start | bytes 110600 | tf_op jit(solution)/shard_map/ppermute | solution.py:46
  49.4 16.4 %collective-permute-start.13 = (bf16[16,3,96]{2,1,0:T(4,128)(2,1)}, bf16[16,3,96]{2,1,0:T(4,128)(2,1)}, u32[]{:S(2)}, u32[]{:S(2)}) collective-permute-start(bf16[16,3,96]{2,1,0:T(4,128)(2,1)} %get-tuple-element.124), channel_id=1, source_target_pairs={{1,2},{2,1},{3,4},{4,3},{5,6},{6,5},{7,8},{8,7},{9,10},{10,9},{11,... | collective-permute-start | bytes 27656 | tf_op jit(solution)/shard_map/ppermute | solution.py:46
  52.0 13.9 %collective-permute-start.14 = (bf16[16,3,96]{2,1,0:T(4,128)(2,1)}, bf16[16,3,96]{2,1,0:T(4,128)(2,1)}, u32[]{:S(2)}, u32[]{:S(2)}) collective-permute-start(bf16[16,3,96]{2,1,0:T(4,128)(2,1)} %get-tuple-element.125), channel_id=1, source_target_pairs={{0,1},{1,0},{2,3},{3,2},{4,5},{5,4},{6,7},{7,6},{8,9},{9,8},{10,11... | collective-permute-start | bytes 27656 | tf_op jit(solution)/shard_map/ppermute | solution.py:46
  60.5 4.7 %collective-permute-start.11 = (bf16[3,3,96]{2,1,0:T(4,128)(2,1)}, bf16[3,3,96]{2,1,0:T(4,128)(2,1)}, u32[]{:S(2)}, u32[]{:S(2)}) collective-permute-start(bf16[3,3,96]{2,1,0:T(4,128)(2,1)} %slice_select_fusion.6), channel_id=1, source_target_pairs={{0,17},{1,16},{2,19},{3,18},{4,21},{5,20},{6,23},{7,22},{8,25},{9,... | collective-permute-start | bytes 5192 | tf_op jit(solution)/shard_map/ppermute | solution.py:46
  61.3 3.8 %collective-permute-start.10 = (bf16[3,3,96]{2,1,0:T(4,128)(2,1)}, bf16[3,3,96]{2,1,0:T(4,128)(2,1)}, u32[]{:S(2)}, u32[]{:S(2)}) collective-permute-start(bf16[3,3,96]{2,1,0:T(4,128)(2,1)} %slice_select_fusion.7), channel_id=1, source_target_pairs={{1,18},{2,17},{3,20},{4,19},{5,22},{6,21},{7,24},{8,23},{9,26},{10... | collective-permute-start | bytes 5192 | tf_op jit(solution)/shard_map/ppermute | solution.py:46
  63.9 4.5 %collective-permute-start.12 = (bf16[3,64,96]{2,1,0:T(8,128)(2,1)}, bf16[3,64,96]{2,1,0:T(8,128)(2,1)}, u32[]{:S(2)}, u32[]{:S(2)}) collective-permute-start(bf16[3,64,96]{2,1,0:T(8,128)(2,1)} %slice_select_fusion.1), channel_id=1, source_target_pairs={{0,16},{1,17},{2,18},{3,19},{4,20},{5,21},{6,22},{7,23},{8,24},{9,... | collective-permute-start | bytes 110600 | tf_op jit(solution)/shard_map/ppermute | solution.py:46
  80.3 24.4 %collective-permute-start.18 = (bf16[16,3,96]{2,1,0:T(4,128)(2,1)S(1)}, bf16[16,3,96]{2,1,0:T(4,128)(2,1)S(1)}, u32[]{:S(2)}, u32[]{:S(2)}) collective-permute-start(bf16[16,3,96]{2,1,0:T(4,128)(2,1)S(1)} %get-tuple-element.122), channel_id=1, source_target_pairs={{1,2},{2,1},{3,4},{4,3},{5,6},{6,5},{7,8},{8,7},{9,10},{10,9},{11,... | collective-permute-start | bytes 27656 | tf_op jit(solution)/shard_map/ppermute | solution.py:46
  81.0 23.8 %collective-permute-start.19 = (bf16[16,3,96]{2,1,0:T(4,128)(2,1)S(1)}, bf16[16,3,96]{2,1,0:T(4,128)(2,1)S(1)}, u32[]{:S(2)}, u32[]{:S(2)}) collective-permute-start(bf16[16,3,96]{2,1,0:T(4,128)(2,1)S(1)} %get-tuple-element.123), channel_id=1, source_target_pairs={{0,1},{1,0},{2,3},{3,2},{4,5},{5,4},{6,7},{7,6},{8,9},{9,8},{10,11... | collective-permute-start | bytes 27656 | tf_op jit(solution)/shard_map/ppermute | solution.py:46
  87.1 17.6 %collective-permute-start.16 = (bf16[3,3,96]{2,1,0:T(4,128)(2,1)S(1)}, bf16[3,3,96]{2,1,0:T(4,128)(2,1)S(1)}, u32[]{:S(2)}, u32[]{:S(2)}) collective-permute-start(bf16[3,3,96]{2,1,0:T(4,128)(2,1)S(1)} %slice_select_fusion.4), channel_id=1, source_target_pairs={{0,17},{1,16},{2,19},{3,18},{4,21},{5,20},{6,23},{7,22},{8,25},{9,... | collective-permute-start | bytes 5192 | tf_op jit(solution)/shard_map/ppermute | solution.py:46
  88.5 16.2 %collective-permute-start.15 = (bf16[3,3,96]{2,1,0:T(4,128)(2,1)S(1)}, bf16[3,3,96]{2,1,0:T(4,128)(2,1)S(1)}, u32[]{:S(2)}, u32[]{:S(2)}) collective-permute-start(bf16[3,3,96]{2,1,0:T(4,128)(2,1)S(1)} %slice_select_fusion.5), channel_id=1, source_target_pairs={{1,18},{2,17},{3,20},{4,19},{5,22},{6,21},{7,24},{8,23},{9,26},{10... | collective-permute-start | bytes 5192 | tf_op jit(solution)/shard_map/ppermute | solution.py:46
  89.4 15.4 %collective-permute-start.17 = (bf16[3,64,96]{2,1,0:T(8,128)(2,1)S(1)}, bf16[3,64,96]{2,1,0:T(8,128)(2,1)S(1)}, u32[]{:S(2)}, u32[]{:S(2)}) collective-permute-start(bf16[3,64,96]{2,1,0:T(8,128)(2,1)S(1)} %slice_select_fusion), channel_id=1, source_target_pairs={{0,16},{1,17},{2,18},{3,19},{4,20},{5,21},{6,22},{7,23},{8,24},{9,... | collective-permute-start | bytes 110600 | tf_op jit(solution)/shard_map/ppermute | solution.py:46
  93.7 11.3 %copy-start.14 = (f32[96]{0:T(128)S(1)}, f32[96]{0:T(128)}, u32[]{:S(2)}) copy-start(f32[96]{0:T(128)} %copy-done.13) | copy-start | bytes 1156
  93.7 11.3 %copy-start.16 = (f32[96]{0:T(128)S(1)}, f32[96]{0:T(128)}, u32[]{:S(2)}) copy-start(f32[96]{0:T(128)} %copy-done.15) | copy-start | bytes 1156
  95.0 21.4 %all-to-all-start = ((bf16[32,39,128]{2,1,0:T(8,128)(2,1)}), bf16[32,39,128]{2,1,0:T(8,128)(2,1)S(1)}, u32[]{:S(2)}, u32[]{:S(2)}) async-start(bf16[32,39,128]{2,1,0:T(8,128)(2,1)} %convert_element_type.100), calls=%async_computation | async-start | bytes 655360 | tf_op jit(solution)/shard_map/all_to_all | solution.py:181
  117.1 10.0 %all-to-all-start.1 = ((f32[32,3,128]{2,1,0:T(4,128)}), f32[32,3,128]{2,1,0:T(4,128)S(1)}, u32[]{:S(2)}, u32[]{:S(2)}) async-start(f32[32,3,128]{2,1,0:T(4,128)} %broadcast_in_dim.2), calls=%async_computation.1 | async-start | bytes 131072 | tf_op jit(solution)/shard_map/all_to_all | solution.py:187
  (86 other events, 729.1 us)

commit v2 on v0

v2 whole, which is shorter than its diff:
```python
import functools
import math

import jax
import jax.numpy as jnp
from jax import lax
from jax.experimental import pallas as pl
from jax.experimental.pallas import tpu as pltpu
from jax.sharding import PartitionSpec as P

epsilon = 1e-06
inv_sqrt_two = 0.7071067811865476
inv_sqrt_two_pi = 0.3989422804014327
LANES = 128
SIDE = 8
f32, bf16 = (jnp.float32, jnp.bfloat16)


def ceil8(n):
    return -(-n // 8) * 8


def combos(row_count):
    listed = [(None, 0), (None, 1), (0, None), (0, 0), (0, 1)]
    if row_count > 2:
        listed += [(1, None), (1, 0), (1, 1)]
    return listed


def partner(index, start, count):
    if start is None:
        return index
    other = index + 1 if (index - start) % 2 == 0 else index - 1
    return other if 0 <= other < count else None


def swap_pairs(row_count, col_count, row_start, col_start):
    pairs = []
    for r in range(row_count):
        for c in range(col_count):
            pr, pc = (partner(r, row_start, row_count), partner(c, col_start, col_count))
            if pr is None:
                pr, pc = (r, c ^ 1)
            elif pc is None:
                pr, pc = (r ^ 1 if row_start is None else pr, c)
            pairs.append((r * col_count + c, pr * col_count + pc))
    return pairs


def exchange(strips, row_count, col_count):
    return [
        lax.ppermute(strip, ("row", "col"), swap_pairs(row_count, col_count, rs, cs))
        for strip, (rs, cs) in zip(strips, combos(row_count))
    ]


class Place:
    def __init__(self, row_count, col_count):
        row, col = (lax.axis_index("row"), lax.axis_index("col"))
        self.even_row, self.even_col = (lax.rem(row, 2) == 0, lax.rem(col, 2) == 0)
        self.has = {
            "above": row > 0,
            "below": row < row_count - 1,
            "left": col > 0,
            "right": col < col_count - 1,
        }
        self.row_count = row_count


def write_strips(place, outs, takes):
    for out, (rs, cs) in zip(outs, combos(place.row_count)):
        at = 0
        for take, radius, rows, cols in takes:
            row_sets = [slice(0, rows)] * 2
            col_sets = [slice(0, cols)] * 2
            if rs is not None:
                row_sets = [slice(rows - radius, rows), slice(0, radius)]
                if rs == 1:
                    row_sets = row_sets[::-1]
            if cs is not None:
                col_sets = [slice(cols - SIDE, cols), slice(0, SIDE)]
                if cs == 1:
                    col_sets = col_sets[::-1]
            count = row_sets[0].stop - row_sets[0].start
            for i in range(count):
                parts = {}
                for er in (0, 1):
                    for ec in (0, 1):
                        key = (row_sets[er].start + i, col_sets[ec].start, col_sets[ec].stop)
                        if key not in parts:
                            parts[key] = take(*key)
                        parts[er, ec] = parts[key]
                if cs is None:
                    pick = [parts[0, 0], parts[1, 0]]
                else:
                    pick = [jnp.where(place.even_col, parts[e, 0], parts[e, 1]) for e in (0, 1)]
                value = pick[0] if rs is None else jnp.where(place.even_row, pick[0], pick[1])
                out[at + i] = value.astype(out.dtype)
            at += count


def strip_shapes(row_count, rows, cols, channels, radii):
    shapes = []
    for rs, cs in combos(row_count):
        height = sum(rows if rs is None else radius for radius in radii)
        shapes.append((height, cols if cs is None else SIDE, channels))
    return shapes


def received(place, strips, row_sections):
    table = dict(zip(combos(place.row_count), strips))
    full_start, band_start = row_sections

    def along(rs, cs, i):
        return table[rs, cs][(full_start if rs is None else band_start) + i].astype(f32)

    def column(rs, side, i):
        if side is None:
            return along(rs, None, i)
        near, far = (along(rs, 0, i), along(rs, 1, i))
        if side == "left":
            return jnp.where(place.even_col, far, near)
        return jnp.where(place.even_col, near, far)

    def read(vertical, side, i):
        if vertical is None:
            value = column(None, side, i)
        elif place.row_count == 2:
            value = column(0, side, i)
        else:
            near, far = (column(0, side, i), column(1, side, i))
            if vertical == "above":
                value = jnp.where(place.even_row, far, near)
            else:
                value = jnp.where(place.even_row, near, far)
        if vertical is not None:
            value = jnp.where(place.has[vertical], value, 0.0)
        if side is not None:
            value = jnp.where(place.has[side], value, 0.0)
        return value

    return read


def assemble(place, target, own, read, radius, rows, cols, channels):
    width = cols + 2 * SIDE
    target[...] = jnp.zeros(target.shape, f32)
    for vertical, start, count in (("above", 0, radius), (None, radius, rows), ("below", radius + rows, radius)):
        for i in range(count):
            base = (start + i) * width
            middle = own(i) if vertical is None else read(vertical, None, i)
            target[base + SIDE : base + SIDE + cols, 0:channels] = middle
            target[base : base + SIDE, 0:channels] = read(vertical, "left", i)
            target[base + SIDE + cols : base + width, 0:channels] = read(vertical, "right", i)


def spread_taps(kernel_ref, layer, target, flipped):
    size, channels = (kernel_ref.shape[1], kernel_ref.shape[3])
    target[...] = jnp.zeros(target.shape, f32)
    for a in range(size):
        for b in range(size):
            t = (size - 1 - a) * size + size - 1 - b if flipped else a * size + b
            row = kernel_ref[layer, a, b : b + 1, :]
            target[t * 8 : t * 8 + 8, 0:channels] = jnp.broadcast_to(row, (8, channels))


def conv_group(src, base, stride, rows_out, taps, size):
    total = [None] * rows_out
    for b in range(size):
        weights = [taps[(a * size + b) * 8 : (a * size + b) * 8 + 8, :] for a in range(size)]
        for i in range(rows_out + size - 1):
            x = src[pl.ds(base + i * stride + b, 8), :]
            for a in range(size):
                r = i - a
                if 0 <= r < rows_out:
                    term = x * weights[a]
                    total[r] = term if total[r] is None else total[r] + term
    return total


def kernel_sums(src, src_base, src_stride, grad, grad_base, grad_stride, rows, cols, size, sums):
    sums[...] = jnp.zeros(sums.shape, f32)

    def group(g, carry):
        at = pl.multiple_of(g * 8, 8)
        grads = [grad[pl.ds(grad_base + i * grad_stride + at, 8), :] for i in range(rows)]
        for b in range(size):
            total = [None] * size
            for i in range(rows + size - 1):
                x = src[pl.ds(src_base + i * src_stride + at + b, 8), :]
                for a in range(size):
                    r = i - a
                    if 0 <= r < rows:
                        term = x * grads[r]
                        total[a] = term if total[a] is None else total[a] + term
            for a in range(size):
                t = (a * size + b) * 8
                sums[t : t + 8, :] += total[a]
        return carry

    lax.fori_loop(0, cols // 8, group, 0)


def lane_total(x):
    high = x.astype(bf16)
    low = (x - high.astype(f32)).astype(bf16)
    both = jnp.concatenate([high, low], axis=1)
    ones = jnp.ones((2 * LANES, LANES), bf16)
    return jnp.dot(both, ones, preferred_element_type=f32)


def layer_norm(conv, channels):
    lane = lax.broadcasted_iota(jnp.int32, conv.shape, 1)
    centred = jnp.where(lane < channels, conv - lane_total(conv) * (1.0 / channels), 0.0)
    variance = lane_total(centred * centred) * (1.0 / channels)
    inverse = lax.rsqrt(variance + epsilon)
    return (centred * inverse, inverse)


def norm_backward(normed_grad, unit, inverse, gain, channels):
    m = normed_grad * gain
    mean = lane_total(m) * (1.0 / channels)
    along = lane_total(m * unit) * (1.0 / channels)
    lane = lax.broadcasted_iota(jnp.int32, m.shape, 1)
    return jnp.where(lane < channels, inverse * (m - mean - unit * along), 0.0)


def gelu_parts(v):
    t = 1.0 / (1.0 + (0.3275911 * inv_sqrt_two) * jnp.abs(v))
    bell = jnp.exp(-0.5 * v * v)
    series = 0.5 * 1.061405429 * t + 0.5 * -1.453152027
    series = series * t + 0.5 * 1.421413741
    series = series * t + 0.5 * -0.284496736
    series = series * t + 0.5 * 0.254829592
    tail = series * t * bell
    cdf = jnp.where(v >= 0.0, 1.0 - tail, tail)
    return (v * cdf, cdf + v * (bell * inv_sqrt_two_pi))


def dot(x, w):
    return jnp.dot(x, w, preferred_element_type=f32)


def dot_leading(x, y):
    return lax.dot_general(x, y, (((0,), (0,)), ((), ())), preferred_element_type=f32)


def pad_lanes(x):
    rows, channels = x.shape
    return jnp.concatenate([x, jnp.zeros((rows, LANES - channels), x.dtype)], axis=1)


def load_weights(up_ref, down_ref, layer, up, down, up_t, down_t):
    channels, units = up_ref.shape[1:]
    up_f = jnp.concatenate([up_ref[layer].astype(f32), jnp.zeros((LANES - channels, units), f32)], axis=0)
    down_f = pad_lanes(down_ref[layer].astype(f32))
    if up is not None:
        up[...] = up_f.astype(bf16)
        down[...] = down_f.astype(bf16)
    if up_t is not None:
        up_t[...] = up_f.T.astype(bf16)
        down_t[...] = down_f.T.astype(bf16)


def round16(x):
    return x.astype(bf16).astype(f32)


def strips_kernel(dims, image, cot, *outs):
    place = Place(dims.row_count, dims.col_count)

    def take(ref):
        return lambda i, lo, hi: ref[i].astype(f32)[lo:hi]

    write_strips(
        place,
        outs,
        [(take(image), 2 * dims.h, dims.rows, dims.cols), (take(cot), dims.h, dims.rows, dims.cols)],
    )


def first_kernel(dims, *refs):
    count = len(combos(dims.row_count))
    image, cot, kernels, gains, up_w, down_w = refs[:6]
    strips = refs[6 : 6 + count]
    refs = refs[6 + count :]
    (output, x0, x1, unit0, inv0, hidden0, slope0, grad1, normed1, pre_grad1, hidden1, gain_sum) = refs[:12]
    outs = refs[12 : 12 + count]
    conv, taps, up, down, up_t, down_t = refs[12 + count :]
    place = Place(dims.row_count, dims.col_count)
    rows, cols, channels, h, size = (dims.rows, dims.cols, dims.channels, dims.h, dims.size)
    ext_rows, ext_cols, wide = (dims.ext_rows, dims.ext_cols, dims.wide)
    read = received(place, strips, (0, 0))
    assemble(place, x0, lambda i: image[i].astype(f32), read, 2 * h, rows, cols, channels)

    spread_taps(kernels, 0, taps, False)
    load_weights(up_w, down_w, 0, up, down, None, None)

    def conv0(g, carry):
        at = pl.multiple_of(g * 8, 8)
        total = conv_group(x0, at + 1, wide, ext_rows, taps, size)
        for r in range(ext_rows):
            conv[pl.ds(r * ext_cols + at, 8), :] = total[r]
            x1[pl.ds(r * ext_cols + at, 8), :] = x0[pl.ds((r + h) * wide + at + 4, 8), :]
        return carry

    lax.fori_loop(0, ext_cols // 8, conv0, 0)
    gain = pad_lanes(gains[0:1, :])
    step = dims.ext_step

    def mix0(k, carry):
        px = pl.ds(pl.multiple_of(k * step, 16), step)
        unit, inverse = layer_norm(conv[px, :], channels)
        unit0[px, :] = unit.astype(bf16)
        inv0[px, :] = inverse
        pre = dot((unit * gain).astype(bf16), up[...])
        value, slope = gelu_parts(pre)
        hidden = value.astype(bf16)
        hidden0[px, :] = hidden
        slope0[px, :] = slope.astype(bf16)
        x1[px, :] = round16(x1[px, :] + dot(hidden, down[...]))
        return carry

    lax.fori_loop(0, ext_rows * ext_cols // step, mix0, 0)
    clear_outside(place, x1, dims)

    spread_taps(kernels, 1, taps, False)
    load_weights(up_w, down_w, 1, up, down, up_t, down_t)

    def conv1(g, carry):
        at = pl.multiple_of(g * 8, 8)
        total = conv_group(x1, at + 1, ext_cols, rows, taps, size)
        for r in range(rows):
            conv[pl.ds(r * cols + at, 8), :] = total[r]
        return carry

    lax.fori_loop(0, cols // 8, conv1, 0)
    gain1 = pad_lanes(gains[1:2, :])
    gain_sum[...] = jnp.zeros(gain_sum.shape, f32)
    lines = dims.line_step
    step1 = lines * cols

    def mix1(k, carry):
        px = pl.ds(pl.multiple_of(k * step1, step1), step1)
        unit, inverse = layer_norm(conv[px, :], channels)
        normed = (unit * gain1).astype(bf16)
        normed1[px, :] = normed
        value, slope = gelu_parts(dot(normed, up[...]))
        hidden = value.astype(bf16)
        hidden1[px, :] = hidden
        branch = dot(hidden, down[...])
        for i in range(lines):
            start = (k * lines + i + h) * ext_cols + 4
            line = x1[pl.ds(start, cols), :] + branch[i * cols : (i + 1) * cols]
            output[k * lines + i] = line[:, :channels].astype(bf16)
        upstream = pad_lanes(cot[pl.ds(k * lines, lines)].reshape(step1, channels))
        pre_grad = (dot(upstream, down_t[...]) * slope).astype(bf16)
        pre_grad1[px, :] = pre_grad
        normed_grad = dot(pre_grad, up_t[...])
        product = normed_grad * unit
        gain_sum[...] += jnp.sum(product.reshape(step1 // 8, 8, LANES), axis=0)
        grad1[px, :] = round16(norm_backward(normed_grad, unit, inverse, gain1, channels))
        return carry

    lax.fori_loop(0, rows // lines, mix1, 0)

    def take(i, lo, hi):
        return grad1[i * cols + lo : i * cols + hi, 0:channels]

    write_strips(place, outs, [(take, 2 * h, rows, cols)])


def clear_outside(place, flat, dims):
    h, ext_rows, ext_cols = (dims.h, dims.ext_rows, dims.ext_cols)
    margin = (ext_cols - dims.cols) // 2

    @pl.when(jnp.logical_not(place.has["above"]))
    def _():
        flat[0 : h * ext_cols, :] = jnp.zeros((h * ext_cols, LANES), f32)

    @pl.when(jnp.logical_not(place.has["below"]))
    def _():
        flat[(ext_rows - h) * ext_cols :, :] = jnp.zeros((h * ext_cols, LANES), f32)

    @pl.when(jnp.logical_not(place.has["left"]))
    def _():
        for r in range(ext_rows):
            flat[r * ext_cols : r * ext_cols + margin, :] = jnp.zeros((margin, LANES), f32)

    @pl.when(jnp.logical_not(place.has["right"]))
    def _():
        for r in range(ext_rows):
            flat[(r + 1) * ext_cols - margin : (r + 1) * ext_cols, :] = jnp.zeros((margin, LANES), f32)


def sums_kernel(dims, x1, grad1, normed1, pre_grad1, hidden1, cot, gain_part, taps_sum, up_sum, down_sum, sums):
    kernel_sums(x1, 1, dims.ext_cols, grad1, 0, dims.cols, dims.rows, dims.cols, dims.size, sums)
    store_sums(dims, sums, gain_part[...], taps_sum)
    upstream = pad_lanes(cot[...].reshape(dims.rows * dims.cols, dims.channels))
    up_sum[...] = dot_leading(normed1[...], pre_grad1[...]).T
    down_sum[...] = dot_leading(upstream, hidden1[...]).T


def store_sums(dims, sums, gain_part, target):
    taps = dims.size * dims.size
    target[...] = jnp.zeros(target.shape, f32)
    for t in range(taps):
        target[t : t + 1, :] = jnp.sum(sums[t * 8 : t * 8 + 8, :], axis=0, keepdims=True)
    target[taps : taps + 1, :] = jnp.sum(gain_part, axis=0, keepdims=True)


def third_kernel(dims, *refs):
    count = len(combos(dims.row_count))
    (grad1, cot, kernels, gains, up_w, down_w, x0, unit0, inv0, hidden0, slope0) = refs[:11]
    (taps_sum1, up_sum1, down_sum1) = refs[11:14]
    strips = refs[14 : 14 + count]
    cot_strips = refs[14 + count : 14 + 2 * count]
    (grad0, middle, packed) = refs[14 + 2 * count : 17 + 2 * count]
    (wide_grad, upstream, own, taps, up_t, down_t, sums, up_acc, down_acc, gain_sum, small, table) = refs[17 + 2 * count :]
    place = Place(dims.row_count, dims.col_count)
    rows, cols, channels, h, size = (dims.rows, dims.cols, dims.channels, dims.h, dims.size)
    ext_rows, ext_cols, wide = (dims.ext_rows, dims.ext_cols, dims.wide)
    read = received(place, strips, (0, 0))
    assemble(
        place, wide_grad, lambda i: grad1[i * cols : (i + 1) * cols, 0:channels], read, 2 * h, rows, cols, channels
    )
    read_cot = received(place, cot_strips, (rows, 2 * h))
    margin = (ext_cols - cols) // 2
    upstream[...] = jnp.zeros(upstream.shape, f32)
    for vertical, start, n in (("above", 0, h), (None, h, rows), ("below", h + rows, h)):
        for i in range(n):
            base = (start + i) * ext_cols
            line = cot[i].astype(f32) if vertical is None else read_cot(vertical, None, i)
            upstream[base + margin : base + margin + cols, 0:channels] = line
            upstream[base : base + margin, 0:channels] = read_cot(vertical, "left", i)[SIDE - margin :]
            upstream[base + margin + cols : base + ext_cols, 0:channels] = read_cot(vertical, "right", i)[:margin]

    spread_taps(kernels, 1, taps, True)
    load_weights(up_w, down_w, 0, None, None, up_t, down_t)

    def conv1(g, carry):
        at = pl.multiple_of(g * 8, 8)
        total = conv_group(wide_grad, at + 1, wide, ext_rows, taps, size)
        col = lax.broadcasted_iota(jnp.int32, (8, LANES), 0) + (at - margin)
        inside = jnp.where(jnp.logical_and(col >= 0, col < cols), 1.0, 0.0)
        for r in range(ext_rows):
            px = pl.ds(r * ext_cols + at, 8)
            upstream[px, :] = upstream[px, :] + total[r]
            own[px, :] = inside if h <= r < h + rows else jnp.zeros((8, LANES), f32)
        return carry

    lax.fori_loop(0, ext_cols // 8, conv1, 0)
    for i in range(rows):
        base = (i + h) * ext_cols + margin
        middle[i * cols : (i + 1) * cols, :] = round16(upstream[base : base + cols, :])

    gain = pad_lanes(gains[0:1, :])
    gain_sum[...] = jnp.zeros(gain_sum.shape, f32)
    up_acc[...] = jnp.zeros(up_acc.shape, f32)
    down_acc[...] = jnp.zeros(down_acc.shape, f32)
    step = dims.ext_step

    def mix0(k, carry):
        px = pl.ds(pl.multiple_of(k * step, 16), step)
        flow = upstream[px, :].astype(bf16)
        mine = own[px, :]
        mine16 = mine.astype(bf16)
        unit = unit0[px, :].astype(f32)
        pre_grad = (dot(flow, down_t[...]) * slope0[px, :].astype(f32)).astype(bf16)
        normed_grad = dot(pre_grad, up_t[...])
        normed = (unit * gain * mine).astype(bf16)
        up_acc[...] += dot_leading(normed, pre_grad)
        down_acc[...] += dot_leading(flow * mine16, hidden0[px, :])
        product = normed_grad * unit * mine
        gain_sum[...] += jnp.sum(product.reshape(step // 8, 8, LANES), axis=0)
        grad0[px, :] = round16(norm_backward(normed_grad, unit, inv0[px, :], gain, channels))
        return carry

    lax.fori_loop(0, ext_rows * ext_cols // step, mix0, 0)
    clear_outside(place, grad0, dims)
    kernel_sums(
        x0, h * wide + SIDE - h, wide, grad0, h * ext_cols + margin, ext_cols, rows, cols, size, sums
    )
    store_sums(dims, sums, gain_sum[...], small)

    layer_rows, part, half, share = (dims.layer_rows, dims.part, dims.half, dims.share)
    units = up_acc.shape[1]
    table[...] = jnp.zeros(table.shape, f32)
    taps_rows = size * size + 1
    for layer, source in ((0, small), (1, taps_sum1)):
        for t in range(taps_rows):
            place_at = layer * taps_rows + t
            line = (place_at // share) * 8 + place_at % share
            table[line : line + 1, :] = source[t : t + 1, :] * dims.factor
    up0 = up_acc[...].T * dims.factor
    down0 = down_acc[...].T * dims.factor
    lane = lax.broadcasted_iota(jnp.int32, (units, LANES), 1)
    tall = wide_grad
    for r in range(dims.row_count):
        for layer, (u, d) in enumerate(((up0, down0), (up_sum1[...] * dims.factor, down_sum1[...] * dims.factor))):
            first = pltpu.roll(u, (LANES - r * half) % LANES, 1) if r else u
            shift = (half - r * half) % LANES
            second = pltpu.roll(d, shift, 1) if shift else d
            joined = jnp.where(lane < half, first, jnp.where(lane < 2 * half, second, 0.0))
            tall[layer * (units + 8) : layer * (units + 8) + units, :] = joined

        def slab(c, carry, r=r):
            dev = r * dims.col_count + c
            rows_of = [tall[pl.ds(layer * (units + 8) + c * part, layer_rows), :] for layer in range(2)]
            whole = jnp.concatenate(rows_of, axis=0)
            extra = table[pl.ds(pl.multiple_of(dev * 8, 8), 8), :]
            quarter = lax.broadcasted_iota(jnp.int32, (8, LANES), 1)
            pieces = [jnp.where(quarter >= 96, pltpu.roll(extra, s, 1), 0.0) for s in (96, 64, 32)]
            pieces.append(jnp.zeros((whole.shape[0] - 24, LANES), f32))
            whole = jnp.where(
                lax.broadcasted_iota(jnp.int32, whole.shape, 1) >= 96, jnp.concatenate(pieces, axis=0), whole
            )
            packed[dev] = whole.astype(bf16)
            return carry

        lax.fori_loop(0, dims.col_count, slab, 0)


def image_kernel(dims, grad0, middle, kernels, out, taps, work):
    rows, cols, size = (dims.rows, dims.cols, dims.size)
    spread_taps(kernels, 0, taps, True)

    def conv0(g, carry):
        at = pl.multiple_of(g * 8, 8)
        total = conv_group(grad0, at + 1, dims.ext_cols, rows, taps, size)
        for r in range(rows):
            work[pl.ds(r * cols + at, 8), :] = middle[pl.ds(r * cols + at, 8), :] + total[r]
        return carry

    lax.fori_loop(0, cols // 8, conv0, 0)
    for r in range(rows):
        out[r] = work[r * cols : (r + 1) * cols, 0 : dims.channels].astype(bf16)


def owner_kernel(dims, got, up_out, down_out, copies):
    total = got[0].astype(f32)
    for d in range(1, got.shape[0]):
        total = total + got[d].astype(f32)
    half, part = (dims.half, dims.part)
    for layer in range(2):
        block = total[layer * dims.layer_rows : (layer + 1) * dims.layer_rows]
        up_out[layer] = block.T[:half, :part]
        down_out[layer] = block[:part, half : 2 * half]
    lane = lax.broadcasted_iota(jnp.int32, (8, LANES), 1)
    line = jnp.where(lane < 32, pltpu.roll(total[0:8], 32, 1), 0.0)
    line = jnp.where(jnp.logical_and(lane >= 32, lane < 64), pltpu.roll(total[8:16], 64, 1), line)
    line = jnp.where(jnp.logical_and(lane >= 64, lane < 96), pltpu.roll(total[16:24], 96, 1), line)
    for d in range(copies.shape[0]):
        copies[d] = line[: dims.share]


def unpack_kernel(dims, every, kernel_out, gain_out):
    size, channels = (dims.size, dims.channels)
    for layer in range(2):
        for t in range(size * size + 1):
            at = layer * (size * size + 1) + t
            row = every[at // dims.share, at % dims.share : at % dims.share + 1, 0:channels]
            if t < size * size:
                kernel_out[layer, t // size, t % size : t % size + 1, :] = row
            else:
                gain_out[layer : layer + 1, :] = row


class Dims:
    pass


def dims_of(image, kernels, up_weights):
    d = Dims()
    d.row_count, d.col_count = (lax.axis_size("row"), lax.axis_size("col"))
    d.rows, d.cols, d.channels = image.shape
    d.size = kernels.shape[1]
    d.h = d.size // 2
    d.ext_rows, d.ext_cols = (d.rows + 2 * d.h, d.cols + 8)
    d.wide = d.cols + 2 * SIDE
    total = d.ext_rows * d.ext_cols
    d.ext_step = max(s for s in range(16, 600, 16) if total % s == 0)
    d.line_step = 4
    d.half = d.channels // d.row_count
    d.part = up_weights.shape[2] // d.col_count
    d.layer_rows = ceil8(d.part)
    d.count = d.row_count * d.col_count
    d.share = -(-2 * (d.size * d.size + 1) // d.count)
    d.factor = 1.0 / math.sqrt(d.rows * d.cols * d.count)
    return d


def run(kernel, outs, scratch, *args):
    shapes = [jax.ShapeDtypeStruct(shape, kind) for shape, kind in outs]
    space = pl.BlockSpec(memory_space=pltpu.VMEM)
    return pl.pallas_call(
        kernel,
        out_shape=shapes,
        in_specs=[space] * len(args),
        out_specs=[space] * len(shapes),
        scratch_shapes=[pltpu.VMEM(shape, kind) for shape, kind in scratch],
        compiler_params=pltpu.CompilerParams(vmem_limit_bytes=48 * 1024 * 1024),
    )(*args)


def per_device(image, kernels, gains, up_weights, down_weights, cotangent):
    d = dims_of(image, kernels, up_weights)
    bind = functools.partial
    rows, cols, channels = image.shape
    units = up_weights.shape[2]
    tile, ext, wide = (rows * cols, d.ext_rows * d.ext_cols, (rows + 4 * d.h) * d.wide)
    taps = ((d.size * d.size * 8, LANES), f32)
    sums_rows = ceil8(d.size * d.size + 1)

    shapes = strip_shapes(d.row_count, rows, cols, channels, (2 * d.h, d.h))
    strips = run(bind(strips_kernel, d), [(s, bf16) for s in shapes], [], image, cotangent)
    strips = exchange(strips, d.row_count, d.col_count)

    grad_shapes = strip_shapes(d.row_count, rows, cols, channels, (2 * d.h,))
    first = run(
        bind(first_kernel, d),
        [
            (image.shape, bf16),
            ((wide, LANES), f32),
            ((ext, LANES), f32),
            ((ext, LANES), bf16),
            ((ext, LANES), f32),
            ((ext, units), bf16),
            ((ext, units), bf16),
            ((tile, LANES), f32),
            ((tile, LANES), bf16),
            ((tile, units), bf16),
            ((tile, units), bf16),
            ((8, LANES), f32),
        ]
        + [(s, bf16) for s in grad_shapes],
        [
            ((ext, LANES), f32),
            taps,
            ((LANES, units), bf16),
            ((units, LANES), bf16),
            ((units, LANES), bf16),
            ((LANES, units), bf16),
        ],
        image,
        cotangent,
        kernels,
        gains,
        up_weights,
        down_weights,
        *strips,
    )
    (output, x0, x1, unit0, inv0, hidden0, slope0, grad1, normed1, pre_grad1, hidden1, gain_part) = first[:12]
    grad_strips = exchange(first[12:], d.row_count, d.col_count)

    taps_sum1, up_sum1, down_sum1 = run(
        bind(sums_kernel, d),
        [((sums_rows, LANES), f32), ((units, LANES), f32), ((units, LANES), f32)],
        [taps],
        x1,
        grad1,
        normed1,
        pre_grad1,
        hidden1,
        cotangent,
        gain_part,
    )

    grad0, middle, packed = run(
        bind(third_kernel, d),
        [((ext, LANES), f32), ((tile, LANES), f32), ((d.count, 2 * d.layer_rows, LANES), bf16)],
        [
            ((max(wide, 2 * (units + 16)), LANES), f32),
            ((ext, LANES), f32),
            ((ext, LANES), f32),
            taps,
            ((units, LANES), bf16),
            ((LANES, units), bf16),
            taps,
            ((LANES, units), f32),
            ((LANES, units), f32),
            ((8, LANES), f32),
            ((sums_rows, LANES), f32),
            ((d.count * 8, LANES), f32),
        ],
        grad1,
        cotangent,
        kernels,
        gains,
        up_weights,
        down_weights,
        x0,
        unit0,
        inv0,
        hidden0,
        slope0,
        taps_sum1,
        up_sum1,
        down_sum1,
        *grad_strips,
        *strips,
    )
    axes = ("row", "col")
    got = lax.all_to_all(packed, axes, 0, 0, tiled=True)
    (gradient,) = run(bind(image_kernel, d), [(image.shape, bf16)], [taps, ((tile, LANES), f32)], grad0, middle, kernels)
    up_out, down_out, copies = run(
        bind(owner_kernel, d),
        [((2, d.half, d.part), f32), ((2, d.part, d.half), f32), ((d.count, d.share, LANES), f32)],
        [],
        got,
    )
    every = lax.all_to_all(copies, axes, 0, 0, tiled=True)
    kernel_out, gain_out = run(bind(unpack_kernel, d), [(kernels.shape, f32), (gains.shape, f32)], [], every)
    return (output, gradient, kernel_out, gain_out, up_out, down_out)


def solution(mesh):
    placed = (P("row", "col", None), P(), P(), P(), P(), P("row", "col", None))
    return jax.shard_map(
        per_device,
        mesh=mesh,
        in_specs=placed,
        out_specs=(
            P("row", "col", None),
            P("row", "col", None),
            P(),
            P(),
            P(None, "row", "col"),
            P(None, "col", "row"),
        ),
        check_vma=False,
    )
```

time: 259 us -> 82.7 us (0.32)
  waiting for transfers between devices: 89 us -> 4.07 us
  Pallas kernels: 0 us -> 36.4 us
  other arithmetic: 30.9 us -> 0 us
  starting transfers between devices: 43.7 us -> 14 us
  blocking collectives: 46.4 us -> 18.5 us
  between operations: 17.3 us -> 0.72 us
  matrix products: 12.3 us -> 0 us
  local copies, waits for them, and re-layouts: 17.6 us -> 8.59 us
    unnamed x6 -> x0, waiting for transfers between devices: 85.1 us -> none
    psum x1 -> x0, blocking collectives: 46.4 us -> none  [per_device(): lax.psum((jnp.stack(kernel_list), jnp.stack(gain_list)), ('row', 'col'))]
    pallas_call x0 -> x7, Pallas kernels: none -> 36.4 us  [run(): pl.pallas_call(kernel, out_shape=shapes, in_specs=[space] * len(args), ou...]
    ppermute x16 -> x10, starting transfers between devices: 43.3 us -> 11.5 us  [exchange(): lax.ppermute(strip, ('row', 'col'), swap_pairs(row_count, col_count, rs,...]
    reduce_sum x10 -> x0, other arithmetic: 19.4 us -> none  [the longest x6 9.92 us: kernel_grad(): jnp.sum(padded_f[tap_row:tap_row + tile_rows, tap_col:tap_col + tile_cols...]
    all_to_all x0 -> x1, blocking collectives: none -> 18.5 us  [per_device(): got = lax.all_to_all(packed, axes, 0, 0, tiled=True)]
    dot_general x12 -> x0, matrix products: 12.3 us -> none  [the longest x4 4.78 us: contract_leading(): lax.dot_general(left, right, (((0,), (0,)), ((), ())), preferred_element_...]
    convert_element_type x8 -> x0, other arithmetic: 10.7 us -> none  [the longest x2 9.48 us: per_device(): gradient = (gradient.astype(jnp.float32) + flipped_conv(padded_grad, kern...]
  transfers between devices with their start and end apart: 21 -> 11, of which waited for: 6 -> 3; matrix products, arithmetic and copies ran while one was open for 11% -> 3% of each run, Pallas kernels for 0% -> 7%
where the time goes in v2:
time: 82.7 us; the launch traced here: 82.3 us
  Pallas kernels  36.4 us (44%)
  blocking collectives  18.5 us (22%)
  starting transfers between devices  14 us (17%)
  local copies, waits for them, and re-layouts  8.59 us (10%)
  waiting for transfers between devices  4.07 us (5%)
    pallas_call x7, Pallas kernels, run(): pl.pallas_call(kernel, out_shape=shapes, in_specs=[space] * len(args), ou...  36.4 us
    all_to_all x1, blocking collectives, per_device(): got = lax.all_to_all(packed, axes, 0, 0, tiled=True)  18.5 us
    ppermute x10, starting transfers between devices, exchange(): lax.ppermute(strip, ('row', 'col'), swap_pairs(row_count, col_count, rs,...  11.5 us
    unnamed x22, local copies, waits for them, and re-layouts  8.59 us
    all_to_all x1, waiting for transfers between devices, per_device(): every = lax.all_to_all(copies, axes, 0, 0, tiled=True)  3.55 us
    all_to_all x1, starting transfers between devices, per_device(): every = lax.all_to_all(copies, axes, 0, 0, tiled=True)  2.55 us
  transfers between devices with their start and end apart: 11, of which 3 were waited for; matrix products, arithmetic and copies ran while one was open for 3% of the time, Pallas kernels for 7%

profile of v2, /device:TPU:0, one launch (start us, length us, event | category | flops | bytes accessed | tf_op | source)
XLA Modules:
  0.0 82.3 jit_solution(5022298488706285325)
XLA Ops:
  0.6 0.9 %copy-done = bf16[16,64,96]{2,1,0:T(8,128)(2,1)S(1)} copy-done((bf16[16,64,96]{2,1,0:T(8,128)(2,1)S(1)}, bf16[16,64,96]{2,1,0:T(8,128)(2,1)}, u32[]{:S(2)}) %copy-start) | copy-done | bytes 196632
  1.6 0.9 %copy-done.4 = bf16[16,64,96]{2,1,0:T(8,128)(2,1)S(1)} copy-done((bf16[16,64,96]{2,1,0:T(8,128)(2,1)S(1)}, bf16[16,64,96]{2,1,0:T(8,128)(2,1)}, u32[]{:S(2)}) %copy-start.4) | copy-done | bytes 196632
  2.6 3.0 %collective-permute-start.2 = (bf16[9,64,96]{2,1,0:T(8,128)(2,1)S(1)}, bf16[9,64,96]{2,1,0:T(8,128)(2,1)S(1)}, u32[]{:S(2)}, u32[]{:S(2)}) collective-permute-start(bf16[9,64,96]{2,1,0:T(8,128)(2,1)S(1)} %get-tuple-element.41), channel_id=1, source_target_pairs={{0,16},{1,17},{2,18},{3,19},{4,20},{5,21},{6,22},{7,23},{8,24},{9,... | collective-permute-start | bytes 331784 | tf_op jit(solution)/shard_map/ppermute | solution.py:52
  5.8 1.6 %collective-permute-start.3 = (bf16[9,8,96]{2,1,0:T(8,128)(2,1)S(1)}, bf16[9,8,96]{2,1,0:T(8,128)(2,1)S(1)}, u32[]{:S(2)}, u32[]{:S(2)}) collective-permute-start(bf16[9,8,96]{2,1,0:T(8,128)(2,1)S(1)} %get-tuple-element.42), channel_id=1, source_target_pairs={{0,17},{1,16},{2,19},{3,18},{4,21},{5,20},{6,23},{7,22},{8,25},{9,... | collective-permute-start | bytes 41480 | tf_op jit(solution)/shard_map/ppermute | solution.py:52
  7.4 1.5 %collective-permute-start.4 = (bf16[9,8,96]{2,1,0:T(8,128)(2,1)S(1)}, bf16[9,8,96]{2,1,0:T(8,128)(2,1)S(1)}, u32[]{:S(2)}, u32[]{:S(2)}) collective-permute-start(bf16[9,8,96]{2,1,0:T(8,128)(2,1)S(1)} %get-tuple-element.43), channel_id=1, source_target_pairs={{0,16},{1,18},{2,17},{3,20},{4,19},{5,22},{6,21},{7,24},{8,23},{9,... | collective-permute-start | bytes 41480 | tf_op jit(solution)/shard_map/ppermute | solution.py:52
  8.9 0.8 copy.12.refs_2_.kernels
  9.7 1.1 %copy.13.refs_5_ = bf16[2,384,96]{2,1,0:T(8,128)(2,1)S(1)} copy(bf16[2,384,96]{1,2,0:T(8,128)(2,1)} %param.10) | data formatting | bytes 294912 | tf_op args[4]
  11.2 0.9 %copy-done.1 = bf16[16,64,96]{2,1,0:T(8,128)(2,1)S(1)} copy-done((bf16[16,64,96]{2,1,0:T(8,128)(2,1)S(1)}, bf16[16,64,96]{2,1,0:T(8,128)(2,1)}, u32[]{:S(2)}) %copy-start.1) | copy-done | bytes 196632
  12.2 0.9 %copy-done.5 = bf16[16,64,96]{2,1,0:T(8,128)(2,1)S(1)} copy-done((bf16[16,64,96]{2,1,0:T(8,128)(2,1)S(1)}, bf16[16,64,96]{2,1,0:T(8,128)(2,1)}, u32[]{:S(2)}) %copy-start.5) | copy-done | bytes 196632
  13.1 0.9 %copy-done.6 = bf16[2,96,384]{2,1,0:T(8,128)(2,1)S(1)} copy-done((bf16[2,96,384]{2,1,0:T(8,128)(2,1)S(1)}, bf16[2,96,384]{2,1,0:T(8,128)(2,1)}, u32[]{:S(2)}) %copy-start.6) | copy-done | bytes 147480
  14.0 0.7 copy-done.8
  14.7 16.3 %shard_map.110 = (bf16[16,64,96]{2,1,0:T(8,128)(2,1)}, f32[2240,128]{1,0:T(8,128)}, f32[1584,128]{1,0:T(8,128)S(1)}, bf16[1584,128]{1,0:T(8,128)(2,1)S(1)}, f32[...) custom-call(bf16[16,64,96]{2,1,0:T(8,128)(2,1)S(1)} %copy-done.5, ...), custom_call_target="tpu_custom_call" | custom-call | tf_op jit(solution)/shard_map/pallas_call | solution.py:596
  31.0 1.5 %collective-permute-start.7 = (bf16[6,64,96]{2,1,0:T(8,128)(2,1)S(1)}, bf16[6,64,96]{2,1,0:T(8,128)(2,1)S(1)}, u32[]{:S(2)}, u32[]{:S(2)}) collective-permute-start(bf16[6,64,96]{2,1,0:T(8,128)(2,1)S(1)} %get-tuple-element.61), channel_id=1, source_target_pairs={{0,16},{1,17},{2,18},{3,19},{4,20},{5,21},{6,22},{7,23},{8,24},{9,... | collective-permute-start | bytes 221192 | tf_op jit(solution)/shard_map/ppermute | solution.py:52
  32.5 1.0 %collective-permute-start.6 = (bf16[16,8,96]{2,1,0:T(8,128)(2,1)S(1)}, bf16[16,8,96]{2,1,0:T(8,128)(2,1)S(1)}, u32[]{:S(2)}, u32[]{:S(2)}) collective-permute-start(bf16[16,8,96]{2,1,0:T(8,128)(2,1)S(1)} %get-tuple-element.60), channel_id=1, source_target_pairs={{0,16},{1,2},{2,1},{3,4},{4,3},{5,6},{6,5},{7,8},{8,7},{9,10},{10,... | collective-permute-start | bytes 73736 | tf_op jit(solution)/shard_map/ppermute | solution.py:52
  33.4 1.6 %collective-permute-start.8 = (bf16[6,8,96]{2,1,0:T(8,128)(2,1)S(1)}, bf16[6,8,96]{2,1,0:T(8,128)(2,1)S(1)}, u32[]{:S(2)}, u32[]{:S(2)}) collective-permute-start(bf16[6,8,96]{2,1,0:T(8,128)(2,1)S(1)} %get-tuple-element.62), channel_id=1, source_target_pairs={{0,17},{1,16},{2,19},{3,18},{4,21},{5,20},{6,23},{7,22},{8,25},{9,... | collective-permute-start | bytes 27656 | tf_op jit(solution)/shard_map/ppermute | solution.py:52
  35.1 1.1 %collective-permute-start.9 = (bf16[6,8,96]{2,1,0:T(8,128)(2,1)S(1)}, bf16[6,8,96]{2,1,0:T(8,128)(2,1)S(1)}, u32[]{:S(2)}, u32[]{:S(2)}) collective-permute-start(bf16[6,8,96]{2,1,0:T(8,128)(2,1)S(1)} %get-tuple-element.63), channel_id=1, source_target_pairs={{0,16},{1,18},{2,17},{3,20},{4,19},{5,22},{6,21},{7,24},{8,23},{9,... | collective-permute-start | bytes 27656 | tf_op jit(solution)/shard_map/ppermute | solution.py:52
  36.2 2.4 %shard_map.111 = (f32[56,128]{1,0:T(8,128)S(1)}, f32[384,128]{1,0:T(8,128)S(1)}, f32[384,128]{1,0:T(8,128)S(1)}) custom-call(f32[1584,128]{1,0:T(8,128)S(1)} %get-tuple-element.51.x1, f32[1024,128]{1,0:T(8,128)S(1)} %get-tuple-element.45.grad1.refs_0_, bf16[1024,128]{1,0:T(8,128)(2,1)S(1)} %get-tuple-element.52.normed1, ...), custom_call_target="tpu_custom_call" | custom-call | tf_op jit(solution)/shard_map/pallas_call | solution.py:596
  38.8 13.0 %shard_map.112 = (f32[1584,128]{1,0:T(8,128)S(1)}, f32[1024,128]{1,0:T(8,128)S(1)}, bf16[32,48,128]{2,1,0:T(8,128)(2,1)S(1)}) custom-call(f32[1024,128]{1,0:T(8,128)S(1)} %get-tuple-element.45.grad1.refs_0_, bf16[16,64,96]{2,1,0:T(8,128)(2,1)S(1)} %copy-done.2, f32[2,7,7,96]{3,2,1,0:T(8,128)S(1)} %copy.12.refs_2_.kernels, f32[2,96]{1,0:T(2,128)S(1)} %copy-done.8, ...), custom_call_target="tpu_custom_call" | custom-call | tf_op jit(solution)/shard_map/pallas_call | solution.py:596
  51.8 18.5 %all_to_all.10.got = bf16[32,48,128]{2,1,0:T(8,128)(2,1)S(1)} all-to-all(bf16[32,48,128]{2,1,0:T(8,128)(2,1)S(1)} %get-tuple-element.66), channel_id=1, replica_groups=mesh['row'=2,'col'=16] {'row','col'}, dimensions={0} | all-to-all | bytes 786432 | tf_op jit(solution)/shard_map/all_to_all | solution.py:704
  70.3 0.8 shard_map.114
  71.1 2.5 %all-to-all-start.1 = ((f32[32,4,128]{2,1,0:T(4,128)}), f32[32,4,128]{2,1,0:T(4,128)S(1)}, u32[]{:S(2)}, u32[]{:S(2)}) async-start(f32[32,4,128]{2,1,0:T(4,128)} %get-tuple-element.67), calls=%async_computation.1 | async-start | bytes 131072 | tf_op jit(solution)/shard_map/all_to_all | solution.py:712
  73.6 3.2 %shard_map.113 = bf16[16,64,96]{2,1,0:T(8,128)(2,1)} custom-call(f32[1584,128]{1,0:T(8,128)S(1)} %get-tuple-element.64.grad0, f32[1024,128]{1,0:T(8,128)S(1)} %get-tuple-element.65.middle, f32[2,7,7,96]{3,2,1,0:T(8,128)S(1)} %copy.12.refs_2_.kernels), custom_call_target="tpu_custom_call" | custom-call | tf_op jit(solution)/shard_map/pallas_call | solution.py:596
  76.8 0.7 copy.18
  77.5 3.5 %all-to-all-done.1.every = f32[32,4,128]{2,1,0:T(4,128)S(1)} async-done(((f32[32,4,128]{2,1,0:T(4,128)}), f32[32,4,128]{2,1,0:T(4,128)S(1)}, u32[]{:S(2)}, u32[]{:S(2)}) %all-to-all-start.1) | async-done | bytes 65568 | tf_op jit(solution)/shard_map/all_to_all | solution.py:712
  (28 shorter events, 2.1 us)
Async XLA Ops:
  0.6 1.0 %copy-start = (bf16[16,64,96]{2,1,0:T(8,128)(2,1)S(1)}, bf16[16,64,96]{2,1,0:T(8,128)(2,1)}, u32[]{:S(2)}) copy-start(bf16[16,64,96]{2,1,0:T(8,128)(2,1)} %refs_1_.3) | copy-start | bytes 589828
  1.6 0.9 %copy-start.4 = (bf16[16,64,96]{2,1,0:T(8,128)(2,1)S(1)}, bf16[16,64,96]{2,1,0:T(8,128)(2,1)}, u32[]{:S(2)}) copy-start(bf16[16,64,96]{2,1,0:T(8,128)(2,1)} %refs_0_.1) | copy-start | bytes 589828
  2.5 33.6 %copy-start.2 = (bf16[16,64,96]{2,1,0:T(8,128)(2,1)S(1)}, bf16[16,64,96]{2,1,0:T(8,128)(2,1)}, u32[]{:S(2)}) copy-start(bf16[16,64,96]{2,1,0:T(8,128)(2,1)} %refs_1_.3) | copy-start | bytes 589828
  2.6 8.6 %collective-permute-start.2 = (bf16[9,64,96]{2,1,0:T(8,128)(2,1)S(1)}, bf16[9,64,96]{2,1,0:T(8,128)(2,1)S(1)}, u32[]{:S(2)}, u32[]{:S(2)}) collective-permute-start(bf16[9,64,96]{2,1,0:T(8,128)(2,1)S(1)} %get-tuple-element.41), channel_id=1, source_target_pairs={{0,16},{1,17},{2,18},{3,19},{4,20},{5,21},{6,22},{7,23},{8,24},{9,... | collective-permute-start | bytes 331784 | tf_op jit(solution)/shard_map/ppermute | solution.py:52
  5.6 5.5 %collective-permute-start = (bf16[32,8,96]{2,1,0:T(8,128)(2,1)S(1)}, bf16[32,8,96]{2,1,0:T(8,128)(2,1)S(1)}, u32[]{:S(2)}, u32[]{:S(2)}) collective-permute-start(bf16[32,8,96]{2,1,0:T(8,128)(2,1)S(1)} %get-tuple-element.39), channel_id=1, source_target_pairs={{0,1},{1,0},{2,3},{3,2},{4,5},{5,4},{6,7},{7,6},{8,9},{9,8},{10,11... | collective-permute-start | bytes 147464 | tf_op jit(solution)/shard_map/ppermute | solution.py:52
  5.6 5.5 %collective-permute-start.1 = (bf16[32,8,96]{2,1,0:T(8,128)(2,1)S(1)}, bf16[32,8,96]{2,1,0:T(8,128)(2,1)S(1)}, u32[]{:S(2)}, u32[]{:S(2)}) collective-permute-start(bf16[32,8,96]{2,1,0:T(8,128)(2,1)S(1)} %get-tuple-element.40), channel_id=1, source_target_pairs={{0,16},{1,2},{2,1},{3,4},{4,3},{5,6},{6,5},{7,8},{8,7},{9,10},{10,... | collective-permute-start | bytes 147464 | tf_op jit(solution)/shard_map/ppermute | solution.py:52
  5.8 5.0 %collective-permute-start.3 = (bf16[9,8,96]{2,1,0:T(8,128)(2,1)S(1)}, bf16[9,8,96]{2,1,0:T(8,128)(2,1)S(1)}, u32[]{:S(2)}, u32[]{:S(2)}) collective-permute-start(bf16[9,8,96]{2,1,0:T(8,128)(2,1)S(1)} %get-tuple-element.42), channel_id=1, source_target_pairs={{0,17},{1,16},{2,19},{3,18},{4,21},{5,20},{6,23},{7,22},{8,25},{9,... | collective-permute-start | bytes 41480 | tf_op jit(solution)/shard_map/ppermute | solution.py:52
  7.4 3.8 %collective-permute-start.4 = (bf16[9,8,96]{2,1,0:T(8,128)(2,1)S(1)}, bf16[9,8,96]{2,1,0:T(8,128)(2,1)S(1)}, u32[]{:S(2)}, u32[]{:S(2)}) collective-permute-start(bf16[9,8,96]{2,1,0:T(8,128)(2,1)S(1)} %get-tuple-element.43), channel_id=1, source_target_pairs={{0,16},{1,18},{2,17},{3,20},{4,19},{5,22},{6,21},{7,24},{8,23},{9,... | collective-permute-start | bytes 41480 | tf_op jit(solution)/shard_map/ppermute | solution.py:52
  11.2 1.0 %copy-start.1 = (bf16[16,64,96]{2,1,0:T(8,128)(2,1)S(1)}, bf16[16,64,96]{2,1,0:T(8,128)(2,1)}, u32[]{:S(2)}) copy-start(bf16[16,64,96]{2,1,0:T(8,128)(2,1)} %refs_1_.3) | copy-start | bytes 589828
  12.2 0.9 %copy-start.5 = (bf16[16,64,96]{2,1,0:T(8,128)(2,1)S(1)}, bf16[16,64,96]{2,1,0:T(8,128)(2,1)}, u32[]{:S(2)}) copy-start(bf16[16,64,96]{2,1,0:T(8,128)(2,1)} %refs_0_.1) | copy-start | bytes 589828
  13.1 0.9 %copy-start.6 = (bf16[2,96,384]{2,1,0:T(8,128)(2,1)S(1)}, bf16[2,96,384]{2,1,0:T(8,128)(2,1)}, u32[]{:S(2)}) copy-start(bf16[2,96,384]{2,1,0:T(8,128)(2,1)} %refs_4_.3) | copy-start | bytes 442372
  14.0 0.7 copy-start.8
  31.0 7.8 %collective-permute-start.7 = (bf16[6,64,96]{2,1,0:T(8,128)(2,1)S(1)}, bf16[6,64,96]{2,1,0:T(8,128)(2,1)S(1)}, u32[]{:S(2)}, u32[]{:S(2)}) collective-permute-start(bf16[6,64,96]{2,1,0:T(8,128)(2,1)S(1)} %get-tuple-element.61), channel_id=1, source_target_pairs={{0,16},{1,17},{2,18},{3,19},{4,20},{5,21},{6,22},{7,23},{8,24},{9,... | collective-permute-start | bytes 221192 | tf_op jit(solution)/shard_map/ppermute | solution.py:52
  32.5 6.3 %collective-permute-start.5 = (bf16[16,8,96]{2,1,0:T(8,128)(2,1)S(1)}, bf16[16,8,96]{2,1,0:T(8,128)(2,1)S(1)}, u32[]{:S(2)}, u32[]{:S(2)}) collective-permute-start(bf16[16,8,96]{2,1,0:T(8,128)(2,1)S(1)} %get-tuple-element.59), channel_id=1, source_target_pairs={{0,1},{1,0},{2,3},{3,2},{4,5},{5,4},{6,7},{7,6},{8,9},{9,8},{10,11... | collective-permute-start | bytes 73736 | tf_op jit(solution)/shard_map/ppermute | solution.py:52
  32.5 6.3 %collective-permute-start.6 = (bf16[16,8,96]{2,1,0:T(8,128)(2,1)S(1)}, bf16[16,8,96]{2,1,0:T(8,128)(2,1)S(1)}, u32[]{:S(2)}, u32[]{:S(2)}) collective-permute-start(bf16[16,8,96]{2,1,0:T(8,128)(2,1)S(1)} %get-tuple-element.60), channel_id=1, source_target_pairs={{0,16},{1,2},{2,1},{3,4},{4,3},{5,6},{6,5},{7,8},{8,7},{9,10},{10,... | collective-permute-start | bytes 73736 | tf_op jit(solution)/shard_map/ppermute | solution.py:52
  33.4 5.2 %collective-permute-start.8 = (bf16[6,8,96]{2,1,0:T(8,128)(2,1)S(1)}, bf16[6,8,96]{2,1,0:T(8,128)(2,1)S(1)}, u32[]{:S(2)}, u32[]{:S(2)}) collective-permute-start(bf16[6,8,96]{2,1,0:T(8,128)(2,1)S(1)} %get-tuple-element.62), channel_id=1, source_target_pairs={{0,17},{1,16},{2,19},{3,18},{4,21},{5,20},{6,23},{7,22},{8,25},{9,... | collective-permute-start | bytes 27656 | tf_op jit(solution)/shard_map/ppermute | solution.py:52
  35.1 3.7 %collective-permute-start.9 = (bf16[6,8,96]{2,1,0:T(8,128)(2,1)S(1)}, bf16[6,8,96]{2,1,0:T(8,128)(2,1)S(1)}, u32[]{:S(2)}, u32[]{:S(2)}) collective-permute-start(bf16[6,8,96]{2,1,0:T(8,128)(2,1)S(1)} %get-tuple-element.63), channel_id=1, source_target_pairs={{0,16},{1,18},{2,17},{3,20},{4,19},{5,22},{6,21},{7,24},{8,23},{9,... | collective-permute-start | bytes 27656 | tf_op jit(solution)/shard_map/ppermute | solution.py:52
  36.2 2.6 %copy-start.3 = (f32[2240,128]{1,0:T(8,128)S(1)}, f32[2240,128]{1,0:T(8,128)}, u32[]{:S(2)}) copy-start(f32[2240,128]{1,0:T(8,128)} %get-tuple-element.46.refs_6_) | copy-start | bytes 3440644
  36.2 2.6 %copy-start.7 = (bf16[2,96,384]{2,1,0:T(8,128)(2,1)S(1)}, bf16[2,96,384]{2,1,0:T(8,128)(2,1)}, u32[]{:S(2)}) copy-start(bf16[2,96,384]{2,1,0:T(8,128)(2,1)} %refs_4_.3) | copy-start | bytes 442372
  71.1 10.0 %all-to-all-start.1 = ((f32[32,4,128]{2,1,0:T(4,128)}), f32[32,4,128]{2,1,0:T(4,128)S(1)}, u32[]{:S(2)}, u32[]{:S(2)}) async-start(f32[32,4,128]{2,1,0:T(4,128)} %get-tuple-element.67), calls=%async_computation.1 | async-start | bytes 131072 | tf_op jit(solution)/shard_map/all_to_all | solution.py:712

commit v3 on v2

--- a/solution.py
+++ b/solution.py
@@ -154,20 +154,23 @@
             target[base + SIDE + cols : base + width, 0:channels] = read(vertical, "right", i)
 
 
-def spread_taps(kernel_ref, layer, target, flipped):
-    size, channels = (kernel_ref.shape[1], kernel_ref.shape[3])
+def spread_taps(kernel_ref, layer, target):
+    size, channels = (kernel_ref.shape[0], kernel_ref.shape[3])
     target[...] = jnp.zeros(target.shape, f32)
     for a in range(size):
         for b in range(size):
-            t = (size - 1 - a) * size + size - 1 - b if flipped else a * size + b
-            row = kernel_ref[layer, a, b : b + 1, :]
+            t = a * size + b
+            row = kernel_ref[a, b, layer : layer + 1, :]
             target[t * 8 : t * 8 + 8, 0:channels] = jnp.broadcast_to(row, (8, channels))
 
 
-def conv_group(src, base, stride, rows_out, taps, size):
+def conv_group(src, base, stride, rows_out, taps, size, flipped=False):
     total = [None] * rows_out
     for b in range(size):
-        weights = [taps[(a * size + b) * 8 : (a * size + b) * 8 + 8, :] for a in range(size)]
+        order = [a * size + b for a in range(size)]
+        if flipped:
+            order = [size * size - 1 - t for t in order]
+        weights = [taps[t * 8 : t * 8 + 8, :] for t in order]
         for i in range(rows_out + size - 1):
             x = src[pl.ds(base + i * stride + b, 8), :]
             for a in range(size):
@@ -250,24 +253,33 @@
     return jnp.concatenate([x, jnp.zeros((rows, LANES - channels), x.dtype)], axis=1)
 
 
-def load_weights(up_ref, down_ref, layer, up, down, up_t, down_t):
+def load_weights(up_ref, down_t_ref, layer, up, down, up_t, down_t):
     channels, units = up_ref.shape[1:]
-    up_f = jnp.concatenate([up_ref[layer].astype(f32), jnp.zeros((LANES - channels, units), f32)], axis=0)
-    down_f = pad_lanes(down_ref[layer].astype(f32))
-    if up is not None:
-        up[...] = up_f.astype(bf16)
-        down[...] = down_f.astype(bf16)
-    if up_t is not None:
-        up_t[...] = up_f.T.astype(bf16)
-        down_t[...] = down_f.T.astype(bf16)
+    blank = jnp.zeros((LANES - channels, units), f32)
+    up_f = jnp.concatenate([up_ref[layer].astype(f32), blank], axis=0)
+    down_f = jnp.concatenate([down_t_ref[layer].astype(f32), blank], axis=0)
+    up[layer] = up_f.astype(bf16)
+    down_t[layer] = down_f.astype(bf16)
+    up_t[layer] = up_f.T.astype(bf16)
+    down[layer] = down_f.T.astype(bf16)
 
 
 def round16(x):
     return x.astype(bf16).astype(f32)
 
 
-def strips_kernel(dims, image, cot, *outs):
+def fetch(sources, targets, sems):
+    copies = [pltpu.make_async_copy(a, b, sems.at[i]) for i, (a, b) in enumerate(zip(sources, targets))]
+    for copy in copies:
+        copy.start()
+    for copy in copies:
+        copy.wait()
+
+
+def strips_kernel(dims, image_in, cot_in, image, cot, *refs):
+    outs, sems = (refs[:-1], refs[-1])
     place = Place(dims.row_count, dims.col_count)
+    fetch((image_in, cot_in), (image, cot), sems)
 
     def take(ref):
         return lambda i, lo, hi: ref[i].astype(f32)[lo:hi]
@@ -279,29 +291,42 @@
     )
 
 
+def weights_kernel(up_in, down_t_in, kernels_in, gains_in, up, down, up_t, down_t, taps0, taps1, gains, *refs):
+    up_w, down_w, kernels, sems = refs
+    fetch((up_in, down_t_in, kernels_in, gains_in), (up_w, down_w, kernels, gains), sems)
+    spread_taps(kernels, 0, taps0)
+    spread_taps(kernels, 1, taps1)
+    for layer in range(2):
+        load_weights(up_w, down_w, layer, up, down, up_t, down_t)
+
+
 def first_kernel(dims, *refs):
     count = len(combos(dims.row_count))
-    image, cot, kernels, gains, up_w, down_w = refs[:6]
-    strips = refs[6 : 6 + count]
-    refs = refs[6 + count :]
+    image, cot, taps0, taps1, gains, up, down, up_t, down_t = refs[:9]
+    strips = refs[9 : 9 + count]
+    refs = refs[9 + count :]
     (output, x0, x1, unit0, inv0, hidden0, slope0, grad1, normed1, pre_grad1, hidden1, gain_sum) = refs[:12]
     outs = refs[12 : 12 + count]
-    conv, taps, up, down, up_t, down_t = refs[12 + count :]
+    (conv,) = refs[12 + count :]
     place = Place(dims.row_count, dims.col_count)
     rows, cols, channels, h, size = (dims.rows, dims.cols, dims.channels, dims.h, dims.size)
     ext_rows, ext_cols, wide = (dims.ext_rows, dims.ext_cols, dims.wide)
+    skip = dims.skipped_rows(place)
     read = received(place, strips, (0, 0))
     assemble(place, x0, lambda i: image[i].astype(f32), read, 2 * h, rows, cols, channels)
 
-    spread_taps(kernels, 0, taps, False)
-    load_weights(up_w, down_w, 0, up, down, None, None)
+    x1[...] = jnp.zeros(x1.shape, f32)
+    if dims.ext_pad > ext_rows * ext_cols:
+        conv[ext_rows * ext_cols :, :] = jnp.zeros((dims.ext_pad - ext_rows * ext_cols, LANES), f32)
+    frame = pl.multiple_of(skip * ext_cols, 8)
 
     def conv0(g, carry):
         at = pl.multiple_of(g * 8, 8)
-        total = conv_group(x0, at + 1, wide, ext_rows, taps, size)
+        base = pl.multiple_of(skip * wide, 8) + at
+        total = conv_group(x0, base + 1, wide, ext_rows, taps0, size)
         for r in range(ext_rows):
             conv[pl.ds(r * ext_cols + at, 8), :] = total[r]
-            x1[pl.ds(r * ext_cols + at, 8), :] = x0[pl.ds((r + h) * wide + at + 4, 8), :]
+            x1[pl.ds(frame + r * ext_cols + at, 8), :] = x0[pl.ds(base + (r + h) * wide + 4, 8), :]
         return carry
 
     lax.fori_loop(0, ext_cols // 8, conv0, 0)
@@ -310,26 +335,24 @@
 
     def mix0(k, carry):
         px = pl.ds(pl.multiple_of(k * step, 16), step)
+        px_frame = pl.ds(frame + pl.multiple_of(k * step, 16), step)
         unit, inverse = layer_norm(conv[px, :], channels)
         unit0[px, :] = unit.astype(bf16)
         inv0[px, :] = inverse
-        pre = dot((unit * gain).astype(bf16), up[...])
+        pre = dot((unit * gain).astype(bf16), up[0])
         value, slope = gelu_parts(pre)
         hidden = value.astype(bf16)
         hidden0[px, :] = hidden
         slope0[px, :] = slope.astype(bf16)
-        x1[px, :] = round16(x1[px, :] + dot(hidden, down[...]))
+        x1[px_frame, :] = round16(x1[px_frame, :] + dot(hidden, down[0]))
         return carry
 
-    lax.fori_loop(0, ext_rows * ext_cols // step, mix0, 0)
+    lax.fori_loop(0, dims.ext_pad // step, mix0, 0)
     clear_outside(place, x1, dims)
-
-    spread_taps(kernels, 1, taps, False)
-    load_weights(up_w, down_w, 1, up, down, up_t, down_t)
 
     def conv1(g, carry):
         at = pl.multiple_of(g * 8, 8)
-        total = conv_group(x1, at + 1, ext_cols, rows, taps, size)
+        total = conv_group(x1, at + 1, ext_cols, rows, taps1, size)
         for r in range(rows):
             conv[pl.ds(r * cols + at, 8), :] = total[r]
         return carry
@@ -345,18 +368,18 @@
         unit, inverse = layer_norm(conv[px, :], channels)
         normed = (unit * gain1).astype(bf16)
         normed1[px, :] = normed
-        value, slope = gelu_parts(dot(normed, up[...]))
+        value, slope = gelu_parts(dot(normed, up[1]))
         hidden = value.astype(bf16)
         hidden1[px, :] = hidden
-        branch = dot(hidden, down[...])
+        branch = dot(hidden, down[1])
         for i in range(lines):
             start = (k * lines + i + h) * ext_cols + 4
             line = x1[pl.ds(start, cols), :] + branch[i * cols : (i + 1) * cols]
             output[k * lines + i] = line[:, :channels].astype(bf16)
         upstream = pad_lanes(cot[pl.ds(k * lines, lines)].reshape(step1, channels))
-        pre_grad = (dot(upstream, down_t[...]) * slope).astype(bf16)
+        pre_grad = (dot(upstream, down_t[1]) * slope).astype(bf16)
         pre_grad1[px, :] = pre_grad
-        normed_grad = dot(pre_grad, up_t[...])
+        normed_grad = dot(pre_grad, up_t[1])
         product = normed_grad * unit
         gain_sum[...] += jnp.sum(product.reshape(step1 // 8, 8, LANES), axis=0)
         grad1[px, :] = round16(norm_backward(normed_grad, unit, inverse, gain1, channels))
@@ -371,7 +394,7 @@
 
 
 def clear_outside(place, flat, dims):
-    h, ext_rows, ext_cols = (dims.h, dims.ext_rows, dims.ext_cols)
+    h, frame_rows, ext_cols = (dims.h, dims.rows + 2 * dims.h, dims.ext_cols)
     margin = (ext_cols - dims.cols) // 2
 
     @pl.when(jnp.logical_not(place.has["above"]))
@@ -380,16 +403,17 @@
 
     @pl.when(jnp.logical_not(place.has["below"]))
     def _():
-        flat[(ext_rows - h) * ext_cols :, :] = jnp.zeros((h * ext_cols, LANES), f32)
+        last = (frame_rows - h) * ext_cols
+        flat[last:, :] = jnp.zeros((flat.shape[0] - last, LANES), f32)
 
     @pl.when(jnp.logical_not(place.has["left"]))
     def _():
-        for r in range(ext_rows):
+        for r in range(frame_rows):
             flat[r * ext_cols : r * ext_cols + margin, :] = jnp.zeros((margin, LANES), f32)
 
     @pl.when(jnp.logical_not(place.has["right"]))
     def _():
-        for r in range(ext_rows):
+        for r in range(frame_rows):
             flat[(r + 1) * ext_cols - margin : (r + 1) * ext_cols, :] = jnp.zeros((margin, LANES), f32)
 
 
@@ -411,48 +435,54 @@
 
 def third_kernel(dims, *refs):
     count = len(combos(dims.row_count))
-    (grad1, cot, kernels, gains, up_w, down_w, x0, unit0, inv0, hidden0, slope0) = refs[:11]
+    (grad1, cot, taps1, gains, up_t, down_t, x0, unit0, inv0, hidden0, slope0) = refs[:11]
     (taps_sum1, up_sum1, down_sum1) = refs[11:14]
     strips = refs[14 : 14 + count]
     cot_strips = refs[14 + count : 14 + 2 * count]
-    (grad0, middle, packed) = refs[14 + 2 * count : 17 + 2 * count]
-    (wide_grad, upstream, own, taps, up_t, down_t, sums, up_acc, down_acc, gain_sum, small, table) = refs[17 + 2 * count :]
+    (grad0, middle, keep, small_keep, send) = refs[14 + 2 * count : 19 + 2 * count]
+    (wide_grad, cot_frame, upstream, own, sums, up_acc, down_acc, gain_sum, small, tall, slabs) = refs[19 + 2 * count :]
     place = Place(dims.row_count, dims.col_count)
     rows, cols, channels, h, size = (dims.rows, dims.cols, dims.channels, dims.h, dims.size)
     ext_rows, ext_cols, wide = (dims.ext_rows, dims.ext_cols, dims.wide)
+    skip = dims.skipped_rows(place)
     read = received(place, strips, (0, 0))
     assemble(
         place, wide_grad, lambda i: grad1[i * cols : (i + 1) * cols, 0:channels], read, 2 * h, rows, cols, channels
     )
     read_cot = received(place, cot_strips, (rows, 2 * h))
     margin = (ext_cols - cols) // 2
-    upstream[...] = jnp.zeros(upstream.shape, f32)
+    cot_frame[...] = jnp.zeros(cot_frame.shape, f32)
     for vertical, start, n in (("above", 0, h), (None, h, rows), ("below", h + rows, h)):
         for i in range(n):
             base = (start + i) * ext_cols
             line = cot[i].astype(f32) if vertical is None else read_cot(vertical, None, i)
-            upstream[base + margin : base + margin + cols, 0:channels] = line
-            upstream[base : base + margin, 0:channels] = read_cot(vertical, "left", i)[SIDE - margin :]
-            upstream[base + margin + cols : base + ext_cols, 0:channels] = read_cot(vertical, "right", i)[:margin]
-
-    spread_taps(kernels, 1, taps, True)
-    load_weights(up_w, down_w, 0, None, None, up_t, down_t)
+            cot_frame[base + margin : base + margin + cols, 0:channels] = line
+            cot_frame[base : base + margin, 0:channels] = read_cot(vertical, "left", i)[SIDE - margin :]
+            cot_frame[base + margin + cols : base + ext_cols, 0:channels] = read_cot(vertical, "right", i)[:margin]
+
+    used = ext_rows * ext_cols
+    if dims.ext_pad > used:
+        upstream[used:, :] = jnp.zeros((dims.ext_pad - used, LANES), f32)
+        own[used:, :] = jnp.zeros((dims.ext_pad - used, LANES), f32)
+    grad0[...] = jnp.zeros(grad0.shape, f32)
+    frame = pl.multiple_of(skip * ext_cols, 8)
 
     def conv1(g, carry):
         at = pl.multiple_of(g * 8, 8)
-        total = conv_group(wide_grad, at + 1, wide, ext_rows, taps, size)
+        total = conv_group(wide_grad, pl.multiple_of(skip * wide, 8) + at + 1, wide, ext_rows, taps1, size, True)
         col = lax.broadcasted_iota(jnp.int32, (8, LANES), 0) + (at - margin)
         inside = jnp.where(jnp.logical_and(col >= 0, col < cols), 1.0, 0.0)
         for r in range(ext_rows):
             px = pl.ds(r * ext_cols + at, 8)
-            upstream[px, :] = upstream[px, :] + total[r]
-            own[px, :] = inside if h <= r < h + rows else jnp.zeros((8, LANES), f32)
+            upstream[px, :] = cot_frame[pl.ds(frame + r * ext_cols + at, 8), :] + total[r]
+            mine = jnp.logical_and(r + skip >= h, r + skip < h + rows)
+            own[px, :] = jnp.where(mine, inside, 0.0)
         return carry
 
     lax.fori_loop(0, ext_cols // 8, conv1, 0)
     for i in range(rows):
-        base = (i + h) * ext_cols + margin
-        middle[i * cols : (i + 1) * cols, :] = round16(upstream[base : base + cols, :])
+        line = upstream[pl.ds((i + h - skip) * ext_cols + margin, cols), :]
+        middle[i * cols : (i + 1) * cols, :] = round16(line)
 
     gain = pad_lanes(gains[0:1, :])
     gain_sum[...] = jnp.zeros(gain_sum.shape, f32)
@@ -464,70 +494,104 @@
         px = pl.ds(pl.multiple_of(k * step, 16), step)
         flow = upstream[px, :].astype(bf16)
         mine = own[px, :]
-        mine16 = mine.astype(bf16)
         unit = unit0[px, :].astype(f32)
-        pre_grad = (dot(flow, down_t[...]) * slope0[px, :].astype(f32)).astype(bf16)
-        normed_grad = dot(pre_grad, up_t[...])
+        pre_grad = (dot(flow, down_t[0]) * slope0[px, :].astype(f32)).astype(bf16)
+        normed_grad = dot(pre_grad, up_t[0])
         normed = (unit * gain * mine).astype(bf16)
         up_acc[...] += dot_leading(normed, pre_grad)
-        down_acc[...] += dot_leading(flow * mine16, hidden0[px, :])
+        down_acc[...] += dot_leading(flow * mine.astype(bf16), hidden0[px, :])
         product = normed_grad * unit * mine
         gain_sum[...] += jnp.sum(product.reshape(step // 8, 8, LANES), axis=0)
-        grad0[px, :] = round16(norm_backward(normed_grad, unit, inv0[px, :], gain, channels))
+        px_frame = pl.ds(frame + pl.multiple_of(k * step, 16), step)
+        grad0[px_frame, :] = round16(norm_backward(normed_grad, unit, inv0[px, :], gain, channels))
         return carry
 
-    lax.fori_loop(0, ext_rows * ext_cols // step, mix0, 0)
+    lax.fori_loop(0, dims.ext_pad // step, mix0, 0)
     clear_outside(place, grad0, dims)
     kernel_sums(
         x0, h * wide + SIDE - h, wide, grad0, h * ext_cols + margin, ext_cols, rows, cols, size, sums
     )
     store_sums(dims, sums, gain_sum[...], small)
 
-    layer_rows, part, half, share = (dims.layer_rows, dims.part, dims.half, dims.share)
+    taps_rows = size * size + 1
+    merged = jnp.concatenate([small[0:taps_rows, :], taps_sum1[0:taps_rows, :]], axis=0) * dims.factor
+    merged = jnp.concatenate([merged, jnp.zeros((dims.small_rows - 2 * taps_rows, LANES), f32)], axis=0)
+    merged = merged.astype(bf16)
+    small_keep[...] = merged.astype(f32)
+
+    layer_rows, part, half = (dims.layer_rows, dims.part, dims.half)
     units = up_acc.shape[1]
-    table[...] = jnp.zeros(table.shape, f32)
-    taps_rows = size * size + 1
-    for layer, source in ((0, small), (1, taps_sum1)):
-        for t in range(taps_rows):
-            place_at = layer * taps_rows + t
-            line = (place_at // share) * 8 + place_at % share
-            table[line : line + 1, :] = source[t : t + 1, :] * dims.factor
     up0 = up_acc[...].T * dims.factor
     down0 = down_acc[...].T * dims.factor
+    up1 = up_sum1[...] * dims.factor
+    down1 = down_sum1[...] * dims.factor
     lane = lax.broadcasted_iota(jnp.int32, (units, LANES), 1)
-    tall = wide_grad
+    slab_rows = 2 * layer_rows
     for r in range(dims.row_count):
-        for layer, (u, d) in enumerate(((up0, down0), (up_sum1[...] * dims.factor, down_sum1[...] * dims.factor))):
-            first = pltpu.roll(u, (LANES - r * half) % LANES, 1) if r else u
+        for layer, (u, d) in enumerate(((up0, down0), (up1, down1))):
+            first = pltpu.roll(u, LANES - r * half, 1) if r else u
             shift = (half - r * half) % LANES
             second = pltpu.roll(d, shift, 1) if shift else d
             joined = jnp.where(lane < half, first, jnp.where(lane < 2 * half, second, 0.0))
             tall[layer * (units + 8) : layer * (units + 8) + units, :] = joined
 
         def slab(c, carry, r=r):
-            dev = r * dims.col_count + c
-            rows_of = [tall[pl.ds(layer * (units + 8) + c * part, layer_rows), :] for layer in range(2)]
-            whole = jnp.concatenate(rows_of, axis=0)
-            extra = table[pl.ds(pl.multiple_of(dev * 8, 8), 8), :]
-            quarter = lax.broadcasted_iota(jnp.int32, (8, LANES), 1)
-            pieces = [jnp.where(quarter >= 96, pltpu.roll(extra, s, 1), 0.0) for s in (96, 64, 32)]
-            pieces.append(jnp.zeros((whole.shape[0] - 24, LANES), f32))
-            whole = jnp.where(
-                lax.broadcasted_iota(jnp.int32, whole.shape, 1) >= 96, jnp.concatenate(pieces, axis=0), whole
-            )
-            packed[dev] = whole.astype(bf16)
+            index = 0
+            for j, (axis, bit) in enumerate(dims.stages):
+                value = (r >> bit) & 1 if axis == "row" else lax.rem(lax.div(c, 1 << bit), 2)
+                index = index + value * (1 << (len(dims.stages) - 1 - j))
+            for layer in range(2):
+                to = pl.multiple_of(index * slab_rows + layer * layer_rows, 8)
+                slabs[pl.ds(to, layer_rows), :] = tall[pl.ds(layer * (units + 8) + c * part, layer_rows), :]
             return carry
 
         lax.fori_loop(0, dims.col_count, slab, 0)
 
-
-def image_kernel(dims, grad0, middle, kernels, out, taps, work):
+    split(dims, place, 0, slabs, merged, keep, send)
+
+
+def split(dims, place, stage, slabs, merged, keep, send):
+    count = slabs.shape[0] // 2
+    axis, bit = dims.stages[stage]
+    mine = lax.rem(lax.div(lax.axis_index(axis), 1 << bit), 2)
+    keep[...] = slabs[pl.ds(pl.multiple_of(mine * count, 16), count), :]
+    send[0:count, :] = slabs[pl.ds(pl.multiple_of((1 - mine) * count, 16), count), :].astype(bf16)
+    send[count:, :] = merged
+
+
+def stage_kernel(dims, stage, keep, small, got, keep_out, small_out, send, total):
+    place = Place(dims.row_count, dims.col_count)
+    count = keep.shape[0]
+    total[...] = keep[...] + got[0:count, :].astype(f32)
+    merged = (small[...] + got[count:, :].astype(f32)).astype(bf16)
+    small_out[...] = merged.astype(f32)
+    split(dims, place, stage, total, merged, keep_out, send)
+
+
+def last_kernel(dims, keep, small, got, kernel_out, gain_out, up_out, down_out):
+    count = keep.shape[0]
+    total = keep[...] + got[0:count, :].astype(f32)
+    merged = small[...] + got[count:, :].astype(f32)
+    size, channels, half, part = (dims.size, dims.channels, dims.half, dims.part)
+    for layer in range(2):
+        block = total[layer * dims.layer_rows : layer * dims.layer_rows + part]
+        up_out[layer] = block[:, :half]
+        down_out[layer] = block[:, half : 2 * half]
+        for t in range(size * size + 1):
+            at = layer * (size * size + 1) + t
+            row = merged[at : at + 1, 0:channels]
+            if t < size * size:
+                kernel_out[t // size, t % size, layer : layer + 1, :] = row
+            else:
+                gain_out[layer : layer + 1, :] = row
+
+
+def image_kernel(dims, grad0, middle, taps0, out, work):
     rows, cols, size = (dims.rows, dims.cols, dims.size)
-    spread_taps(kernels, 0, taps, True)
 
     def conv0(g, carry):
         at = pl.multiple_of(g * 8, 8)
-        total = conv_group(grad0, at + 1, dims.ext_cols, rows, taps, size)
+        total = conv_group(grad0, at + 1, dims.ext_cols, rows, taps0, size, True)
         for r in range(rows):
             work[pl.ds(r * cols + at, 8), :] = middle[pl.ds(r * cols + at, 8), :] + total[r]
         return carry
@@ -537,37 +601,11 @@
         out[r] = work[r * cols : (r + 1) * cols, 0 : dims.channels].astype(bf16)
 
 
-def owner_kernel(dims, got, up_out, down_out, copies):
-    total = got[0].astype(f32)
-    for d in range(1, got.shape[0]):
-        total = total + got[d].astype(f32)
-    half, part = (dims.half, dims.part)
-    for layer in range(2):
-        block = total[layer * dims.layer_rows : (layer + 1) * dims.layer_rows]
-        up_out[layer] = block.T[:half, :part]
-        down_out[layer] = block[:part, half : 2 * half]
-    lane = lax.broadcasted_iota(jnp.int32, (8, LANES), 1)
-    line = jnp.where(lane < 32, pltpu.roll(total[0:8], 32, 1), 0.0)
-    line = jnp.where(jnp.logical_and(lane >= 32, lane < 64), pltpu.roll(total[8:16], 64, 1), line)
-    line = jnp.where(jnp.logical_and(lane >= 64, lane < 96), pltpu.roll(total[16:24], 96, 1), line)
-    for d in range(copies.shape[0]):
-        copies[d] = line[: dims.share]
-
-
-def unpack_kernel(dims, every, kernel_out, gain_out):
-    size, channels = (dims.size, dims.channels)
-    for layer in range(2):
-        for t in range(size * size + 1):
-            at = layer * (size * size + 1) + t
-            row = every[at // dims.share, at % dims.share : at % dims.share + 1, 0:channels]
-            if t < size * size:
-                kernel_out[layer, t // size, t % size : t % size + 1, :] = row
-            else:
-                gain_out[layer : layer + 1, :] = row
-
-
 class Dims:
-    pass
+    def skipped_rows(self, place):
+        if self.row_count > 2:
+            return 0
+        return jnp.where(place.has["above"], 0, self.h)
 
 
 def dims_of(image, kernels, up_weights):
@@ -576,30 +614,47 @@
     d.rows, d.cols, d.channels = image.shape
     d.size = kernels.shape[1]
     d.h = d.size // 2
-    d.ext_rows, d.ext_cols = (d.rows + 2 * d.h, d.cols + 8)
+    d.ext_rows, d.ext_cols = (d.rows + (d.h if d.row_count == 2 else 2 * d.h), d.cols + 8)
     d.wide = d.cols + 2 * SIDE
-    total = d.ext_rows * d.ext_cols
-    d.ext_step = max(s for s in range(16, 600, 16) if total % s == 0)
+    d.ext_pad = -(-d.ext_rows * d.ext_cols // 16) * 16
+    d.ext_step = max(s for s in range(16, 700, 16) if d.ext_pad % s == 0)
     d.line_step = 4
     d.half = d.channels // d.row_count
     d.part = up_weights.shape[2] // d.col_count
     d.layer_rows = ceil8(d.part)
     d.count = d.row_count * d.col_count
-    d.share = -(-2 * (d.size * d.size + 1) // d.count)
+    d.small_rows = -(-2 * (d.size * d.size + 1) // 16) * 16
     d.factor = 1.0 / math.sqrt(d.rows * d.cols * d.count)
+    row_bits, col_bits = (d.row_count.bit_length() - 1, d.col_count.bit_length() - 1)
+    d.stages = [("col", 0)] + [("row", b) for b in range(row_bits)] + [("col", b) for b in range(1, col_bits)]
     return d
 
 
-def run(kernel, outs, scratch, *args):
+def halving_pairs(d, stage):
+    axis, bit = d.stages[stage]
+    pairs = []
+    for r in range(d.row_count):
+        for c in range(d.col_count):
+            pr, pc = (r ^ (1 << bit), c) if axis == "row" else (r, c ^ (1 << bit))
+            pairs.append((r * d.col_count + c, pr * d.col_count + pc))
+    return pairs
+
+
+def run(kernel, outs, scratch, *args, in_hbm=0, sems=0, busy_us=1):
     shapes = [jax.ShapeDtypeStruct(shape, kind) for shape, kind in outs]
     space = pl.BlockSpec(memory_space=pltpu.VMEM)
+    far = pl.BlockSpec(memory_space=pltpu.HBM)
+    held = [pltpu.VMEM(shape, kind) for shape, kind in scratch]
+    if sems:
+        held.append(pltpu.SemaphoreType.DMA((sems,)))
     return pl.pallas_call(
         kernel,
         out_shape=shapes,
-        in_specs=[space] * len(args),
+        in_specs=[far] * in_hbm + [space] * (len(args) - in_hbm),
         out_specs=[space] * len(shapes),
-        scratch_shapes=[pltpu.VMEM(shape, kind) for shape, kind in scratch],
-        compiler_params=pltpu.CompilerParams(vmem_limit_bytes=48 * 1024 * 1024),
+        scratch_shapes=held,
+        compiler_params=pltpu.CompilerParams(vmem_limit_bytes=32 * 1024 * 1024),
+        cost_estimate=pl.CostEstimate(flops=int(busy_us * 1e9), bytes_accessed=1 << 18, transcendentals=0),
     )(*args)
 
 
@@ -608,13 +663,42 @@
     bind = functools.partial
     rows, cols, channels = image.shape
     units = up_weights.shape[2]
-    tile, ext, wide = (rows * cols, d.ext_rows * d.ext_cols, (rows + 4 * d.h) * d.wide)
+    tile, ext, wide = (rows * cols, d.ext_pad, (rows + 4 * d.h) * d.wide)
+    frame = (rows + 2 * d.h) * d.ext_cols + 16
     taps = ((d.size * d.size * 8, LANES), f32)
     sums_rows = ceil8(d.size * d.size + 1)
 
     shapes = strip_shapes(d.row_count, rows, cols, channels, (2 * d.h, d.h))
-    strips = run(bind(strips_kernel, d), [(s, bf16) for s in shapes], [], image, cotangent)
+    image, cot, *strips = run(
+        bind(strips_kernel, d),
+        [(image.shape, bf16), (image.shape, bf16)] + [(s, bf16) for s in shapes],
+        [],
+        image,
+        cotangent,
+        in_hbm=2,
+        sems=2,
+    )
     strips = exchange(strips, d.row_count, d.col_count)
+    up, down, up_t, down_t, taps0, taps1, gains = run(
+        weights_kernel,
+        [
+            ((2, LANES, units), bf16),
+            ((2, units, LANES), bf16),
+            ((2, units, LANES), bf16),
+            ((2, LANES, units), bf16),
+            taps,
+            taps,
+            (gains.shape, f32),
+        ],
+        [((2, channels, units), bf16), ((2, channels, units), bf16), ((d.size, d.size, 2, channels), f32)],
+        up_weights,
+        jnp.swapaxes(down_weights, 1, 2),
+        jnp.transpose(kernels, (1, 2, 0, 3)),
+        gains,
+        in_hbm=4,
+        sems=4,
+        busy_us=2,
+    )
 
     grad_shapes = strip_shapes(d.row_count, rows, cols, channels, (2 * d.h,))
     first = run(
@@ -622,7 +706,7 @@
         [
             (image.shape, bf16),
             ((wide, LANES), f32),
-            ((ext, LANES), f32),
+            ((frame, LANES), f32),
             ((ext, LANES), bf16),
             ((ext, LANES), f32),
             ((ext, units), bf16),
@@ -634,21 +718,18 @@
             ((8, LANES), f32),
         ]
         + [(s, bf16) for s in grad_shapes],
-        [
-            ((ext, LANES), f32),
-            taps,
-            ((LANES, units), bf16),
-            ((units, LANES), bf16),
-            ((units, LANES), bf16),
-            ((LANES, units), bf16),
-        ],
+        [((ext, LANES), f32)],
         image,
-        cotangent,
-        kernels,
+        cot,
+        taps0,
+        taps1,
         gains,
-        up_weights,
-        down_weights,
+        up,
+        down,
+        up_t,
+        down_t,
         *strips,
+        busy_us=15,
     )
     (output, x0, x1, unit0, inv0, hidden0, slope0, grad1, normed1, pre_grad1, hidden1, gain_part) = first[:12]
     grad_strips = exchange(first[12:], d.row_count, d.col_count)
@@ -662,33 +743,35 @@
         normed1,
         pre_grad1,
         hidden1,
-        cotangent,
+        cot,
         gain_part,
-    )
-
-    grad0, middle, packed = run(
+        busy_us=3,
+    )
+
+    held = d.count // 2 * 2 * d.layer_rows
+    small = ((d.small_rows, LANES), f32)
+    grad0, middle, keep, sums, send = run(
         bind(third_kernel, d),
-        [((ext, LANES), f32), ((tile, LANES), f32), ((d.count, 2 * d.layer_rows, LANES), bf16)],
+        [((frame, LANES), f32), ((tile, LANES), f32), ((held, LANES), f32), small, ((held + d.small_rows, LANES), bf16)],
         [
-            ((max(wide, 2 * (units + 16)), LANES), f32),
+            ((wide, LANES), f32),
+            ((frame, LANES), f32),
             ((ext, LANES), f32),
             ((ext, LANES), f32),
-            taps,
-            ((units, LANES), bf16),
-            ((LANES, units), bf16),
             taps,
             ((LANES, units), f32),
             ((LANES, units), f32),
             ((8, LANES), f32),
             ((sums_rows, LANES), f32),
-            ((d.count * 8, LANES), f32),
+            ((2 * (units + 8), LANES), f32),
+            ((2 * held, LANES), f32),
         ],
         grad1,
-        cotangent,
-        kernels,
+        cot,
+        taps1,
         gains,
-        up_weights,
-        down_weights,
+        up_t,
+        down_t,
         x0,
         unit0,
         inv0,
@@ -699,19 +782,39 @@
         down_sum1,
         *grad_strips,
         *strips,
+        busy_us=12,
+    )
+    (gradient,) = run(
+        bind(image_kernel, d), [(image.shape, bf16)], [((tile, LANES), f32)], grad0, middle, taps0, busy_us=3
     )
     axes = ("row", "col")
-    got = lax.all_to_all(packed, axes, 0, 0, tiled=True)
-    (gradient,) = run(bind(image_kernel, d), [(image.shape, bf16)], [taps, ((tile, LANES), f32)], grad0, middle, kernels)
-    up_out, down_out, copies = run(
-        bind(owner_kernel, d),
-        [((2, d.half, d.part), f32), ((2, d.part, d.half), f32), ((d.count, d.share, LANES), f32)],
+    for stage in range(len(d.stages)):
+        got = lax.ppermute(send, axes, halving_pairs(d, stage))
+        if stage + 1 < len(d.stages):
+            held //= 2
+            keep, sums, send = run(
+                bind(stage_kernel, d, stage + 1),
+                [((held, LANES), f32), small, ((held + d.small_rows, LANES), bf16)],
+                [((2 * held, LANES), f32)],
+                keep,
+                sums,
+                got,
+            )
+    kernel_out, gain_out, up_out, down_out = run(
+        bind(last_kernel, d),
+        [
+            ((d.size, d.size, 2, channels), f32),
+            (gains.shape, f32),
+            ((2, d.part, d.half), f32),
+            ((2, d.part, d.half), f32),
+        ],
         [],
+        keep,
+        sums,
         got,
     )
-    every = lax.all_to_all(copies, axes, 0, 0, tiled=True)
-    kernel_out, gain_out = run(bind(unpack_kernel, d), [(kernels.shape, f32), (gains.shape, f32)], [], every)
-    return (output, gradient, kernel_out, gain_out, up_out, down_out)
+    kernel_out = jnp.transpose(kernel_out, (2, 0, 1, 3))
+    return (output, gradient, kernel_out, gain_out, jnp.swapaxes(up_out, 1, 2), down_out)
 
 
 def solution(mesh):

time: 82.7 us -> 67.5 us (0.82)
  blocking collectives: 18.5 us -> 0 us
  waiting for transfers between devices: 4.07 us -> 20.5 us
  Pallas kernels: 36.4 us -> 29.7 us
  local copies, waits for them, and re-layouts: 8.59 us -> 1.91 us
    all_to_all x1 -> x0, blocking collectives: 18.5 us -> none  [per_device(): got = lax.all_to_all(packed, axes, 0, 0, tiled=True)]
    ppermute x0 -> x5, waiting for transfers between devices: none -> 13.2 us  [per_device(): got = lax.ppermute(send, axes, halving_pairs(d, stage))]
    ppermute x10, waiting for transfers between devices: 0.52 us -> 7.27 us  [exchange(): lax.ppermute(strip, ('row', 'col'), swap_pairs(row_count, col_count, rs,...]
    unnamed x22 -> x12, local copies, waits for them, and re-layouts: 8.59 us -> 1.91 us
    pallas_call x7 -> x11, Pallas kernels: 36.4 us -> 29.7 us  [run(): pl.pallas_call(kernel, out_shape=shapes, in_specs=[far] * in_hbm + [space...]
    ppermute x0 -> x5, starting transfers between devices: none -> 4.57 us  [per_device(): got = lax.ppermute(send, axes, halving_pairs(d, stage))]
    all_to_all x1 -> x0, waiting for transfers between devices: 3.55 us -> none  [per_device(): every = lax.all_to_all(copies, axes, 0, 0, tiled=True)]
    all_to_all x1 -> x0, starting transfers between devices: 2.55 us -> none  [per_device(): every = lax.all_to_all(copies, axes, 0, 0, tiled=True)]
  transfers between devices with their start and end apart: 11 -> 15, of which waited for: 3 -> 7; matrix products, arithmetic and copies ran while one was open for 3% -> 0% of each run, Pallas kernels for 7% -> 9%
where the time goes in v3:
time: 67.5 us; the launch traced here: 67.3 us
  Pallas kernels  29.7 us (44%)
  waiting for transfers between devices  20.5 us (30%)
  starting transfers between devices  14.5 us (21%)
  local copies, waits for them, and re-layouts  1.91 us (3%)
  between operations  0.77 us (1%)
    pallas_call x11, Pallas kernels, run(): pl.pallas_call(kernel, out_shape=shapes, in_specs=[far] * in_hbm + [space...  29.7 us
    ppermute x5, waiting for transfers between devices, per_device(): got = lax.ppermute(send, axes, halving_pairs(d, stage))  13.2 us
    ppermute x10, starting transfers between devices, exchange(): lax.ppermute(strip, ('row', 'col'), swap_pairs(row_count, col_count, rs,...  9.93 us
    ppermute x10, waiting for transfers between devices, exchange(): lax.ppermute(strip, ('row', 'col'), swap_pairs(row_count, col_count, rs,...  7.27 us
    ppermute x5, starting transfers between devices, per_device(): got = lax.ppermute(send, axes, halving_pairs(d, stage))  4.57 us
    unnamed x12, local copies, waits for them, and re-layouts  1.91 us
  transfers between devices with their start and end apart: 15, of which 7 were waited for; matrix products, arithmetic and copies ran while one was open for 0% of the time, Pallas kernels for 9%

profile of v3, /device:TPU:0, one launch (start us, length us, event | category | flops | bytes accessed | tf_op | source)
XLA Modules:
  0.0 67.3 jit_solution(5625099710687884428)
XLA Ops:
  0.6 0.9 %copy-done = bf16[16,64,96]{2,1,0:T(8,128)(2,1)S(1)} copy-done((bf16[16,64,96]{2,1,0:T(8,128)(2,1)S(1)}, bf16[16,64,96]{2,1,0:T(8,128)(2,1)}, u32[]{:S(2)}) %copy-start) | copy-done | bytes 196632
  1.6 0.9 %copy-done.1 = bf16[16,64,96]{2,1,0:T(8,128)(2,1)S(1)} copy-done((bf16[16,64,96]{2,1,0:T(8,128)(2,1)S(1)}, bf16[16,64,96]{2,1,0:T(8,128)(2,1)}, u32[]{:S(2)}) %copy-start.1) | copy-done | bytes 196632
  2.7 2.4 %collective-permute-start.3 = (bf16[9,8,96]{2,1,0:T(8,128)(2,1)S(1)}, bf16[9,8,96]{2,1,0:T(8,128)(2,1)S(1)}, u32[]{:S(2)}, u32[]{:S(2)}) collective-permute-start(bf16[9,8,96]{2,1,0:T(8,128)(2,1)S(1)} %get-tuple-element.73), channel_id=1, source_target_pairs={{0,17},{1,16},{2,19},{3,18},{4,21},{5,20},{6,23},{7,22},{8,25},{9,... | collective-permute-start | bytes 41480 | tf_op jit(solution)/shard_map/ppermute | solution.py:52
  5.2 0.6 collective-permute-start.4
  5.8 1.1 %collective-permute-start = (bf16[32,8,96]{2,1,0:T(8,128)(2,1)S(1)}, bf16[32,8,96]{2,1,0:T(8,128)(2,1)S(1)}, u32[]{:S(2)}, u32[]{:S(2)}) collective-permute-start(bf16[32,8,96]{2,1,0:T(8,128)(2,1)S(1)} %get-tuple-element.70), channel_id=1, source_target_pairs={{0,1},{1,0},{2,3},{3,2},{4,5},{5,4},{6,7},{7,6},{8,9},{9,8},{10,11... | collective-permute-start | bytes 147464 | tf_op jit(solution)/shard_map/ppermute | solution.py:52
  6.9 1.4 %collective-permute-start.1 = (bf16[32,8,96]{2,1,0:T(8,128)(2,1)S(1)}, bf16[32,8,96]{2,1,0:T(8,128)(2,1)S(1)}, u32[]{:S(2)}, u32[]{:S(2)}) collective-permute-start(bf16[32,8,96]{2,1,0:T(8,128)(2,1)S(1)} %get-tuple-element.71), channel_id=1, source_target_pairs={{0,16},{1,2},{2,1},{3,4},{4,3},{5,6},{6,5},{7,8},{8,7},{9,10},{10,... | collective-permute-start | bytes 147464 | tf_op jit(solution)/shard_map/ppermute | solution.py:52
  8.3 0.6 collective-permute-start.2
  8.9 0.7 %shard_map.110 = (bf16[2,128,384]{2,1,0:T(8,128)(2,1)S(1)}, bf16[2,384,128]{2,1,0:T(8,128)(2,1)S(1)}, bf16[2,384,128]{2,1,0:T(8,128)(2,1)S(1)}, bf16[2,128,384]{...) custom-call(bf16[2,96,384]{2,1,0:T(8,128)(2,1)S(1)} %copy-done.2, ...), custom_call_target="tpu_custom_call" | custom-call | flops 2000000000 | bytes 262144 | tf_op jit(solution)/shard_map/pallas_call | solution.py:650
  9.7 1.9 %collective-permute-done.1.refs_10_.refs_20_ = bf16[32,8,96]{2,1,0:T(8,128)(2,1)S(1)} collective-permute-done((bf16[32,8,96]{2,1,0:T(8,128)(2,1)S(1)}, bf16[32,8,96]{2,1,0:T(8,128)(2,1)S(1)}, u32[]{:S(2)}, u32[]{:S(2)}) %collective-permute-start.1) | collective-permute-done | bytes 49184 | tf_op jit(solution)/shard_map/ppermute | solution.py:52
  11.6 2.9 %collective-permute-done.2.refs_11_.refs_21_ = bf16[9,64,96]{2,1,0:T(8,128)(2,1)S(1)} collective-permute-done((bf16[9,64,96]{2,1,0:T(8,128)(2,1)S(1)}, bf16[9,64,96]{2,1,0:T(8,128)(2,1)S(1)}, u32[]{:S(2)}, u32[]{:S(2)}) %collective-permute-start.2) | collective-permute-done | bytes 110624 | tf_op jit(solution)/shard_map/ppermute | solution.py:52
  14.5 14.0 %shard_map.111 = (bf16[16,64,96]{2,1,0:T(8,128)(2,1)}, f32[2240,128]{1,0:T(8,128)S(1)}, f32[1600,128]{1,0:T(8,128)S(1)}, bf16[1376,128]{1,0:T(8,128)(2,1)S(1)}, ...) custom-call(bf16[16,64,96]{2,1,0:T(8,128)(2,1)S(1)} %get-tuple-eleme, ...), custom_call_target="tpu_custom_call" | custom-call | flops 15000000512 | bytes 262144 | tf_op jit(solution)/shard_map/pallas_call | solution.py:650
  28.5 0.9 %collective-permute-start.8 = (bf16[6,8,96]{2,1,0:T(8,128)(2,1)S(1)}, bf16[6,8,96]{2,1,0:T(8,128)(2,1)S(1)}, u32[]{:S(2)}, u32[]{:S(2)}) collective-permute-start(bf16[6,8,96]{2,1,0:T(8,128)(2,1)S(1)} %get-tuple-element.93), channel_id=1, source_target_pairs={{0,17},{1,16},{2,19},{3,18},{4,21},{5,20},{6,23},{7,22},{8,25},{9,... | collective-permute-start | bytes 27656 | tf_op jit(solution)/shard_map/ppermute | solution.py:52
  30.2 1.4 %collective-permute-start.6 = (bf16[16,8,96]{2,1,0:T(8,128)(2,1)S(1)}, bf16[16,8,96]{2,1,0:T(8,128)(2,1)S(1)}, u32[]{:S(2)}, u32[]{:S(2)}) collective-permute-start(bf16[16,8,96]{2,1,0:T(8,128)(2,1)S(1)} %get-tuple-element.91), channel_id=1, source_target_pairs={{0,16},{1,2},{2,1},{3,4},{4,3},{5,6},{6,5},{7,8},{8,7},{9,10},{10,... | collective-permute-start | bytes 73736 | tf_op jit(solution)/shard_map/ppermute | solution.py:52
  32.2 2.4 %shard_map.112 = (f32[56,128]{1,0:T(8,128)S(1)}, f32[384,128]{1,0:T(8,128)S(1)}, f32[384,128]{1,0:T(8,128)S(1)}) custom-call(f32[1600,128]{1,0:T(8,128)S(1)} %get-tuple-element.82.x1, f32[1024,128]{1,0:T(8,128)S(1)} %get-tuple-element.76.grad1.refs_0_, bf16[1024,128]{1,0:T(8,128)(2,1)S(1)} %get-tuple-element.83.normed1, ...), custom_call_target="tpu_custom_call" | custom-call | flops 3000000000 | bytes 262144 | tf_op jit(solution)/shard_map/pallas_call | solution.py:650
  34.7 2.4 %collective-permute-done.7.refs_16_ = bf16[6,64,96]{2,1,0:T(8,128)(2,1)S(1)} collective-permute-done((bf16[6,64,96]{2,1,0:T(8,128)(2,1)S(1)}, bf16[6,64,96]{2,1,0:T(8,128)(2,1)S(1)}, u32[]{:S(2)}, u32[]{:S(2)}) %collective-permute-start.7) | collective-permute-done | bytes 73760 | tf_op jit(solution)/shard_map/ppermute | solution.py:52
  37.1 8.5 %shard_map.113 = (f32[1600,128]{1,0:T(8,128)S(1)}, f32[1024,128]{1,0:T(8,128)S(1)}, f32[768,128]{1,0:T(8,128)S(1)}, f32[112,128]{1,0:T(8,128)S(1)}, bf16[880,128]{1,0:T(8,128)(2,1)S(1)}) custom-call(f32[1024,128]{1,0:T(8,128)S(1)} %get-tuple-element.76.grad1.refs_0_, bf16[16,64,96]{2,1,0:T(8,128)(2,1)S(1)} %get-tuple-element.62.refs_1_.cot, ...), custom_call_target="tpu_custom_call" | custom-call | flops 12000000000 | bytes 262144 | tf_op jit(solution)/shard_map/pallas_call | solution.py:650
  45.7 1.5 %collective-permute-done.10.got = bf16[880,128]{1,0:T(8,128)(2,1)S(1)} collective-permute-done((bf16[880,128]{1,0:T(8,128)(2,1)S(1)}, bf16[880,128]{1,0:T(8,128)(2,1)S(1)}, u32[]{:S(2)}, u32[]{:S(2)}) %collective-permute-start.10) | collective-permute-done | bytes 225312 | tf_op jit(solution)/shard_map/ppermute | solution.py:792
  47.5 5.3 %collective-permute-done.11.got = bf16[496,128]{1,0:T(8,128)(2,1)S(1)} collective-permute-done((bf16[496,128]{1,0:T(8,128)(2,1)S(1)}, bf16[496,128]{1,0:T(8,128)(2,1)S(1)}, u32[]{:S(2)}, u32[]{:S(2)}) %collective-permute-start.11) | collective-permute-done | bytes 127008 | tf_op jit(solution)/shard_map/ppermute | solution.py:792
  53.4 3.9 %collective-permute-done.12.got = bf16[304,128]{1,0:T(8,128)(2,1)S(1)} collective-permute-done((bf16[304,128]{1,0:T(8,128)(2,1)S(1)}, bf16[304,128]{1,0:T(8,128)(2,1)S(1)}, u32[]{:S(2)}, u32[]{:S(2)}) %collective-permute-start.12) | collective-permute-done | bytes 77856 | tf_op jit(solution)/shard_map/ppermute | solution.py:792
  57.3 1.6 %collective-permute-start.13 = (bf16[208,128]{1,0:T(8,128)(2,1)S(1)}, bf16[208,128]{1,0:T(8,128)(2,1)S(1)}, u32[]{:S(2)}, u32[]{:S(2)}) collective-permute-start(bf16[208,128]{1,0:T(8,128)(2,1)S(1)} %get-tuple-element.108), channel_id=1, source_target_pairs={{0,4},{1,5},{2,6},{3,7},{4,0},{5,1},{6,2},{7,3},{8,12},{9,13},{10,... | collective-permute-start | bytes 159752 | tf_op jit(solution)/shard_map/ppermute | solution.py:792
  59.0 2.6 %collective-permute-done.13.got = bf16[208,128]{1,0:T(8,128)(2,1)S(1)} collective-permute-done((bf16[208,128]{1,0:T(8,128)(2,1)S(1)}, bf16[208,128]{1,0:T(8,128)(2,1)S(1)}, u32[]{:S(2)}, u32[]{:S(2)}) %collective-permute-start.13) | collective-permute-done | bytes 53280 | tf_op jit(solution)/shard_map/ppermute | solution.py:792
  61.5 2.1 %collective-permute-start.14 = (bf16[160,128]{1,0:T(8,128)(2,1)S(1)}, bf16[160,128]{1,0:T(8,128)(2,1)S(1)}, u32[]{:S(2)}, u32[]{:S(2)}) collective-permute-start(bf16[160,128]{1,0:T(8,128)(2,1)S(1)} %get-tuple-element.111), channel_id=1, source_target_pairs={{0,8},{1,9},{2,10},{3,11},{4,12},{5,13},{6,14},{7,15},{8,0},{9,1},... | collective-permute-start | bytes 122888 | tf_op jit(solution)/shard_map/ppermute | solution.py:792
  63.6 3.1 %shard_map.114 = bf16[16,64,96]{2,1,0:T(8,128)(2,1)} custom-call(f32[1600,128]{1,0:T(8,128)S(1)} %get-tuple-element.95.grad0, f32[1024,128]{1,0:T(8,128)S(1)} %get-tuple-element.96.middle, f32[392,128]{1,0:T(8,128)S(1)} %get-tuple-element.63.refs_2_.taps0), custom_call_target="tpu_custom_call" | custom-call | flops 3000000000 | bytes 262144 | tf_op jit(solution)/shard_map/pallas_call | solution.py:650
  66.7 0.7 %shard_map.119 = (f32[7,7,2,96]{3,2,1,0:T(2,128)}, f32[2,96]{1,0:T(2,128)}, f32[2,24,48]{2,1,0:T(8,128)}, f32[2,24,48]{2,1,0:T(8,128)}) custom-call(f32[48,128]{1,0:T(8,128)S(1)} %get-tuple-element.109.keep, f32[112,128]{1,0:T(8,128)S(1)} %get-tuple-element.110.small, bf16[160,128]{1,0:T(8,128)(2,1)S(1)} %collective-permute-done.14.got), custom_call_target="tpu_custom_call" | custom-call | flops 1000000000 | bytes 262144 | tf_op jit(solution)/shard_map/pallas_call | solution.py:650
  (29 shorter events, 2.7 us)
Async XLA Ops:
  0.6 1.0 %copy-start = (bf16[16,64,96]{2,1,0:T(8,128)(2,1)S(1)}, bf16[16,64,96]{2,1,0:T(8,128)(2,1)}, u32[]{:S(2)}) copy-start(bf16[16,64,96]{2,1,0:T(8,128)(2,1)} %image_in.1) | copy-start | bytes 589828
  1.6 0.9 %copy-start.1 = (bf16[16,64,96]{2,1,0:T(8,128)(2,1)S(1)}, bf16[16,64,96]{2,1,0:T(8,128)(2,1)}, u32[]{:S(2)}) copy-start(bf16[16,64,96]{2,1,0:T(8,128)(2,1)} %cot_in.1) | copy-start | bytes 589828
  2.5 6.4 %copy-start.2 = (bf16[2,96,384]{2,1,0:T(8,128)(2,1)S(1)}, bf16[2,96,384]{2,1,0:T(8,128)(2,1)}, u32[]{:S(2)}) copy-start(bf16[2,96,384]{2,1,0:T(8,128)(2,1)} %up_in.1) | copy-start | bytes 442372
  2.5 6.4 %copy-start.3 = (bf16[2,384,96]{1,2,0:T(8,128)(2,1)S(1)}, bf16[2,384,96]{1,2,0:T(8,128)(2,1)}, u32[]{:S(2)}) copy-start(bf16[2,384,96]{1,2,0:T(8,128)(2,1)} %param.10) | copy-start | bytes 442372
  2.5 6.4 %copy-start.4 = (f32[2,7,7,96]{3,0,2,1:T(2,128)S(1)}, f32[2,7,7,96]{3,0,2,1:T(2,128)}, u32[]{:S(2)}) copy-start(f32[2,7,7,96]{3,0,2,1:T(2,128)} %param.7) | copy-start | bytes 112900
  2.5 6.4 %copy-start.5 = (f32[2,96]{1,0:T(2,128)S(1)}, f32[2,96]{1,0:T(2,128)}, u32[]{:S(2)}) copy-start(f32[2,96]{1,0:T(2,128)} %gains_in.1) | copy-start | bytes 2308
  2.7 6.9 %collective-permute-start.3 = (bf16[9,8,96]{2,1,0:T(8,128)(2,1)S(1)}, bf16[9,8,96]{2,1,0:T(8,128)(2,1)S(1)}, u32[]{:S(2)}, u32[]{:S(2)}) collective-permute-start(bf16[9,8,96]{2,1,0:T(8,128)(2,1)S(1)} %get-tuple-element.73), channel_id=1, source_target_pairs={{0,17},{1,16},{2,19},{3,18},{4,21},{5,20},{6,23},{7,22},{8,25},{9,... | collective-permute-start | bytes 41480 | tf_op jit(solution)/shard_map/ppermute | solution.py:52
  5.2 4.5 %collective-permute-start.4 = (bf16[9,8,96]{2,1,0:T(8,128)(2,1)S(1)}, bf16[9,8,96]{2,1,0:T(8,128)(2,1)S(1)}, u32[]{:S(2)}, u32[]{:S(2)}) collective-permute-start(bf16[9,8,96]{2,1,0:T(8,128)(2,1)S(1)} %get-tuple-element.74), channel_id=1, source_target_pairs={{0,16},{1,18},{2,17},{3,20},{4,19},{5,22},{6,21},{7,24},{8,23},{9,... | collective-permute-start | bytes 41480 | tf_op jit(solution)/shard_map/ppermute | solution.py:52
  5.8 3.9 %collective-permute-start = (bf16[32,8,96]{2,1,0:T(8,128)(2,1)S(1)}, bf16[32,8,96]{2,1,0:T(8,128)(2,1)S(1)}, u32[]{:S(2)}, u32[]{:S(2)}) collective-permute-start(bf16[32,8,96]{2,1,0:T(8,128)(2,1)S(1)} %get-tuple-element.70), channel_id=1, source_target_pairs={{0,1},{1,0},{2,3},{3,2},{4,5},{5,4},{6,7},{7,6},{8,9},{9,8},{10,11... | collective-permute-start | bytes 147464 | tf_op jit(solution)/shard_map/ppermute | solution.py:52
  6.9 4.7 %collective-permute-start.1 = (bf16[32,8,96]{2,1,0:T(8,128)(2,1)S(1)}, bf16[32,8,96]{2,1,0:T(8,128)(2,1)S(1)}, u32[]{:S(2)}, u32[]{:S(2)}) collective-permute-start(bf16[32,8,96]{2,1,0:T(8,128)(2,1)S(1)} %get-tuple-element.71), channel_id=1, source_target_pairs={{0,16},{1,2},{2,1},{3,4},{4,3},{5,6},{6,5},{7,8},{8,7},{9,10},{10,... | collective-permute-start | bytes 147464 | tf_op jit(solution)/shard_map/ppermute | solution.py:52
  8.3 6.2 %collective-permute-start.2 = (bf16[9,64,96]{2,1,0:T(8,128)(2,1)S(1)}, bf16[9,64,96]{2,1,0:T(8,128)(2,1)S(1)}, u32[]{:S(2)}, u32[]{:S(2)}) collective-permute-start(bf16[9,64,96]{2,1,0:T(8,128)(2,1)S(1)} %get-tuple-element.72), channel_id=1, source_target_pairs={{0,16},{1,17},{2,18},{3,19},{4,20},{5,21},{6,22},{7,23},{8,24},{9,... | collective-permute-start | bytes 331784 | tf_op jit(solution)/shard_map/ppermute | solution.py:52
  28.5 6.2 %collective-permute-start.8 = (bf16[6,8,96]{2,1,0:T(8,128)(2,1)S(1)}, bf16[6,8,96]{2,1,0:T(8,128)(2,1)S(1)}, u32[]{:S(2)}, u32[]{:S(2)}) collective-permute-start(bf16[6,8,96]{2,1,0:T(8,128)(2,1)S(1)} %get-tuple-element.93), channel_id=1, source_target_pairs={{0,17},{1,16},{2,19},{3,18},{4,21},{5,20},{6,23},{7,22},{8,25},{9,... | collective-permute-start | bytes 27656 | tf_op jit(solution)/shard_map/ppermute | solution.py:52
  29.3 5.3 %collective-permute-start.9 = (bf16[6,8,96]{2,1,0:T(8,128)(2,1)S(1)}, bf16[6,8,96]{2,1,0:T(8,128)(2,1)S(1)}, u32[]{:S(2)}, u32[]{:S(2)}) collective-permute-start(bf16[6,8,96]{2,1,0:T(8,128)(2,1)S(1)} %get-tuple-element.94), channel_id=1, source_target_pairs={{0,16},{1,18},{2,17},{3,20},{4,19},{5,22},{6,21},{7,24},{8,23},{9,... | collective-permute-start | bytes 27656 | tf_op jit(solution)/shard_map/ppermute | solution.py:52
  29.8 4.9 %collective-permute-start.5 = (bf16[16,8,96]{2,1,0:T(8,128)(2,1)S(1)}, bf16[16,8,96]{2,1,0:T(8,128)(2,1)S(1)}, u32[]{:S(2)}, u32[]{:S(2)}) collective-permute-start(bf16[16,8,96]{2,1,0:T(8,128)(2,1)S(1)} %get-tuple-element.90), channel_id=1, source_target_pairs={{0,1},{1,0},{2,3},{3,2},{4,5},{5,4},{6,7},{7,6},{8,9},{9,8},{10,11... | collective-permute-start | bytes 73736 | tf_op jit(solution)/shard_map/ppermute | solution.py:52
  30.2 4.5 %collective-permute-start.6 = (bf16[16,8,96]{2,1,0:T(8,128)(2,1)S(1)}, bf16[16,8,96]{2,1,0:T(8,128)(2,1)S(1)}, u32[]{:S(2)}, u32[]{:S(2)}) collective-permute-start(bf16[16,8,96]{2,1,0:T(8,128)(2,1)S(1)} %get-tuple-element.91), channel_id=1, source_target_pairs={{0,16},{1,2},{2,1},{3,4},{4,3},{5,6},{6,5},{7,8},{8,7},{9,10},{10,... | collective-permute-start | bytes 73736 | tf_op jit(solution)/shard_map/ppermute | solution.py:52
  31.6 5.5 %collective-permute-start.7 = (bf16[6,64,96]{2,1,0:T(8,128)(2,1)S(1)}, bf16[6,64,96]{2,1,0:T(8,128)(2,1)S(1)}, u32[]{:S(2)}, u32[]{:S(2)}) collective-permute-start(bf16[6,64,96]{2,1,0:T(8,128)(2,1)S(1)} %get-tuple-element.92), channel_id=1, source_target_pairs={{0,16},{1,17},{2,18},{3,19},{4,20},{5,21},{6,22},{7,23},{8,24},{9,... | collective-permute-start | bytes 221192 | tf_op jit(solution)/shard_map/ppermute | solution.py:52
  45.6 1.5 %collective-permute-start.10 = (bf16[880,128]{1,0:T(8,128)(2,1)S(1)}, bf16[880,128]{1,0:T(8,128)(2,1)S(1)}, u32[]{:S(2)}, u32[]{:S(2)}) collective-permute-start(bf16[880,128]{1,0:T(8,128)(2,1)S(1)} %get-tuple-element.99), channel_id=1, source_target_pairs={{0,1},{1,0},{2,3},{3,2},{4,5},{5,4},{6,7},{7,6},{8,9},{9,8},{10,11... | collective-permute-start | bytes 675848 | tf_op jit(solution)/shard_map/ppermute | solution.py:792
  47.3 5.5 %collective-permute-start.11 = (bf16[496,128]{1,0:T(8,128)(2,1)S(1)}, bf16[496,128]{1,0:T(8,128)(2,1)S(1)}, u32[]{:S(2)}, u32[]{:S(2)}) collective-permute-start(bf16[496,128]{1,0:T(8,128)(2,1)S(1)} %get-tuple-element.102), channel_id=1, source_target_pairs={{0,16},{1,17},{2,18},{3,19},{4,20},{5,21},{6,22},{7,23},{8,24},{9,... | collective-permute-start | bytes 380936 | tf_op jit(solution)/shard_map/ppermute | solution.py:792
  52.8 4.5 %collective-permute-start.12 = (bf16[304,128]{1,0:T(8,128)(2,1)S(1)}, bf16[304,128]{1,0:T(8,128)(2,1)S(1)}, u32[]{:S(2)}, u32[]{:S(2)}) collective-permute-start(bf16[304,128]{1,0:T(8,128)(2,1)S(1)} %get-tuple-element.105), channel_id=1, source_target_pairs={{0,2},{1,3},{2,0},{3,1},{4,6},{5,7},{6,4},{7,5},{8,10},{9,11},{10,... | collective-permute-start | bytes 233480 | tf_op jit(solution)/shard_map/ppermute | solution.py:792
  57.3 4.2 %collective-permute-start.13 = (bf16[208,128]{1,0:T(8,128)(2,1)S(1)}, bf16[208,128]{1,0:T(8,128)(2,1)S(1)}, u32[]{:S(2)}, u32[]{:S(2)}) collective-permute-start(bf16[208,128]{1,0:T(8,128)(2,1)S(1)} %get-tuple-element.108), channel_id=1, source_target_pairs={{0,4},{1,5},{2,6},{3,7},{4,0},{5,1},{6,2},{7,3},{8,12},{9,13},{10,... | collective-permute-start | bytes 159752 | tf_op jit(solution)/shard_map/ppermute | solution.py:792
  61.5 5.1 %collective-permute-start.14 = (bf16[160,128]{1,0:T(8,128)(2,1)S(1)}, bf16[160,128]{1,0:T(8,128)(2,1)S(1)}, u32[]{:S(2)}, u32[]{:S(2)}) collective-permute-start(bf16[160,128]{1,0:T(8,128)(2,1)S(1)} %get-tuple-element.111), channel_id=1, source_target_pairs={{0,8},{1,9},{2,10},{3,11},{4,12},{5,13},{6,14},{7,15},{8,0},{9,1},... | collective-permute-start | bytes 122888 | tf_op jit(solution)/shard_map/ppermute | solution.py:792

commit v4 on v3

--- a/solution.py
+++ b/solution.py
@@ -11,6 +11,7 @@
 epsilon = 1e-06
 inv_sqrt_two = 0.7071067811865476
 inv_sqrt_two_pi = 0.3989422804014327
+log2_e = 1.4426950408889634
 LANES = 128
 SIDE = 8
 f32, bf16 = (jnp.float32, jnp.bfloat16)
@@ -47,11 +48,12 @@
     return pairs
 
 
-def exchange(strips, row_count, col_count):
-    return [
-        lax.ppermute(strip, ("row", "col"), swap_pairs(row_count, col_count, rs, cs))
-        for strip, (rs, cs) in zip(strips, combos(row_count))
-    ]
+def exchange(bands, others, row_count, col_count):
+    got = {}
+    for strips, pairs in ((bands, band_combos(row_count)), (others, other_combos(row_count))):
+        for strip, (rs, cs) in zip(strips, pairs):
+            got[rs, cs] = lax.ppermute(strip, ("row", "col"), swap_pairs(row_count, col_count, rs, cs))
+    return [got[pair] for pair in combos(row_count)]
 
 
 class Place:
@@ -67,8 +69,16 @@
         self.row_count = row_count
 
 
-def write_strips(place, outs, takes):
-    for out, (rs, cs) in zip(outs, combos(place.row_count)):
+def band_combos(row_count):
+    return [pair for pair in combos(row_count) if pair[1] is None]
+
+
+def other_combos(row_count):
+    return [pair for pair in combos(row_count) if pair[1] is not None]
+
+
+def write_strips(place, outs, takes, pairs):
+    for out, (rs, cs) in zip(outs, pairs):
         at = 0
         for take, radius, rows, cols in takes:
             row_sets = [slice(0, rows)] * 2
@@ -99,9 +109,9 @@
             at += count
 
 
-def strip_shapes(row_count, rows, cols, channels, radii):
+def strip_shapes(pairs, rows, cols, channels, radii):
     shapes = []
-    for rs, cs in combos(row_count):
+    for rs, cs in pairs:
         height = sum(rows if rs is None else radius for radius in radii)
         shapes.append((height, cols if cs is None else SIDE, channels))
     return shapes
@@ -156,12 +166,18 @@
 
 def spread_taps(kernel_ref, layer, target):
     size, channels = (kernel_ref.shape[0], kernel_ref.shape[3])
-    target[...] = jnp.zeros(target.shape, f32)
     for a in range(size):
         for b in range(size):
             t = a * size + b
-            row = kernel_ref[a, b, layer : layer + 1, :]
-            target[t * 8 : t * 8 + 8, 0:channels] = jnp.broadcast_to(row, (8, channels))
+            row = pad_lanes(kernel_ref[a, b, layer : layer + 1, :])
+            target[t * 16 : t * 16 + 16, :] = jnp.broadcast_to(row, (16, LANES)).astype(bf16)
+
+
+def tree_sum(terms):
+    while len(terms) > 1:
+        pairs = [terms[i] + terms[i + 1] for i in range(0, len(terms) - 1, 2)]
+        terms = pairs + ([terms[-1]] if len(terms) % 2 else [])
+    return terms[0]
 
 
 def conv_group(src, base, stride, rows_out, taps, size, flipped=False):
@@ -170,38 +186,38 @@
         order = [a * size + b for a in range(size)]
         if flipped:
             order = [size * size - 1 - t for t in order]
-        weights = [taps[t * 8 : t * 8 + 8, :] for t in order]
+        weights = [taps[t * 16 : t * 16 + 16, :] for t in order]
+        window = []
         for i in range(rows_out + size - 1):
-            x = src[pl.ds(base + i * stride + b, 8), :]
-            for a in range(size):
-                r = i - a
-                if 0 <= r < rows_out:
-                    term = x * weights[a]
-                    total[r] = term if total[r] is None else total[r] + term
+            window.append(src[pl.ds(base + i * stride + b, 16), :].astype(bf16))
+            r = i - size + 1
+            if r >= 0:
+                term = tree_sum([window[r + a] * weights[a] for a in range(size)]).astype(f32)
+                total[r] = term if total[r] is None else total[r] + term
     return total
+
+
+def group_start(g, cols):
+    return pl.multiple_of(jnp.minimum(g * 16, cols - 16), 8)
 
 
 def kernel_sums(src, src_base, src_stride, grad, grad_base, grad_stride, rows, cols, size, sums):
     sums[...] = jnp.zeros(sums.shape, f32)
 
     def group(g, carry):
-        at = pl.multiple_of(g * 8, 8)
-        grads = [grad[pl.ds(grad_base + i * grad_stride + at, 8), :] for i in range(rows)]
+        at = pl.multiple_of(g * 16, 16)
+        grads = [grad[pl.ds(grad_base + i * grad_stride + at, 16), :].astype(bf16) for i in range(rows)]
         for b in range(size):
-            total = [None] * size
-            for i in range(rows + size - 1):
-                x = src[pl.ds(src_base + i * src_stride + at + b, 8), :]
-                for a in range(size):
-                    r = i - a
-                    if 0 <= r < rows:
-                        term = x * grads[r]
-                        total[a] = term if total[a] is None else total[a] + term
+            lines = [
+                src[pl.ds(src_base + i * src_stride + at + b, 16), :].astype(bf16) for i in range(rows + size - 1)
+            ]
             for a in range(size):
+                term = tree_sum([lines[r + a] * grads[r] for r in range(rows)]).astype(f32)
                 t = (a * size + b) * 8
-                sums[t : t + 8, :] += total[a]
+                sums[t : t + 8, :] += term[0:8] + term[8:16]
         return carry
 
-    lax.fori_loop(0, cols // 8, group, 0)
+    lax.fori_loop(0, cols // 16, group, 0)
 
 
 def lane_total(x):
@@ -229,8 +245,10 @@
 
 
 def gelu_parts(v):
-    t = 1.0 / (1.0 + (0.3275911 * inv_sqrt_two) * jnp.abs(v))
-    bell = jnp.exp(-0.5 * v * v)
+    d = 1.0 + (0.3275911 * inv_sqrt_two) * jnp.abs(v)
+    t = pl.reciprocal(d, approx=True)
+    t = t * (2.0 - d * t)
+    bell = jnp.exp2(v * v * (-0.5 * log2_e))
     series = 0.5 * 1.061405429 * t + 0.5 * -1.453152027
     series = series * t + 0.5 * 1.421413741
     series = series * t + 0.5 * -0.284496736
@@ -276,19 +294,37 @@
         copy.wait()
 
 
-def strips_kernel(dims, image_in, cot_in, image, cot, *refs):
+def image_take(ref):
+    return lambda i, lo, hi: ref[i].astype(f32)[lo:hi]
+
+
+def flat_take(ref, cols, channels):
+    return lambda i, lo, hi: ref[i * cols + lo : i * cols + hi, 0:channels]
+
+
+def bands_kernel(dims, image_in, image, *refs):
     outs, sems = (refs[:-1], refs[-1])
     place = Place(dims.row_count, dims.col_count)
-    fetch((image_in, cot_in), (image, cot), sems)
-
-    def take(ref):
-        return lambda i, lo, hi: ref[i].astype(f32)[lo:hi]
-
-    write_strips(
-        place,
-        outs,
-        [(take(image), 2 * dims.h, dims.rows, dims.cols), (take(cot), dims.h, dims.rows, dims.cols)],
-    )
+    fetch((image_in,), (image,), sems)
+    takes = [(image_take(image), 2 * dims.h, dims.rows, dims.cols)]
+    write_strips(place, outs, takes, band_combos(dims.row_count))
+
+
+def others_kernel(dims, image, *refs):
+    outs = refs[len(band_combos(dims.row_count)) :]
+    place = Place(dims.row_count, dims.col_count)
+    takes = [(image_take(image), 2 * dims.h, dims.rows, dims.cols)]
+    write_strips(place, outs, takes, other_combos(dims.row_count))
+
+
+def grad_others_kernel(dims, grad1, cot, *refs):
+    outs = refs[len(band_combos(dims.row_count)) :]
+    place = Place(dims.row_count, dims.col_count)
+    takes = [
+        (flat_take(grad1, dims.cols, dims.channels), 2 * dims.h, dims.rows, dims.cols),
+        (image_take(cot), dims.h, dims.rows, dims.cols),
+    ]
+    write_strips(place, outs, takes, other_combos(dims.row_count))
 
 
 def weights_kernel(up_in, down_t_in, kernels_in, gains_in, up, down, up_t, down_t, taps0, taps1, gains, *refs):
@@ -306,8 +342,7 @@
     strips = refs[9 : 9 + count]
     refs = refs[9 + count :]
     (output, x0, x1, unit0, inv0, hidden0, slope0, grad1, normed1, pre_grad1, hidden1, gain_sum) = refs[:12]
-    outs = refs[12 : 12 + count]
-    (conv,) = refs[12 + count :]
+    outs, conv = (refs[12:-1], refs[-1])
     place = Place(dims.row_count, dims.col_count)
     rows, cols, channels, h, size = (dims.rows, dims.cols, dims.channels, dims.h, dims.size)
     ext_rows, ext_cols, wide = (dims.ext_rows, dims.ext_cols, dims.wide)
@@ -321,15 +356,15 @@
     frame = pl.multiple_of(skip * ext_cols, 8)
 
     def conv0(g, carry):
-        at = pl.multiple_of(g * 8, 8)
+        at = group_start(g, ext_cols)
         base = pl.multiple_of(skip * wide, 8) + at
         total = conv_group(x0, base + 1, wide, ext_rows, taps0, size)
         for r in range(ext_rows):
-            conv[pl.ds(r * ext_cols + at, 8), :] = total[r]
-            x1[pl.ds(frame + r * ext_cols + at, 8), :] = x0[pl.ds(base + (r + h) * wide + 4, 8), :]
+            conv[pl.ds(r * ext_cols + at, 16), :] = total[r]
+            x1[pl.ds(frame + r * ext_cols + at, 16), :] = x0[pl.ds(base + (r + h) * wide + 4, 16), :]
         return carry
 
-    lax.fori_loop(0, ext_cols // 8, conv0, 0)
+    lax.fori_loop(0, -(-ext_cols // 16), conv0, 0)
     gain = pad_lanes(gains[0:1, :])
     step = dims.ext_step
 
@@ -351,13 +386,13 @@
     clear_outside(place, x1, dims)
 
     def conv1(g, carry):
-        at = pl.multiple_of(g * 8, 8)
+        at = group_start(g, cols)
         total = conv_group(x1, at + 1, ext_cols, rows, taps1, size)
         for r in range(rows):
-            conv[pl.ds(r * cols + at, 8), :] = total[r]
+            conv[pl.ds(r * cols + at, 16), :] = total[r]
         return carry
 
-    lax.fori_loop(0, cols // 8, conv1, 0)
+    lax.fori_loop(0, -(-cols // 16), conv1, 0)
     gain1 = pad_lanes(gains[1:2, :])
     gain_sum[...] = jnp.zeros(gain_sum.shape, f32)
     lines = dims.line_step
@@ -387,10 +422,8 @@
 
     lax.fori_loop(0, rows // lines, mix1, 0)
 
-    def take(i, lo, hi):
-        return grad1[i * cols + lo : i * cols + hi, 0:channels]
-
-    write_strips(place, outs, [(take, 2 * h, rows, cols)])
+    takes = [(flat_take(grad1, cols, channels), 2 * h, rows, cols), (image_take(cot), h, rows, cols)]
+    write_strips(place, outs, takes, band_combos(dims.row_count))
 
 
 def clear_outside(place, flat, dims):
@@ -438,9 +471,8 @@
     (grad1, cot, taps1, gains, up_t, down_t, x0, unit0, inv0, hidden0, slope0) = refs[:11]
     (taps_sum1, up_sum1, down_sum1) = refs[11:14]
     strips = refs[14 : 14 + count]
-    cot_strips = refs[14 + count : 14 + 2 * count]
-    (grad0, middle, keep, small_keep, send) = refs[14 + 2 * count : 19 + 2 * count]
-    (wide_grad, cot_frame, upstream, own, sums, up_acc, down_acc, gain_sum, small, tall, slabs) = refs[19 + 2 * count :]
+    (grad0, middle, keep, small_keep, send) = refs[14 + count : 19 + count]
+    (wide_grad, cot_frame, upstream, own, sums, up_acc, down_acc, gain_sum, small, tall, slabs) = refs[19 + count :]
     place = Place(dims.row_count, dims.col_count)
     rows, cols, channels, h, size = (dims.rows, dims.cols, dims.channels, dims.h, dims.size)
     ext_rows, ext_cols, wide = (dims.ext_rows, dims.ext_cols, dims.wide)
@@ -449,7 +481,7 @@
     assemble(
         place, wide_grad, lambda i: grad1[i * cols : (i + 1) * cols, 0:channels], read, 2 * h, rows, cols, channels
     )
-    read_cot = received(place, cot_strips, (rows, 2 * h))
+    read_cot = received(place, strips, (rows, 2 * h))
     margin = (ext_cols - cols) // 2
     cot_frame[...] = jnp.zeros(cot_frame.shape, f32)
     for vertical, start, n in (("above", 0, h), (None, h, rows), ("below", h + rows, h)):
@@ -468,18 +500,18 @@
     frame = pl.multiple_of(skip * ext_cols, 8)
 
     def conv1(g, carry):
-        at = pl.multiple_of(g * 8, 8)
+        at = group_start(g, ext_cols)
         total = conv_group(wide_grad, pl.multiple_of(skip * wide, 8) + at + 1, wide, ext_rows, taps1, size, True)
-        col = lax.broadcasted_iota(jnp.int32, (8, LANES), 0) + (at - margin)
+        col = lax.broadcasted_iota(jnp.int32, (16, LANES), 0) + (at - margin)
         inside = jnp.where(jnp.logical_and(col >= 0, col < cols), 1.0, 0.0)
         for r in range(ext_rows):
-            px = pl.ds(r * ext_cols + at, 8)
-            upstream[px, :] = cot_frame[pl.ds(frame + r * ext_cols + at, 8), :] + total[r]
+            px = pl.ds(r * ext_cols + at, 16)
+            upstream[px, :] = cot_frame[pl.ds(frame + r * ext_cols + at, 16), :] + total[r]
             mine = jnp.logical_and(r + skip >= h, r + skip < h + rows)
             own[px, :] = jnp.where(mine, inside, 0.0)
         return carry
 
-    lax.fori_loop(0, ext_cols // 8, conv1, 0)
+    lax.fori_loop(0, -(-ext_cols // 16), conv1, 0)
     for i in range(rows):
         line = upstream[pl.ds((i + h - skip) * ext_cols + margin, cols), :]
         middle[i * cols : (i + 1) * cols, :] = round16(line)
@@ -559,7 +591,8 @@
     send[count:, :] = merged
 
 
-def stage_kernel(dims, stage, keep, small, got, keep_out, small_out, send, total):
+def stage_kernel(dims, stage, keep, small, got, *refs):
+    keep_out, small_out, send, total = refs[-4:]
     place = Place(dims.row_count, dims.col_count)
     count = keep.shape[0]
     total[...] = keep[...] + got[0:count, :].astype(f32)
@@ -586,19 +619,20 @@
                 gain_out[layer : layer + 1, :] = row
 
 
-def image_kernel(dims, grad0, middle, taps0, out, work):
+def image_kernel(dims, grad0, middle, taps0, after, out, ready, work):
     rows, cols, size = (dims.rows, dims.cols, dims.size)
 
     def conv0(g, carry):
-        at = pl.multiple_of(g * 8, 8)
+        at = group_start(g, cols)
         total = conv_group(grad0, at + 1, dims.ext_cols, rows, taps0, size, True)
         for r in range(rows):
-            work[pl.ds(r * cols + at, 8), :] = middle[pl.ds(r * cols + at, 8), :] + total[r]
+            work[pl.ds(r * cols + at, 16), :] = middle[pl.ds(r * cols + at, 16), :] + total[r]
         return carry
 
-    lax.fori_loop(0, cols // 8, conv0, 0)
+    lax.fori_loop(0, -(-cols // 16), conv0, 0)
     for r in range(rows):
         out[r] = work[r * cols : (r + 1) * cols, 0 : dims.channels].astype(bf16)
+    ready[...] = jnp.zeros(ready.shape, f32)
 
 
 class Dims:
@@ -665,20 +699,20 @@
     units = up_weights.shape[2]
     tile, ext, wide = (rows * cols, d.ext_pad, (rows + 4 * d.h) * d.wide)
     frame = (rows + 2 * d.h) * d.ext_cols + 16
-    taps = ((d.size * d.size * 8, LANES), f32)
+    taps = ((d.size * d.size * 16, LANES), bf16)
+    tap_sums = ((d.size * d.size * 8, LANES), f32)
     sums_rows = ceil8(d.size * d.size + 1)
 
-    shapes = strip_shapes(d.row_count, rows, cols, channels, (2 * d.h, d.h))
-    image, cot, *strips = run(
-        bind(strips_kernel, d),
-        [(image.shape, bf16), (image.shape, bf16)] + [(s, bf16) for s in shapes],
-        [],
-        image,
-        cotangent,
-        in_hbm=2,
-        sems=2,
-    )
-    strips = exchange(strips, d.row_count, d.col_count)
+    bands, others = (band_combos(d.row_count), other_combos(d.row_count))
+
+    def strips_of(pairs, radii):
+        return [(shape, bf16) for shape in strip_shapes(pairs, rows, cols, channels, radii)]
+
+    image, *band_strips = run(
+        bind(bands_kernel, d), [(image.shape, bf16)] + strips_of(bands, (2 * d.h,)), [], image, in_hbm=1, sems=1
+    )
+    other_strips = run(bind(others_kernel, d), strips_of(others, (2 * d.h,)), [], image, *band_strips)
+    strips = exchange(band_strips, other_strips, d.row_count, d.col_count)
     up, down, up_t, down_t, taps0, taps1, gains = run(
         weights_kernel,
         [
@@ -700,7 +734,6 @@
         busy_us=2,
     )
 
-    grad_shapes = strip_shapes(d.row_count, rows, cols, channels, (2 * d.h,))
     first = run(
         bind(first_kernel, d),
         [
@@ -717,10 +750,10 @@
             ((tile, units), bf16),
             ((8, LANES), f32),
         ]
-        + [(s, bf16) for s in grad_shapes],
+        + strips_of(bands, (2 * d.h, d.h)),
         [((ext, LANES), f32)],
         image,
-        cot,
+        cotangent,
         taps0,
         taps1,
         gains,
@@ -732,18 +765,22 @@
         busy_us=15,
     )
     (output, x0, x1, unit0, inv0, hidden0, slope0, grad1, normed1, pre_grad1, hidden1, gain_part) = first[:12]
-    grad_strips = exchange(first[12:], d.row_count, d.col_count)
+    band_strips = first[12:]
+    other_strips = run(
+        bind(grad_others_kernel, d), strips_of(others, (2 * d.h, d.h)), [], grad1, cotangent, *band_strips
+    )
+    strips = exchange(band_strips, other_strips, d.row_count, d.col_count)
 
     taps_sum1, up_sum1, down_sum1 = run(
         bind(sums_kernel, d),
         [((sums_rows, LANES), f32), ((units, LANES), f32), ((units, LANES), f32)],
-        [taps],
+        [tap_sums],
         x1,
         grad1,
         normed1,
         pre_grad1,
         hidden1,
-        cot,
+        cotangent,
         gain_part,
         busy_us=3,
     )
@@ -758,7 +795,7 @@
             ((frame, LANES), f32),
             ((ext, LANES), f32),
             ((ext, LANES), f32),
-            taps,
+            tap_sums,
             ((LANES, units), f32),
             ((LANES, units), f32),
             ((8, LANES), f32),
@@ -767,7 +804,7 @@
             ((2 * held, LANES), f32),
         ],
         grad1,
-        cot,
+        cotangent,
         taps1,
         gains,
         up_t,
@@ -780,16 +817,25 @@
         taps_sum1,
         up_sum1,
         down_sum1,
-        *grad_strips,
         *strips,
         busy_us=12,
-    )
-    (gradient,) = run(
-        bind(image_kernel, d), [(image.shape, bf16)], [((tile, LANES), f32)], grad0, middle, taps0, busy_us=3
     )
     axes = ("row", "col")
     for stage in range(len(d.stages)):
         got = lax.ppermute(send, axes, halving_pairs(d, stage))
+        if stage == 1:
+            gradient, *ready = run(
+                bind(image_kernel, d),
+                [(image.shape, bf16), ((8, LANES), f32)],
+                [((tile, LANES), f32)],
+                grad0,
+                middle,
+                taps0,
+                sums,
+                busy_us=3,
+            )
+        else:
+            ready = []
         if stage + 1 < len(d.stages):
             held //= 2
             keep, sums, send = run(
@@ -799,6 +845,7 @@
                 keep,
                 sums,
                 got,
+                *ready,
             )
     kernel_out, gain_out, up_out, down_out = run(
         bind(last_kernel, d),

time: 67.5 us -> 60.2 us (0.89)
  waiting for transfers between devices: 20.5 us -> 14 us
  starting transfers between devices: 14.5 us -> 20 us
  Pallas kernels: 29.7 us -> 24.4 us
  local copies, waits for them, and re-layouts: 1.91 us -> 0.96 us
    pallas_call x11 -> x13, Pallas kernels: 29.7 us -> 24.4 us  [run(): pl.pallas_call(kernel, out_shape=shapes, in_specs=[far] * in_hbm + [space...]
    ppermute x5, starting transfers between devices: 4.57 us -> 8.88 us  [per_device(): got = lax.ppermute(send, axes, halving_pairs(d, stage))]
    ppermute x10, waiting for transfers between devices: 7.27 us -> 3.71 us  [exchange(): lax.ppermute(strip, ('row', 'col'), swap_pairs(row_count, col_count, rs,...]
    ppermute x5, waiting for transfers between devices: 13.2 us -> 10.2 us  [per_device(): got = lax.ppermute(send, axes, halving_pairs(d, stage))]
    ppermute x10, starting transfers between devices: 9.93 us -> 11.1 us  [exchange(): lax.ppermute(strip, ('row', 'col'), swap_pairs(row_count, col_count, rs,...]
    unnamed x12, local copies, waits for them, and re-layouts: 1.91 us -> 0.96 us
  transfers between devices with their start and end apart: 15 -> 15, of which waited for: 7 -> 7; matrix products, arithmetic and copies ran while one was open for 0% -> 0% of each run, Pallas kernels for 9% -> 8%
where the time goes in v4:
time: 60.2 us; the launch traced here: 60 us
  Pallas kernels  24.4 us (41%)
  starting transfers between devices  20 us (33%)
  waiting for transfers between devices  14 us (23%)
  local copies, waits for them, and re-layouts  0.96 us (2%)
  between operations  0.78 us (1%)
    pallas_call x13, Pallas kernels, run(): pl.pallas_call(kernel, out_shape=shapes, in_specs=[far] * in_hbm + [space...  24.4 us
    ppermute x10, starting transfers between devices, exchange(): lax.ppermute(strip, ('row', 'col'), swap_pairs(row_count, col_count, rs,...  11.1 us
    ppermute x5, waiting for transfers between devices, per_device(): got = lax.ppermute(send, axes, halving_pairs(d, stage))  10.2 us
    ppermute x5, starting transfers between devices, per_device(): got = lax.ppermute(send, axes, halving_pairs(d, stage))  8.88 us
    ppermute x10, waiting for transfers between devices, exchange(): lax.ppermute(strip, ('row', 'col'), swap_pairs(row_count, col_count, rs,...  3.71 us
  transfers between devices with their start and end apart: 15, of which 7 were waited for; matrix products, arithmetic and copies ran while one was open for 0% of the time, Pallas kernels for 8%

profile of v4, /device:TPU:0, one launch (start us, length us, event | category | flops | bytes accessed | tf_op | source)
XLA Modules:
  0.0 60.0 jit_solution(13540720224275772941)
XLA Ops:
  0.6 0.9 %copy-done = bf16[16,64,96]{2,1,0:T(8,128)(2,1)S(1)} copy-done((bf16[16,64,96]{2,1,0:T(8,128)(2,1)S(1)}, bf16[16,64,96]{2,1,0:T(8,128)(2,1)}, u32[]{:S(2)}) %copy-start) | copy-done | bytes 196632
  1.6 3.0 %collective-permute-start.2 = (bf16[6,64,96]{2,1,0:T(8,128)(2,1)S(1)}, bf16[6,64,96]{2,1,0:T(8,128)(2,1)S(1)}, u32[]{:S(2)}, u32[]{:S(2)}) collective-permute-start(bf16[6,64,96]{2,1,0:T(8,128)(2,1)S(1)} %get-tuple-element.70.refs_0_), channel_id=1, source_target_pairs={{0,16},{1,17},{2,18},{3,19},{4,20},{5,21},{6,22},{7,23},{8,24},{9,... | collective-permute-start | bytes 221192 | tf_op jit(solution)/shard_map/ppermute | solution.py:55
  4.8 1.2 %collective-permute-start.4 = (bf16[6,8,96]{2,1,0:T(8,128)(2,1)S(1)}, bf16[6,8,96]{2,1,0:T(8,128)(2,1)S(1)}, u32[]{:S(2)}, u32[]{:S(2)}) collective-permute-start(bf16[6,8,96]{2,1,0:T(8,128)(2,1)S(1)} %get-tuple-element.74), channel_id=1, source_target_pairs={{0,16},{1,18},{2,17},{3,20},{4,19},{5,22},{6,21},{7,24},{8,23},{9,... | collective-permute-start | bytes 27656 | tf_op jit(solution)/shard_map/ppermute | solution.py:55
  6.0 1.1 %collective-permute-start = (bf16[16,8,96]{2,1,0:T(8,128)(2,1)S(1)}, bf16[16,8,96]{2,1,0:T(8,128)(2,1)S(1)}, u32[]{:S(2)}, u32[]{:S(2)}) collective-permute-start(bf16[16,8,96]{2,1,0:T(8,128)(2,1)S(1)} %get-tuple-element.71), channel_id=1, source_target_pairs={{0,1},{1,0},{2,3},{3,2},{4,5},{5,4},{6,7},{7,6},{8,9},{9,8},{10,11... | collective-permute-start | bytes 73736 | tf_op jit(solution)/shard_map/ppermute | solution.py:55
  7.0 0.9 %collective-permute-start.1 = (bf16[16,8,96]{2,1,0:T(8,128)(2,1)S(1)}, bf16[16,8,96]{2,1,0:T(8,128)(2,1)S(1)}, u32[]{:S(2)}, u32[]{:S(2)}) collective-permute-start(bf16[16,8,96]{2,1,0:T(8,128)(2,1)S(1)} %get-tuple-element.72), channel_id=1, source_target_pairs={{0,16},{1,2},{2,1},{3,4},{4,3},{5,6},{6,5},{7,8},{8,7},{9,10},{10,... | collective-permute-start | bytes 73736 | tf_op jit(solution)/shard_map/ppermute | solution.py:55
  8.7 2.2 %collective-permute-done.1.refs_10_ = bf16[16,8,96]{2,1,0:T(8,128)(2,1)S(1)} collective-permute-done((bf16[16,8,96]{2,1,0:T(8,128)(2,1)S(1)}, bf16[16,8,96]{2,1,0:T(8,128)(2,1)S(1)}, u32[]{:S(2)}, u32[]{:S(2)}) %collective-permute-start.1) | collective-permute-done | bytes 24608 | tf_op jit(solution)/shard_map/ppermute | solution.py:55
  10.9 12.3 %shard_map.112 = (bf16[16,64,96]{2,1,0:T(8,128)(2,1)}, f32[2240,128]{1,0:T(8,128)S(1)}, f32[1600,128]{1,0:T(8,128)S(1)}, bf16[1376,128]{1,0:T(8,128)(2,1)S(1)}, ...) custom-call(bf16[16,64,96]{2,1,0:T(8,128)(2,1)S(1)} %get-tuple-eleme, ...), custom_call_target="tpu_custom_call" | custom-call | flops 15000000512 | bytes 262144 | tf_op jit(solution)/shard_map/pallas_call | solution.py:684
  23.3 0.9 %collective-permute-start.7 = (bf16[9,64,96]{2,1,0:T(8,128)(2,1)S(1)}, bf16[9,64,96]{2,1,0:T(8,128)(2,1)S(1)}, u32[]{:S(2)}, u32[]{:S(2)}) collective-permute-start(bf16[9,64,96]{2,1,0:T(8,128)(2,1)S(1)} %get-tuple-element.90.refs_0_), channel_id=1, source_target_pairs={{0,16},{1,17},{2,18},{3,19},{4,20},{5,21},{6,22},{7,23},{8,24},{9,... | collective-permute-start | bytes 331784 | tf_op jit(solution)/shard_map/ppermute | solution.py:55
  24.4 1.1 %collective-permute-start.9 = (bf16[9,8,96]{2,1,0:T(8,128)(2,1)S(1)}, bf16[9,8,96]{2,1,0:T(8,128)(2,1)S(1)}, u32[]{:S(2)}, u32[]{:S(2)}) collective-permute-start(bf16[9,8,96]{2,1,0:T(8,128)(2,1)S(1)} %get-tuple-element.94), channel_id=1, source_target_pairs={{0,16},{1,18},{2,17},{3,20},{4,19},{5,22},{6,21},{7,24},{8,23},{9,... | collective-permute-start | bytes 41480 | tf_op jit(solution)/shard_map/ppermute | solution.py:55
  25.5 1.6 %collective-permute-start.5 = (bf16[32,8,96]{2,1,0:T(8,128)(2,1)S(1)}, bf16[32,8,96]{2,1,0:T(8,128)(2,1)S(1)}, u32[]{:S(2)}, u32[]{:S(2)}) collective-permute-start(bf16[32,8,96]{2,1,0:T(8,128)(2,1)S(1)} %get-tuple-element.91), channel_id=1, source_target_pairs={{0,1},{1,0},{2,3},{3,2},{4,5},{5,4},{6,7},{7,6},{8,9},{9,8},{10,11... | collective-permute-start | bytes 147464 | tf_op jit(solution)/shard_map/ppermute | solution.py:55
  27.1 1.1 %collective-permute-start.6 = (bf16[32,8,96]{2,1,0:T(8,128)(2,1)S(1)}, bf16[32,8,96]{2,1,0:T(8,128)(2,1)S(1)}, u32[]{:S(2)}, u32[]{:S(2)}) collective-permute-start(bf16[32,8,96]{2,1,0:T(8,128)(2,1)S(1)} %get-tuple-element.92), channel_id=1, source_target_pairs={{0,16},{1,2},{2,1},{3,4},{4,3},{5,6},{6,5},{7,8},{8,7},{9,10},{10,... | collective-permute-start | bytes 147464 | tf_op jit(solution)/shard_map/ppermute | solution.py:55
  28.2 1.7 %shard_map.113 = (f32[56,128]{1,0:T(8,128)S(1)}, f32[384,128]{1,0:T(8,128)S(1)}, f32[384,128]{1,0:T(8,128)S(1)}) custom-call(f32[1600,128]{1,0:T(8,128)S(1)} %get-tuple-element.82.x1, f32[1024,128]{1,0:T(8,128)S(1)} %get-tuple-element.76.grad1.refs_0_, bf16[1024,128]{1,0:T(8,128)(2,1)S(1)} %get-tuple-element.83.normed1, ...), custom_call_target="tpu_custom_call" | custom-call | flops 3000000000 | bytes 262144 | tf_op jit(solution)/shard_map/pallas_call | solution.py:684
  29.9 1.5 %collective-permute-done.6.refs_15_ = bf16[32,8,96]{2,1,0:T(8,128)(2,1)S(1)} collective-permute-done((bf16[32,8,96]{2,1,0:T(8,128)(2,1)S(1)}, bf16[32,8,96]{2,1,0:T(8,128)(2,1)S(1)}, u32[]{:S(2)}, u32[]{:S(2)}) %collective-permute-start.6) | collective-permute-done | bytes 49184 | tf_op jit(solution)/shard_map/ppermute | solution.py:55
  31.4 6.6 %shard_map.115 = (f32[1600,128]{1,0:T(8,128)S(1)}, f32[1024,128]{1,0:T(8,128)S(1)}, f32[768,128]{1,0:T(8,128)S(1)}, f32[112,128]{1,0:T(8,128)S(1)}, bf16[880,128]{1,0:T(8,128)(2,1)S(1)}) custom-call(f32[1024,128]{1,0:T(8,128)S(1)} %get-tuple-element.76.grad1.refs_0_, bf16[16,64,96]{2,1,0:T(8,128)(2,1)S(1)} %copy-done.1, ...), custom_call_target="tpu_custom_call" | custom-call | flops 12000000000 | bytes 262144 | tf_op jit(solution)/shard_map/pallas_call | solution.py:684
  38.0 1.4 %collective-permute-done.10.got = bf16[880,128]{1,0:T(8,128)(2,1)S(1)} collective-permute-done((bf16[880,128]{1,0:T(8,128)(2,1)S(1)}, bf16[880,128]{1,0:T(8,128)(2,1)S(1)}, u32[]{:S(2)}, u32[]{:S(2)}) %collective-permute-start.10) | collective-permute-done | bytes 225312 | tf_op jit(solution)/shard_map/ppermute | solution.py:825
  39.6 1.1 %collective-permute-start.11 = (bf16[496,128]{1,0:T(8,128)(2,1)S(1)}, bf16[496,128]{1,0:T(8,128)(2,1)S(1)}, u32[]{:S(2)}, u32[]{:S(2)}) collective-permute-start(bf16[496,128]{1,0:T(8,128)(2,1)S(1)} %get-tuple-element.103), channel_id=1, source_target_pairs={{0,16},{1,17},{2,18},{3,19},{4,20},{5,21},{6,22},{7,23},{8,24},{9,... | collective-permute-start | bytes 380936 | tf_op jit(solution)/shard_map/ppermute | solution.py:825
  40.7 2.1 %shard_map.117 = (bf16[16,64,96]{2,1,0:T(8,128)(2,1)}, f32[8,128]{1,0:T(8,128)S(1)}) custom-call(f32[1600,128]{1,0:T(8,128)S(1)} %get-tuple-element.95.grad0, f32[1024,128]{1,0:T(8,128)S(1)} %get-tuple-element.96.middle, bf16[784,128]{1,0:T(8,128)(2,1)S(1)} %get-tuple-element.63.refs_2_.taps0, f32[112,128]{1,0:T(8,128)S(1)} %get-tuple-element.100.after.small), custom_call_target="tpu_custom_call" | custom-call | flops 3000000000 | bytes 262144 | tf_op jit(solution)/shard_map/pallas_call | solution.py:684
  42.8 2.3 %collective-permute-done.11.got = bf16[496,128]{1,0:T(8,128)(2,1)S(1)} collective-permute-done((bf16[496,128]{1,0:T(8,128)(2,1)S(1)}, bf16[496,128]{1,0:T(8,128)(2,1)S(1)}, u32[]{:S(2)}, u32[]{:S(2)}) %collective-permute-start.11) | collective-permute-done | bytes 127008 | tf_op jit(solution)/shard_map/ppermute | solution.py:825
  45.1 2.0 %collective-permute-start.12 = (bf16[304,128]{1,0:T(8,128)(2,1)S(1)}, bf16[304,128]{1,0:T(8,128)(2,1)S(1)}, u32[]{:S(2)}, u32[]{:S(2)}) collective-permute-start(bf16[304,128]{1,0:T(8,128)(2,1)S(1)} %get-tuple-element.107), channel_id=1, source_target_pairs={{0,2},{1,3},{2,0},{3,1},{4,6},{5,7},{6,4},{7,5},{8,10},{9,11},{10,... | collective-permute-start | bytes 233480 | tf_op jit(solution)/shard_map/ppermute | solution.py:825
  47.1 2.4 %collective-permute-done.12.got = bf16[304,128]{1,0:T(8,128)(2,1)S(1)} collective-permute-done((bf16[304,128]{1,0:T(8,128)(2,1)S(1)}, bf16[304,128]{1,0:T(8,128)(2,1)S(1)}, u32[]{:S(2)}, u32[]{:S(2)}) %collective-permute-start.12) | collective-permute-done | bytes 77856 | tf_op jit(solution)/shard_map/ppermute | solution.py:825
  49.6 2.2 %collective-permute-start.13 = (bf16[208,128]{1,0:T(8,128)(2,1)S(1)}, bf16[208,128]{1,0:T(8,128)(2,1)S(1)}, u32[]{:S(2)}, u32[]{:S(2)}) collective-permute-start(bf16[208,128]{1,0:T(8,128)(2,1)S(1)} %get-tuple-element.110), channel_id=1, source_target_pairs={{0,4},{1,5},{2,6},{3,7},{4,0},{5,1},{6,2},{7,3},{8,12},{9,13},{10,... | collective-permute-start | bytes 159752 | tf_op jit(solution)/shard_map/ppermute | solution.py:825
  51.8 2.1 %collective-permute-done.13.got = bf16[208,128]{1,0:T(8,128)(2,1)S(1)} collective-permute-done((bf16[208,128]{1,0:T(8,128)(2,1)S(1)}, bf16[208,128]{1,0:T(8,128)(2,1)S(1)}, u32[]{:S(2)}, u32[]{:S(2)}) %collective-permute-start.13) | collective-permute-done | bytes 53280 | tf_op jit(solution)/shard_map/ppermute | solution.py:825
  53.9 3.5 %collective-permute-start.14 = (bf16[160,128]{1,0:T(8,128)(2,1)S(1)}, bf16[160,128]{1,0:T(8,128)(2,1)S(1)}, u32[]{:S(2)}, u32[]{:S(2)}) collective-permute-start(bf16[160,128]{1,0:T(8,128)(2,1)S(1)} %get-tuple-element.113), channel_id=1, source_target_pairs={{0,8},{1,9},{2,10},{3,11},{4,12},{5,13},{6,14},{7,15},{8,0},{9,1},... | collective-permute-start | bytes 122888 | tf_op jit(solution)/shard_map/ppermute | solution.py:825
  57.4 2.0 %collective-permute-done.14.got = bf16[160,128]{1,0:T(8,128)(2,1)S(1)} collective-permute-done((bf16[160,128]{1,0:T(8,128)(2,1)S(1)}, bf16[160,128]{1,0:T(8,128)(2,1)S(1)}, u32[]{:S(2)}, u32[]{:S(2)}) %collective-permute-start.14) | collective-permute-done | bytes 40992 | tf_op jit(solution)/shard_map/ppermute | solution.py:825
  (31 shorter events, 2.0 us)
Async XLA Ops:
  0.6 1.0 %copy-start = (bf16[16,64,96]{2,1,0:T(8,128)(2,1)S(1)}, bf16[16,64,96]{2,1,0:T(8,128)(2,1)}, u32[]{:S(2)}) copy-start(bf16[16,64,96]{2,1,0:T(8,128)(2,1)} %image_in.1) | copy-start | bytes 589828
  1.6 9.3 %collective-permute-start.2 = (bf16[6,64,96]{2,1,0:T(8,128)(2,1)S(1)}, bf16[6,64,96]{2,1,0:T(8,128)(2,1)S(1)}, u32[]{:S(2)}, u32[]{:S(2)}) collective-permute-start(bf16[6,64,96]{2,1,0:T(8,128)(2,1)S(1)} %get-tuple-element.70.refs_0_), channel_id=1, source_target_pairs={{0,16},{1,17},{2,18},{3,19},{4,20},{5,21},{6,22},{7,23},{8,24},{9,... | collective-permute-start | bytes 221192 | tf_op jit(solution)/shard_map/ppermute | solution.py:55
  4.7 3.3 %copy-start.2 = (bf16[2,96,384]{2,1,0:T(8,128)(2,1)S(1)}, bf16[2,96,384]{2,1,0:T(8,128)(2,1)}, u32[]{:S(2)}) copy-start(bf16[2,96,384]{2,1,0:T(8,128)(2,1)} %up_in.1) | copy-start | bytes 442372
  4.7 3.3 %copy-start.3 = (bf16[2,384,96]{1,2,0:T(8,128)(2,1)S(1)}, bf16[2,384,96]{1,2,0:T(8,128)(2,1)}, u32[]{:S(2)}) copy-start(bf16[2,384,96]{1,2,0:T(8,128)(2,1)} %param.10) | copy-start | bytes 442372
  4.7 3.3 %copy-start.4 = (f32[2,7,7,96]{3,0,2,1:T(2,128)S(1)}, f32[2,7,7,96]{3,0,2,1:T(2,128)}, u32[]{:S(2)}) copy-start(f32[2,7,7,96]{3,0,2,1:T(2,128)} %param.7) | copy-start | bytes 112900
  4.7 3.3 %copy-start.5 = (f32[2,96]{1,0:T(2,128)S(1)}, f32[2,96]{1,0:T(2,128)}, u32[]{:S(2)}) copy-start(f32[2,96]{1,0:T(2,128)} %gains_in.1) | copy-start | bytes 2308
  4.7 4.0 %collective-permute-start.3 = (bf16[6,8,96]{2,1,0:T(8,128)(2,1)S(1)}, bf16[6,8,96]{2,1,0:T(8,128)(2,1)S(1)}, u32[]{:S(2)}, u32[]{:S(2)}) collective-permute-start(bf16[6,8,96]{2,1,0:T(8,128)(2,1)S(1)} %get-tuple-element.73), channel_id=1, source_target_pairs={{0,17},{1,16},{2,19},{3,18},{4,21},{5,20},{6,23},{7,22},{8,25},{9,... | collective-permute-start | bytes 27656 | tf_op jit(solution)/shard_map/ppermute | solution.py:55
  4.8 3.9 %collective-permute-start.4 = (bf16[6,8,96]{2,1,0:T(8,128)(2,1)S(1)}, bf16[6,8,96]{2,1,0:T(8,128)(2,1)S(1)}, u32[]{:S(2)}, u32[]{:S(2)}) collective-permute-start(bf16[6,8,96]{2,1,0:T(8,128)(2,1)S(1)} %get-tuple-element.74), channel_id=1, source_target_pairs={{0,16},{1,18},{2,17},{3,20},{4,19},{5,22},{6,21},{7,24},{8,23},{9,... | collective-permute-start | bytes 27656 | tf_op jit(solution)/shard_map/ppermute | solution.py:55
  6.0 2.8 %collective-permute-start = (bf16[16,8,96]{2,1,0:T(8,128)(2,1)S(1)}, bf16[16,8,96]{2,1,0:T(8,128)(2,1)S(1)}, u32[]{:S(2)}, u32[]{:S(2)}) collective-permute-start(bf16[16,8,96]{2,1,0:T(8,128)(2,1)S(1)} %get-tuple-element.71), channel_id=1, source_target_pairs={{0,1},{1,0},{2,3},{3,2},{4,5},{5,4},{6,7},{7,6},{8,9},{9,8},{10,11... | collective-permute-start | bytes 73736 | tf_op jit(solution)/shard_map/ppermute | solution.py:55
  7.0 3.9 %collective-permute-start.1 = (bf16[16,8,96]{2,1,0:T(8,128)(2,1)S(1)}, bf16[16,8,96]{2,1,0:T(8,128)(2,1)S(1)}, u32[]{:S(2)}, u32[]{:S(2)}) collective-permute-start(bf16[16,8,96]{2,1,0:T(8,128)(2,1)S(1)} %get-tuple-element.72), channel_id=1, source_target_pairs={{0,16},{1,2},{2,1},{3,4},{4,3},{5,6},{6,5},{7,8},{8,7},{9,10},{10,... | collective-permute-start | bytes 73736 | tf_op jit(solution)/shard_map/ppermute | solution.py:55
  8.0 3.0 %copy-start.1 = (bf16[16,64,96]{2,1,0:T(8,128)(2,1)S(1)}, bf16[16,64,96]{2,1,0:T(8,128)(2,1)}, u32[]{:S(2)}) copy-start(bf16[16,64,96]{2,1,0:T(8,128)(2,1)} %refs_1_.3) | copy-start | bytes 589828
  23.3 8.1 %collective-permute-start.7 = (bf16[9,64,96]{2,1,0:T(8,128)(2,1)S(1)}, bf16[9,64,96]{2,1,0:T(8,128)(2,1)S(1)}, u32[]{:S(2)}, u32[]{:S(2)}) collective-permute-start(bf16[9,64,96]{2,1,0:T(8,128)(2,1)S(1)} %get-tuple-element.90.refs_0_), channel_id=1, source_target_pairs={{0,16},{1,17},{2,18},{3,19},{4,20},{5,21},{6,22},{7,23},{8,24},{9,... | collective-permute-start | bytes 331784 | tf_op jit(solution)/shard_map/ppermute | solution.py:55
  24.3 5.6 %collective-permute-start.8 = (bf16[9,8,96]{2,1,0:T(8,128)(2,1)S(1)}, bf16[9,8,96]{2,1,0:T(8,128)(2,1)S(1)}, u32[]{:S(2)}, u32[]{:S(2)}) collective-permute-start(bf16[9,8,96]{2,1,0:T(8,128)(2,1)S(1)} %get-tuple-element.93), channel_id=1, source_target_pairs={{0,17},{1,16},{2,19},{3,18},{4,21},{5,20},{6,23},{7,22},{8,25},{9,... | collective-permute-start | bytes 41480 | tf_op jit(solution)/shard_map/ppermute | solution.py:55
  24.4 5.5 %collective-permute-start.9 = (bf16[9,8,96]{2,1,0:T(8,128)(2,1)S(1)}, bf16[9,8,96]{2,1,0:T(8,128)(2,1)S(1)}, u32[]{:S(2)}, u32[]{:S(2)}) collective-permute-start(bf16[9,8,96]{2,1,0:T(8,128)(2,1)S(1)} %get-tuple-element.94), channel_id=1, source_target_pairs={{0,16},{1,18},{2,17},{3,20},{4,19},{5,22},{6,21},{7,24},{8,23},{9,... | collective-permute-start | bytes 41480 | tf_op jit(solution)/shard_map/ppermute | solution.py:55
  25.5 4.4 %collective-permute-start.5 = (bf16[32,8,96]{2,1,0:T(8,128)(2,1)S(1)}, bf16[32,8,96]{2,1,0:T(8,128)(2,1)S(1)}, u32[]{:S(2)}, u32[]{:S(2)}) collective-permute-start(bf16[32,8,96]{2,1,0:T(8,128)(2,1)S(1)} %get-tuple-element.91), channel_id=1, source_target_pairs={{0,1},{1,0},{2,3},{3,2},{4,5},{5,4},{6,7},{7,6},{8,9},{9,8},{10,11... | collective-permute-start | bytes 147464 | tf_op jit(solution)/shard_map/ppermute | solution.py:55
  27.1 4.3 %collective-permute-start.6 = (bf16[32,8,96]{2,1,0:T(8,128)(2,1)S(1)}, bf16[32,8,96]{2,1,0:T(8,128)(2,1)S(1)}, u32[]{:S(2)}, u32[]{:S(2)}) collective-permute-start(bf16[32,8,96]{2,1,0:T(8,128)(2,1)S(1)} %get-tuple-element.92), channel_id=1, source_target_pairs={{0,16},{1,2},{2,1},{3,4},{4,3},{5,6},{6,5},{7,8},{8,7},{9,10},{10,... | collective-permute-start | bytes 147464 | tf_op jit(solution)/shard_map/ppermute | solution.py:55
  37.9 1.5 %collective-permute-start.10 = (bf16[880,128]{1,0:T(8,128)(2,1)S(1)}, bf16[880,128]{1,0:T(8,128)(2,1)S(1)}, u32[]{:S(2)}, u32[]{:S(2)}) collective-permute-start(bf16[880,128]{1,0:T(8,128)(2,1)S(1)} %get-tuple-element.99), channel_id=1, source_target_pairs={{0,1},{1,0},{2,3},{3,2},{4,5},{5,4},{6,7},{7,6},{8,9},{9,8},{10,11... | collective-permute-start | bytes 675848 | tf_op jit(solution)/shard_map/ppermute | solution.py:825
  39.6 5.5 %collective-permute-start.11 = (bf16[496,128]{1,0:T(8,128)(2,1)S(1)}, bf16[496,128]{1,0:T(8,128)(2,1)S(1)}, u32[]{:S(2)}, u32[]{:S(2)}) collective-permute-start(bf16[496,128]{1,0:T(8,128)(2,1)S(1)} %get-tuple-element.103), channel_id=1, source_target_pairs={{0,16},{1,17},{2,18},{3,19},{4,20},{5,21},{6,22},{7,23},{8,24},{9,... | collective-permute-start | bytes 380936 | tf_op jit(solution)/shard_map/ppermute | solution.py:825
  45.1 4.5 %collective-permute-start.12 = (bf16[304,128]{1,0:T(8,128)(2,1)S(1)}, bf16[304,128]{1,0:T(8,128)(2,1)S(1)}, u32[]{:S(2)}, u32[]{:S(2)}) collective-permute-start(bf16[304,128]{1,0:T(8,128)(2,1)S(1)} %get-tuple-element.107), channel_id=1, source_target_pairs={{0,2},{1,3},{2,0},{3,1},{4,6},{5,7},{6,4},{7,5},{8,10},{9,11},{10,... | collective-permute-start | bytes 233480 | tf_op jit(solution)/shard_map/ppermute | solution.py:825
  49.6 4.3 %collective-permute-start.13 = (bf16[208,128]{1,0:T(8,128)(2,1)S(1)}, bf16[208,128]{1,0:T(8,128)(2,1)S(1)}, u32[]{:S(2)}, u32[]{:S(2)}) collective-permute-start(bf16[208,128]{1,0:T(8,128)(2,1)S(1)} %get-tuple-element.110), channel_id=1, source_target_pairs={{0,4},{1,5},{2,6},{3,7},{4,0},{5,1},{6,2},{7,3},{8,12},{9,13},{10,... | collective-permute-start | bytes 159752 | tf_op jit(solution)/shard_map/ppermute | solution.py:825
  53.9 5.4 %collective-permute-start.14 = (bf16[160,128]{1,0:T(8,128)(2,1)S(1)}, bf16[160,128]{1,0:T(8,128)(2,1)S(1)}, u32[]{:S(2)}, u32[]{:S(2)}) collective-permute-start(bf16[160,128]{1,0:T(8,128)(2,1)S(1)} %get-tuple-element.113), channel_id=1, source_target_pairs={{0,8},{1,9},{2,10},{3,11},{4,12},{5,13},{6,14},{7,15},{8,0},{9,1},... | collective-permute-start | bytes 122888 | tf_op jit(solution)/shard_map/ppermute | solution.py:825

commit v5 on v4

--- a/solution.py
+++ b/solution.py
@@ -220,28 +220,39 @@
     lax.fori_loop(0, cols // 16, group, 0)
 
 
+def diagonal(first, second):
+    top = jnp.concatenate([first, jnp.zeros((first.shape[0], second.shape[1]), first.dtype)], axis=1)
+    bottom = jnp.concatenate([jnp.zeros((second.shape[0], first.shape[1]), first.dtype), second], axis=1)
+    return jnp.concatenate([top, bottom], axis=0)
+
+
 def lane_total(x):
     high = x.astype(bf16)
     low = (x - high.astype(f32)).astype(bf16)
     both = jnp.concatenate([high, low], axis=1)
-    ones = jnp.ones((2 * LANES, LANES), bf16)
-    return jnp.dot(both, ones, preferred_element_type=f32)
-
-
-def layer_norm(conv, channels):
-    lane = lax.broadcasted_iota(jnp.int32, conv.shape, 1)
-    centred = jnp.where(lane < channels, conv - lane_total(conv) * (1.0 / channels), 0.0)
-    variance = lane_total(centred * centred) * (1.0 / channels)
-    inverse = lax.rsqrt(variance + epsilon)
-    return (centred * inverse, inverse)
-
-
-def norm_backward(normed_grad, unit, inverse, gain, channels):
+    return dot(both, jnp.ones((2 * LANES, LANES), bf16))
+
+
+def paired_dot(x, y, weights):
+    total = dot(jnp.concatenate([x.astype(bf16), y.astype(bf16)], axis=1), weights)
+    half = weights.shape[1] // 2
+    return (total[:, :half], total[:, half:])
+
+
+def layer_norm(parts, channels, ones):
+    lane = lax.broadcasted_iota(jnp.int32, parts[0].shape, 1)
+    centred = [jnp.where(lane < channels, x - lane_total(x) * (1.0 / channels), 0.0) for x in parts]
+    variances = paired_dot(centred[0] * centred[0], centred[1] * centred[1], ones)
+    inverses = [lax.rsqrt(v * (1.0 / channels) + epsilon) for v in variances]
+    return ([c * i for c, i in zip(centred, inverses)], inverses)
+
+
+def norm_backward(normed_grad, unit, inverse, gain, channels, ones):
     m = normed_grad * gain
-    mean = lane_total(m) * (1.0 / channels)
-    along = lane_total(m * unit) * (1.0 / channels)
+    mean, along = paired_dot(m, m * unit, ones)
     lane = lax.broadcasted_iota(jnp.int32, m.shape, 1)
-    return jnp.where(lane < channels, inverse * (m - mean - unit * along), 0.0)
+    centred = m - (mean + unit * along) * (1.0 / channels)
+    return jnp.where(lane < channels, inverse * centred, 0.0)
 
 
 def gelu_parts(v):
@@ -271,15 +282,8 @@
     return jnp.concatenate([x, jnp.zeros((rows, LANES - channels), x.dtype)], axis=1)
 
 
-def load_weights(up_ref, down_t_ref, layer, up, down, up_t, down_t):
-    channels, units = up_ref.shape[1:]
-    blank = jnp.zeros((LANES - channels, units), f32)
-    up_f = jnp.concatenate([up_ref[layer].astype(f32), blank], axis=0)
-    down_f = jnp.concatenate([down_t_ref[layer].astype(f32), blank], axis=0)
-    up[layer] = up_f.astype(bf16)
-    down_t[layer] = down_f.astype(bf16)
-    up_t[layer] = up_f.T.astype(bf16)
-    down[layer] = down_f.T.astype(bf16)
+def pieces(total, size):
+    return [(start, min(size, total - start)) for start in range(0, total, size)]
 
 
 def round16(x):
@@ -327,18 +331,31 @@
     write_strips(place, outs, takes, other_combos(dims.row_count))
 
 
-def weights_kernel(up_in, down_t_in, kernels_in, gains_in, up, down, up_t, down_t, taps0, taps1, gains, *refs):
-    up_w, down_w, kernels, sems = refs
+def weights_kernel(up_in, down_t_in, kernels_in, gains_in, *refs):
+    forward0, back0, forward1, back1, grad_in0, grad_out0, taps0, taps1, gains, up_w, down_w, kernels, sems = refs
     fetch((up_in, down_t_in, kernels_in, gains_in), (up_w, down_w, kernels, gains), sems)
     spread_taps(kernels, 0, taps0)
     spread_taps(kernels, 1, taps1)
+    channels, units = up_w.shape[1:]
+    blank = jnp.zeros((LANES - channels, units), f32)
+    wide, tall = ([], [])
     for layer in range(2):
-        load_weights(up_w, down_w, layer, up, down, up_t, down_t)
+        for ref in (up_w, down_w):
+            full = jnp.concatenate([ref[layer].astype(f32), blank], axis=0)
+            wide.append(full.astype(bf16))
+            tall.append(full.T.astype(bf16))
+    (up0, down_t0, up1, down_t1), (up_t0, down0, up_t1, down1) = (wide, tall)
+    forward0[...] = diagonal(up0, up0)
+    back0[...] = diagonal(down0, down0)
+    forward1[...] = diagonal(up1, down_t1)
+    back1[...] = diagonal(down1, up_t1)
+    grad_in0[...] = diagonal(down_t0, down_t0)
+    grad_out0[...] = diagonal(up_t0, up_t0)
 
 
 def first_kernel(dims, *refs):
     count = len(combos(dims.row_count))
-    image, cot, taps0, taps1, gains, up, down, up_t, down_t = refs[:9]
+    image, cot, taps0, taps1, gains, forward0, back0, forward1, back1 = refs[:9]
     strips = refs[9 : 9 + count]
     refs = refs[9 + count :]
     (output, x0, x1, unit0, inv0, hidden0, slope0, grad1, normed1, pre_grad1, hidden1, gain_sum) = refs[:12]
@@ -366,23 +383,24 @@
 
     lax.fori_loop(0, -(-ext_cols // 16), conv0, 0)
     gain = pad_lanes(gains[0:1, :])
-    step = dims.ext_step
-
-    def mix0(k, carry):
-        px = pl.ds(pl.multiple_of(k * step, 16), step)
-        px_frame = pl.ds(frame + pl.multiple_of(k * step, 16), step)
-        unit, inverse = layer_norm(conv[px, :], channels)
-        unit0[px, :] = unit.astype(bf16)
-        inv0[px, :] = inverse
-        pre = dot((unit * gain).astype(bf16), up[0])
-        value, slope = gelu_parts(pre)
-        hidden = value.astype(bf16)
-        hidden0[px, :] = hidden
-        slope0[px, :] = slope.astype(bf16)
-        x1[px_frame, :] = round16(x1[px_frame, :] + dot(hidden, down[0]))
-        return carry
-
-    lax.fori_loop(0, dims.ext_pad // step, mix0, 0)
+    ones = diagonal(jnp.ones((LANES, LANES), bf16), jnp.ones((LANES, LANES), bf16))
+    half = dims.ext_pad // 2
+    for start, n in pieces(half, dims.piece):
+        spans = [(start, n), (half + start, n)]
+        units, inverses = layer_norm([conv[at : at + n, :] for at, n in spans], channels, ones)
+        pres = paired_dot(units[0] * gain, units[1] * gain, forward0[...])
+        hiddens = []
+        for (at, n), unit, inverse, pre in zip(spans, units, inverses, pres):
+            unit0[at : at + n, :] = unit.astype(bf16)
+            inv0[at : at + n, :] = inverse
+            value, slope = gelu_parts(pre)
+            hiddens.append(value.astype(bf16))
+            hidden0[at : at + n, :] = hiddens[-1]
+            slope0[at : at + n, :] = slope.astype(bf16)
+        branches = paired_dot(hiddens[0], hiddens[1], back0[...])
+        for (at, n), branch in zip(spans, branches):
+            px = pl.ds(frame + at, n)
+            x1[px, :] = round16(x1[px, :] + branch)
     clear_outside(place, x1, dims)
 
     def conv1(g, carry):
@@ -396,31 +414,29 @@
     gain1 = pad_lanes(gains[1:2, :])
     gain_sum[...] = jnp.zeros(gain_sum.shape, f32)
     lines = dims.line_step
-    step1 = lines * cols
-
-    def mix1(k, carry):
-        px = pl.ds(pl.multiple_of(k * step1, step1), step1)
-        unit, inverse = layer_norm(conv[px, :], channels)
+    step = lines * cols
+    for k in range(rows // lines):
+        px = slice(k * step, (k + 1) * step)
+        middle = k * step + step // 2
+        units, inverses = layer_norm([conv[k * step : middle, :], conv[middle : (k + 1) * step, :]], channels, ones)
+        unit, inverse = (jnp.concatenate(units, axis=0), jnp.concatenate(inverses, axis=0))
         normed = (unit * gain1).astype(bf16)
         normed1[px, :] = normed
-        value, slope = gelu_parts(dot(normed, up[1]))
+        upstream = pad_lanes(cot[k * lines : (k + 1) * lines].reshape(step, channels))
+        pre, hidden_grad = paired_dot(normed, upstream, forward1[...])
+        value, slope = gelu_parts(pre)
         hidden = value.astype(bf16)
         hidden1[px, :] = hidden
-        branch = dot(hidden, down[1])
+        pre_grad = (hidden_grad * slope).astype(bf16)
+        pre_grad1[px, :] = pre_grad
+        branch, normed_grad = paired_dot(hidden, pre_grad, back1[...])
         for i in range(lines):
             start = (k * lines + i + h) * ext_cols + 4
-            line = x1[pl.ds(start, cols), :] + branch[i * cols : (i + 1) * cols]
+            line = x1[start : start + cols, :] + branch[i * cols : (i + 1) * cols]
             output[k * lines + i] = line[:, :channels].astype(bf16)
-        upstream = pad_lanes(cot[pl.ds(k * lines, lines)].reshape(step1, channels))
-        pre_grad = (dot(upstream, down_t[1]) * slope).astype(bf16)
-        pre_grad1[px, :] = pre_grad
-        normed_grad = dot(pre_grad, up_t[1])
         product = normed_grad * unit
-        gain_sum[...] += jnp.sum(product.reshape(step1 // 8, 8, LANES), axis=0)
-        grad1[px, :] = round16(norm_backward(normed_grad, unit, inverse, gain1, channels))
-        return carry
-
-    lax.fori_loop(0, rows // lines, mix1, 0)
+        gain_sum[...] += jnp.sum(product.reshape(step // 8, 8, LANES), axis=0)
+        grad1[px, :] = round16(norm_backward(normed_grad, unit, inverse, gain1, channels, ones))
 
     takes = [(flat_take(grad1, cols, channels), 2 * h, rows, cols), (image_take(cot), h, rows, cols)]
     write_strips(place, outs, takes, band_combos(dims.row_count))
@@ -468,7 +484,7 @@
 
 def third_kernel(dims, *refs):
     count = len(combos(dims.row_count))
-    (grad1, cot, taps1, gains, up_t, down_t, x0, unit0, inv0, hidden0, slope0) = refs[:11]
+    (grad1, cot, taps1, gains, grad_in0, grad_out0, x0, unit0, inv0, hidden0, slope0) = refs[:11]
     (taps_sum1, up_sum1, down_sum1) = refs[11:14]
     strips = refs[14 : 14 + count]
     (grad0, middle, keep, small_keep, send) = refs[14 + count : 19 + count]
@@ -520,25 +536,26 @@
     gain_sum[...] = jnp.zeros(gain_sum.shape, f32)
     up_acc[...] = jnp.zeros(up_acc.shape, f32)
     down_acc[...] = jnp.zeros(down_acc.shape, f32)
-    step = dims.ext_step
-
-    def mix0(k, carry):
-        px = pl.ds(pl.multiple_of(k * step, 16), step)
-        flow = upstream[px, :].astype(bf16)
-        mine = own[px, :]
-        unit = unit0[px, :].astype(f32)
-        pre_grad = (dot(flow, down_t[0]) * slope0[px, :].astype(f32)).astype(bf16)
-        normed_grad = dot(pre_grad, up_t[0])
-        normed = (unit * gain * mine).astype(bf16)
-        up_acc[...] += dot_leading(normed, pre_grad)
-        down_acc[...] += dot_leading(flow * mine.astype(bf16), hidden0[px, :])
-        product = normed_grad * unit * mine
-        gain_sum[...] += jnp.sum(product.reshape(step // 8, 8, LANES), axis=0)
-        px_frame = pl.ds(frame + pl.multiple_of(k * step, 16), step)
-        grad0[px_frame, :] = round16(norm_backward(normed_grad, unit, inv0[px, :], gain, channels))
-        return carry
-
-    lax.fori_loop(0, dims.ext_pad // step, mix0, 0)
+    ones = diagonal(jnp.ones((LANES, LANES), bf16), jnp.ones((LANES, LANES), bf16))
+    half_px = dims.ext_pad // 2
+    for start, n in pieces(half_px, dims.piece):
+        spans = [(start, n), (half_px + start, n)]
+        flows = [upstream[at : at + n, :].astype(bf16) for at, n in spans]
+        hidden_grads = paired_dot(flows[0], flows[1], grad_in0[...])
+        pre_grads = [
+            (grad * slope0[at : at + n, :].astype(f32)).astype(bf16) for grad, (at, n) in zip(hidden_grads, spans)
+        ]
+        normed_grads = paired_dot(pre_grads[0], pre_grads[1], grad_out0[...])
+        for (at, n), flow, pre_grad, normed_grad in zip(spans, flows, pre_grads, normed_grads):
+            mine = own[at : at + n, :]
+            unit = unit0[at : at + n, :].astype(f32)
+            normed = (unit * gain * mine).astype(bf16)
+            up_acc[...] += dot_leading(normed, pre_grad)
+            down_acc[...] += dot_leading(flow * mine.astype(bf16), hidden0[at : at + n, :])
+            product = normed_grad * unit * mine
+            gain_sum[...] += jnp.sum(product.reshape(n // 8, 8, LANES), axis=0)
+            grad = norm_backward(normed_grad, unit, inv0[at : at + n, :], gain, channels, ones)
+            grad0[pl.ds(frame + at, n), :] = round16(grad)
     clear_outside(place, grad0, dims)
     kernel_sums(
         x0, h * wide + SIDE - h, wide, grad0, h * ext_cols + margin, ext_cols, rows, cols, size, sums
@@ -601,10 +618,20 @@
     split(dims, place, stage, total, merged, keep_out, send)
 
 
-def last_kernel(dims, keep, small, got, kernel_out, gain_out, up_out, down_out):
+def group_kernel(dims, keep, small, got, packed):
     count = keep.shape[0]
-    total = keep[...] + got[0:count, :].astype(f32)
-    merged = small[...] + got[count:, :].astype(f32)
+    total = (keep[...] + got[0:count, :].astype(f32)).astype(bf16)
+    merged = (small[...] + got[count:, :].astype(f32)).astype(bf16)
+    slab = count // 4
+    for k in range(4):
+        packed[k, 0:slab, :] = total[k * slab : (k + 1) * slab]
+        packed[k, slab:, :] = merged
+
+
+def last_kernel(dims, got, kernel_out, gain_out, up_out, down_out):
+    every = (got[0].astype(f32) + got[1].astype(f32)) + (got[2].astype(f32) + got[3].astype(f32))
+    count = 2 * dims.layer_rows
+    total, merged = (every[0:count], every[count:])
     size, channels, half, part = (dims.size, dims.channels, dims.half, dims.part)
     for layer in range(2):
         block = total[layer * dims.layer_rows : layer * dims.layer_rows + part]
@@ -650,8 +677,8 @@
     d.h = d.size // 2
     d.ext_rows, d.ext_cols = (d.rows + (d.h if d.row_count == 2 else 2 * d.h), d.cols + 8)
     d.wide = d.cols + 2 * SIDE
-    d.ext_pad = -(-d.ext_rows * d.ext_cols // 16) * 16
-    d.ext_step = max(s for s in range(16, 700, 16) if d.ext_pad % s == 0)
+    d.ext_pad = -(-d.ext_rows * d.ext_cols // 32) * 32
+    d.piece = 176
     d.line_step = 4
     d.half = d.channels // d.row_count
     d.part = up_weights.shape[2] // d.col_count
@@ -660,7 +687,9 @@
     d.small_rows = -(-2 * (d.size * d.size + 1) // 16) * 16
     d.factor = 1.0 / math.sqrt(d.rows * d.cols * d.count)
     row_bits, col_bits = (d.row_count.bit_length() - 1, d.col_count.bit_length() - 1)
-    d.stages = [("col", 0)] + [("row", b) for b in range(row_bits)] + [("col", b) for b in range(1, col_bits)]
+    d.stages = [("col", 0)] + [("row", b) for b in range(row_bits)] + [("col", b) for b in range(1, col_bits - 2)]
+    d.stages += [("col", col_bits - 1), ("col", col_bits - 2)]
+    d.swaps = len(d.stages) - 2
     return d
 
 
@@ -713,17 +742,10 @@
     )
     other_strips = run(bind(others_kernel, d), strips_of(others, (2 * d.h,)), [], image, *band_strips)
     strips = exchange(band_strips, other_strips, d.row_count, d.col_count)
-    up, down, up_t, down_t, taps0, taps1, gains = run(
+    mixing = [((2 * LANES, 2 * units), bf16), ((2 * units, 2 * LANES), bf16)]
+    forward0, back0, forward1, back1, grad_in0, grad_out0, taps0, taps1, gains = run(
         weights_kernel,
-        [
-            ((2, LANES, units), bf16),
-            ((2, units, LANES), bf16),
-            ((2, units, LANES), bf16),
-            ((2, LANES, units), bf16),
-            taps,
-            taps,
-            (gains.shape, f32),
-        ],
+        mixing * 3 + [taps, taps, (gains.shape, f32)],
         [((2, channels, units), bf16), ((2, channels, units), bf16), ((d.size, d.size, 2, channels), f32)],
         up_weights,
         jnp.swapaxes(down_weights, 1, 2),
@@ -757,10 +779,10 @@
         taps0,
         taps1,
         gains,
-        up,
-        down,
-        up_t,
-        down_t,
+        forward0,
+        back0,
+        forward1,
+        back1,
         *strips,
         busy_us=15,
     )
@@ -807,8 +829,8 @@
         cotangent,
         taps1,
         gains,
-        up_t,
-        down_t,
+        grad_in0,
+        grad_out0,
         x0,
         unit0,
         inv0,
@@ -821,7 +843,7 @@
         busy_us=12,
     )
     axes = ("row", "col")
-    for stage in range(len(d.stages)):
+    for stage in range(d.swaps):
         got = lax.ppermute(send, axes, halving_pairs(d, stage))
         if stage == 1:
             gradient, *ready = run(
@@ -836,7 +858,7 @@
             )
         else:
             ready = []
-        if stage + 1 < len(d.stages):
+        if stage + 1 < d.swaps:
             held //= 2
             keep, sums, send = run(
                 bind(stage_kernel, d, stage + 1),
@@ -847,6 +869,12 @@
                 got,
                 *ready,
             )
+    (packed,) = run(
+        bind(group_kernel, d), [((4, held // 4 + d.small_rows, LANES), bf16)], [], keep, sums, got
+    )
+    stride = d.col_count // 4
+    groups = [[first + stride * k for k in range(4)] for first in range(stride)]
+    got = lax.all_to_all(packed, "col", 0, 0, axis_index_groups=groups, tiled=True)
     kernel_out, gain_out, up_out, down_out = run(
         bind(last_kernel, d),
         [
@@ -856,8 +884,6 @@
             ((2, d.part, d.half), f32),
         ],
         [],
-        keep,
-        sums,
         got,
     )
     kernel_out = jnp.transpose(kernel_out, (2, 0, 1, 3))

time: 60.2 us -> 61.6 us (1.023)
  blocking collectives: 0 us -> 11.5 us
  starting transfers between devices: 20 us -> 14.3 us
  waiting for transfers between devices: 14 us -> 9.9 us
    all_to_all x0 -> x1, blocking collectives: none -> 11.5 us  [per_device(): lax.all_to_all(packed, 'col', 0, 0, axis_index_groups=groups, tiled=True)]
    ppermute x5 -> x3, starting transfers between devices: 8.88 us -> 3.21 us  [per_device(): got = lax.ppermute(send, axes, halving_pairs(d, stage))]
    ppermute x5 -> x3, waiting for transfers between devices: 10.2 us -> 6.2 us  [per_device(): got = lax.ppermute(send, axes, halving_pairs(d, stage))]
    pallas_call x13 -> x12, Pallas kernels: 24.4 us -> 24 us  [run(): pl.pallas_call(kernel, out_shape=shapes, in_specs=[far] * in_hbm + [space...]
  transfers between devices with their start and end apart: 15 -> 13, of which waited for: 7 -> 5; matrix products, arithmetic and copies ran while one was open for 0% -> 0% of each run, Pallas kernels for 8% -> 7%
where the time goes in v5:
time: 61.6 us; the launch traced here: 61.5 us
  Pallas kernels  24 us (39%)
  starting transfers between devices  14.3 us (23%)
  blocking collectives  11.5 us (19%)
  waiting for transfers between devices  9.9 us (16%)
  local copies, waits for them, and re-layouts  0.96 us (2%)
  between operations  0.78 us (1%)
    pallas_call x12, Pallas kernels, run(): pl.pallas_call(kernel, out_shape=shapes, in_specs=[far] * in_hbm + [space...  24 us
    all_to_all x1, blocking collectives, per_device(): lax.all_to_all(packed, 'col', 0, 0, axis_index_groups=groups, tiled=True)  11.5 us
    ppermute x10, starting transfers between devices, exchange(): lax.ppermute(strip, ('row', 'col'), swap_pairs(row_count, col_count, rs,...  11.1 us
    ppermute x3, waiting for transfers between devices, per_device(): got = lax.ppermute(send, axes, halving_pairs(d, stage))  6.2 us
    ppermute x10, waiting for transfers between devices, exchange(): lax.ppermute(strip, ('row', 'col'), swap_pairs(row_count, col_count, rs,...  3.71 us
    ppermute x3, starting transfers between devices, per_device(): got = lax.ppermute(send, axes, halving_pairs(d, stage))  3.21 us
  transfers between devices with their start and end apart: 13, of which 5 were waited for; matrix products, arithmetic and copies ran while one was open for 0% of the time, Pallas kernels for 7%

profile of v5, /device:TPU:0, one launch (start us, length us, event | category | flops | bytes accessed | tf_op | source)
XLA Modules:
  0.0 61.5 jit_solution(12584713040184312770)
XLA Ops:
  0.6 0.9 %copy-done = bf16[16,64,96]{2,1,0:T(8,128)(2,1)S(1)} copy-done((bf16[16,64,96]{2,1,0:T(8,128)(2,1)S(1)}, bf16[16,64,96]{2,1,0:T(8,128)(2,1)}, u32[]{:S(2)}) %copy-start) | copy-done | bytes 196632
  1.6 3.0 %collective-permute-start.2 = (bf16[6,64,96]{2,1,0:T(8,128)(2,1)S(1)}, bf16[6,64,96]{2,1,0:T(8,128)(2,1)S(1)}, u32[]{:S(2)}, u32[]{:S(2)}) collective-permute-start(bf16[6,64,96]{2,1,0:T(8,128)(2,1)S(1)} %get-tuple-element.66.refs_0_), channel_id=1, source_target_pairs={{0,16},{1,17},{2,18},{3,19},{4,20},{5,21},{6,22},{7,23},{8,24},{9,... | collective-permute-start | bytes 221192 | tf_op jit(solution)/shard_map/ppermute | solution.py:55
  4.8 1.2 %collective-permute-start.4 = (bf16[6,8,96]{2,1,0:T(8,128)(2,1)S(1)}, bf16[6,8,96]{2,1,0:T(8,128)(2,1)S(1)}, u32[]{:S(2)}, u32[]{:S(2)}) collective-permute-start(bf16[6,8,96]{2,1,0:T(8,128)(2,1)S(1)} %get-tuple-element.70), channel_id=1, source_target_pairs={{0,16},{1,18},{2,17},{3,20},{4,19},{5,22},{6,21},{7,24},{8,23},{9,... | collective-permute-start | bytes 27656 | tf_op jit(solution)/shard_map/ppermute | solution.py:55
  6.0 1.1 %collective-permute-start = (bf16[16,8,96]{2,1,0:T(8,128)(2,1)S(1)}, bf16[16,8,96]{2,1,0:T(8,128)(2,1)S(1)}, u32[]{:S(2)}, u32[]{:S(2)}) collective-permute-start(bf16[16,8,96]{2,1,0:T(8,128)(2,1)S(1)} %get-tuple-element.67), channel_id=1, source_target_pairs={{0,1},{1,0},{2,3},{3,2},{4,5},{5,4},{6,7},{7,6},{8,9},{9,8},{10,11... | collective-permute-start | bytes 73736 | tf_op jit(solution)/shard_map/ppermute | solution.py:55
  7.0 0.9 %collective-permute-start.1 = (bf16[16,8,96]{2,1,0:T(8,128)(2,1)S(1)}, bf16[16,8,96]{2,1,0:T(8,128)(2,1)S(1)}, u32[]{:S(2)}, u32[]{:S(2)}) collective-permute-start(bf16[16,8,96]{2,1,0:T(8,128)(2,1)S(1)} %get-tuple-element.68), channel_id=1, source_target_pairs={{0,16},{1,2},{2,1},{3,4},{4,3},{5,6},{6,5},{7,8},{8,7},{9,10},{10,... | collective-permute-start | bytes 73736 | tf_op jit(solution)/shard_map/ppermute | solution.py:55
  8.0 0.8 %shard_map.110 = (bf16[256,768]{1,0:T(8,128)(2,1)S(1)}, bf16[768,256]{1,0:T(8,128)(2,1)S(1)}, bf16[256,768]{1,0:T(8,128)(2,1)S(1)}, bf16[768,256]{1,0:T(8,128)(2...) custom-call(bf16[2,96,384]{2,1,0:T(8,128)(2,1)S(1)} %copy-done.2, ...), custom_call_target="tpu_custom_call" | custom-call | flops 2000000000 | bytes 262144 | tf_op jit(solution)/shard_map/pallas_call | solution.py:713
  8.8 2.2 %collective-permute-done.1.refs_10_ = bf16[16,8,96]{2,1,0:T(8,128)(2,1)S(1)} collective-permute-done((bf16[16,8,96]{2,1,0:T(8,128)(2,1)S(1)}, bf16[16,8,96]{2,1,0:T(8,128)(2,1)S(1)}, u32[]{:S(2)}, u32[]{:S(2)}) %collective-permute-start.1) | collective-permute-done | bytes 24608 | tf_op jit(solution)/shard_map/ppermute | solution.py:55
  10.9 11.8 %shard_map.112 = (bf16[16,64,96]{2,1,0:T(8,128)(2,1)}, f32[2240,128]{1,0:T(8,128)S(1)}, f32[1600,128]{1,0:T(8,128)S(1)}, bf16[1376,128]{1,0:T(8,128)(2,1)S(1)}, ...) custom-call(bf16[16,64,96]{2,1,0:T(8,128)(2,1)S(1)} %get-tuple-eleme, ...), custom_call_target="tpu_custom_call" | custom-call | flops 15000000512 | bytes 262144 | tf_op jit(solution)/shard_map/pallas_call | solution.py:713
  22.8 0.9 %collective-permute-start.7 = (bf16[9,64,96]{2,1,0:T(8,128)(2,1)S(1)}, bf16[9,64,96]{2,1,0:T(8,128)(2,1)S(1)}, u32[]{:S(2)}, u32[]{:S(2)}) collective-permute-start(bf16[9,64,96]{2,1,0:T(8,128)(2,1)S(1)} %get-tuple-element.88.refs_0_), channel_id=1, source_target_pairs={{0,16},{1,17},{2,18},{3,19},{4,20},{5,21},{6,22},{7,23},{8,24},{9,... | collective-permute-start | bytes 331784 | tf_op jit(solution)/shard_map/ppermute | solution.py:55
  23.9 1.1 %collective-permute-start.9 = (bf16[9,8,96]{2,1,0:T(8,128)(2,1)S(1)}, bf16[9,8,96]{2,1,0:T(8,128)(2,1)S(1)}, u32[]{:S(2)}, u32[]{:S(2)}) collective-permute-start(bf16[9,8,96]{2,1,0:T(8,128)(2,1)S(1)} %get-tuple-element.92), channel_id=1, source_target_pairs={{0,16},{1,18},{2,17},{3,20},{4,19},{5,22},{6,21},{7,24},{8,23},{9,... | collective-permute-start | bytes 41480 | tf_op jit(solution)/shard_map/ppermute | solution.py:55
  25.0 1.6 %collective-permute-start.5 = (bf16[32,8,96]{2,1,0:T(8,128)(2,1)S(1)}, bf16[32,8,96]{2,1,0:T(8,128)(2,1)S(1)}, u32[]{:S(2)}, u32[]{:S(2)}) collective-permute-start(bf16[32,8,96]{2,1,0:T(8,128)(2,1)S(1)} %get-tuple-element.89), channel_id=1, source_target_pairs={{0,1},{1,0},{2,3},{3,2},{4,5},{5,4},{6,7},{7,6},{8,9},{9,8},{10,11... | collective-permute-start | bytes 147464 | tf_op jit(solution)/shard_map/ppermute | solution.py:55
  26.6 1.1 %collective-permute-start.6 = (bf16[32,8,96]{2,1,0:T(8,128)(2,1)S(1)}, bf16[32,8,96]{2,1,0:T(8,128)(2,1)S(1)}, u32[]{:S(2)}, u32[]{:S(2)}) collective-permute-start(bf16[32,8,96]{2,1,0:T(8,128)(2,1)S(1)} %get-tuple-element.90), channel_id=1, source_target_pairs={{0,16},{1,2},{2,1},{3,4},{4,3},{5,6},{6,5},{7,8},{8,7},{9,10},{10,... | collective-permute-start | bytes 147464 | tf_op jit(solution)/shard_map/ppermute | solution.py:55
  27.7 1.7 %shard_map.113 = (f32[56,128]{1,0:T(8,128)S(1)}, f32[384,128]{1,0:T(8,128)S(1)}, f32[384,128]{1,0:T(8,128)S(1)}) custom-call(f32[1600,128]{1,0:T(8,128)S(1)} %get-tuple-element.80.x1, f32[1024,128]{1,0:T(8,128)S(1)} %get-tuple-element.72.grad1.refs_0_, bf16[1024,128]{1,0:T(8,128)(2,1)S(1)} %get-tuple-element.81.normed1, ...), custom_call_target="tpu_custom_call" | custom-call | flops 3000000000 | bytes 262144 | tf_op jit(solution)/shard_map/pallas_call | solution.py:713
  29.4 1.5 %collective-permute-done.6.refs_15_ = bf16[32,8,96]{2,1,0:T(8,128)(2,1)S(1)} collective-permute-done((bf16[32,8,96]{2,1,0:T(8,128)(2,1)S(1)}, bf16[32,8,96]{2,1,0:T(8,128)(2,1)S(1)}, u32[]{:S(2)}, u32[]{:S(2)}) %collective-permute-start.6) | collective-permute-done | bytes 49184 | tf_op jit(solution)/shard_map/ppermute | solution.py:55
  30.9 6.7 %shard_map.115 = (f32[1600,128]{1,0:T(8,128)S(1)}, f32[1024,128]{1,0:T(8,128)S(1)}, f32[768,128]{1,0:T(8,128)S(1)}, f32[112,128]{1,0:T(8,128)S(1)}, bf16[880,128]{1,0:T(8,128)(2,1)S(1)}) custom-call(f32[1024,128]{1,0:T(8,128)S(1)} %get-tuple-element.72.grad1.refs_0_, bf16[16,64,96]{2,1,0:T(8,128)(2,1)S(1)} %copy-done.1, ...), custom_call_target="tpu_custom_call" | custom-call | flops 12000000000 | bytes 262144 | tf_op jit(solution)/shard_map/pallas_call | solution.py:713
  37.5 0.1 collective-permute-start.10
  37.6 1.4 %collective-permute-done.10.got = bf16[880,128]{1,0:T(8,128)(2,1)S(1)} collective-permute-done((bf16[880,128]{1,0:T(8,128)(2,1)S(1)}, bf16[880,128]{1,0:T(8,128)(2,1)S(1)}, u32[]{:S(2)}, u32[]{:S(2)}) %collective-permute-start.10) | collective-permute-done | bytes 225312 | tf_op jit(solution)/shard_map/ppermute | solution.py:847
  39.2 1.1 %collective-permute-start.11 = (bf16[496,128]{1,0:T(8,128)(2,1)S(1)}, bf16[496,128]{1,0:T(8,128)(2,1)S(1)}, u32[]{:S(2)}, u32[]{:S(2)}) collective-permute-start(bf16[496,128]{1,0:T(8,128)(2,1)S(1)} %get-tuple-element.101), channel_id=1, source_target_pairs={{0,16},{1,17},{2,18},{3,19},{4,20},{5,21},{6,22},{7,23},{8,24},{9,... | collective-permute-start | bytes 380936 | tf_op jit(solution)/shard_map/ppermute | solution.py:847
  40.3 2.1 %shard_map.117 = (bf16[16,64,96]{2,1,0:T(8,128)(2,1)}, f32[8,128]{1,0:T(8,128)S(1)}) custom-call(f32[1600,128]{1,0:T(8,128)S(1)} %get-tuple-element.93.grad0, f32[1024,128]{1,0:T(8,128)S(1)} %get-tuple-element.94.middle, bf16[784,128]{1,0:T(8,128)(2,1)S(1)} %get-tuple-element.59.refs_2_.taps0, f32[112,128]{1,0:T(8,128)S(1)} %get-tuple-element.98.after.small), custom_call_target="tpu_custom_call" | custom-call | flops 3000000000 | bytes 262144 | tf_op jit(solution)/shard_map/pallas_call | solution.py:713
  42.4 2.3 %collective-permute-done.11.got = bf16[496,128]{1,0:T(8,128)(2,1)S(1)} collective-permute-done((bf16[496,128]{1,0:T(8,128)(2,1)S(1)}, bf16[496,128]{1,0:T(8,128)(2,1)S(1)}, u32[]{:S(2)}, u32[]{:S(2)}) %collective-permute-start.11) | collective-permute-done | bytes 127008 | tf_op jit(solution)/shard_map/ppermute | solution.py:847
  44.7 2.0 %collective-permute-start.12 = (bf16[304,128]{1,0:T(8,128)(2,1)S(1)}, bf16[304,128]{1,0:T(8,128)(2,1)S(1)}, u32[]{:S(2)}, u32[]{:S(2)}) collective-permute-start(bf16[304,128]{1,0:T(8,128)(2,1)S(1)} %get-tuple-element.105), channel_id=1, source_target_pairs={{0,2},{1,3},{2,0},{3,1},{4,6},{5,7},{6,4},{7,5},{8,10},{9,11},{10,... | collective-permute-start | bytes 233480 | tf_op jit(solution)/shard_map/ppermute | solution.py:847
  46.7 2.5 %collective-permute-done.12.got = bf16[304,128]{1,0:T(8,128)(2,1)S(1)} collective-permute-done((bf16[304,128]{1,0:T(8,128)(2,1)S(1)}, bf16[304,128]{1,0:T(8,128)(2,1)S(1)}, u32[]{:S(2)}, u32[]{:S(2)}) %collective-permute-start.12) | collective-permute-done | bytes 77856 | tf_op jit(solution)/shard_map/ppermute | solution.py:847
  49.2 11.5 %all_to_all.5.got = bf16[4,160,128]{2,1,0:T(8,128)(2,1)S(1)} all-to-all(bf16[4,160,128]{2,1,0:T(8,128)(2,1)S(1)} %shard_map.119), channel_id=1, replica_groups={{0,4,8,12},{1,5,9,13},{2,6,10,14},{3,7,11,15},{16,20,24,28},{17,21,25,2..., dimensions={0} | all-to-all | bytes 327680 | tf_op jit(solution)/shard_map/all_to_all | solution.py:877
  60.8 0.7 %shard_map.120 = (f32[7,7,2,96]{3,2,1,0:T(2,128)}, f32[2,96]{1,0:T(2,128)}, f32[2,24,48]{2,1,0:T(8,128)}, f32[2,24,48]{2,1,0:T(8,128)}) custom-call(bf16[4,160,128]{2,1,0:T(8,128)(2,1)S(1)} %all_to_all.5.got), custom_call_target="tpu_custom_call" | custom-call | flops 1000000000 | bytes 262144 | tf_op jit(solution)/shard_map/pallas_call | solution.py:713
  (27 shorter events, 0.5 us)
Async XLA Ops:
  0.6 1.0 %copy-start = (bf16[16,64,96]{2,1,0:T(8,128)(2,1)S(1)}, bf16[16,64,96]{2,1,0:T(8,128)(2,1)}, u32[]{:S(2)}) copy-start(bf16[16,64,96]{2,1,0:T(8,128)(2,1)} %image_in.1) | copy-start | bytes 589828
  1.6 9.3 %collective-permute-start.2 = (bf16[6,64,96]{2,1,0:T(8,128)(2,1)S(1)}, bf16[6,64,96]{2,1,0:T(8,128)(2,1)S(1)}, u32[]{:S(2)}, u32[]{:S(2)}) collective-permute-start(bf16[6,64,96]{2,1,0:T(8,128)(2,1)S(1)} %get-tuple-element.66.refs_0_), channel_id=1, source_target_pairs={{0,16},{1,17},{2,18},{3,19},{4,20},{5,21},{6,22},{7,23},{8,24},{9,... | collective-permute-start | bytes 221192 | tf_op jit(solution)/shard_map/ppermute | solution.py:55
  4.7 3.3 %copy-start.2 = (bf16[2,96,384]{2,1,0:T(8,128)(2,1)S(1)}, bf16[2,96,384]{2,1,0:T(8,128)(2,1)}, u32[]{:S(2)}) copy-start(bf16[2,96,384]{2,1,0:T(8,128)(2,1)} %up_in.1) | copy-start | bytes 442372
  4.7 3.3 %copy-start.3 = (bf16[2,384,96]{1,2,0:T(8,128)(2,1)S(1)}, bf16[2,384,96]{1,2,0:T(8,128)(2,1)}, u32[]{:S(2)}) copy-start(bf16[2,384,96]{1,2,0:T(8,128)(2,1)} %param.10) | copy-start | bytes 442372
  4.7 3.3 %copy-start.4 = (f32[2,7,7,96]{3,0,2,1:T(2,128)S(1)}, f32[2,7,7,96]{3,0,2,1:T(2,128)}, u32[]{:S(2)}) copy-start(f32[2,7,7,96]{3,0,2,1:T(2,128)} %param.7) | copy-start | bytes 112900
  4.7 3.3 %copy-start.5 = (f32[2,96]{1,0:T(2,128)S(1)}, f32[2,96]{1,0:T(2,128)}, u32[]{:S(2)}) copy-start(f32[2,96]{1,0:T(2,128)} %gains_in.1) | copy-start | bytes 2308
  4.7 4.0 %collective-permute-start.3 = (bf16[6,8,96]{2,1,0:T(8,128)(2,1)S(1)}, bf16[6,8,96]{2,1,0:T(8,128)(2,1)S(1)}, u32[]{:S(2)}, u32[]{:S(2)}) collective-permute-start(bf16[6,8,96]{2,1,0:T(8,128)(2,1)S(1)} %get-tuple-element.69), channel_id=1, source_target_pairs={{0,17},{1,16},{2,19},{3,18},{4,21},{5,20},{6,23},{7,22},{8,25},{9,... | collective-permute-start | bytes 27656 | tf_op jit(solution)/shard_map/ppermute | solution.py:55
  4.8 4.0 %collective-permute-start.4 = (bf16[6,8,96]{2,1,0:T(8,128)(2,1)S(1)}, bf16[6,8,96]{2,1,0:T(8,128)(2,1)S(1)}, u32[]{:S(2)}, u32[]{:S(2)}) collective-permute-start(bf16[6,8,96]{2,1,0:T(8,128)(2,1)S(1)} %get-tuple-element.70), channel_id=1, source_target_pairs={{0,16},{1,18},{2,17},{3,20},{4,19},{5,22},{6,21},{7,24},{8,23},{9,... | collective-permute-start | bytes 27656 | tf_op jit(solution)/shard_map/ppermute | solution.py:55
  6.0 2.8 %collective-permute-start = (bf16[16,8,96]{2,1,0:T(8,128)(2,1)S(1)}, bf16[16,8,96]{2,1,0:T(8,128)(2,1)S(1)}, u32[]{:S(2)}, u32[]{:S(2)}) collective-permute-start(bf16[16,8,96]{2,1,0:T(8,128)(2,1)S(1)} %get-tuple-element.67), channel_id=1, source_target_pairs={{0,1},{1,0},{2,3},{3,2},{4,5},{5,4},{6,7},{7,6},{8,9},{9,8},{10,11... | collective-permute-start | bytes 73736 | tf_op jit(solution)/shard_map/ppermute | solution.py:55
  7.0 3.9 %collective-permute-start.1 = (bf16[16,8,96]{2,1,0:T(8,128)(2,1)S(1)}, bf16[16,8,96]{2,1,0:T(8,128)(2,1)S(1)}, u32[]{:S(2)}, u32[]{:S(2)}) collective-permute-start(bf16[16,8,96]{2,1,0:T(8,128)(2,1)S(1)} %get-tuple-element.68), channel_id=1, source_target_pairs={{0,16},{1,2},{2,1},{3,4},{4,3},{5,6},{6,5},{7,8},{8,7},{9,10},{10,... | collective-permute-start | bytes 73736 | tf_op jit(solution)/shard_map/ppermute | solution.py:55
  8.0 3.0 %copy-start.1 = (bf16[16,64,96]{2,1,0:T(8,128)(2,1)S(1)}, bf16[16,64,96]{2,1,0:T(8,128)(2,1)}, u32[]{:S(2)}) copy-start(bf16[16,64,96]{2,1,0:T(8,128)(2,1)} %refs_1_.3) | copy-start | bytes 589828
  22.8 8.1 %collective-permute-start.7 = (bf16[9,64,96]{2,1,0:T(8,128)(2,1)S(1)}, bf16[9,64,96]{2,1,0:T(8,128)(2,1)S(1)}, u32[]{:S(2)}, u32[]{:S(2)}) collective-permute-start(bf16[9,64,96]{2,1,0:T(8,128)(2,1)S(1)} %get-tuple-element.88.refs_0_), channel_id=1, source_target_pairs={{0,16},{1,17},{2,18},{3,19},{4,20},{5,21},{6,22},{7,23},{8,24},{9,... | collective-permute-start | bytes 331784 | tf_op jit(solution)/shard_map/ppermute | solution.py:55
  23.8 5.6 %collective-permute-start.8 = (bf16[9,8,96]{2,1,0:T(8,128)(2,1)S(1)}, bf16[9,8,96]{2,1,0:T(8,128)(2,1)S(1)}, u32[]{:S(2)}, u32[]{:S(2)}) collective-permute-start(bf16[9,8,96]{2,1,0:T(8,128)(2,1)S(1)} %get-tuple-element.91), channel_id=1, source_target_pairs={{0,17},{1,16},{2,19},{3,18},{4,21},{5,20},{6,23},{7,22},{8,25},{9,... | collective-permute-start | bytes 41480 | tf_op jit(solution)/shard_map/ppermute | solution.py:55
  23.9 5.5 %collective-permute-start.9 = (bf16[9,8,96]{2,1,0:T(8,128)(2,1)S(1)}, bf16[9,8,96]{2,1,0:T(8,128)(2,1)S(1)}, u32[]{:S(2)}, u32[]{:S(2)}) collective-permute-start(bf16[9,8,96]{2,1,0:T(8,128)(2,1)S(1)} %get-tuple-element.92), channel_id=1, source_target_pairs={{0,16},{1,18},{2,17},{3,20},{4,19},{5,22},{6,21},{7,24},{8,23},{9,... | collective-permute-start | bytes 41480 | tf_op jit(solution)/shard_map/ppermute | solution.py:55
  25.0 4.4 %collective-permute-start.5 = (bf16[32,8,96]{2,1,0:T(8,128)(2,1)S(1)}, bf16[32,8,96]{2,1,0:T(8,128)(2,1)S(1)}, u32[]{:S(2)}, u32[]{:S(2)}) collective-permute-start(bf16[32,8,96]{2,1,0:T(8,128)(2,1)S(1)} %get-tuple-element.89), channel_id=1, source_target_pairs={{0,1},{1,0},{2,3},{3,2},{4,5},{5,4},{6,7},{7,6},{8,9},{9,8},{10,11... | collective-permute-start | bytes 147464 | tf_op jit(solution)/shard_map/ppermute | solution.py:55
  26.6 4.3 %collective-permute-start.6 = (bf16[32,8,96]{2,1,0:T(8,128)(2,1)S(1)}, bf16[32,8,96]{2,1,0:T(8,128)(2,1)S(1)}, u32[]{:S(2)}, u32[]{:S(2)}) collective-permute-start(bf16[32,8,96]{2,1,0:T(8,128)(2,1)S(1)} %get-tuple-element.90), channel_id=1, source_target_pairs={{0,16},{1,2},{2,1},{3,4},{4,3},{5,6},{6,5},{7,8},{8,7},{9,10},{10,... | collective-permute-start | bytes 147464 | tf_op jit(solution)/shard_map/ppermute | solution.py:55
  37.5 1.5 %collective-permute-start.10 = (bf16[880,128]{1,0:T(8,128)(2,1)S(1)}, bf16[880,128]{1,0:T(8,128)(2,1)S(1)}, u32[]{:S(2)}, u32[]{:S(2)}) collective-permute-start(bf16[880,128]{1,0:T(8,128)(2,1)S(1)} %get-tuple-element.97), channel_id=1, source_target_pairs={{0,1},{1,0},{2,3},{3,2},{4,5},{5,4},{6,7},{7,6},{8,9},{9,8},{10,11... | collective-permute-start | bytes 675848 | tf_op jit(solution)/shard_map/ppermute | solution.py:847
  39.2 5.5 %collective-permute-start.11 = (bf16[496,128]{1,0:T(8,128)(2,1)S(1)}, bf16[496,128]{1,0:T(8,128)(2,1)S(1)}, u32[]{:S(2)}, u32[]{:S(2)}) collective-permute-start(bf16[496,128]{1,0:T(8,128)(2,1)S(1)} %get-tuple-element.101), channel_id=1, source_target_pairs={{0,16},{1,17},{2,18},{3,19},{4,20},{5,21},{6,22},{7,23},{8,24},{9,... | collective-permute-start | bytes 380936 | tf_op jit(solution)/shard_map/ppermute | solution.py:847
  44.7 4.5 %collective-permute-start.12 = (bf16[304,128]{1,0:T(8,128)(2,1)S(1)}, bf16[304,128]{1,0:T(8,128)(2,1)S(1)}, u32[]{:S(2)}, u32[]{:S(2)}) collective-permute-start(bf16[304,128]{1,0:T(8,128)(2,1)S(1)} %get-tuple-element.105), channel_id=1, source_target_pairs={{0,2},{1,3},{2,0},{3,1},{4,6},{5,7},{6,4},{7,5},{8,10},{9,11},{10,... | collective-permute-start | bytes 233480 | tf_op jit(solution)/shard_map/ppermute | solution.py:847

commit v6 on v5

--- a/solution.py
+++ b/solution.py
@@ -466,7 +466,10 @@
             flat[(r + 1) * ext_cols - margin : (r + 1) * ext_cols, :] = jnp.zeros((margin, LANES), f32)
 
 
-def sums_kernel(dims, x1, grad1, normed1, pre_grad1, hidden1, cot, gain_part, taps_sum, up_sum, down_sum, sums):
+def sums_kernel(
+    dims, x1, grad1, normed1, pre_grad1, hidden1, cot, gain_part, final, taps_sum, up_sum, down_sum, output, sums
+):
+    output[...] = final[...]
     kernel_sums(x1, 1, dims.ext_cols, grad1, 0, dims.cols, dims.rows, dims.cols, dims.size, sums)
     store_sums(dims, sums, gain_part[...], taps_sum)
     upstream = pad_lanes(cot[...].reshape(dims.rows * dims.cols, dims.channels))
@@ -596,42 +599,54 @@
 
         lax.fori_loop(0, dims.col_count, slab, 0)
 
-    split(dims, place, 0, slabs, merged, keep, send)
-
-
-def split(dims, place, stage, slabs, merged, keep, send):
-    count = slabs.shape[0] // 2
-    axis, bit = dims.stages[stage]
-    mine = lax.rem(lax.div(lax.axis_index(axis), 1 << bit), 2)
+    split(dims, 0, slabs, merged, keep, (send,))
+
+
+def split(dims, stage, slabs, merged, keep, sends):
+    group = dims.groups[stage]
+    count = slabs.shape[0] >> len(group)
+    mine = 0
+    for axis, bit in group:
+        mine = mine * 2 + lax.rem(lax.div(lax.axis_index(axis), 1 << bit), 2)
     keep[...] = slabs[pl.ds(pl.multiple_of(mine * count, 16), count), :]
-    send[0:count, :] = slabs[pl.ds(pl.multiple_of((1 - mine) * count, 16), count), :].astype(bf16)
-    send[count:, :] = merged
-
-
-def stage_kernel(dims, stage, keep, small, got, *refs):
-    keep_out, small_out, send, total = refs[-4:]
-    place = Place(dims.row_count, dims.col_count)
+    for mask, send in enumerate(sends, 1):
+        other = 0
+        for j in range(len(group)):
+            weight = 1 << j
+            digit = lax.rem(lax.div(mine, weight), 2)
+            other = other + weight * (1 - digit if mask & weight else digit)
+        send[0:count, :] = slabs[pl.ds(pl.multiple_of(other * count, 16), count), :].astype(bf16)
+        send[count:, :] = merged
+
+
+def gather_up(keep, small, gots):
     count = keep.shape[0]
-    total[...] = keep[...] + got[0:count, :].astype(f32)
-    merged = (small[...] + got[count:, :].astype(f32)).astype(bf16)
+    slabs = [keep[...]] + [got[0:count, :].astype(f32) for got in gots]
+    sums = [small[...]] + [got[count:, :].astype(f32) for got in gots]
+    if len(gots) == 1:
+        return (slabs[0] + slabs[1], sums[0] + sums[1])
+    return tuple((x[0] + x[1]) + (x[2] + x[3]) for x in (slabs, sums))
+
+
+def stage_kernel(dims, stage, keep, small, *refs):
+    before, after = (len_sends(dims.groups[stage - 1]), len_sends(dims.groups[stage]))
+    gots = refs[:before]
+    keep_out, small_out = refs[-3 - after : -1 - after]
+    sends, total = (refs[-1 - after : -1], refs[-1])
+    slabs, merged = gather_up(keep, small, gots)
+    total[...] = slabs
+    merged = merged.astype(bf16)
     small_out[...] = merged.astype(f32)
-    split(dims, place, stage, total, merged, keep_out, send)
-
-
-def group_kernel(dims, keep, small, got, packed):
-    count = keep.shape[0]
-    total = (keep[...] + got[0:count, :].astype(f32)).astype(bf16)
-    merged = (small[...] + got[count:, :].astype(f32)).astype(bf16)
-    slab = count // 4
-    for k in range(4):
-        packed[k, 0:slab, :] = total[k * slab : (k + 1) * slab]
-        packed[k, slab:, :] = merged
-
-
-def last_kernel(dims, got, kernel_out, gain_out, up_out, down_out):
-    every = (got[0].astype(f32) + got[1].astype(f32)) + (got[2].astype(f32) + got[3].astype(f32))
-    count = 2 * dims.layer_rows
-    total, merged = (every[0:count], every[count:])
+    split(dims, stage, total, merged, keep_out, sends)
+
+
+def len_sends(group):
+    return (1 << len(group)) - 1
+
+
+def last_kernel(dims, keep, small, *refs):
+    gots, (kernel_out, gain_out, up_out, down_out) = (refs[:-4], refs[-4:])
+    total, merged = gather_up(keep, small, gots)
     size, channels, half, part = (dims.size, dims.channels, dims.half, dims.part)
     for layer in range(2):
         block = total[layer * dims.layer_rows : layer * dims.layer_rows + part]
@@ -687,19 +702,21 @@
     d.small_rows = -(-2 * (d.size * d.size + 1) // 16) * 16
     d.factor = 1.0 / math.sqrt(d.rows * d.cols * d.count)
     row_bits, col_bits = (d.row_count.bit_length() - 1, d.col_count.bit_length() - 1)
-    d.stages = [("col", 0)] + [("row", b) for b in range(row_bits)] + [("col", b) for b in range(1, col_bits - 2)]
-    d.stages += [("col", col_bits - 1), ("col", col_bits - 2)]
-    d.swaps = len(d.stages) - 2
+    bits = [("row", b) for b in range(row_bits)] + [("col", b) for b in range(1, col_bits)]
+    d.groups = [[("col", 0)]] + [bits[i : i + 2] for i in range(0, len(bits), 2)]
+    d.stages = [bit for group in d.groups for bit in group]
     return d
 
 
-def halving_pairs(d, stage):
-    axis, bit = d.stages[stage]
+def swap_by(d, group, mask):
+    flip = {"row": 0, "col": 0}
+    for j, (axis, bit) in enumerate(group):
+        if mask >> (len(group) - 1 - j) & 1:
+            flip[axis] |= 1 << bit
     pairs = []
     for r in range(d.row_count):
         for c in range(d.col_count):
-            pr, pc = (r ^ (1 << bit), c) if axis == "row" else (r, c ^ (1 << bit))
-            pairs.append((r * d.col_count + c, pr * d.col_count + pc))
+            pairs.append((r * d.col_count + c, (r ^ flip["row"]) * d.col_count + (c ^ flip["col"])))
     return pairs
 
 
@@ -786,16 +803,16 @@
         *strips,
         busy_us=15,
     )
-    (output, x0, x1, unit0, inv0, hidden0, slope0, grad1, normed1, pre_grad1, hidden1, gain_part) = first[:12]
+    (final, x0, x1, unit0, inv0, hidden0, slope0, grad1, normed1, pre_grad1, hidden1, gain_part) = first[:12]
     band_strips = first[12:]
     other_strips = run(
         bind(grad_others_kernel, d), strips_of(others, (2 * d.h, d.h)), [], grad1, cotangent, *band_strips
     )
     strips = exchange(band_strips, other_strips, d.row_count, d.col_count)
 
-    taps_sum1, up_sum1, down_sum1 = run(
+    taps_sum1, up_sum1, down_sum1, output = run(
         bind(sums_kernel, d),
-        [((sums_rows, LANES), f32), ((units, LANES), f32), ((units, LANES), f32)],
+        [((sums_rows, LANES), f32), ((units, LANES), f32), ((units, LANES), f32), (image.shape, bf16)],
         [tap_sums],
         x1,
         grad1,
@@ -804,6 +821,7 @@
         hidden1,
         cotangent,
         gain_part,
+        final,
         busy_us=3,
     )
 
@@ -843,8 +861,10 @@
         busy_us=12,
     )
     axes = ("row", "col")
-    for stage in range(d.swaps):
-        got = lax.ppermute(send, axes, halving_pairs(d, stage))
+    sends = [send]
+    for stage, group in enumerate(d.groups):
+        gots = [lax.ppermute(x, axes, swap_by(d, group, mask)) for mask, x in enumerate(sends, 1)]
+        ready = []
         if stage == 1:
             gradient, *ready = run(
                 bind(image_kernel, d),
@@ -856,25 +876,18 @@
                 sums,
                 busy_us=3,
             )
-        else:
-            ready = []
-        if stage + 1 < d.swaps:
-            held //= 2
-            keep, sums, send = run(
+        if stage + 1 < len(d.groups):
+            after = d.groups[stage + 1]
+            whole, held = (held, held >> len(after))
+            keep, sums, *sends = run(
                 bind(stage_kernel, d, stage + 1),
-                [((held, LANES), f32), small, ((held + d.small_rows, LANES), bf16)],
-                [((2 * held, LANES), f32)],
+                [((held, LANES), f32), small] + [((held + d.small_rows, LANES), bf16)] * len_sends(after),
+                [((whole, LANES), f32)],
                 keep,
                 sums,
-                got,
+                *gots,
                 *ready,
             )
-    (packed,) = run(
-        bind(group_kernel, d), [((4, held // 4 + d.small_rows, LANES), bf16)], [], keep, sums, got
-    )
-    stride = d.col_count // 4
-    groups = [[first + stride * k for k in range(4)] for first in range(stride)]
-    got = lax.all_to_all(packed, "col", 0, 0, axis_index_groups=groups, tiled=True)
     kernel_out, gain_out, up_out, down_out = run(
         bind(last_kernel, d),
         [
@@ -884,7 +897,9 @@
             ((2, d.part, d.half), f32),
         ],
         [],
-        got,
+        keep,
+        sums,
+        *gots,
     )
     kernel_out = jnp.transpose(kernel_out, (2, 0, 1, 3))
     return (output, gradient, kernel_out, gain_out, jnp.swapaxes(up_out, 1, 2), down_out)

time: 61.6 us -> 57.2 us (0.929)
  blocking collectives: 11.5 us -> 0 us
  starting transfers between devices: 14.3 us -> 19.3 us
  waiting for transfers between devices: 9.9 us -> 11.8 us
    all_to_all x1 -> x0, blocking collectives: 11.5 us -> none  [per_device(): lax.all_to_all(packed, 'col', 0, 0, axis_index_groups=groups, tiled=True)]
    ppermute x3 -> x7, starting transfers between devices: 3.21 us -> 8.15 us  [per_device(): lax.ppermute(x, axes, swap_by(d, group, mask))]
    ppermute x3 -> x7, waiting for transfers between devices: 6.2 us -> 8.77 us  [per_device(): lax.ppermute(x, axes, swap_by(d, group, mask))]
    ppermute x10, waiting for transfers between devices: 3.71 us -> 3.04 us  [exchange(): lax.ppermute(strip, ('row', 'col'), swap_pairs(row_count, col_count, rs,...]
    pallas_call x12 -> x11, Pallas kernels: 24 us -> 24.2 us  [run(): pl.pallas_call(kernel, out_shape=shapes, in_specs=[far] * in_hbm + [space...]
  transfers between devices with their start and end apart: 13 -> 17, of which waited for: 5 -> 8; matrix products, arithmetic and copies ran while one was open for 0% -> 0% of each run, Pallas kernels for 7% -> 9%
where the time goes in v6:
time: 57.2 us; the launch traced here: 57.1 us
  Pallas kernels  24.2 us (42%)
  starting transfers between devices  19.3 us (34%)
  waiting for transfers between devices  11.8 us (21%)
  local copies, waits for them, and re-layouts  0.96 us (2%)
  between operations  0.76 us (1%)
    pallas_call x11, Pallas kernels, run(): pl.pallas_call(kernel, out_shape=shapes, in_specs=[far] * in_hbm + [space...  24.2 us
    ppermute x10, starting transfers between devices, exchange(): lax.ppermute(strip, ('row', 'col'), swap_pairs(row_count, col_count, rs,...  11.1 us
    ppermute x7, waiting for transfers between devices, per_device(): lax.ppermute(x, axes, swap_by(d, group, mask))  8.77 us
    ppermute x7, starting transfers between devices, per_device(): lax.ppermute(x, axes, swap_by(d, group, mask))  8.15 us
    ppermute x10, waiting for transfers between devices, exchange(): lax.ppermute(strip, ('row', 'col'), swap_pairs(row_count, col_count, rs,...  3.04 us
  transfers between devices with their start and end apart: 17, of which 8 were waited for; matrix products, arithmetic and copies ran while one was open for 0% of the time, Pallas kernels for 9%

profile of v6, /device:TPU:0, one launch (start us, length us, event | category | flops | bytes accessed | tf_op | source)
XLA Modules:
  0.0 57.1 jit_solution(7421894025728164848)
XLA Ops:
  0.6 0.9 %copy-done = bf16[16,64,96]{2,1,0:T(8,128)(2,1)S(1)} copy-done((bf16[16,64,96]{2,1,0:T(8,128)(2,1)S(1)}, bf16[16,64,96]{2,1,0:T(8,128)(2,1)}, u32[]{:S(2)}) %copy-start) | copy-done | bytes 196632
  1.6 3.0 %collective-permute-start.2 = (bf16[6,64,96]{2,1,0:T(8,128)(2,1)S(1)}, bf16[6,64,96]{2,1,0:T(8,128)(2,1)S(1)}, u32[]{:S(2)}, u32[]{:S(2)}) collective-permute-start(bf16[6,64,96]{2,1,0:T(8,128)(2,1)S(1)} %get-tuple-element.71.refs_0_), channel_id=1, source_target_pairs={{0,16},{1,17},{2,18},{3,19},{4,20},{5,21},{6,22},{7,23},{8,24},{9,... | collective-permute-start | bytes 221192 | tf_op jit(solution)/shard_map/ppermute | solution.py:55
  4.8 1.2 %collective-permute-start.4 = (bf16[6,8,96]{2,1,0:T(8,128)(2,1)S(1)}, bf16[6,8,96]{2,1,0:T(8,128)(2,1)S(1)}, u32[]{:S(2)}, u32[]{:S(2)}) collective-permute-start(bf16[6,8,96]{2,1,0:T(8,128)(2,1)S(1)} %get-tuple-element.75), channel_id=1, source_target_pairs={{0,16},{1,18},{2,17},{3,20},{4,19},{5,22},{6,21},{7,24},{8,23},{9,... | collective-permute-start | bytes 27656 | tf_op jit(solution)/shard_map/ppermute | solution.py:55
  6.0 1.1 %collective-permute-start = (bf16[16,8,96]{2,1,0:T(8,128)(2,1)S(1)}, bf16[16,8,96]{2,1,0:T(8,128)(2,1)S(1)}, u32[]{:S(2)}, u32[]{:S(2)}) collective-permute-start(bf16[16,8,96]{2,1,0:T(8,128)(2,1)S(1)} %get-tuple-element.72), channel_id=1, source_target_pairs={{0,1},{1,0},{2,3},{3,2},{4,5},{5,4},{6,7},{7,6},{8,9},{9,8},{10,11... | collective-permute-start | bytes 73736 | tf_op jit(solution)/shard_map/ppermute | solution.py:55
  7.0 0.9 %collective-permute-start.1 = (bf16[16,8,96]{2,1,0:T(8,128)(2,1)S(1)}, bf16[16,8,96]{2,1,0:T(8,128)(2,1)S(1)}, u32[]{:S(2)}, u32[]{:S(2)}) collective-permute-start(bf16[16,8,96]{2,1,0:T(8,128)(2,1)S(1)} %get-tuple-element.73), channel_id=1, source_target_pairs={{0,16},{1,2},{2,1},{3,4},{4,3},{5,6},{6,5},{7,8},{8,7},{9,10},{10,... | collective-permute-start | bytes 73736 | tf_op jit(solution)/shard_map/ppermute | solution.py:55
  8.8 2.2 %collective-permute-done.1.refs_10_ = bf16[16,8,96]{2,1,0:T(8,128)(2,1)S(1)} collective-permute-done((bf16[16,8,96]{2,1,0:T(8,128)(2,1)S(1)}, bf16[16,8,96]{2,1,0:T(8,128)(2,1)S(1)}, u32[]{:S(2)}, u32[]{:S(2)}) %collective-permute-start.1) | collective-permute-done | bytes 24608 | tf_op jit(solution)/shard_map/ppermute | solution.py:55
  10.9 11.4 %shard_map.112 = (bf16[16,64,96]{2,1,0:T(8,128)(2,1)S(1)}, f32[2240,128]{1,0:T(8,128)S(1)}, f32[1600,128]{1,0:T(8,128)S(1)}, bf16[1376,128]{1,0:T(8,128)(2,1)S(1...) custom-call(bf16[16,64,96]{2,1,0:T(8,128)(2,1)S(1)} %get-tuple-eleme, ...), custom_call_target="tpu_custom_call" | custom-call | flops 15000000512 | bytes 262144 | tf_op jit(solution)/shard_map/pallas_call | solution.py:730
  22.4 1.0 %collective-permute-start.7 = (bf16[9,64,96]{2,1,0:T(8,128)(2,1)S(1)}, bf16[9,64,96]{2,1,0:T(8,128)(2,1)S(1)}, u32[]{:S(2)}, u32[]{:S(2)}) collective-permute-start(bf16[9,64,96]{2,1,0:T(8,128)(2,1)S(1)} %get-tuple-element.94.refs_0_), channel_id=1, source_target_pairs={{0,16},{1,17},{2,18},{3,19},{4,20},{5,21},{6,22},{7,23},{8,24},{9,... | collective-permute-start | bytes 331784 | tf_op jit(solution)/shard_map/ppermute | solution.py:55
  23.5 1.2 %collective-permute-start.9 = (bf16[9,8,96]{2,1,0:T(8,128)(2,1)S(1)}, bf16[9,8,96]{2,1,0:T(8,128)(2,1)S(1)}, u32[]{:S(2)}, u32[]{:S(2)}) collective-permute-start(bf16[9,8,96]{2,1,0:T(8,128)(2,1)S(1)} %get-tuple-element.98), channel_id=1, source_target_pairs={{0,16},{1,18},{2,17},{3,20},{4,19},{5,22},{6,21},{7,24},{8,23},{9,... | collective-permute-start | bytes 41480 | tf_op jit(solution)/shard_map/ppermute | solution.py:55
  24.7 1.6 %collective-permute-start.5 = (bf16[32,8,96]{2,1,0:T(8,128)(2,1)S(1)}, bf16[32,8,96]{2,1,0:T(8,128)(2,1)S(1)}, u32[]{:S(2)}, u32[]{:S(2)}) collective-permute-start(bf16[32,8,96]{2,1,0:T(8,128)(2,1)S(1)} %get-tuple-element.95), channel_id=1, source_target_pairs={{0,1},{1,0},{2,3},{3,2},{4,5},{5,4},{6,7},{7,6},{8,9},{9,8},{10,11... | collective-permute-start | bytes 147464 | tf_op jit(solution)/shard_map/ppermute | solution.py:55
  26.2 1.1 %collective-permute-start.6 = (bf16[32,8,96]{2,1,0:T(8,128)(2,1)S(1)}, bf16[32,8,96]{2,1,0:T(8,128)(2,1)S(1)}, u32[]{:S(2)}, u32[]{:S(2)}) collective-permute-start(bf16[32,8,96]{2,1,0:T(8,128)(2,1)S(1)} %get-tuple-element.96), channel_id=1, source_target_pairs={{0,16},{1,2},{2,1},{3,4},{4,3},{5,6},{6,5},{7,8},{8,7},{9,10},{10,... | collective-permute-start | bytes 147464 | tf_op jit(solution)/shard_map/ppermute | solution.py:55
  27.3 2.3 %shard_map.113 = (f32[56,128]{1,0:T(8,128)S(1)}, f32[384,128]{1,0:T(8,128)S(1)}, f32[384,128]{1,0:T(8,128)S(1)}, bf16[16,64,96]{2,1,0:T(8,128)(2,1)}) custom-call(f32[1600,128]{1,0:T(8,128)S(1)} %get-tuple-element.76.x1, f32[1024,128]{1,0:T(8,128)S(1)} %get-tuple-element.77.grad1.refs_0_, bf16[1024,128]{1,0:T(8,128)(2,1)S(1)} %get-tuple-element.78.normed1, ...), custom_call_target="tpu_custom_call" | custom-call | flops 3000000000 | bytes 262144 | tf_op jit(solution)/shard_map/pallas_call | solution.py:730
  29.7 0.8 %collective-permute-done.6.refs_15_ = bf16[32,8,96]{2,1,0:T(8,128)(2,1)S(1)} collective-permute-done((bf16[32,8,96]{2,1,0:T(8,128)(2,1)S(1)}, bf16[32,8,96]{2,1,0:T(8,128)(2,1)S(1)}, u32[]{:S(2)}, u32[]{:S(2)}) %collective-permute-start.6) | collective-permute-done | bytes 49184 | tf_op jit(solution)/shard_map/ppermute | solution.py:55
  30.5 6.7 %shard_map.115 = (f32[1600,128]{1,0:T(8,128)S(1)}, f32[1024,128]{1,0:T(8,128)S(1)}, f32[768,128]{1,0:T(8,128)S(1)}, f32[112,128]{1,0:T(8,128)S(1)}, bf16[880,128]{1,0:T(8,128)(2,1)S(1)}) custom-call(f32[1024,128]{1,0:T(8,128)S(1)} %get-tuple-element.77.grad1.refs_0_, bf16[16,64,96]{2,1,0:T(8,128)(2,1)S(1)} %copy-done.1, ...), custom_call_target="tpu_custom_call" | custom-call | flops 12000000000 | bytes 262144 | tf_op jit(solution)/shard_map/pallas_call | solution.py:730
  37.3 1.4 %collective-permute-done.10.refs_0_ = bf16[880,128]{1,0:T(8,128)(2,1)S(1)} collective-permute-done((bf16[880,128]{1,0:T(8,128)(2,1)S(1)}, bf16[880,128]{1,0:T(8,128)(2,1)S(1)}, u32[]{:S(2)}, u32[]{:S(2)}) %collective-permute-start.10) | collective-permute-done | bytes 225312 | tf_op jit(solution)/shard_map/ppermute | solution.py:866
  38.8 1.8 %collective-permute-start.11 = (bf16[304,128]{1,0:T(8,128)(2,1)S(1)}, bf16[304,128]{1,0:T(8,128)(2,1)S(1)}, u32[]{:S(2)}, u32[]{:S(2)}) collective-permute-start(bf16[304,128]{1,0:T(8,128)(2,1)S(1)} %get-tuple-element.107), channel_id=1, source_target_pairs={{0,2},{1,3},{2,0},{3,1},{4,6},{5,7},{6,4},{7,5},{8,10},{9,11},{10,... | collective-permute-start | bytes 233480 | tf_op jit(solution)/shard_map/ppermute | solution.py:866
  40.6 1.3 %collective-permute-start.12 = (bf16[304,128]{1,0:T(8,128)(2,1)S(1)}, bf16[304,128]{1,0:T(8,128)(2,1)S(1)}, u32[]{:S(2)}, u32[]{:S(2)}) collective-permute-start(bf16[304,128]{1,0:T(8,128)(2,1)S(1)} %get-tuple-element.108), channel_id=1, source_target_pairs={{0,16},{1,17},{2,18},{3,19},{4,20},{5,21},{6,22},{7,23},{8,24},{9,... | collective-permute-start | bytes 233480 | tf_op jit(solution)/shard_map/ppermute | solution.py:866
  42.4 2.1 %shard_map.117 = (bf16[16,64,96]{2,1,0:T(8,128)(2,1)}, f32[8,128]{1,0:T(8,128)S(1)}) custom-call(f32[1600,128]{1,0:T(8,128)S(1)} %get-tuple-element.99.grad0, f32[1024,128]{1,0:T(8,128)S(1)} %get-tuple-element.100.middle, bf16[784,128]{1,0:T(8,128)(2,1)S(1)} %get-tuple-element.64.refs_2_.taps0, f32[112,128]{1,0:T(8,128)S(1)} %get-tuple-element.104.after.small), custom_call_target="tpu_custom_call" | custom-call | flops 3000000000 | bytes 262144 | tf_op jit(solution)/shard_map/pallas_call | solution.py:730
  44.5 1.3 %collective-permute-done.12.refs_1_ = bf16[304,128]{1,0:T(8,128)(2,1)S(1)} collective-permute-done((bf16[304,128]{1,0:T(8,128)(2,1)S(1)}, bf16[304,128]{1,0:T(8,128)(2,1)S(1)}, u32[]{:S(2)}, u32[]{:S(2)}) %collective-permute-start.12) | collective-permute-done | bytes 77856 | tf_op jit(solution)/shard_map/ppermute | solution.py:866
  45.8 1.4 %collective-permute-done.13.refs_2_ = bf16[304,128]{1,0:T(8,128)(2,1)S(1)} collective-permute-done((bf16[304,128]{1,0:T(8,128)(2,1)S(1)}, bf16[304,128]{1,0:T(8,128)(2,1)S(1)}, u32[]{:S(2)}, u32[]{:S(2)}) %collective-permute-start.13) | collective-permute-done | bytes 77856 | tf_op jit(solution)/shard_map/ppermute | solution.py:866
  47.2 2.7 %collective-permute-start.14 = (bf16[160,128]{1,0:T(8,128)(2,1)S(1)}, bf16[160,128]{1,0:T(8,128)(2,1)S(1)}, u32[]{:S(2)}, u32[]{:S(2)}) collective-permute-start(bf16[160,128]{1,0:T(8,128)(2,1)S(1)} %get-tuple-element.113), channel_id=1, source_target_pairs={{0,8},{1,9},{2,10},{3,11},{4,12},{5,13},{6,14},{7,15},{8,0},{9,1},... | collective-permute-start | bytes 122888 | tf_op jit(solution)/shard_map/ppermute | solution.py:866
  50.6 1.1 %collective-permute-start.16 = (bf16[160,128]{1,0:T(8,128)(2,1)S(1)}, bf16[160,128]{1,0:T(8,128)(2,1)S(1)}, u32[]{:S(2)}, u32[]{:S(2)}) collective-permute-start(bf16[160,128]{1,0:T(8,128)(2,1)S(1)} %get-tuple-element.115), channel_id=1, source_target_pairs={{0,12},{1,13},{2,14},{3,15},{4,8},{5,9},{6,10},{7,11},{8,4},{9,5},... | collective-permute-start | bytes 122888 | tf_op jit(solution)/shard_map/ppermute | solution.py:866
  52.3 1.8 %collective-permute-done.15.refs_1_ = bf16[160,128]{1,0:T(8,128)(2,1)S(1)} collective-permute-done((bf16[160,128]{1,0:T(8,128)(2,1)S(1)}, bf16[160,128]{1,0:T(8,128)(2,1)S(1)}, u32[]{:S(2)}, u32[]{:S(2)}) %collective-permute-start.15) | collective-permute-done | bytes 40992 | tf_op jit(solution)/shard_map/ppermute | solution.py:866
  54.1 2.2 %collective-permute-done.16.refs_2_ = bf16[160,128]{1,0:T(8,128)(2,1)S(1)} collective-permute-done((bf16[160,128]{1,0:T(8,128)(2,1)S(1)}, bf16[160,128]{1,0:T(8,128)(2,1)S(1)}, u32[]{:S(2)}, u32[]{:S(2)}) %collective-permute-start.16) | collective-permute-done | bytes 40992 | tf_op jit(solution)/shard_map/ppermute | solution.py:866
  (33 shorter events, 3.8 us)
Async XLA Ops:
  0.6 1.0 %copy-start = (bf16[16,64,96]{2,1,0:T(8,128)(2,1)S(1)}, bf16[16,64,96]{2,1,0:T(8,128)(2,1)}, u32[]{:S(2)}) copy-start(bf16[16,64,96]{2,1,0:T(8,128)(2,1)} %image_in.1) | copy-start | bytes 589828
  1.6 9.3 %collective-permute-start.2 = (bf16[6,64,96]{2,1,0:T(8,128)(2,1)S(1)}, bf16[6,64,96]{2,1,0:T(8,128)(2,1)S(1)}, u32[]{:S(2)}, u32[]{:S(2)}) collective-permute-start(bf16[6,64,96]{2,1,0:T(8,128)(2,1)S(1)} %get-tuple-element.71.refs_0_), channel_id=1, source_target_pairs={{0,16},{1,17},{2,18},{3,19},{4,20},{5,21},{6,22},{7,23},{8,24},{9,... | collective-permute-start | bytes 221192 | tf_op jit(solution)/shard_map/ppermute | solution.py:55
  4.7 3.3 %copy-start.2 = (bf16[2,96,384]{2,1,0:T(8,128)(2,1)S(1)}, bf16[2,96,384]{2,1,0:T(8,128)(2,1)}, u32[]{:S(2)}) copy-start(bf16[2,96,384]{2,1,0:T(8,128)(2,1)} %up_in.1) | copy-start | bytes 442372
  4.7 3.3 %copy-start.3 = (bf16[2,384,96]{1,2,0:T(8,128)(2,1)S(1)}, bf16[2,384,96]{1,2,0:T(8,128)(2,1)}, u32[]{:S(2)}) copy-start(bf16[2,384,96]{1,2,0:T(8,128)(2,1)} %param.10) | copy-start | bytes 442372
  4.7 3.3 %copy-start.4 = (f32[2,7,7,96]{3,0,2,1:T(2,128)S(1)}, f32[2,7,7,96]{3,0,2,1:T(2,128)}, u32[]{:S(2)}) copy-start(f32[2,7,7,96]{3,0,2,1:T(2,128)} %param.7) | copy-start | bytes 112900
  4.7 3.3 %copy-start.5 = (f32[2,96]{1,0:T(2,128)S(1)}, f32[2,96]{1,0:T(2,128)}, u32[]{:S(2)}) copy-start(f32[2,96]{1,0:T(2,128)} %gains_in.1) | copy-start | bytes 2308
  4.7 4.0 %collective-permute-start.3 = (bf16[6,8,96]{2,1,0:T(8,128)(2,1)S(1)}, bf16[6,8,96]{2,1,0:T(8,128)(2,1)S(1)}, u32[]{:S(2)}, u32[]{:S(2)}) collective-permute-start(bf16[6,8,96]{2,1,0:T(8,128)(2,1)S(1)} %get-tuple-element.74), channel_id=1, source_target_pairs={{0,17},{1,16},{2,19},{3,18},{4,21},{5,20},{6,23},{7,22},{8,25},{9,... | collective-permute-start | bytes 27656 | tf_op jit(solution)/shard_map/ppermute | solution.py:55
  4.8 4.0 %collective-permute-start.4 = (bf16[6,8,96]{2,1,0:T(8,128)(2,1)S(1)}, bf16[6,8,96]{2,1,0:T(8,128)(2,1)S(1)}, u32[]{:S(2)}, u32[]{:S(2)}) collective-permute-start(bf16[6,8,96]{2,1,0:T(8,128)(2,1)S(1)} %get-tuple-element.75), channel_id=1, source_target_pairs={{0,16},{1,18},{2,17},{3,20},{4,19},{5,22},{6,21},{7,24},{8,23},{9,... | collective-permute-start | bytes 27656 | tf_op jit(solution)/shard_map/ppermute | solution.py:55
  6.0 2.8 %collective-permute-start = (bf16[16,8,96]{2,1,0:T(8,128)(2,1)S(1)}, bf16[16,8,96]{2,1,0:T(8,128)(2,1)S(1)}, u32[]{:S(2)}, u32[]{:S(2)}) collective-permute-start(bf16[16,8,96]{2,1,0:T(8,128)(2,1)S(1)} %get-tuple-element.72), channel_id=1, source_target_pairs={{0,1},{1,0},{2,3},{3,2},{4,5},{5,4},{6,7},{7,6},{8,9},{9,8},{10,11... | collective-permute-start | bytes 73736 | tf_op jit(solution)/shard_map/ppermute | solution.py:55
  7.0 3.9 %collective-permute-start.1 = (bf16[16,8,96]{2,1,0:T(8,128)(2,1)S(1)}, bf16[16,8,96]{2,1,0:T(8,128)(2,1)S(1)}, u32[]{:S(2)}, u32[]{:S(2)}) collective-permute-start(bf16[16,8,96]{2,1,0:T(8,128)(2,1)S(1)} %get-tuple-element.73), channel_id=1, source_target_pairs={{0,16},{1,2},{2,1},{3,4},{4,3},{5,6},{6,5},{7,8},{8,7},{9,10},{10,... | collective-permute-start | bytes 73736 | tf_op jit(solution)/shard_map/ppermute | solution.py:55
  8.0 3.0 %copy-start.1 = (bf16[16,64,96]{2,1,0:T(8,128)(2,1)S(1)}, bf16[16,64,96]{2,1,0:T(8,128)(2,1)}, u32[]{:S(2)}) copy-start(bf16[16,64,96]{2,1,0:T(8,128)(2,1)} %refs_1_.3) | copy-start | bytes 589828
  22.4 8.1 %collective-permute-start.7 = (bf16[9,64,96]{2,1,0:T(8,128)(2,1)S(1)}, bf16[9,64,96]{2,1,0:T(8,128)(2,1)S(1)}, u32[]{:S(2)}, u32[]{:S(2)}) collective-permute-start(bf16[9,64,96]{2,1,0:T(8,128)(2,1)S(1)} %get-tuple-element.94.refs_0_), channel_id=1, source_target_pairs={{0,16},{1,17},{2,18},{3,19},{4,20},{5,21},{6,22},{7,23},{8,24},{9,... | collective-permute-start | bytes 331784 | tf_op jit(solution)/shard_map/ppermute | solution.py:55
  23.4 6.2 %collective-permute-start.8 = (bf16[9,8,96]{2,1,0:T(8,128)(2,1)S(1)}, bf16[9,8,96]{2,1,0:T(8,128)(2,1)S(1)}, u32[]{:S(2)}, u32[]{:S(2)}) collective-permute-start(bf16[9,8,96]{2,1,0:T(8,128)(2,1)S(1)} %get-tuple-element.97), channel_id=1, source_target_pairs={{0,17},{1,16},{2,19},{3,18},{4,21},{5,20},{6,23},{7,22},{8,25},{9,... | collective-permute-start | bytes 41480 | tf_op jit(solution)/shard_map/ppermute | solution.py:55
  23.5 6.1 %collective-permute-start.9 = (bf16[9,8,96]{2,1,0:T(8,128)(2,1)S(1)}, bf16[9,8,96]{2,1,0:T(8,128)(2,1)S(1)}, u32[]{:S(2)}, u32[]{:S(2)}) collective-permute-start(bf16[9,8,96]{2,1,0:T(8,128)(2,1)S(1)} %get-tuple-element.98), channel_id=1, source_target_pairs={{0,16},{1,18},{2,17},{3,20},{4,19},{5,22},{6,21},{7,24},{8,23},{9,... | collective-permute-start | bytes 41480 | tf_op jit(solution)/shard_map/ppermute | solution.py:55
  24.7 5.0 %collective-permute-start.5 = (bf16[32,8,96]{2,1,0:T(8,128)(2,1)S(1)}, bf16[32,8,96]{2,1,0:T(8,128)(2,1)S(1)}, u32[]{:S(2)}, u32[]{:S(2)}) collective-permute-start(bf16[32,8,96]{2,1,0:T(8,128)(2,1)S(1)} %get-tuple-element.95), channel_id=1, source_target_pairs={{0,1},{1,0},{2,3},{3,2},{4,5},{5,4},{6,7},{7,6},{8,9},{9,8},{10,11... | collective-permute-start | bytes 147464 | tf_op jit(solution)/shard_map/ppermute | solution.py:55
  26.2 4.3 %collective-permute-start.6 = (bf16[32,8,96]{2,1,0:T(8,128)(2,1)S(1)}, bf16[32,8,96]{2,1,0:T(8,128)(2,1)S(1)}, u32[]{:S(2)}, u32[]{:S(2)}) collective-permute-start(bf16[32,8,96]{2,1,0:T(8,128)(2,1)S(1)} %get-tuple-element.96), channel_id=1, source_target_pairs={{0,16},{1,2},{2,1},{3,4},{4,3},{5,6},{6,5},{7,8},{8,7},{9,10},{10,... | collective-permute-start | bytes 147464 | tf_op jit(solution)/shard_map/ppermute | solution.py:55
  37.2 1.5 %collective-permute-start.10 = (bf16[880,128]{1,0:T(8,128)(2,1)S(1)}, bf16[880,128]{1,0:T(8,128)(2,1)S(1)}, u32[]{:S(2)}, u32[]{:S(2)}) collective-permute-start(bf16[880,128]{1,0:T(8,128)(2,1)S(1)} %get-tuple-element.103), channel_id=1, source_target_pairs={{0,1},{1,0},{2,3},{3,2},{4,5},{5,4},{6,7},{7,6},{8,9},{9,8},{10,11... | collective-permute-start | bytes 675848 | tf_op jit(solution)/shard_map/ppermute | solution.py:866
  38.8 5.7 %collective-permute-start.11 = (bf16[304,128]{1,0:T(8,128)(2,1)S(1)}, bf16[304,128]{1,0:T(8,128)(2,1)S(1)}, u32[]{:S(2)}, u32[]{:S(2)}) collective-permute-start(bf16[304,128]{1,0:T(8,128)(2,1)S(1)} %get-tuple-element.107), channel_id=1, source_target_pairs={{0,2},{1,3},{2,0},{3,1},{4,6},{5,7},{6,4},{7,5},{8,10},{9,11},{10,... | collective-permute-start | bytes 233480 | tf_op jit(solution)/shard_map/ppermute | solution.py:866
  40.6 5.2 %collective-permute-start.12 = (bf16[304,128]{1,0:T(8,128)(2,1)S(1)}, bf16[304,128]{1,0:T(8,128)(2,1)S(1)}, u32[]{:S(2)}, u32[]{:S(2)}) collective-permute-start(bf16[304,128]{1,0:T(8,128)(2,1)S(1)} %get-tuple-element.108), channel_id=1, source_target_pairs={{0,16},{1,17},{2,18},{3,19},{4,20},{5,21},{6,22},{7,23},{8,24},{9,... | collective-permute-start | bytes 233480 | tf_op jit(solution)/shard_map/ppermute | solution.py:866
  41.9 5.3 %collective-permute-start.13 = (bf16[304,128]{1,0:T(8,128)(2,1)S(1)}, bf16[304,128]{1,0:T(8,128)(2,1)S(1)}, u32[]{:S(2)}, u32[]{:S(2)}) collective-permute-start(bf16[304,128]{1,0:T(8,128)(2,1)S(1)} %get-tuple-element.109), channel_id=1, source_target_pairs={{0,18},{1,19},{2,16},{3,17},{4,22},{5,23},{6,20},{7,21},{8,26},{9,... | collective-permute-start | bytes 233480 | tf_op jit(solution)/shard_map/ppermute | solution.py:866
  47.2 5.1 %collective-permute-start.14 = (bf16[160,128]{1,0:T(8,128)(2,1)S(1)}, bf16[160,128]{1,0:T(8,128)(2,1)S(1)}, u32[]{:S(2)}, u32[]{:S(2)}) collective-permute-start(bf16[160,128]{1,0:T(8,128)(2,1)S(1)} %get-tuple-element.113), channel_id=1, source_target_pairs={{0,8},{1,9},{2,10},{3,11},{4,12},{5,13},{6,14},{7,15},{8,0},{9,1},... | collective-permute-start | bytes 122888 | tf_op jit(solution)/shard_map/ppermute | solution.py:866
  49.9 4.3 %collective-permute-start.15 = (bf16[160,128]{1,0:T(8,128)(2,1)S(1)}, bf16[160,128]{1,0:T(8,128)(2,1)S(1)}, u32[]{:S(2)}, u32[]{:S(2)}) collective-permute-start(bf16[160,128]{1,0:T(8,128)(2,1)S(1)} %get-tuple-element.114), channel_id=1, source_target_pairs={{0,4},{1,5},{2,6},{3,7},{4,0},{5,1},{6,2},{7,3},{8,12},{9,13},{10,... | collective-permute-start | bytes 122888 | tf_op jit(solution)/shard_map/ppermute | solution.py:866
  50.6 5.8 %collective-permute-start.16 = (bf16[160,128]{1,0:T(8,128)(2,1)S(1)}, bf16[160,128]{1,0:T(8,128)(2,1)S(1)}, u32[]{:S(2)}, u32[]{:S(2)}) collective-permute-start(bf16[160,128]{1,0:T(8,128)(2,1)S(1)} %get-tuple-element.115), channel_id=1, source_target_pairs={{0,12},{1,13},{2,14},{3,15},{4,8},{5,9},{6,10},{7,11},{8,4},{9,5},... | collective-permute-start | bytes 122888 | tf_op jit(solution)/shard_map/ppermute | solution.py:866

commit v7 on v6

--- a/solution.py
+++ b/solution.py
@@ -21,11 +21,8 @@
     return -(-n // 8) * 8
 
 
-def combos(row_count):
-    listed = [(None, 0), (None, 1), (0, None), (0, 0), (0, 1)]
-    if row_count > 2:
-        listed += [(1, None), (1, 0), (1, 1)]
-    return listed
+def band_starts(row_count):
+    return [0] if row_count == 2 else [0, 1]
 
 
 def partner(index, start, count):
@@ -48,12 +45,15 @@
     return pairs
 
 
-def exchange(bands, others, row_count, col_count):
-    got = {}
-    for strips, pairs in ((bands, band_combos(row_count)), (others, other_combos(row_count))):
-        for strip, (rs, cs) in zip(strips, pairs):
-            got[rs, cs] = lax.ppermute(strip, ("row", "col"), swap_pairs(row_count, col_count, rs, cs))
-    return [got[pair] for pair in combos(row_count)]
+def swap_bands(bands, row_count, col_count):
+    axes = ("row", "col")
+    starts = band_starts(row_count)
+    return [lax.ppermute(x, axes, swap_pairs(row_count, col_count, s, None)) for x, s in zip(bands, starts)]
+
+
+def swap_columns(strips, row_count, col_count):
+    axes = ("row", "col")
+    return [lax.ppermute(x, axes, swap_pairs(row_count, col_count, None, s)) for s, x in enumerate(strips)]
 
 
 class Place:
@@ -68,100 +68,61 @@
         }
         self.row_count = row_count
 
-
-def band_combos(row_count):
-    return [pair for pair in combos(row_count) if pair[1] is None]
-
-
-def other_combos(row_count):
-    return [pair for pair in combos(row_count) if pair[1] is not None]
-
-
-def write_strips(place, outs, takes, pairs):
-    for out, (rs, cs) in zip(outs, pairs):
+    def pick_band(self, bands, vertical):
+        if self.row_count == 2:
+            return lambda i: bands[0][i]
+        near, far = ((0, 1) if vertical == "below" else (1, 0))
+        return lambda i: jnp.where(self.even_row, bands[near][i].astype(f32), bands[far][i].astype(f32))
+
+
+def write_bands(place, outs, takes):
+    for out, start in zip(outs, band_starts(place.row_count)):
         at = 0
-        for take, radius, rows, cols in takes:
-            row_sets = [slice(0, rows)] * 2
-            col_sets = [slice(0, cols)] * 2
-            if rs is not None:
-                row_sets = [slice(rows - radius, rows), slice(0, radius)]
-                if rs == 1:
-                    row_sets = row_sets[::-1]
-            if cs is not None:
-                col_sets = [slice(cols - SIDE, cols), slice(0, SIDE)]
-                if cs == 1:
-                    col_sets = col_sets[::-1]
-            count = row_sets[0].stop - row_sets[0].start
-            for i in range(count):
-                parts = {}
-                for er in (0, 1):
-                    for ec in (0, 1):
-                        key = (row_sets[er].start + i, col_sets[ec].start, col_sets[ec].stop)
-                        if key not in parts:
-                            parts[key] = take(*key)
-                        parts[er, ec] = parts[key]
-                if cs is None:
-                    pick = [parts[0, 0], parts[1, 0]]
-                else:
-                    pick = [jnp.where(place.even_col, parts[e, 0], parts[e, 1]) for e in (0, 1)]
-                value = pick[0] if rs is None else jnp.where(place.even_row, pick[0], pick[1])
+        for take, radius, rows in takes:
+            for i in range(radius):
+                low, high = (take(i), take(rows - radius + i))
+                value = jnp.where(place.even_row, high, low) if start == 0 else jnp.where(place.even_row, low, high)
                 out[at + i] = value.astype(out.dtype)
-            at += count
-
-
-def strip_shapes(pairs, rows, cols, channels, radii):
-    shapes = []
-    for rs, cs in pairs:
-        height = sum(rows if rs is None else radius for radius in radii)
-        shapes.append((height, cols if cs is None else SIDE, channels))
-    return shapes
-
-
-def received(place, strips, row_sections):
-    table = dict(zip(combos(place.row_count), strips))
-    full_start, band_start = row_sections
-
-    def along(rs, cs, i):
-        return table[rs, cs][(full_start if rs is None else band_start) + i].astype(f32)
-
-    def column(rs, side, i):
-        if side is None:
-            return along(rs, None, i)
-        near, far = (along(rs, 0, i), along(rs, 1, i))
-        if side == "left":
-            return jnp.where(place.even_col, far, near)
-        return jnp.where(place.even_col, near, far)
-
-    def read(vertical, side, i):
-        if vertical is None:
-            value = column(None, side, i)
-        elif place.row_count == 2:
-            value = column(0, side, i)
-        else:
-            near, far = (column(0, side, i), column(1, side, i))
-            if vertical == "above":
-                value = jnp.where(place.even_row, far, near)
-            else:
-                value = jnp.where(place.even_row, near, far)
-        if vertical is not None:
-            value = jnp.where(place.has[vertical], value, 0.0)
-        if side is not None:
-            value = jnp.where(place.has[side], value, 0.0)
-        return value
-
-    return read
-
-
-def assemble(place, target, own, read, radius, rows, cols, channels):
-    width = cols + 2 * SIDE
+            at += radius
+
+
+def tall_rows(place, bands, at, own, radius, rows):
+    listed = []
+    for i in range(radius):
+        listed.append((place.pick_band(bands, "above"), at + i, "above"))
+    for i in range(rows):
+        listed.append((own, i, None))
+    for i in range(radius):
+        listed.append((place.pick_band(bands, "below"), at + i, "below"))
+    for take, i, vertical in listed:
+        value = take(i).astype(f32)
+        yield value if vertical is None else jnp.where(place.has[vertical], value, 0.0)
+
+
+def write_columns(place, outs, row, value):
+    cols = value.shape[0]
+    first, last = (value[0:SIDE], value[cols - SIDE : cols])
+    outs[0][row] = jnp.where(place.even_col, last, first).astype(bf16)
+    outs[1][row] = jnp.where(place.even_col, first, last).astype(bf16)
+
+
+def side_columns(place, strips, row, side):
+    near, far = (strips[0][row].astype(f32), strips[1][row].astype(f32))
+    if side == "left":
+        value = jnp.where(place.even_col, far, near)
+    else:
+        value = jnp.where(place.even_col, near, far)
+    return jnp.where(place.has[side], value, 0.0)
+
+
+def frame_rows(place, target, tall, strips, at, rows, cols, margin, channels):
+    width = cols + 2 * margin
     target[...] = jnp.zeros(target.shape, f32)
-    for vertical, start, count in (("above", 0, radius), (None, radius, rows), ("below", radius + rows, radius)):
-        for i in range(count):
-            base = (start + i) * width
-            middle = own(i) if vertical is None else read(vertical, None, i)
-            target[base + SIDE : base + SIDE + cols, 0:channels] = middle
-            target[base : base + SIDE, 0:channels] = read(vertical, "left", i)
-            target[base + SIDE + cols : base + width, 0:channels] = read(vertical, "right", i)
+    for i in range(rows):
+        base = i * width
+        target[base + margin : base + margin + cols, :] = tall[i * cols : (i + 1) * cols, :]
+        target[base : base + margin, 0:channels] = side_columns(place, strips, at + i, "left")[SIDE - margin :]
+        target[base + margin + cols : base + width, 0:channels] = side_columns(place, strips, at + i, "right")[:margin]
 
 
 def spread_taps(kernel_ref, layer, target):
@@ -256,15 +217,14 @@
 
 
 def gelu_parts(v):
-    d = 1.0 + (0.3275911 * inv_sqrt_two) * jnp.abs(v)
-    t = pl.reciprocal(d, approx=True)
-    t = t * (2.0 - d * t)
+    p = 0.3275911 * inv_sqrt_two
+    c1, c2, c3, c4, c5 = (
+        0.5 * c / p ** (k + 1)
+        for k, c in enumerate((0.254829592, -0.284496736, 1.421413741, -1.453152027, 1.061405429))
+    )
+    t = pl.reciprocal(jnp.abs(v) + 1.0 / p, approx=True)
     bell = jnp.exp2(v * v * (-0.5 * log2_e))
-    series = 0.5 * 1.061405429 * t + 0.5 * -1.453152027
-    series = series * t + 0.5 * 1.421413741
-    series = series * t + 0.5 * -0.284496736
-    series = series * t + 0.5 * 0.254829592
-    tail = series * t * bell
+    tail = ((((c5 * t + c4) * t + c3) * t + c2) * t + c1) * t * bell
     cdf = jnp.where(v >= 0.0, 1.0 - tail, tail)
     return (v * cdf, cdf + v * (bell * inv_sqrt_two_pi))
 
@@ -298,37 +258,60 @@
         copy.wait()
 
 
-def image_take(ref):
-    return lambda i, lo, hi: ref[i].astype(f32)[lo:hi]
-
-
-def flat_take(ref, cols, channels):
-    return lambda i, lo, hi: ref[i * cols + lo : i * cols + hi, 0:channels]
-
-
 def bands_kernel(dims, image_in, image, *refs):
     outs, sems = (refs[:-1], refs[-1])
     place = Place(dims.row_count, dims.col_count)
     fetch((image_in,), (image,), sems)
-    takes = [(image_take(image), 2 * dims.h, dims.rows, dims.cols)]
-    write_strips(place, outs, takes, band_combos(dims.row_count))
-
-
-def others_kernel(dims, image, *refs):
-    outs = refs[len(band_combos(dims.row_count)) :]
+    write_bands(place, outs, [(lambda i: image[i].astype(f32), 2 * dims.h, dims.rows)])
+
+
+def columns_kernel(dims, image, *refs):
+    bands, (tall, first, second) = (refs[:-3], refs[-3:])
     place = Place(dims.row_count, dims.col_count)
-    takes = [(image_take(image), 2 * dims.h, dims.rows, dims.cols)]
-    write_strips(place, outs, takes, other_combos(dims.row_count))
-
-
-def grad_others_kernel(dims, grad1, cot, *refs):
-    outs = refs[len(band_combos(dims.row_count)) :]
+    cols, channels = (dims.cols, dims.channels)
+    tall[...] = jnp.zeros(tall.shape, f32)
+    for i, value in enumerate(tall_rows(place, bands, 0, lambda i: image[i], 2 * dims.h, dims.rows)):
+        tall[i * cols : (i + 1) * cols, 0:channels] = value
+        write_columns(place, (first, second), i, value)
+
+
+def grad_columns_kernel(dims, grad1, cot, *refs):
+    bands, (tall, tall_cot, first, second) = (refs[:-4], refs[-4:])
     place = Place(dims.row_count, dims.col_count)
-    takes = [
-        (flat_take(grad1, dims.cols, dims.channels), 2 * dims.h, dims.rows, dims.cols),
-        (image_take(cot), dims.h, dims.rows, dims.cols),
-    ]
-    write_strips(place, outs, takes, other_combos(dims.row_count))
+    cols, channels, h, rows = (dims.cols, dims.channels, dims.h, dims.rows)
+    tall[...] = jnp.zeros(tall.shape, f32)
+    tall_cot[...] = jnp.zeros(tall_cot.shape, f32)
+
+    def own(i):
+        return grad1[i * cols : (i + 1) * cols, 0:channels]
+
+    for i, value in enumerate(tall_rows(place, bands, 0, own, 2 * h, rows)):
+        tall[i * cols : (i + 1) * cols, 0:channels] = value
+        write_columns(place, (first, second), i, value)
+    for i, value in enumerate(tall_rows(place, bands, 2 * h, lambda i: cot[i], h, rows)):
+        tall_cot[i * cols : (i + 1) * cols, 0:channels] = value
+        write_columns(place, (first, second), rows + 4 * h + i, value)
+
+
+def middle_groups(ext_cols):
+    starts = list(range(16, ext_cols - 16 - 8 + 1, 16))
+    return (starts, [0, ext_cols - 16])
+
+
+def middle_kernel(dims, flipped, tall, taps, out):
+    cols, ext_rows, margin = (dims.cols, dims.ext_rows, (dims.ext_cols - dims.cols) // 2)
+    skip = dims.skipped_rows(Place(dims.row_count, dims.col_count))
+    width = dims.middle_cols
+
+    def group(g, carry):
+        at = pl.multiple_of(g * 16, 16)
+        base = pl.multiple_of(skip * cols, 8) + at + 16 - margin - dims.h
+        total = conv_group(tall, base, cols, ext_rows, taps, dims.size, flipped)
+        for r in range(ext_rows):
+            out[pl.ds(r * width + at, 16), :] = total[r]
+        return carry
+
+    lax.fori_loop(0, width // 16, group, 0)
 
 
 def weights_kernel(up_in, down_t_in, kernels_in, gains_in, *refs):
@@ -354,18 +337,16 @@
 
 
 def first_kernel(dims, *refs):
-    count = len(combos(dims.row_count))
-    image, cot, taps0, taps1, gains, forward0, back0, forward1, back1 = refs[:9]
-    strips = refs[9 : 9 + count]
-    refs = refs[9 + count :]
+    tall, done, cot, taps0, taps1, gains, forward0, back0, forward1, back1 = refs[:10]
+    strips = refs[10:12]
+    refs = refs[12:]
     (output, x0, x1, unit0, inv0, hidden0, slope0, grad1, normed1, pre_grad1, hidden1, gain_sum) = refs[:12]
     outs, conv = (refs[12:-1], refs[-1])
     place = Place(dims.row_count, dims.col_count)
     rows, cols, channels, h, size = (dims.rows, dims.cols, dims.channels, dims.h, dims.size)
     ext_rows, ext_cols, wide = (dims.ext_rows, dims.ext_cols, dims.wide)
     skip = dims.skipped_rows(place)
-    read = received(place, strips, (0, 0))
-    assemble(place, x0, lambda i: image[i].astype(f32), read, 2 * h, rows, cols, channels)
+    frame_rows(place, x0, tall, strips, 0, rows + 4 * h, cols, SIDE, channels)
 
     x1[...] = jnp.zeros(x1.shape, f32)
     if dims.ext_pad > ext_rows * ext_cols:
@@ -373,15 +354,19 @@
     frame = pl.multiple_of(skip * ext_cols, 8)
 
     def conv0(g, carry):
-        at = group_start(g, ext_cols)
+        at = pl.multiple_of(g * (ext_cols - 16), 8)
         base = pl.multiple_of(skip * wide, 8) + at
         total = conv_group(x0, base + 1, wide, ext_rows, taps0, size)
         for r in range(ext_rows):
             conv[pl.ds(r * ext_cols + at, 16), :] = total[r]
-            x1[pl.ds(frame + r * ext_cols + at, 16), :] = x0[pl.ds(base + (r + h) * wide + 4, 16), :]
         return carry
 
-    lax.fori_loop(0, -(-ext_cols // 16), conv0, 0)
+    lax.fori_loop(0, 2, conv0, 0)
+    for r in range(ext_rows):
+        width = dims.middle_cols
+        conv[r * ext_cols + 16 : r * ext_cols + 16 + width, :] = done[r * width : (r + 1) * width, :]
+        line = x0[pl.ds(skip * wide + (r + h) * wide + 4, ext_cols), :]
+        x1[pl.ds(frame + r * ext_cols, ext_cols), :] = line
     gain = pad_lanes(gains[0:1, :])
     ones = diagonal(jnp.ones((LANES, LANES), bf16), jnp.ones((LANES, LANES), bf16))
     half = dims.ext_pad // 2
@@ -438,8 +423,10 @@
         gain_sum[...] += jnp.sum(product.reshape(step // 8, 8, LANES), axis=0)
         grad1[px, :] = round16(norm_backward(normed_grad, unit, inverse, gain1, channels, ones))
 
-    takes = [(flat_take(grad1, cols, channels), 2 * h, rows, cols), (image_take(cot), h, rows, cols)]
-    write_strips(place, outs, takes, band_combos(dims.row_count))
+    def own(i):
+        return grad1[i * cols : (i + 1) * cols, 0:channels]
+
+    write_bands(place, outs, [(own, 2 * h, rows), (lambda i: cot[i].astype(f32), h, rows)])
 
 
 def clear_outside(place, flat, dims):
@@ -486,30 +473,18 @@
 
 
 def third_kernel(dims, *refs):
-    count = len(combos(dims.row_count))
-    (grad1, cot, taps1, gains, grad_in0, grad_out0, x0, unit0, inv0, hidden0, slope0) = refs[:11]
-    (taps_sum1, up_sum1, down_sum1) = refs[11:14]
-    strips = refs[14 : 14 + count]
-    (grad0, middle, keep, small_keep, send) = refs[14 + count : 19 + count]
-    (wide_grad, cot_frame, upstream, own, sums, up_acc, down_acc, gain_sum, small, tall, slabs) = refs[19 + count :]
+    (tall, tall_cot, done, taps1, gains, grad_in0, grad_out0, x0, unit0, inv0, hidden0, slope0) = refs[:12]
+    (taps_sum1, up_sum1, down_sum1) = refs[12:15]
+    strips = refs[15:17]
+    (grad0, middle, keep, small_keep, send) = refs[17:22]
+    (wide_grad, cot_frame, upstream, own, sums, up_acc, down_acc, gain_sum, small, table, slabs) = refs[22:]
     place = Place(dims.row_count, dims.col_count)
     rows, cols, channels, h, size = (dims.rows, dims.cols, dims.channels, dims.h, dims.size)
     ext_rows, ext_cols, wide = (dims.ext_rows, dims.ext_cols, dims.wide)
     skip = dims.skipped_rows(place)
-    read = received(place, strips, (0, 0))
-    assemble(
-        place, wide_grad, lambda i: grad1[i * cols : (i + 1) * cols, 0:channels], read, 2 * h, rows, cols, channels
-    )
-    read_cot = received(place, strips, (rows, 2 * h))
     margin = (ext_cols - cols) // 2
-    cot_frame[...] = jnp.zeros(cot_frame.shape, f32)
-    for vertical, start, n in (("above", 0, h), (None, h, rows), ("below", h + rows, h)):
-        for i in range(n):
-            base = (start + i) * ext_cols
-            line = cot[i].astype(f32) if vertical is None else read_cot(vertical, None, i)
-            cot_frame[base + margin : base + margin + cols, 0:channels] = line
-            cot_frame[base : base + margin, 0:channels] = read_cot(vertical, "left", i)[SIDE - margin :]
-            cot_frame[base + margin + cols : base + ext_cols, 0:channels] = read_cot(vertical, "right", i)[:margin]
+    frame_rows(place, wide_grad, tall, strips, 0, rows + 4 * h, cols, SIDE, channels)
+    frame_rows(place, cot_frame, tall_cot, strips, rows + 4 * h, rows + 2 * h, cols, margin, channels)
 
     used = ext_rows * ext_cols
     if dims.ext_pad > used:
@@ -519,18 +494,21 @@
     frame = pl.multiple_of(skip * ext_cols, 8)
 
     def conv1(g, carry):
-        at = group_start(g, ext_cols)
+        at = pl.multiple_of(g * (ext_cols - 16), 8)
         total = conv_group(wide_grad, pl.multiple_of(skip * wide, 8) + at + 1, wide, ext_rows, taps1, size, True)
-        col = lax.broadcasted_iota(jnp.int32, (16, LANES), 0) + (at - margin)
-        inside = jnp.where(jnp.logical_and(col >= 0, col < cols), 1.0, 0.0)
         for r in range(ext_rows):
-            px = pl.ds(r * ext_cols + at, 16)
-            upstream[px, :] = cot_frame[pl.ds(frame + r * ext_cols + at, 16), :] + total[r]
-            mine = jnp.logical_and(r + skip >= h, r + skip < h + rows)
-            own[px, :] = jnp.where(mine, inside, 0.0)
+            upstream[pl.ds(r * ext_cols + at, 16), :] = total[r]
         return carry
 
-    lax.fori_loop(0, -(-ext_cols // 16), conv1, 0)
+    lax.fori_loop(0, 2, conv1, 0)
+    col = lax.broadcasted_iota(jnp.int32, (ext_cols, LANES), 0) - margin
+    inside = jnp.where(jnp.logical_and(col >= 0, col < cols), 1.0, 0.0)
+    for r in range(ext_rows):
+        px, width = (slice(r * ext_cols, (r + 1) * ext_cols), dims.middle_cols)
+        upstream[r * ext_cols + 16 : r * ext_cols + 16 + width, :] = done[r * width : (r + 1) * width, :]
+        upstream[px, :] = upstream[px, :] + cot_frame[pl.ds(frame + r * ext_cols, ext_cols), :]
+        mine = jnp.logical_and(r + skip >= h, r + skip < h + rows)
+        own[px, :] = jnp.where(mine, inside, 0.0)
     for i in range(rows):
         line = upstream[pl.ds((i + h - skip) * ext_cols + margin, cols), :]
         middle[i * cols : (i + 1) * cols, :] = round16(line)
@@ -567,8 +545,7 @@
 
     taps_rows = size * size + 1
     merged = jnp.concatenate([small[0:taps_rows, :], taps_sum1[0:taps_rows, :]], axis=0) * dims.factor
-    merged = jnp.concatenate([merged, jnp.zeros((dims.small_rows - 2 * taps_rows, LANES), f32)], axis=0)
-    merged = merged.astype(bf16)
+    merged = fold_rows(merged, dims.small_rows, 3 * 32).astype(bf16)
     small_keep[...] = merged.astype(f32)
 
     layer_rows, part, half = (dims.layer_rows, dims.part, dims.half)
@@ -578,28 +555,58 @@
     up1 = up_sum1[...] * dims.factor
     down1 = down_sum1[...] * dims.factor
     lane = lax.broadcasted_iota(jnp.int32, (units, LANES), 1)
-    slab_rows = 2 * layer_rows
     for r in range(dims.row_count):
         for layer, (u, d) in enumerate(((up0, down0), (up1, down1))):
             first = pltpu.roll(u, LANES - r * half, 1) if r else u
             shift = (half - r * half) % LANES
             second = pltpu.roll(d, shift, 1) if shift else d
             joined = jnp.where(lane < half, first, jnp.where(lane < 2 * half, second, 0.0))
-            tall[layer * (units + 8) : layer * (units + 8) + units, :] = joined
+            table[layer * (units + 8) : layer * (units + 8) + units, :] = joined
 
         def slab(c, carry, r=r):
             index = 0
             for j, (axis, bit) in enumerate(dims.stages):
                 value = (r >> bit) & 1 if axis == "row" else lax.rem(lax.div(c, 1 << bit), 2)
                 index = index + value * (1 << (len(dims.stages) - 1 - j))
-            for layer in range(2):
-                to = pl.multiple_of(index * slab_rows + layer * layer_rows, 8)
-                slabs[pl.ds(to, layer_rows), :] = tall[pl.ds(layer * (units + 8) + c * part, layer_rows), :]
+            blocks = [table[pl.ds(layer * (units + 8) + c * part, layer_rows), :] for layer in range(2)]
+            whole = fold_rows(jnp.concatenate(blocks, axis=0), dims.slab_rows, 2 * half)
+            slabs[pl.ds(pl.multiple_of(index * dims.slab_rows, 8), dims.slab_rows), :] = whole
             return carry
 
         lax.fori_loop(0, dims.col_count, slab, 0)
 
     split(dims, 0, slabs, merged, keep, (send,))
+
+
+def fold_rows(x, rows, used):
+    n = x.shape[0]
+    if rows >= n:
+        return pad_rows(x, rows)
+    assert used <= 96
+    stride = ceil8(n - rows)
+    rest = pad_rows(x[rows:], stride)
+    pieces_of = pad_rows(jnp.concatenate([pltpu.roll(rest, 96 - 32 * k, 1) for k in range(3)], axis=0), rows)
+    lane = lax.broadcasted_iota(jnp.int32, (rows, LANES), 1)
+    return jnp.where(lane < 96, x[:rows], pieces_of)
+
+
+def pad_rows(x, rows):
+    if rows == x.shape[0]:
+        return x
+    return jnp.concatenate([x, jnp.zeros((rows - x.shape[0], LANES), x.dtype)], axis=0)
+
+
+def unfold_rows(x, n):
+    rows = x.shape[0]
+    if rows >= n:
+        return x[:n]
+    stride = ceil8(n - rows)
+    lane = lax.broadcasted_iota(jnp.int32, (stride, LANES), 1)
+    rest = jnp.zeros((stride, LANES), x.dtype)
+    for k in range(3):
+        moved = pltpu.roll(x[k * stride : (k + 1) * stride], 32 + 32 * k, 1)
+        rest = jnp.where(jnp.logical_and(lane >= 32 * k, lane < 32 * k + 32), moved, rest)
+    return jnp.concatenate([x, rest[: n - rows]], axis=0)
 
 
 def split(dims, stage, slabs, merged, keep, sends):
@@ -608,21 +615,22 @@
     mine = 0
     for axis, bit in group:
         mine = mine * 2 + lax.rem(lax.div(lax.axis_index(axis), 1 << bit), 2)
-    keep[...] = slabs[pl.ds(pl.multiple_of(mine * count, 16), count), :]
+    keep[...] = slabs[pl.ds(pl.multiple_of(mine * count, 8), count), :]
+    sums_rows = merged.shape[0]
     for mask, send in enumerate(sends, 1):
         other = 0
         for j in range(len(group)):
             weight = 1 << j
             digit = lax.rem(lax.div(mine, weight), 2)
             other = other + weight * (1 - digit if mask & weight else digit)
-        send[0:count, :] = slabs[pl.ds(pl.multiple_of(other * count, 16), count), :].astype(bf16)
-        send[count:, :] = merged
+        send[0:sums_rows, :] = merged
+        send[sums_rows:, :] = slabs[pl.ds(pl.multiple_of(other * count, 8), count), :].astype(bf16)
 
 
 def gather_up(keep, small, gots):
-    count = keep.shape[0]
-    slabs = [keep[...]] + [got[0:count, :].astype(f32) for got in gots]
-    sums = [small[...]] + [got[count:, :].astype(f32) for got in gots]
+    count = small.shape[0]
+    slabs = [keep[...]] + [got[count:, :].astype(f32) for got in gots]
+    sums = [small[...]] + [got[0:count, :].astype(f32) for got in gots]
     if len(gots) == 1:
         return (slabs[0] + slabs[1], sums[0] + sums[1])
     return tuple((x[0] + x[1]) + (x[2] + x[3]) for x in (slabs, sums))
@@ -647,6 +655,8 @@
 def last_kernel(dims, keep, small, *refs):
     gots, (kernel_out, gain_out, up_out, down_out) = (refs[:-4], refs[-4:])
     total, merged = gather_up(keep, small, gots)
+    total = unfold_rows(total, 2 * dims.layer_rows)
+    merged = unfold_rows(merged, 2 * (dims.size * dims.size + 1))
     size, channels, half, part = (dims.size, dims.channels, dims.half, dims.part)
     for layer in range(2):
         block = total[layer * dims.layer_rows : layer * dims.layer_rows + part]
@@ -699,7 +709,9 @@
     d.part = up_weights.shape[2] // d.col_count
     d.layer_rows = ceil8(d.part)
     d.count = d.row_count * d.col_count
-    d.small_rows = -(-2 * (d.size * d.size + 1) // 16) * 16
+    d.small_rows = 80 if d.size == 7 and d.channels <= 96 else -(-2 * (d.size * d.size + 1) // 16) * 16
+    d.slab_rows = 40 if d.layer_rows == 24 and 2 * d.half <= 96 else 2 * d.layer_rows
+    d.middle_cols = (d.cols - 16) // 16 * 16
     d.factor = 1.0 / math.sqrt(d.rows * d.cols * d.count)
     row_bits, col_bits = (d.row_count.bit_length() - 1, d.col_count.bit_length() - 1)
     bits = [("row", b) for b in range(row_bits)] + [("col", b) for b in range(1, col_bits)]
@@ -749,16 +761,21 @@
     tap_sums = ((d.size * d.size * 8, LANES), f32)
     sums_rows = ceil8(d.size * d.size + 1)
 
-    bands, others = (band_combos(d.row_count), other_combos(d.row_count))
-
-    def strips_of(pairs, radii):
-        return [(shape, bf16) for shape in strip_shapes(pairs, rows, cols, channels, radii)]
-
-    image, *band_strips = run(
-        bind(bands_kernel, d), [(image.shape, bf16)] + strips_of(bands, (2 * d.h,)), [], image, in_hbm=1, sems=1
-    )
-    other_strips = run(bind(others_kernel, d), strips_of(others, (2 * d.h,)), [], image, *band_strips)
-    strips = exchange(band_strips, other_strips, d.row_count, d.col_count)
+    counts = (d.row_count, d.col_count)
+    band_count, tall_rows_count = (len(band_starts(d.row_count)), rows + 4 * d.h)
+    tall = ((tall_rows_count * cols, LANES), f32)
+    done = ((d.ext_rows * d.middle_cols, LANES), f32)
+
+    def bands_of(height):
+        return [((height, cols, channels), bf16)] * band_count
+
+    def columns_of(height):
+        return [((height, SIDE, channels), bf16)] * 2
+
+    image, *bands = run(
+        bind(bands_kernel, d), [(image.shape, bf16)] + bands_of(2 * d.h), [], image, in_hbm=1, sems=1
+    )
+    bands = swap_bands(bands, *counts)
     mixing = [((2 * LANES, 2 * units), bf16), ((2 * units, 2 * LANES), bf16)]
     forward0, back0, forward1, back1, grad_in0, grad_out0, taps0, taps1, gains = run(
         weights_kernel,
@@ -773,6 +790,11 @@
         busy_us=2,
     )
 
+    tall_image, *strips = run(
+        bind(columns_kernel, d), [tall] + columns_of(tall_rows_count), [], image, *bands
+    )
+    strips = swap_columns(strips, *counts)
+    (done0,) = run(bind(middle_kernel, d, False), [done], [], tall_image, taps0, busy_us=2)
     first = run(
         bind(first_kernel, d),
         [
@@ -789,9 +811,10 @@
             ((tile, units), bf16),
             ((8, LANES), f32),
         ]
-        + strips_of(bands, (2 * d.h, d.h)),
+        + bands_of(3 * d.h),
         [((ext, LANES), f32)],
-        image,
+        tall_image,
+        done0,
         cotangent,
         taps0,
         taps1,
@@ -804,11 +827,7 @@
         busy_us=15,
     )
     (final, x0, x1, unit0, inv0, hidden0, slope0, grad1, normed1, pre_grad1, hidden1, gain_part) = first[:12]
-    band_strips = first[12:]
-    other_strips = run(
-        bind(grad_others_kernel, d), strips_of(others, (2 * d.h, d.h)), [], grad1, cotangent, *band_strips
-    )
-    strips = exchange(band_strips, other_strips, d.row_count, d.col_count)
+    bands = swap_bands(first[12:], *counts)
 
     taps_sum1, up_sum1, down_sum1, output = run(
         bind(sums_kernel, d),
@@ -825,7 +844,17 @@
         busy_us=3,
     )
 
-    held = d.count // 2 * 2 * d.layer_rows
+    tall_grad, tall_cot, *strips = run(
+        bind(grad_columns_kernel, d),
+        [tall, (((rows + 2 * d.h) * cols, LANES), f32)] + columns_of(2 * rows + 6 * d.h),
+        [],
+        grad1,
+        cotangent,
+        *bands,
+    )
+    strips = swap_columns(strips, *counts)
+    (done1,) = run(bind(middle_kernel, d, True), [done], [], tall_grad, taps1, busy_us=2)
+    held = d.count // 2 * d.slab_rows
     small = ((d.small_rows, LANES), f32)
     grad0, middle, keep, sums, send = run(
         bind(third_kernel, d),
@@ -843,8 +872,9 @@
             ((2 * (units + 8), LANES), f32),
             ((2 * held, LANES), f32),
         ],
-        grad1,
-        cotangent,
+        tall_grad,
+        tall_cot,
+        done1,
         taps1,
         gains,
         grad_in0,

time: 57.2 us -> 60.4 us (1.056)
  waiting for transfers between devices: 11.8 us -> 15.9 us
  starting transfers between devices: 19.3 us -> 17.1 us
  Pallas kernels: 24.2 us -> 25.4 us
    ppermute x10 -> x6, waiting for transfers between devices: 3.04 us -> 6.76 us  [the longest x2 3.82 us: swap_bands(): lax.ppermute(x, axes, swap_pairs(row_count, col_count, s, None))]
    ppermute x10 -> x6, starting transfers between devices: 11.1 us -> 8.8 us  [the longest x2 4.96 us: swap_bands(): lax.ppermute(x, axes, swap_pairs(row_count, col_count, s, None))]
    pallas_call x11 -> x13, Pallas kernels: 24.2 us -> 25.4 us  [run(): pl.pallas_call(kernel, out_shape=shapes, in_specs=[far] * in_hbm + [space...]
  transfers between devices with their start and end apart: 17 -> 13, of which waited for: 8 -> 10; matrix products, arithmetic and copies ran while one was open for 0% -> 0% of each run, Pallas kernels for 9% -> 12%
where the time goes in v7:
time: 60.4 us; the launch traced here: 60.2 us
  Pallas kernels  25.4 us (42%)
  starting transfers between devices  17.1 us (28%)
  waiting for transfers between devices  15.9 us (26%)
  local copies, waits for them, and re-layouts  0.96 us (2%)
  between operations  0.75 us (1%)
    pallas_call x13, Pallas kernels, run(): pl.pallas_call(kernel, out_shape=shapes, in_specs=[far] * in_hbm + [space...  25.4 us
    ppermute x7, waiting for transfers between devices, per_device(): lax.ppermute(x, axes, swap_by(d, group, mask))  9.18 us
    ppermute x7, starting transfers between devices, per_device(): lax.ppermute(x, axes, swap_by(d, group, mask))  8.34 us
    ppermute x2, starting transfers between devices, swap_bands(): lax.ppermute(x, axes, swap_pairs(row_count, col_count, s, None))  4.96 us
    ppermute x4, starting transfers between devices, swap_columns(): lax.ppermute(x, axes, swap_pairs(row_count, col_count, None, s))  3.83 us
    ppermute x2, waiting for transfers between devices, swap_bands(): lax.ppermute(x, axes, swap_pairs(row_count, col_count, s, None))  3.82 us
    ppermute x4, waiting for transfers between devices, swap_columns(): lax.ppermute(x, axes, swap_pairs(row_count, col_count, None, s))  2.94 us
  transfers between devices with their start and end apart: 13, of which 10 were waited for; matrix products, arithmetic and copies ran while one was open for 0% of the time, Pallas kernels for 12%

profile of v7, /device:TPU:0, one launch (start us, length us, event | category | flops | bytes accessed | tf_op | source)
XLA Modules:
  0.0 60.2 jit_solution(5374354531661185106)
XLA Ops:
  0.6 0.9 %copy-done = bf16[16,64,96]{2,1,0:T(8,128)(2,1)S(1)} copy-done((bf16[16,64,96]{2,1,0:T(8,128)(2,1)S(1)}, bf16[16,64,96]{2,1,0:T(8,128)(2,1)}, u32[]{:S(2)}) %copy-start) | copy-done | bytes 196632
  1.7 3.0 %collective-permute-start = (bf16[6,64,96]{2,1,0:T(8,128)(2,1)S(1)}, bf16[6,64,96]{2,1,0:T(8,128)(2,1)S(1)}, u32[]{:S(2)}, u32[]{:S(2)}) collective-permute-start(bf16[6,64,96]{2,1,0:T(8,128)(2,1)S(1)} %get-tuple-element.63), channel_id=1, source_target_pairs={{0,16},{1,17},{2,18},{3,19},{4,20},{5,21},{6,22},{7,23},{8,24},{9,... | collective-permute-start | bytes 221192 | tf_op jit(solution)/shard_map/ppermute | solution.py:51
  5.4 2.0 %collective-permute-done.refs_0_ = bf16[6,64,96]{2,1,0:T(8,128)(2,1)S(1)} collective-permute-done((bf16[6,64,96]{2,1,0:T(8,128)(2,1)S(1)}, bf16[6,64,96]{2,1,0:T(8,128)(2,1)S(1)}, u32[]{:S(2)}, u32[]{:S(2)}) %collective-permute-start) | collective-permute-done | bytes 73760 | tf_op jit(solution)/shard_map/ppermute | solution.py:51
  7.7 1.9 %collective-permute-start.2 = (bf16[28,8,96]{2,1,0:T(8,128)(2,1)S(1)}, bf16[28,8,96]{2,1,0:T(8,128)(2,1)S(1)}, u32[]{:S(2)}, u32[]{:S(2)}) collective-permute-start(bf16[28,8,96]{2,1,0:T(8,128)(2,1)S(1)} %get-tuple-element.73), channel_id=1, source_target_pairs={{0,16},{1,2},{2,1},{3,4},{4,3},{5,6},{6,5},{7,8},{8,7},{9,10},{10,... | collective-permute-start | bytes 129032 | tf_op jit(solution)/shard_map/ppermute | solution.py:56
  9.6 1.1 %shard_map.112.refs_1_ = f32[912,128]{1,0:T(8,128)S(1)} custom-call(f32[1792,128]{1,0:T(8,128)S(1)} %get-tuple-element.64.tall.refs_0_, bf16[784,128]{1,0:T(8,128)(2,1)S(1)} %get-tuple-element.65.taps.refs_3_.taps0), custom_call_target="tpu_custom_call" | custom-call | flops 2000000000 | bytes 262144 | tf_op jit(solution)/shard_map/pallas_call | solution.py:742
  10.7 1.2 %collective-permute-done.2.refs_11_ = bf16[28,8,96]{2,1,0:T(8,128)(2,1)S(1)} collective-permute-done((bf16[28,8,96]{2,1,0:T(8,128)(2,1)S(1)}, bf16[28,8,96]{2,1,0:T(8,128)(2,1)S(1)}, u32[]{:S(2)}, u32[]{:S(2)}) %collective-permute-start.2) | collective-permute-done | bytes 43040 | tf_op jit(solution)/shard_map/ppermute | solution.py:56
  11.9 9.6 %shard_map.113 = (bf16[16,64,96]{2,1,0:T(8,128)(2,1)S(1)}, f32[2240,128]{1,0:T(8,128)S(1)}, f32[1600,128]{1,0:T(8,128)S(1)}, bf16[1376,128]{1,0:T(8,128)(2,1)S(1...) custom-call(f32[1792,128]{1,0:T(8,128)S(1)} %get-tuple-element.64.ta, ...), custom_call_target="tpu_custom_call" | custom-call | flops 15000000512 | bytes 262144 | tf_op jit(solution)/shard_map/pallas_call | solution.py:742
  21.5 2.0 %collective-permute-start.3 = (bf16[9,64,96]{2,1,0:T(8,128)(2,1)S(1)}, bf16[9,64,96]{2,1,0:T(8,128)(2,1)S(1)}, u32[]{:S(2)}, u32[]{:S(2)}) collective-permute-start(bf16[9,64,96]{2,1,0:T(8,128)(2,1)S(1)} %get-tuple-element.82), channel_id=1, source_target_pairs={{0,16},{1,17},{2,18},{3,19},{4,20},{5,21},{6,22},{7,23},{8,24},{9,... | collective-permute-start | bytes 331784 | tf_op jit(solution)/shard_map/ppermute | solution.py:51
  23.5 2.3 %shard_map.114 = (f32[56,128]{1,0:T(8,128)S(1)}, f32[384,128]{1,0:T(8,128)S(1)}, f32[384,128]{1,0:T(8,128)S(1)}, bf16[16,64,96]{2,1,0:T(8,128)(2,1)}) custom-call(f32[1600,128]{1,0:T(8,128)S(1)} %get-tuple-element.74.x1, f32[1024,128]{1,0:T(8,128)S(1)} %get-tuple-element.75.grad1, bf16[1024,128]{1,0:T(8,128)(2,1)S(1)} %get-tuple-element.76.normed1, ...), custom_call_target="tpu_custom_call" | custom-call | flops 3000000000 | bytes 262144 | tf_op jit(solution)/shard_map/pallas_call | solution.py:742
  25.8 1.8 %collective-permute-done.3.refs_0_ = bf16[9,64,96]{2,1,0:T(8,128)(2,1)S(1)} collective-permute-done((bf16[9,64,96]{2,1,0:T(8,128)(2,1)S(1)}, bf16[9,64,96]{2,1,0:T(8,128)(2,1)S(1)}, u32[]{:S(2)}, u32[]{:S(2)}) %collective-permute-start.3) | collective-permute-done | bytes 110624 | tf_op jit(solution)/shard_map/ppermute | solution.py:51
  27.9 1.8 %collective-permute-start.5 = (bf16[50,8,96]{2,1,0:T(8,128)(2,1)S(1)}, bf16[50,8,96]{2,1,0:T(8,128)(2,1)S(1)}, u32[]{:S(2)}, u32[]{:S(2)}) collective-permute-start(bf16[50,8,96]{2,1,0:T(8,128)(2,1)S(1)} %get-tuple-element.96), channel_id=1, source_target_pairs={{0,16},{1,2},{2,1},{3,4},{4,3},{5,6},{6,5},{7,8},{8,7},{9,10},{10,... | collective-permute-start | bytes 230408 | tf_op jit(solution)/shard_map/ppermute | solution.py:56
  29.7 1.2 %shard_map.116.refs_2_ = f32[912,128]{1,0:T(8,128)S(1)} custom-call(f32[1792,128]{1,0:T(8,128)S(1)} %get-tuple-element.83.tall.refs_0_, bf16[784,128]{1,0:T(8,128)(2,1)S(1)} %get-tuple-element.66.refs_4_.taps.refs_3_), custom_call_target="tpu_custom_call" | custom-call | flops 2000000000 | bytes 262144 | tf_op jit(solution)/shard_map/pallas_call | solution.py:742
  31.0 1.7 %collective-permute-done.5.refs_16_ = bf16[50,8,96]{2,1,0:T(8,128)(2,1)S(1)} collective-permute-done((bf16[50,8,96]{2,1,0:T(8,128)(2,1)S(1)}, bf16[50,8,96]{2,1,0:T(8,128)(2,1)S(1)}, u32[]{:S(2)}, u32[]{:S(2)}) %collective-permute-start.5) | collective-permute-done | bytes 76832 | tf_op jit(solution)/shard_map/ppermute | solution.py:56
  32.7 7.1 %shard_map.117 = (f32[1600,128]{1,0:T(8,128)S(1)}, f32[1024,128]{1,0:T(8,128)S(1)}, f32[640,128]{1,0:T(8,128)S(1)}, f32[80,128]{1,0:T(8,128)S(1)}, bf16[720,128]{1,0:T(8,128)(2,1)S(1)}) custom-call(f32[1792,128]{1,0:T(8,128)S(1)} %get-tuple-element.83.tall.refs_0_, f32[1408,128]{1,0:T(8,128)S(1)} %get-tuple-element.84.refs_1_, ...), custom_call_target="tpu_custom_call" | custom-call | flops 12000000000 | bytes 262144 | tf_op jit(solution)/shard_map/pallas_call | solution.py:742
  39.9 1.3 %collective-permute-done.6.refs_0_ = bf16[720,128]{1,0:T(8,128)(2,1)S(1)} collective-permute-done((bf16[720,128]{1,0:T(8,128)(2,1)S(1)}, bf16[720,128]{1,0:T(8,128)(2,1)S(1)}, u32[]{:S(2)}, u32[]{:S(2)}) %collective-permute-start.6) | collective-permute-done | bytes 184352 | tf_op jit(solution)/shard_map/ppermute | solution.py:896
  41.3 2.2 %collective-permute-start.7 = (bf16[240,128]{1,0:T(8,128)(2,1)S(1)}, bf16[240,128]{1,0:T(8,128)(2,1)S(1)}, u32[]{:S(2)}, u32[]{:S(2)}) collective-permute-start(bf16[240,128]{1,0:T(8,128)(2,1)S(1)} %get-tuple-element.105), channel_id=1, source_target_pairs={{0,2},{1,3},{2,0},{3,1},{4,6},{5,7},{6,4},{7,5},{8,10},{9,11},{10,... | collective-permute-start | bytes 184328 | tf_op jit(solution)/shard_map/ppermute | solution.py:896
  43.5 1.5 %collective-permute-start.8 = (bf16[240,128]{1,0:T(8,128)(2,1)S(1)}, bf16[240,128]{1,0:T(8,128)(2,1)S(1)}, u32[]{:S(2)}, u32[]{:S(2)}) collective-permute-start(bf16[240,128]{1,0:T(8,128)(2,1)S(1)} %get-tuple-element.106), channel_id=1, source_target_pairs={{0,16},{1,17},{2,18},{3,19},{4,20},{5,21},{6,22},{7,23},{8,24},{9,... | collective-permute-start | bytes 184328 | tf_op jit(solution)/shard_map/ppermute | solution.py:896
  45.0 2.1 %shard_map.119 = (bf16[16,64,96]{2,1,0:T(8,128)(2,1)}, f32[8,128]{1,0:T(8,128)S(1)}) custom-call(f32[1600,128]{1,0:T(8,128)S(1)} %get-tuple-element.97.grad0, f32[1024,128]{1,0:T(8,128)S(1)} %get-tuple-element.98.middle, bf16[784,128]{1,0:T(8,128)(2,1)S(1)} %get-tuple-element.65.taps.refs_3_.taps0, f32[80,128]{1,0:T(8,128)S(1)} %get-tuple-element.102.after.small), custom_call_target="tpu_custom_call" | custom-call | flops 3000000000 | bytes 262144 | tf_op jit(solution)/shard_map/pallas_call | solution.py:742
  47.1 1.1 %collective-permute-done.8.refs_1_ = bf16[240,128]{1,0:T(8,128)(2,1)S(1)} collective-permute-done((bf16[240,128]{1,0:T(8,128)(2,1)S(1)}, bf16[240,128]{1,0:T(8,128)(2,1)S(1)}, u32[]{:S(2)}, u32[]{:S(2)}) %collective-permute-start.8) | collective-permute-done | bytes 61472 | tf_op jit(solution)/shard_map/ppermute | solution.py:896
  48.2 1.9 %collective-permute-done.9.refs_2_ = bf16[240,128]{1,0:T(8,128)(2,1)S(1)} collective-permute-done((bf16[240,128]{1,0:T(8,128)(2,1)S(1)}, bf16[240,128]{1,0:T(8,128)(2,1)S(1)}, u32[]{:S(2)}, u32[]{:S(2)}) %collective-permute-start.9) | collective-permute-done | bytes 61472 | tf_op jit(solution)/shard_map/ppermute | solution.py:896
  50.2 2.7 %collective-permute-start.10 = (bf16[120,128]{1,0:T(8,128)(2,1)S(1)}, bf16[120,128]{1,0:T(8,128)(2,1)S(1)}, u32[]{:S(2)}, u32[]{:S(2)}) collective-permute-start(bf16[120,128]{1,0:T(8,128)(2,1)S(1)} %get-tuple-element.111), channel_id=1, source_target_pairs={{0,8},{1,9},{2,10},{3,11},{4,12},{5,13},{6,14},{7,15},{8,0},{9,1},... | collective-permute-start | bytes 92168 | tf_op jit(solution)/shard_map/ppermute | solution.py:896
  52.8 0.9 %collective-permute-start.11 = (bf16[120,128]{1,0:T(8,128)(2,1)S(1)}, bf16[120,128]{1,0:T(8,128)(2,1)S(1)}, u32[]{:S(2)}, u32[]{:S(2)}) collective-permute-start(bf16[120,128]{1,0:T(8,128)(2,1)S(1)} %get-tuple-element.112), channel_id=1, source_target_pairs={{0,4},{1,5},{2,6},{3,7},{4,0},{5,1},{6,2},{7,3},{8,12},{9,13},{10,... | collective-permute-start | bytes 92168 | tf_op jit(solution)/shard_map/ppermute | solution.py:896
  55.0 1.7 %collective-permute-done.11.refs_1_ = bf16[120,128]{1,0:T(8,128)(2,1)S(1)} collective-permute-done((bf16[120,128]{1,0:T(8,128)(2,1)S(1)}, bf16[120,128]{1,0:T(8,128)(2,1)S(1)}, u32[]{:S(2)}, u32[]{:S(2)}) %collective-permute-start.11) | collective-permute-done | bytes 30752 | tf_op jit(solution)/shard_map/ppermute | solution.py:896
  56.7 2.7 %collective-permute-done.12.refs_2_ = bf16[120,128]{1,0:T(8,128)(2,1)S(1)} collective-permute-done((bf16[120,128]{1,0:T(8,128)(2,1)S(1)}, bf16[120,128]{1,0:T(8,128)(2,1)S(1)}, u32[]{:S(2)}, u32[]{:S(2)}) %collective-permute-start.12) | collective-permute-done | bytes 30752 | tf_op jit(solution)/shard_map/ppermute | solution.py:896
  (27 shorter events, 3.7 us)
Async XLA Ops:
  0.6 1.0 %copy-start = (bf16[16,64,96]{2,1,0:T(8,128)(2,1)S(1)}, bf16[16,64,96]{2,1,0:T(8,128)(2,1)}, u32[]{:S(2)}) copy-start(bf16[16,64,96]{2,1,0:T(8,128)(2,1)} %image_in.1) | copy-start | bytes 589828
  1.6 3.1 %copy-start.2 = (bf16[2,96,384]{2,1,0:T(8,128)(2,1)S(1)}, bf16[2,96,384]{2,1,0:T(8,128)(2,1)}, u32[]{:S(2)}) copy-start(bf16[2,96,384]{2,1,0:T(8,128)(2,1)} %up_in.1) | copy-start | bytes 442372
  1.6 3.1 %copy-start.3 = (bf16[2,384,96]{1,2,0:T(8,128)(2,1)S(1)}, bf16[2,384,96]{1,2,0:T(8,128)(2,1)}, u32[]{:S(2)}) copy-start(bf16[2,384,96]{1,2,0:T(8,128)(2,1)} %param.10) | copy-start | bytes 442372
  1.6 3.1 %copy-start.4 = (f32[2,7,7,96]{3,0,2,1:T(2,128)S(1)}, f32[2,7,7,96]{3,0,2,1:T(2,128)}, u32[]{:S(2)}) copy-start(f32[2,7,7,96]{3,0,2,1:T(2,128)} %param.7) | copy-start | bytes 112900
  1.6 3.1 %copy-start.5 = (f32[2,96]{1,0:T(2,128)S(1)}, f32[2,96]{1,0:T(2,128)}, u32[]{:S(2)}) copy-start(f32[2,96]{1,0:T(2,128)} %gains_in.1) | copy-start | bytes 2308
  1.7 5.8 %collective-permute-start = (bf16[6,64,96]{2,1,0:T(8,128)(2,1)S(1)}, bf16[6,64,96]{2,1,0:T(8,128)(2,1)S(1)}, u32[]{:S(2)}, u32[]{:S(2)}) collective-permute-start(bf16[6,64,96]{2,1,0:T(8,128)(2,1)S(1)} %get-tuple-element.63), channel_id=1, source_target_pairs={{0,16},{1,17},{2,18},{3,19},{4,20},{5,21},{6,22},{7,23},{8,24},{9,... | collective-permute-start | bytes 221192 | tf_op jit(solution)/shard_map/ppermute | solution.py:51
  7.6 3.1 %collective-permute-start.1 = (bf16[28,8,96]{2,1,0:T(8,128)(2,1)S(1)}, bf16[28,8,96]{2,1,0:T(8,128)(2,1)S(1)}, u32[]{:S(2)}, u32[]{:S(2)}) collective-permute-start(bf16[28,8,96]{2,1,0:T(8,128)(2,1)S(1)} %get-tuple-element.72), channel_id=1, source_target_pairs={{0,1},{1,0},{2,3},{3,2},{4,5},{5,4},{6,7},{7,6},{8,9},{9,8},{10,11... | collective-permute-start | bytes 129032 | tf_op jit(solution)/shard_map/ppermute | solution.py:56
  7.7 4.2 %collective-permute-start.2 = (bf16[28,8,96]{2,1,0:T(8,128)(2,1)S(1)}, bf16[28,8,96]{2,1,0:T(8,128)(2,1)S(1)}, u32[]{:S(2)}, u32[]{:S(2)}) collective-permute-start(bf16[28,8,96]{2,1,0:T(8,128)(2,1)S(1)} %get-tuple-element.73), channel_id=1, source_target_pairs={{0,16},{1,2},{2,1},{3,4},{4,3},{5,6},{6,5},{7,8},{8,7},{9,10},{10,... | collective-permute-start | bytes 129032 | tf_op jit(solution)/shard_map/ppermute | solution.py:56
  9.6 2.4 %copy-start.1 = (bf16[16,64,96]{2,1,0:T(8,128)(2,1)S(1)}, bf16[16,64,96]{2,1,0:T(8,128)(2,1)}, u32[]{:S(2)}) copy-start(bf16[16,64,96]{2,1,0:T(8,128)(2,1)} %cot.3) | copy-start | bytes 589828
  21.5 6.1 %collective-permute-start.3 = (bf16[9,64,96]{2,1,0:T(8,128)(2,1)S(1)}, bf16[9,64,96]{2,1,0:T(8,128)(2,1)S(1)}, u32[]{:S(2)}, u32[]{:S(2)}) collective-permute-start(bf16[9,64,96]{2,1,0:T(8,128)(2,1)S(1)} %get-tuple-element.82), channel_id=1, source_target_pairs={{0,16},{1,17},{2,18},{3,19},{4,20},{5,21},{6,22},{7,23},{8,24},{9,... | collective-permute-start | bytes 331784 | tf_op jit(solution)/shard_map/ppermute | solution.py:51
  27.9 3.1 %collective-permute-start.4 = (bf16[50,8,96]{2,1,0:T(8,128)(2,1)S(1)}, bf16[50,8,96]{2,1,0:T(8,128)(2,1)S(1)}, u32[]{:S(2)}, u32[]{:S(2)}) collective-permute-start(bf16[50,8,96]{2,1,0:T(8,128)(2,1)S(1)} %get-tuple-element.95), channel_id=1, source_target_pairs={{0,1},{1,0},{2,3},{3,2},{4,5},{5,4},{6,7},{7,6},{8,9},{9,8},{10,11... | collective-permute-start | bytes 230408 | tf_op jit(solution)/shard_map/ppermute | solution.py:56
  27.9 4.7 %collective-permute-start.5 = (bf16[50,8,96]{2,1,0:T(8,128)(2,1)S(1)}, bf16[50,8,96]{2,1,0:T(8,128)(2,1)S(1)}, u32[]{:S(2)}, u32[]{:S(2)}) collective-permute-start(bf16[50,8,96]{2,1,0:T(8,128)(2,1)S(1)} %get-tuple-element.96), channel_id=1, source_target_pairs={{0,16},{1,2},{2,1},{3,4},{4,3},{5,6},{6,5},{7,8},{8,7},{9,10},{10,... | collective-permute-start | bytes 230408 | tf_op jit(solution)/shard_map/ppermute | solution.py:56
  39.7 1.5 %collective-permute-start.6 = (bf16[720,128]{1,0:T(8,128)(2,1)S(1)}, bf16[720,128]{1,0:T(8,128)(2,1)S(1)}, u32[]{:S(2)}, u32[]{:S(2)}) collective-permute-start(bf16[720,128]{1,0:T(8,128)(2,1)S(1)} %get-tuple-element.101), channel_id=1, source_target_pairs={{0,1},{1,0},{2,3},{3,2},{4,5},{5,4},{6,7},{7,6},{8,9},{9,8},{10,11... | collective-permute-start | bytes 552968 | tf_op jit(solution)/shard_map/ppermute | solution.py:896
  41.3 5.8 %collective-permute-start.7 = (bf16[240,128]{1,0:T(8,128)(2,1)S(1)}, bf16[240,128]{1,0:T(8,128)(2,1)S(1)}, u32[]{:S(2)}, u32[]{:S(2)}) collective-permute-start(bf16[240,128]{1,0:T(8,128)(2,1)S(1)} %get-tuple-element.105), channel_id=1, source_target_pairs={{0,2},{1,3},{2,0},{3,1},{4,6},{5,7},{6,4},{7,5},{8,10},{9,11},{10,... | collective-permute-start | bytes 184328 | tf_op jit(solution)/shard_map/ppermute | solution.py:896
  43.5 4.7 %collective-permute-start.8 = (bf16[240,128]{1,0:T(8,128)(2,1)S(1)}, bf16[240,128]{1,0:T(8,128)(2,1)S(1)}, u32[]{:S(2)}, u32[]{:S(2)}) collective-permute-start(bf16[240,128]{1,0:T(8,128)(2,1)S(1)} %get-tuple-element.106), channel_id=1, source_target_pairs={{0,16},{1,17},{2,18},{3,19},{4,20},{5,21},{6,22},{7,23},{8,24},{9,... | collective-permute-start | bytes 184328 | tf_op jit(solution)/shard_map/ppermute | solution.py:896
  45.0 5.1 %collective-permute-start.9 = (bf16[240,128]{1,0:T(8,128)(2,1)S(1)}, bf16[240,128]{1,0:T(8,128)(2,1)S(1)}, u32[]{:S(2)}, u32[]{:S(2)}) collective-permute-start(bf16[240,128]{1,0:T(8,128)(2,1)S(1)} %get-tuple-element.107), channel_id=1, source_target_pairs={{0,18},{1,19},{2,16},{3,17},{4,22},{5,23},{6,20},{7,21},{8,26},{9,... | collective-permute-start | bytes 184328 | tf_op jit(solution)/shard_map/ppermute | solution.py:896
  50.2 4.9 %collective-permute-start.10 = (bf16[120,128]{1,0:T(8,128)(2,1)S(1)}, bf16[120,128]{1,0:T(8,128)(2,1)S(1)}, u32[]{:S(2)}, u32[]{:S(2)}) collective-permute-start(bf16[120,128]{1,0:T(8,128)(2,1)S(1)} %get-tuple-element.111), channel_id=1, source_target_pairs={{0,8},{1,9},{2,10},{3,11},{4,12},{5,13},{6,14},{7,15},{8,0},{9,1},... | collective-permute-start | bytes 92168 | tf_op jit(solution)/shard_map/ppermute | solution.py:896
  52.8 3.9 %collective-permute-start.11 = (bf16[120,128]{1,0:T(8,128)(2,1)S(1)}, bf16[120,128]{1,0:T(8,128)(2,1)S(1)}, u32[]{:S(2)}, u32[]{:S(2)}) collective-permute-start(bf16[120,128]{1,0:T(8,128)(2,1)S(1)} %get-tuple-element.112), channel_id=1, source_target_pairs={{0,4},{1,5},{2,6},{3,7},{4,0},{5,1},{6,2},{7,3},{8,12},{9,13},{10,... | collective-permute-start | bytes 92168 | tf_op jit(solution)/shard_map/ppermute | solution.py:896
  53.8 5.7 %collective-permute-start.12 = (bf16[120,128]{1,0:T(8,128)(2,1)S(1)}, bf16[120,128]{1,0:T(8,128)(2,1)S(1)}, u32[]{:S(2)}, u32[]{:S(2)}) collective-permute-start(bf16[120,128]{1,0:T(8,128)(2,1)S(1)} %get-tuple-element.113), channel_id=1, source_target_pairs={{0,12},{1,13},{2,14},{3,15},{4,8},{5,9},{6,10},{7,11},{8,4},{9,5},... | collective-permute-start | bytes 92168 | tf_op jit(solution)/shard_map/ppermute | solution.py:896

commit v8 on v6

--- a/solution.py
+++ b/solution.py
@@ -256,15 +256,14 @@
 
 
 def gelu_parts(v):
-    d = 1.0 + (0.3275911 * inv_sqrt_two) * jnp.abs(v)
-    t = pl.reciprocal(d, approx=True)
-    t = t * (2.0 - d * t)
+    p = 0.3275911 * inv_sqrt_two
+    c1, c2, c3, c4, c5 = (
+        0.5 * c / p ** (k + 1)
+        for k, c in enumerate((0.254829592, -0.284496736, 1.421413741, -1.453152027, 1.061405429))
+    )
+    t = pl.reciprocal(jnp.abs(v) + 1.0 / p, approx=True)
     bell = jnp.exp2(v * v * (-0.5 * log2_e))
-    series = 0.5 * 1.061405429 * t + 0.5 * -1.453152027
-    series = series * t + 0.5 * 1.421413741
-    series = series * t + 0.5 * -0.284496736
-    series = series * t + 0.5 * 0.254829592
-    tail = series * t * bell
+    tail = ((((c5 * t + c4) * t + c3) * t + c2) * t + c1) * t * bell
     cdf = jnp.where(v >= 0.0, 1.0 - tail, tail)
     return (v * cdf, cdf + v * (bell * inv_sqrt_two_pi))
 
@@ -567,8 +566,7 @@
 
     taps_rows = size * size + 1
     merged = jnp.concatenate([small[0:taps_rows, :], taps_sum1[0:taps_rows, :]], axis=0) * dims.factor
-    merged = jnp.concatenate([merged, jnp.zeros((dims.small_rows - 2 * taps_rows, LANES), f32)], axis=0)
-    merged = merged.astype(bf16)
+    merged = fold_rows(merged, dims.small_rows, channels).astype(bf16)
     small_keep[...] = merged.astype(f32)
 
     layer_rows, part, half = (dims.layer_rows, dims.part, dims.half)
@@ -602,6 +600,37 @@
     split(dims, 0, slabs, merged, keep, (send,))
 
 
+def fold_rows(x, rows, used):
+    n = x.shape[0]
+    if rows >= n:
+        return pad_rows(x, rows)
+    assert used <= 96
+    stride = ceil8(n - rows)
+    rest = pad_rows(x[rows:], stride)
+    pieces_of = pad_rows(jnp.concatenate([pltpu.roll(rest, 96 - 32 * k, 1) for k in range(3)], axis=0), rows)
+    lane = lax.broadcasted_iota(jnp.int32, (rows, LANES), 1)
+    return jnp.where(lane < 96, x[:rows], pieces_of)
+
+
+def pad_rows(x, rows):
+    if rows == x.shape[0]:
+        return x
+    return jnp.concatenate([x, jnp.zeros((rows - x.shape[0], LANES), x.dtype)], axis=0)
+
+
+def unfold_rows(x, n):
+    rows = x.shape[0]
+    if rows >= n:
+        return x[:n]
+    stride = ceil8(n - rows)
+    lane = lax.broadcasted_iota(jnp.int32, (stride, LANES), 1)
+    rest = jnp.zeros((stride, LANES), x.dtype)
+    for k in range(3):
+        moved = pltpu.roll(x[k * stride : (k + 1) * stride], 32 + 32 * k, 1)
+        rest = jnp.where(jnp.logical_and(lane >= 32 * k, lane < 32 * k + 32), moved, rest)
+    return jnp.concatenate([x, rest[: n - rows]], axis=0)
+
+
 def split(dims, stage, slabs, merged, keep, sends):
     group = dims.groups[stage]
     count = slabs.shape[0] >> len(group)
@@ -647,6 +676,7 @@
 def last_kernel(dims, keep, small, *refs):
     gots, (kernel_out, gain_out, up_out, down_out) = (refs[:-4], refs[-4:])
     total, merged = gather_up(keep, small, gots)
+    merged = unfold_rows(merged, 2 * (dims.size * dims.size + 1))
     size, channels, half, part = (dims.size, dims.channels, dims.half, dims.part)
     for layer in range(2):
         block = total[layer * dims.layer_rows : layer * dims.layer_rows + part]
@@ -699,7 +729,7 @@
     d.part = up_weights.shape[2] // d.col_count
     d.layer_rows = ceil8(d.part)
     d.count = d.row_count * d.col_count
-    d.small_rows = -(-2 * (d.size * d.size + 1) // 16) * 16
+    d.small_rows = 80 if d.size == 7 and d.channels <= 96 else -(-2 * (d.size * d.size + 1) // 16) * 16
     d.factor = 1.0 / math.sqrt(d.rows * d.cols * d.count)
     row_bits, col_bits = (d.row_count.bit_length() - 1, d.col_count.bit_length() - 1)
     bits = [("row", b) for b in range(row_bits)] + [("col", b) for b in range(1, col_bits)]

time: 57.2 us -> 56 us (0.979)
  Pallas kernels: 24.2 us -> 23.5 us
    pallas_call x11, Pallas kernels: 24.2 us -> 23.5 us  [run(): pl.pallas_call(kernel, out_shape=shapes, in_specs=[far] * in_hbm + [space...]
where the time goes in v8:
time: 56 us; the launch traced here: 55.9 us
  Pallas kernels  23.5 us (42%)
  starting transfers between devices  19.3 us (34%)
  waiting for transfers between devices  11.4 us (20%)
  local copies, waits for them, and re-layouts  0.96 us (2%)
  between operations  0.76 us (1%)
    pallas_call x11, Pallas kernels, run(): pl.pallas_call(kernel, out_shape=shapes, in_specs=[far] * in_hbm + [space...  23.5 us
    ppermute x10, starting transfers between devices, exchange(): lax.ppermute(strip, ('row', 'col'), swap_pairs(row_count, col_count, rs,...  11.1 us
    ppermute x7, waiting for transfers between devices, per_device(): lax.ppermute(x, axes, swap_by(d, group, mask))  8.32 us
    ppermute x7, starting transfers between devices, per_device(): lax.ppermute(x, axes, swap_by(d, group, mask))  8.15 us
    ppermute x10, waiting for transfers between devices, exchange(): lax.ppermute(strip, ('row', 'col'), swap_pairs(row_count, col_count, rs,...  3.04 us
  transfers between devices with their start and end apart: 17, of which 8 were waited for; matrix products, arithmetic and copies ran while one was open for 0% of the time, Pallas kernels for 9%

profile of v8, /device:TPU:0, one launch (start us, length us, event | category | flops | bytes accessed | tf_op | source)
XLA Modules:
  0.0 55.9 jit_solution(3401771539510294696)
XLA Ops:
  0.6 0.9 %copy-done = bf16[16,64,96]{2,1,0:T(8,128)(2,1)S(1)} copy-done((bf16[16,64,96]{2,1,0:T(8,128)(2,1)S(1)}, bf16[16,64,96]{2,1,0:T(8,128)(2,1)}, u32[]{:S(2)}) %copy-start) | copy-done | bytes 196632
  1.6 3.0 %collective-permute-start.2 = (bf16[6,64,96]{2,1,0:T(8,128)(2,1)S(1)}, bf16[6,64,96]{2,1,0:T(8,128)(2,1)S(1)}, u32[]{:S(2)}, u32[]{:S(2)}) collective-permute-start(bf16[6,64,96]{2,1,0:T(8,128)(2,1)S(1)} %get-tuple-element.71.refs_0_), channel_id=1, source_target_pairs={{0,16},{1,17},{2,18},{3,19},{4,20},{5,21},{6,22},{7,23},{8,24},{9,... | collective-permute-start | bytes 221192 | tf_op jit(solution)/shard_map/ppermute | solution.py:55
  4.8 1.2 %collective-permute-start.4 = (bf16[6,8,96]{2,1,0:T(8,128)(2,1)S(1)}, bf16[6,8,96]{2,1,0:T(8,128)(2,1)S(1)}, u32[]{:S(2)}, u32[]{:S(2)}) collective-permute-start(bf16[6,8,96]{2,1,0:T(8,128)(2,1)S(1)} %get-tuple-element.75), channel_id=1, source_target_pairs={{0,16},{1,18},{2,17},{3,20},{4,19},{5,22},{6,21},{7,24},{8,23},{9,... | collective-permute-start | bytes 27656 | tf_op jit(solution)/shard_map/ppermute | solution.py:55
  6.0 1.1 %collective-permute-start = (bf16[16,8,96]{2,1,0:T(8,128)(2,1)S(1)}, bf16[16,8,96]{2,1,0:T(8,128)(2,1)S(1)}, u32[]{:S(2)}, u32[]{:S(2)}) collective-permute-start(bf16[16,8,96]{2,1,0:T(8,128)(2,1)S(1)} %get-tuple-element.72), channel_id=1, source_target_pairs={{0,1},{1,0},{2,3},{3,2},{4,5},{5,4},{6,7},{7,6},{8,9},{9,8},{10,11... | collective-permute-start | bytes 73736 | tf_op jit(solution)/shard_map/ppermute | solution.py:55
  7.0 0.9 %collective-permute-start.1 = (bf16[16,8,96]{2,1,0:T(8,128)(2,1)S(1)}, bf16[16,8,96]{2,1,0:T(8,128)(2,1)S(1)}, u32[]{:S(2)}, u32[]{:S(2)}) collective-permute-start(bf16[16,8,96]{2,1,0:T(8,128)(2,1)S(1)} %get-tuple-element.73), channel_id=1, source_target_pairs={{0,16},{1,2},{2,1},{3,4},{4,3},{5,6},{6,5},{7,8},{8,7},{9,10},{10,... | collective-permute-start | bytes 73736 | tf_op jit(solution)/shard_map/ppermute | solution.py:55
  8.8 2.2 %collective-permute-done.1.refs_10_ = bf16[16,8,96]{2,1,0:T(8,128)(2,1)S(1)} collective-permute-done((bf16[16,8,96]{2,1,0:T(8,128)(2,1)S(1)}, bf16[16,8,96]{2,1,0:T(8,128)(2,1)S(1)}, u32[]{:S(2)}, u32[]{:S(2)}) %collective-permute-start.1) | collective-permute-done | bytes 24608 | tf_op jit(solution)/shard_map/ppermute | solution.py:55
  10.9 10.7 %shard_map.112 = (bf16[16,64,96]{2,1,0:T(8,128)(2,1)S(1)}, f32[2240,128]{1,0:T(8,128)S(1)}, f32[1600,128]{1,0:T(8,128)S(1)}, bf16[1376,128]{1,0:T(8,128)(2,1)S(1...) custom-call(bf16[16,64,96]{2,1,0:T(8,128)(2,1)S(1)} %get-tuple-eleme, ...), custom_call_target="tpu_custom_call" | custom-call | flops 15000000512 | bytes 262144 | tf_op jit(solution)/shard_map/pallas_call | solution.py:760
  21.7 1.0 %collective-permute-start.7 = (bf16[9,64,96]{2,1,0:T(8,128)(2,1)S(1)}, bf16[9,64,96]{2,1,0:T(8,128)(2,1)S(1)}, u32[]{:S(2)}, u32[]{:S(2)}) collective-permute-start(bf16[9,64,96]{2,1,0:T(8,128)(2,1)S(1)} %get-tuple-element.94.refs_0_), channel_id=1, source_target_pairs={{0,16},{1,17},{2,18},{3,19},{4,20},{5,21},{6,22},{7,23},{8,24},{9,... | collective-permute-start | bytes 331784 | tf_op jit(solution)/shard_map/ppermute | solution.py:55
  22.8 1.2 %collective-permute-start.9 = (bf16[9,8,96]{2,1,0:T(8,128)(2,1)S(1)}, bf16[9,8,96]{2,1,0:T(8,128)(2,1)S(1)}, u32[]{:S(2)}, u32[]{:S(2)}) collective-permute-start(bf16[9,8,96]{2,1,0:T(8,128)(2,1)S(1)} %get-tuple-element.98), channel_id=1, source_target_pairs={{0,16},{1,18},{2,17},{3,20},{4,19},{5,22},{6,21},{7,24},{8,23},{9,... | collective-permute-start | bytes 41480 | tf_op jit(solution)/shard_map/ppermute | solution.py:55
  24.0 1.6 %collective-permute-start.5 = (bf16[32,8,96]{2,1,0:T(8,128)(2,1)S(1)}, bf16[32,8,96]{2,1,0:T(8,128)(2,1)S(1)}, u32[]{:S(2)}, u32[]{:S(2)}) collective-permute-start(bf16[32,8,96]{2,1,0:T(8,128)(2,1)S(1)} %get-tuple-element.95), channel_id=1, source_target_pairs={{0,1},{1,0},{2,3},{3,2},{4,5},{5,4},{6,7},{7,6},{8,9},{9,8},{10,11... | collective-permute-start | bytes 147464 | tf_op jit(solution)/shard_map/ppermute | solution.py:55
  25.5 1.1 %collective-permute-start.6 = (bf16[32,8,96]{2,1,0:T(8,128)(2,1)S(1)}, bf16[32,8,96]{2,1,0:T(8,128)(2,1)S(1)}, u32[]{:S(2)}, u32[]{:S(2)}) collective-permute-start(bf16[32,8,96]{2,1,0:T(8,128)(2,1)S(1)} %get-tuple-element.96), channel_id=1, source_target_pairs={{0,16},{1,2},{2,1},{3,4},{4,3},{5,6},{6,5},{7,8},{8,7},{9,10},{10,... | collective-permute-start | bytes 147464 | tf_op jit(solution)/shard_map/ppermute | solution.py:55
  26.6 2.3 %shard_map.113 = (f32[56,128]{1,0:T(8,128)S(1)}, f32[384,128]{1,0:T(8,128)S(1)}, f32[384,128]{1,0:T(8,128)S(1)}, bf16[16,64,96]{2,1,0:T(8,128)(2,1)}) custom-call(f32[1600,128]{1,0:T(8,128)S(1)} %get-tuple-element.76.x1, f32[1024,128]{1,0:T(8,128)S(1)} %get-tuple-element.77.grad1.refs_0_, bf16[1024,128]{1,0:T(8,128)(2,1)S(1)} %get-tuple-element.78.normed1, ...), custom_call_target="tpu_custom_call" | custom-call | flops 3000000000 | bytes 262144 | tf_op jit(solution)/shard_map/pallas_call | solution.py:760
  28.9 0.8 %collective-permute-done.6.refs_15_ = bf16[32,8,96]{2,1,0:T(8,128)(2,1)S(1)} collective-permute-done((bf16[32,8,96]{2,1,0:T(8,128)(2,1)S(1)}, bf16[32,8,96]{2,1,0:T(8,128)(2,1)S(1)}, u32[]{:S(2)}, u32[]{:S(2)}) %collective-permute-start.6) | collective-permute-done | bytes 49184 | tf_op jit(solution)/shard_map/ppermute | solution.py:55
  29.8 6.6 %shard_map.115 = (f32[1600,128]{1,0:T(8,128)S(1)}, f32[1024,128]{1,0:T(8,128)S(1)}, f32[768,128]{1,0:T(8,128)S(1)}, f32[80,128]{1,0:T(8,128)S(1)}, bf16[848,128]{1,0:T(8,128)(2,1)S(1)}) custom-call(f32[1024,128]{1,0:T(8,128)S(1)} %get-tuple-element.77.grad1.refs_0_, bf16[16,64,96]{2,1,0:T(8,128)(2,1)S(1)} %copy-done.1, ...), custom_call_target="tpu_custom_call" | custom-call | flops 12000000000 | bytes 262144 | tf_op jit(solution)/shard_map/pallas_call | solution.py:760
  36.6 1.4 %collective-permute-done.10.refs_0_ = bf16[848,128]{1,0:T(8,128)(2,1)S(1)} collective-permute-done((bf16[848,128]{1,0:T(8,128)(2,1)S(1)}, bf16[848,128]{1,0:T(8,128)(2,1)S(1)}, u32[]{:S(2)}, u32[]{:S(2)}) %collective-permute-start.10) | collective-permute-done | bytes 217120 | tf_op jit(solution)/shard_map/ppermute | solution.py:896
  38.0 1.8 %collective-permute-start.11 = (bf16[272,128]{1,0:T(8,128)(2,1)S(1)}, bf16[272,128]{1,0:T(8,128)(2,1)S(1)}, u32[]{:S(2)}, u32[]{:S(2)}) collective-permute-start(bf16[272,128]{1,0:T(8,128)(2,1)S(1)} %get-tuple-element.107), channel_id=1, source_target_pairs={{0,2},{1,3},{2,0},{3,1},{4,6},{5,7},{6,4},{7,5},{8,10},{9,11},{10,... | collective-permute-start | bytes 208904 | tf_op jit(solution)/shard_map/ppermute | solution.py:896
  39.9 1.3 %collective-permute-start.12 = (bf16[272,128]{1,0:T(8,128)(2,1)S(1)}, bf16[272,128]{1,0:T(8,128)(2,1)S(1)}, u32[]{:S(2)}, u32[]{:S(2)}) collective-permute-start(bf16[272,128]{1,0:T(8,128)(2,1)S(1)} %get-tuple-element.108), channel_id=1, source_target_pairs={{0,16},{1,17},{2,18},{3,19},{4,20},{5,21},{6,22},{7,23},{8,24},{9,... | collective-permute-start | bytes 208904 | tf_op jit(solution)/shard_map/ppermute | solution.py:896
  41.6 2.1 %shard_map.117 = (bf16[16,64,96]{2,1,0:T(8,128)(2,1)}, f32[8,128]{1,0:T(8,128)S(1)}) custom-call(f32[1600,128]{1,0:T(8,128)S(1)} %get-tuple-element.99.grad0, f32[1024,128]{1,0:T(8,128)S(1)} %get-tuple-element.100.middle, bf16[784,128]{1,0:T(8,128)(2,1)S(1)} %get-tuple-element.64.refs_2_.taps0, f32[80,128]{1,0:T(8,128)S(1)} %get-tuple-element.104.after.small), custom_call_target="tpu_custom_call" | custom-call | flops 3000000000 | bytes 262144 | tf_op jit(solution)/shard_map/pallas_call | solution.py:760
  43.7 1.1 %collective-permute-done.12.refs_1_ = bf16[272,128]{1,0:T(8,128)(2,1)S(1)} collective-permute-done((bf16[272,128]{1,0:T(8,128)(2,1)S(1)}, bf16[272,128]{1,0:T(8,128)(2,1)S(1)}, u32[]{:S(2)}, u32[]{:S(2)}) %collective-permute-start.12) | collective-permute-done | bytes 69664 | tf_op jit(solution)/shard_map/ppermute | solution.py:896
  44.8 1.5 %collective-permute-done.13.refs_2_ = bf16[272,128]{1,0:T(8,128)(2,1)S(1)} collective-permute-done((bf16[272,128]{1,0:T(8,128)(2,1)S(1)}, bf16[272,128]{1,0:T(8,128)(2,1)S(1)}, u32[]{:S(2)}, u32[]{:S(2)}) %collective-permute-start.13) | collective-permute-done | bytes 69664 | tf_op jit(solution)/shard_map/ppermute | solution.py:896
  46.4 2.7 %collective-permute-start.14 = (bf16[128,128]{1,0:T(8,128)(2,1)S(1)}, bf16[128,128]{1,0:T(8,128)(2,1)S(1)}, u32[]{:S(2)}, u32[]{:S(2)}) collective-permute-start(bf16[128,128]{1,0:T(8,128)(2,1)S(1)} %get-tuple-element.113), channel_id=1, source_target_pairs={{0,8},{1,9},{2,10},{3,11},{4,12},{5,13},{6,14},{7,15},{8,0},{9,1},... | collective-permute-start | bytes 98312 | tf_op jit(solution)/shard_map/ppermute | solution.py:896
  49.4 1.4 %collective-permute-start.16 = (bf16[128,128]{1,0:T(8,128)(2,1)S(1)}, bf16[128,128]{1,0:T(8,128)(2,1)S(1)}, u32[]{:S(2)}, u32[]{:S(2)}) collective-permute-start(bf16[128,128]{1,0:T(8,128)(2,1)S(1)} %get-tuple-element.115), channel_id=1, source_target_pairs={{0,12},{1,13},{2,14},{3,15},{4,8},{5,9},{6,10},{7,11},{8,4},{9,5},... | collective-permute-start | bytes 98312 | tf_op jit(solution)/shard_map/ppermute | solution.py:896
  51.3 1.7 %collective-permute-done.15.refs_1_ = bf16[128,128]{1,0:T(8,128)(2,1)S(1)} collective-permute-done((bf16[128,128]{1,0:T(8,128)(2,1)S(1)}, bf16[128,128]{1,0:T(8,128)(2,1)S(1)}, u32[]{:S(2)}, u32[]{:S(2)}) %collective-permute-start.15) | collective-permute-done | bytes 32800 | tf_op jit(solution)/shard_map/ppermute | solution.py:896
  53.0 2.1 %collective-permute-done.16.refs_2_ = bf16[128,128]{1,0:T(8,128)(2,1)S(1)} collective-permute-done((bf16[128,128]{1,0:T(8,128)(2,1)S(1)}, bf16[128,128]{1,0:T(8,128)(2,1)S(1)}, u32[]{:S(2)}, u32[]{:S(2)}) %collective-permute-start.16) | collective-permute-done | bytes 32800 | tf_op jit(solution)/shard_map/ppermute | solution.py:896
  (33 shorter events, 3.4 us)
Async XLA Ops:
  0.6 1.0 %copy-start = (bf16[16,64,96]{2,1,0:T(8,128)(2,1)S(1)}, bf16[16,64,96]{2,1,0:T(8,128)(2,1)}, u32[]{:S(2)}) copy-start(bf16[16,64,96]{2,1,0:T(8,128)(2,1)} %image_in.1) | copy-start | bytes 589828
  1.6 9.3 %collective-permute-start.2 = (bf16[6,64,96]{2,1,0:T(8,128)(2,1)S(1)}, bf16[6,64,96]{2,1,0:T(8,128)(2,1)S(1)}, u32[]{:S(2)}, u32[]{:S(2)}) collective-permute-start(bf16[6,64,96]{2,1,0:T(8,128)(2,1)S(1)} %get-tuple-element.71.refs_0_), channel_id=1, source_target_pairs={{0,16},{1,17},{2,18},{3,19},{4,20},{5,21},{6,22},{7,23},{8,24},{9,... | collective-permute-start | bytes 221192 | tf_op jit(solution)/shard_map/ppermute | solution.py:55
  4.7 3.3 %copy-start.2 = (bf16[2,96,384]{2,1,0:T(8,128)(2,1)S(1)}, bf16[2,96,384]{2,1,0:T(8,128)(2,1)}, u32[]{:S(2)}) copy-start(bf16[2,96,384]{2,1,0:T(8,128)(2,1)} %up_in.1) | copy-start | bytes 442372
  4.7 3.3 %copy-start.3 = (bf16[2,384,96]{1,2,0:T(8,128)(2,1)S(1)}, bf16[2,384,96]{1,2,0:T(8,128)(2,1)}, u32[]{:S(2)}) copy-start(bf16[2,384,96]{1,2,0:T(8,128)(2,1)} %param.10) | copy-start | bytes 442372
  4.7 3.3 %copy-start.4 = (f32[2,7,7,96]{3,0,2,1:T(2,128)S(1)}, f32[2,7,7,96]{3,0,2,1:T(2,128)}, u32[]{:S(2)}) copy-start(f32[2,7,7,96]{3,0,2,1:T(2,128)} %param.7) | copy-start | bytes 112900
  4.7 3.3 %copy-start.5 = (f32[2,96]{1,0:T(2,128)S(1)}, f32[2,96]{1,0:T(2,128)}, u32[]{:S(2)}) copy-start(f32[2,96]{1,0:T(2,128)} %gains_in.1) | copy-start | bytes 2308
  4.7 4.0 %collective-permute-start.3 = (bf16[6,8,96]{2,1,0:T(8,128)(2,1)S(1)}, bf16[6,8,96]{2,1,0:T(8,128)(2,1)S(1)}, u32[]{:S(2)}, u32[]{:S(2)}) collective-permute-start(bf16[6,8,96]{2,1,0:T(8,128)(2,1)S(1)} %get-tuple-element.74), channel_id=1, source_target_pairs={{0,17},{1,16},{2,19},{3,18},{4,21},{5,20},{6,23},{7,22},{8,25},{9,... | collective-permute-start | bytes 27656 | tf_op jit(solution)/shard_map/ppermute | solution.py:55
  4.8 4.0 %collective-permute-start.4 = (bf16[6,8,96]{2,1,0:T(8,128)(2,1)S(1)}, bf16[6,8,96]{2,1,0:T(8,128)(2,1)S(1)}, u32[]{:S(2)}, u32[]{:S(2)}) collective-permute-start(bf16[6,8,96]{2,1,0:T(8,128)(2,1)S(1)} %get-tuple-element.75), channel_id=1, source_target_pairs={{0,16},{1,18},{2,17},{3,20},{4,19},{5,22},{6,21},{7,24},{8,23},{9,... | collective-permute-start | bytes 27656 | tf_op jit(solution)/shard_map/ppermute | solution.py:55
  6.0 2.8 %collective-permute-start = (bf16[16,8,96]{2,1,0:T(8,128)(2,1)S(1)}, bf16[16,8,96]{2,1,0:T(8,128)(2,1)S(1)}, u32[]{:S(2)}, u32[]{:S(2)}) collective-permute-start(bf16[16,8,96]{2,1,0:T(8,128)(2,1)S(1)} %get-tuple-element.72), channel_id=1, source_target_pairs={{0,1},{1,0},{2,3},{3,2},{4,5},{5,4},{6,7},{7,6},{8,9},{9,8},{10,11... | collective-permute-start | bytes 73736 | tf_op jit(solution)/shard_map/ppermute | solution.py:55
  7.0 3.9 %collective-permute-start.1 = (bf16[16,8,96]{2,1,0:T(8,128)(2,1)S(1)}, bf16[16,8,96]{2,1,0:T(8,128)(2,1)S(1)}, u32[]{:S(2)}, u32[]{:S(2)}) collective-permute-start(bf16[16,8,96]{2,1,0:T(8,128)(2,1)S(1)} %get-tuple-element.73), channel_id=1, source_target_pairs={{0,16},{1,2},{2,1},{3,4},{4,3},{5,6},{6,5},{7,8},{8,7},{9,10},{10,... | collective-permute-start | bytes 73736 | tf_op jit(solution)/shard_map/ppermute | solution.py:55
  8.0 3.0 %copy-start.1 = (bf16[16,64,96]{2,1,0:T(8,128)(2,1)S(1)}, bf16[16,64,96]{2,1,0:T(8,128)(2,1)}, u32[]{:S(2)}) copy-start(bf16[16,64,96]{2,1,0:T(8,128)(2,1)} %refs_1_.3) | copy-start | bytes 589828
  21.7 8.1 %collective-permute-start.7 = (bf16[9,64,96]{2,1,0:T(8,128)(2,1)S(1)}, bf16[9,64,96]{2,1,0:T(8,128)(2,1)S(1)}, u32[]{:S(2)}, u32[]{:S(2)}) collective-permute-start(bf16[9,64,96]{2,1,0:T(8,128)(2,1)S(1)} %get-tuple-element.94.refs_0_), channel_id=1, source_target_pairs={{0,16},{1,17},{2,18},{3,19},{4,20},{5,21},{6,22},{7,23},{8,24},{9,... | collective-permute-start | bytes 331784 | tf_op jit(solution)/shard_map/ppermute | solution.py:55
  22.7 6.2 %collective-permute-start.8 = (bf16[9,8,96]{2,1,0:T(8,128)(2,1)S(1)}, bf16[9,8,96]{2,1,0:T(8,128)(2,1)S(1)}, u32[]{:S(2)}, u32[]{:S(2)}) collective-permute-start(bf16[9,8,96]{2,1,0:T(8,128)(2,1)S(1)} %get-tuple-element.97), channel_id=1, source_target_pairs={{0,17},{1,16},{2,19},{3,18},{4,21},{5,20},{6,23},{7,22},{8,25},{9,... | collective-permute-start | bytes 41480 | tf_op jit(solution)/shard_map/ppermute | solution.py:55
  22.8 6.1 %collective-permute-start.9 = (bf16[9,8,96]{2,1,0:T(8,128)(2,1)S(1)}, bf16[9,8,96]{2,1,0:T(8,128)(2,1)S(1)}, u32[]{:S(2)}, u32[]{:S(2)}) collective-permute-start(bf16[9,8,96]{2,1,0:T(8,128)(2,1)S(1)} %get-tuple-element.98), channel_id=1, source_target_pairs={{0,16},{1,18},{2,17},{3,20},{4,19},{5,22},{6,21},{7,24},{8,23},{9,... | collective-permute-start | bytes 41480 | tf_op jit(solution)/shard_map/ppermute | solution.py:55
  24.0 5.0 %collective-permute-start.5 = (bf16[32,8,96]{2,1,0:T(8,128)(2,1)S(1)}, bf16[32,8,96]{2,1,0:T(8,128)(2,1)S(1)}, u32[]{:S(2)}, u32[]{:S(2)}) collective-permute-start(bf16[32,8,96]{2,1,0:T(8,128)(2,1)S(1)} %get-tuple-element.95), channel_id=1, source_target_pairs={{0,1},{1,0},{2,3},{3,2},{4,5},{5,4},{6,7},{7,6},{8,9},{9,8},{10,11... | collective-permute-start | bytes 147464 | tf_op jit(solution)/shard_map/ppermute | solution.py:55
  25.5 4.3 %collective-permute-start.6 = (bf16[32,8,96]{2,1,0:T(8,128)(2,1)S(1)}, bf16[32,8,96]{2,1,0:T(8,128)(2,1)S(1)}, u32[]{:S(2)}, u32[]{:S(2)}) collective-permute-start(bf16[32,8,96]{2,1,0:T(8,128)(2,1)S(1)} %get-tuple-element.96), channel_id=1, source_target_pairs={{0,16},{1,2},{2,1},{3,4},{4,3},{5,6},{6,5},{7,8},{8,7},{9,10},{10,... | collective-permute-start | bytes 147464 | tf_op jit(solution)/shard_map/ppermute | solution.py:55
  36.4 1.5 %collective-permute-start.10 = (bf16[848,128]{1,0:T(8,128)(2,1)S(1)}, bf16[848,128]{1,0:T(8,128)(2,1)S(1)}, u32[]{:S(2)}, u32[]{:S(2)}) collective-permute-start(bf16[848,128]{1,0:T(8,128)(2,1)S(1)} %get-tuple-element.103), channel_id=1, source_target_pairs={{0,1},{1,0},{2,3},{3,2},{4,5},{5,4},{6,7},{7,6},{8,9},{9,8},{10,11... | collective-permute-start | bytes 651272 | tf_op jit(solution)/shard_map/ppermute | solution.py:896
  38.0 5.7 %collective-permute-start.11 = (bf16[272,128]{1,0:T(8,128)(2,1)S(1)}, bf16[272,128]{1,0:T(8,128)(2,1)S(1)}, u32[]{:S(2)}, u32[]{:S(2)}) collective-permute-start(bf16[272,128]{1,0:T(8,128)(2,1)S(1)} %get-tuple-element.107), channel_id=1, source_target_pairs={{0,2},{1,3},{2,0},{3,1},{4,6},{5,7},{6,4},{7,5},{8,10},{9,11},{10,... | collective-permute-start | bytes 208904 | tf_op jit(solution)/shard_map/ppermute | solution.py:896
  39.9 4.9 %collective-permute-start.12 = (bf16[272,128]{1,0:T(8,128)(2,1)S(1)}, bf16[272,128]{1,0:T(8,128)(2,1)S(1)}, u32[]{:S(2)}, u32[]{:S(2)}) collective-permute-start(bf16[272,128]{1,0:T(8,128)(2,1)S(1)} %get-tuple-element.108), channel_id=1, source_target_pairs={{0,16},{1,17},{2,18},{3,19},{4,20},{5,21},{6,22},{7,23},{8,24},{9,... | collective-permute-start | bytes 208904 | tf_op jit(solution)/shard_map/ppermute | solution.py:896
  41.1 5.2 %collective-permute-start.13 = (bf16[272,128]{1,0:T(8,128)(2,1)S(1)}, bf16[272,128]{1,0:T(8,128)(2,1)S(1)}, u32[]{:S(2)}, u32[]{:S(2)}) collective-permute-start(bf16[272,128]{1,0:T(8,128)(2,1)S(1)} %get-tuple-element.109), channel_id=1, source_target_pairs={{0,18},{1,19},{2,16},{3,17},{4,22},{5,23},{6,20},{7,21},{8,26},{9,... | collective-permute-start | bytes 208904 | tf_op jit(solution)/shard_map/ppermute | solution.py:896
  46.4 5.0 %collective-permute-start.14 = (bf16[128,128]{1,0:T(8,128)(2,1)S(1)}, bf16[128,128]{1,0:T(8,128)(2,1)S(1)}, u32[]{:S(2)}, u32[]{:S(2)}) collective-permute-start(bf16[128,128]{1,0:T(8,128)(2,1)S(1)} %get-tuple-element.113), channel_id=1, source_target_pairs={{0,8},{1,9},{2,10},{3,11},{4,12},{5,13},{6,14},{7,15},{8,0},{9,1},... | collective-permute-start | bytes 98312 | tf_op jit(solution)/shard_map/ppermute | solution.py:896
  49.0 4.0 %collective-permute-start.15 = (bf16[128,128]{1,0:T(8,128)(2,1)S(1)}, bf16[128,128]{1,0:T(8,128)(2,1)S(1)}, u32[]{:S(2)}, u32[]{:S(2)}) collective-permute-start(bf16[128,128]{1,0:T(8,128)(2,1)S(1)} %get-tuple-element.114), channel_id=1, source_target_pairs={{0,4},{1,5},{2,6},{3,7},{4,0},{5,1},{6,2},{7,3},{8,12},{9,13},{10,... | collective-permute-start | bytes 98312 | tf_op jit(solution)/shard_map/ppermute | solution.py:896
  49.4 5.7 %collective-permute-start.16 = (bf16[128,128]{1,0:T(8,128)(2,1)S(1)}, bf16[128,128]{1,0:T(8,128)(2,1)S(1)}, u32[]{:S(2)}, u32[]{:S(2)}) collective-permute-start(bf16[128,128]{1,0:T(8,128)(2,1)S(1)} %get-tuple-element.115), channel_id=1, source_target_pairs={{0,12},{1,13},{2,14},{3,15},{4,8},{5,9},{6,10},{7,11},{8,4},{9,5},... | collective-permute-start | bytes 98312 | tf_op jit(solution)/shard_map/ppermute | solution.py:896

commit v9 on v8

--- a/solution.py
+++ b/solution.py
@@ -490,7 +490,7 @@
     (taps_sum1, up_sum1, down_sum1) = refs[11:14]
     strips = refs[14 : 14 + count]
     (grad0, middle, keep, small_keep, send) = refs[14 + count : 19 + count]
-    (wide_grad, cot_frame, upstream, own, sums, up_acc, down_acc, gain_sum, small, tall, slabs) = refs[19 + count :]
+    (wide_grad, cot_frame, upstream, own, sums, normed0, flow0, pre_grad0, gain_sum, small, tall, slabs) = refs[19 + count :]
     place = Place(dims.row_count, dims.col_count)
     rows, cols, channels, h, size = (dims.rows, dims.cols, dims.channels, dims.h, dims.size)
     ext_rows, ext_cols, wide = (dims.ext_rows, dims.ext_cols, dims.wide)
@@ -536,8 +536,6 @@
 
     gain = pad_lanes(gains[0:1, :])
     gain_sum[...] = jnp.zeros(gain_sum.shape, f32)
-    up_acc[...] = jnp.zeros(up_acc.shape, f32)
-    down_acc[...] = jnp.zeros(down_acc.shape, f32)
     ones = diagonal(jnp.ones((LANES, LANES), bf16), jnp.ones((LANES, LANES), bf16))
     half_px = dims.ext_pad // 2
     for start, n in pieces(half_px, dims.piece):
@@ -551,9 +549,9 @@
         for (at, n), flow, pre_grad, normed_grad in zip(spans, flows, pre_grads, normed_grads):
             mine = own[at : at + n, :]
             unit = unit0[at : at + n, :].astype(f32)
-            normed = (unit * gain * mine).astype(bf16)
-            up_acc[...] += dot_leading(normed, pre_grad)
-            down_acc[...] += dot_leading(flow * mine.astype(bf16), hidden0[at : at + n, :])
+            normed0[at : at + n, :] = (unit * gain * mine).astype(bf16)
+            flow0[at : at + n, :] = flow * mine.astype(bf16)
+            pre_grad0[at : at + n, :] = pre_grad
             product = normed_grad * unit * mine
             gain_sum[...] += jnp.sum(product.reshape(n // 8, 8, LANES), axis=0)
             grad = norm_backward(normed_grad, unit, inv0[at : at + n, :], gain, channels, ones)
@@ -570,9 +568,9 @@
     small_keep[...] = merged.astype(f32)
 
     layer_rows, part, half = (dims.layer_rows, dims.part, dims.half)
-    units = up_acc.shape[1]
-    up0 = up_acc[...].T * dims.factor
-    down0 = down_acc[...].T * dims.factor
+    units = hidden0.shape[1]
+    up0 = dot_leading(normed0[...], pre_grad0[...]).T * dims.factor
+    down0 = dot_leading(flow0[...], hidden0[...]).T * dims.factor
     up1 = up_sum1[...] * dims.factor
     down1 = down_sum1[...] * dims.factor
     lane = lax.broadcasted_iota(jnp.int32, (units, LANES), 1)
@@ -585,17 +583,13 @@
             joined = jnp.where(lane < half, first, jnp.where(lane < 2 * half, second, 0.0))
             tall[layer * (units + 8) : layer * (units + 8) + units, :] = joined
 
-        def slab(c, carry, r=r):
+        for c in range(dims.col_count):
             index = 0
-            for j, (axis, bit) in enumerate(dims.stages):
-                value = (r >> bit) & 1 if axis == "row" else lax.rem(lax.div(c, 1 << bit), 2)
-                index = index + value * (1 << (len(dims.stages) - 1 - j))
+            for axis, bit in dims.stages:
+                index = 2 * index + ((r if axis == "row" else c) >> bit & 1)
             for layer in range(2):
-                to = pl.multiple_of(index * slab_rows + layer * layer_rows, 8)
-                slabs[pl.ds(to, layer_rows), :] = tall[pl.ds(layer * (units + 8) + c * part, layer_rows), :]
-            return carry
-
-        lax.fori_loop(0, dims.col_count, slab, 0)
+                to, at = (index * slab_rows + layer * layer_rows, layer * (units + 8) + c * part)
+                slabs[to : to + layer_rows, :] = tall[at : at + layer_rows, :]
 
     split(dims, 0, slabs, merged, keep, (send,))
 
@@ -866,8 +860,9 @@
             ((ext, LANES), f32),
             ((ext, LANES), f32),
             tap_sums,
-            ((LANES, units), f32),
-            ((LANES, units), f32),
+            ((ext, LANES), bf16),
+            ((ext, LANES), bf16),
+            ((ext, units), bf16),
             ((8, LANES), f32),
             ((sums_rows, LANES), f32),
             ((2 * (units + 8), LANES), f32),

time: 56 us -> 55.9 us (level)
  no operation moved by 1% of the time
where the time goes in v9:
time: 55.9 us; the launch traced here: 55.7 us
  Pallas kernels  23.4 us (42%)
  starting transfers between devices  19.3 us (35%)
  waiting for transfers between devices  11.4 us (20%)
  local copies, waits for them, and re-layouts  0.96 us (2%)
  between operations  0.76 us (1%)
    pallas_call x11, Pallas kernels, run(): pl.pallas_call(kernel, out_shape=shapes, in_specs=[far] * in_hbm + [space...  23.4 us
    ppermute x10, starting transfers between devices, exchange(): lax.ppermute(strip, ('row', 'col'), swap_pairs(row_count, col_count, rs,...  11.1 us
    ppermute x7, waiting for transfers between devices, per_device(): lax.ppermute(x, axes, swap_by(d, group, mask))  8.32 us
    ppermute x7, starting transfers between devices, per_device(): lax.ppermute(x, axes, swap_by(d, group, mask))  8.15 us
    ppermute x10, waiting for transfers between devices, exchange(): lax.ppermute(strip, ('row', 'col'), swap_pairs(row_count, col_count, rs,...  3.04 us
  transfers between devices with their start and end apart: 17, of which 8 were waited for; matrix products, arithmetic and copies ran while one was open for 0% of the time, Pallas kernels for 9%

profile of v9, /device:TPU:0, one launch (start us, length us, event | category | flops | bytes accessed | tf_op | source)
XLA Modules:
  0.0 55.7 jit_solution(2974818933527954965)
XLA Ops:
  0.6 0.9 %copy-done = bf16[16,64,96]{2,1,0:T(8,128)(2,1)S(1)} copy-done((bf16[16,64,96]{2,1,0:T(8,128)(2,1)S(1)}, bf16[16,64,96]{2,1,0:T(8,128)(2,1)}, u32[]{:S(2)}) %copy-start) | copy-done | bytes 196632
  1.6 3.0 %collective-permute-start.2 = (bf16[6,64,96]{2,1,0:T(8,128)(2,1)S(1)}, bf16[6,64,96]{2,1,0:T(8,128)(2,1)S(1)}, u32[]{:S(2)}, u32[]{:S(2)}) collective-permute-start(bf16[6,64,96]{2,1,0:T(8,128)(2,1)S(1)} %get-tuple-element.71.refs_0_), channel_id=1, source_target_pairs={{0,16},{1,17},{2,18},{3,19},{4,20},{5,21},{6,22},{7,23},{8,24},{9,... | collective-permute-start | bytes 221192 | tf_op jit(solution)/shard_map/ppermute | solution.py:55
  4.8 1.2 %collective-permute-start.4 = (bf16[6,8,96]{2,1,0:T(8,128)(2,1)S(1)}, bf16[6,8,96]{2,1,0:T(8,128)(2,1)S(1)}, u32[]{:S(2)}, u32[]{:S(2)}) collective-permute-start(bf16[6,8,96]{2,1,0:T(8,128)(2,1)S(1)} %get-tuple-element.75), channel_id=1, source_target_pairs={{0,16},{1,18},{2,17},{3,20},{4,19},{5,22},{6,21},{7,24},{8,23},{9,... | collective-permute-start | bytes 27656 | tf_op jit(solution)/shard_map/ppermute | solution.py:55
  6.0 1.1 %collective-permute-start = (bf16[16,8,96]{2,1,0:T(8,128)(2,1)S(1)}, bf16[16,8,96]{2,1,0:T(8,128)(2,1)S(1)}, u32[]{:S(2)}, u32[]{:S(2)}) collective-permute-start(bf16[16,8,96]{2,1,0:T(8,128)(2,1)S(1)} %get-tuple-element.72), channel_id=1, source_target_pairs={{0,1},{1,0},{2,3},{3,2},{4,5},{5,4},{6,7},{7,6},{8,9},{9,8},{10,11... | collective-permute-start | bytes 73736 | tf_op jit(solution)/shard_map/ppermute | solution.py:55
  7.0 0.9 %collective-permute-start.1 = (bf16[16,8,96]{2,1,0:T(8,128)(2,1)S(1)}, bf16[16,8,96]{2,1,0:T(8,128)(2,1)S(1)}, u32[]{:S(2)}, u32[]{:S(2)}) collective-permute-start(bf16[16,8,96]{2,1,0:T(8,128)(2,1)S(1)} %get-tuple-element.73), channel_id=1, source_target_pairs={{0,16},{1,2},{2,1},{3,4},{4,3},{5,6},{6,5},{7,8},{8,7},{9,10},{10,... | collective-permute-start | bytes 73736 | tf_op jit(solution)/shard_map/ppermute | solution.py:55
  8.8 2.2 %collective-permute-done.1.refs_10_ = bf16[16,8,96]{2,1,0:T(8,128)(2,1)S(1)} collective-permute-done((bf16[16,8,96]{2,1,0:T(8,128)(2,1)S(1)}, bf16[16,8,96]{2,1,0:T(8,128)(2,1)S(1)}, u32[]{:S(2)}, u32[]{:S(2)}) %collective-permute-start.1) | collective-permute-done | bytes 24608 | tf_op jit(solution)/shard_map/ppermute | solution.py:55
  10.9 10.7 %shard_map.112 = (bf16[16,64,96]{2,1,0:T(8,128)(2,1)S(1)}, f32[2240,128]{1,0:T(8,128)S(1)}, f32[1600,128]{1,0:T(8,128)S(1)}, bf16[1376,128]{1,0:T(8,128)(2,1)S(1...) custom-call(bf16[16,64,96]{2,1,0:T(8,128)(2,1)S(1)} %get-tuple-eleme, ...), custom_call_target="tpu_custom_call" | custom-call | flops 15000000512 | bytes 262144 | tf_op jit(solution)/shard_map/pallas_call | solution.py:754
  21.7 1.0 %collective-permute-start.7 = (bf16[9,64,96]{2,1,0:T(8,128)(2,1)S(1)}, bf16[9,64,96]{2,1,0:T(8,128)(2,1)S(1)}, u32[]{:S(2)}, u32[]{:S(2)}) collective-permute-start(bf16[9,64,96]{2,1,0:T(8,128)(2,1)S(1)} %get-tuple-element.94.refs_0_), channel_id=1, source_target_pairs={{0,16},{1,17},{2,18},{3,19},{4,20},{5,21},{6,22},{7,23},{8,24},{9,... | collective-permute-start | bytes 331784 | tf_op jit(solution)/shard_map/ppermute | solution.py:55
  22.8 1.2 %collective-permute-start.9 = (bf16[9,8,96]{2,1,0:T(8,128)(2,1)S(1)}, bf16[9,8,96]{2,1,0:T(8,128)(2,1)S(1)}, u32[]{:S(2)}, u32[]{:S(2)}) collective-permute-start(bf16[9,8,96]{2,1,0:T(8,128)(2,1)S(1)} %get-tuple-element.98), channel_id=1, source_target_pairs={{0,16},{1,18},{2,17},{3,20},{4,19},{5,22},{6,21},{7,24},{8,23},{9,... | collective-permute-start | bytes 41480 | tf_op jit(solution)/shard_map/ppermute | solution.py:55
  24.0 1.6 %collective-permute-start.5 = (bf16[32,8,96]{2,1,0:T(8,128)(2,1)S(1)}, bf16[32,8,96]{2,1,0:T(8,128)(2,1)S(1)}, u32[]{:S(2)}, u32[]{:S(2)}) collective-permute-start(bf16[32,8,96]{2,1,0:T(8,128)(2,1)S(1)} %get-tuple-element.95), channel_id=1, source_target_pairs={{0,1},{1,0},{2,3},{3,2},{4,5},{5,4},{6,7},{7,6},{8,9},{9,8},{10,11... | collective-permute-start | bytes 147464 | tf_op jit(solution)/shard_map/ppermute | solution.py:55
  25.5 1.1 %collective-permute-start.6 = (bf16[32,8,96]{2,1,0:T(8,128)(2,1)S(1)}, bf16[32,8,96]{2,1,0:T(8,128)(2,1)S(1)}, u32[]{:S(2)}, u32[]{:S(2)}) collective-permute-start(bf16[32,8,96]{2,1,0:T(8,128)(2,1)S(1)} %get-tuple-element.96), channel_id=1, source_target_pairs={{0,16},{1,2},{2,1},{3,4},{4,3},{5,6},{6,5},{7,8},{8,7},{9,10},{10,... | collective-permute-start | bytes 147464 | tf_op jit(solution)/shard_map/ppermute | solution.py:55
  26.6 2.3 %shard_map.113 = (f32[56,128]{1,0:T(8,128)S(1)}, f32[384,128]{1,0:T(8,128)S(1)}, f32[384,128]{1,0:T(8,128)S(1)}, bf16[16,64,96]{2,1,0:T(8,128)(2,1)}) custom-call(f32[1600,128]{1,0:T(8,128)S(1)} %get-tuple-element.76.x1, f32[1024,128]{1,0:T(8,128)S(1)} %get-tuple-element.77.grad1.refs_0_, bf16[1024,128]{1,0:T(8,128)(2,1)S(1)} %get-tuple-element.78.normed1, ...), custom_call_target="tpu_custom_call" | custom-call | flops 3000000000 | bytes 262144 | tf_op jit(solution)/shard_map/pallas_call | solution.py:754
  28.9 0.8 %collective-permute-done.6.refs_15_ = bf16[32,8,96]{2,1,0:T(8,128)(2,1)S(1)} collective-permute-done((bf16[32,8,96]{2,1,0:T(8,128)(2,1)S(1)}, bf16[32,8,96]{2,1,0:T(8,128)(2,1)S(1)}, u32[]{:S(2)}, u32[]{:S(2)}) %collective-permute-start.6) | collective-permute-done | bytes 49184 | tf_op jit(solution)/shard_map/ppermute | solution.py:55
  29.8 6.5 %shard_map.115 = (f32[1600,128]{1,0:T(8,128)S(1)}, f32[1024,128]{1,0:T(8,128)S(1)}, f32[768,128]{1,0:T(8,128)S(1)}, f32[80,128]{1,0:T(8,128)S(1)}, bf16[848,128]{1,0:T(8,128)(2,1)S(1)}) custom-call(f32[1024,128]{1,0:T(8,128)S(1)} %get-tuple-element.77.grad1.refs_0_, bf16[16,64,96]{2,1,0:T(8,128)(2,1)S(1)} %copy-done.1, ...), custom_call_target="tpu_custom_call" | custom-call | flops 12000000000 | bytes 262144 | tf_op jit(solution)/shard_map/pallas_call | solution.py:754
  36.4 1.4 %collective-permute-done.10.refs_0_ = bf16[848,128]{1,0:T(8,128)(2,1)S(1)} collective-permute-done((bf16[848,128]{1,0:T(8,128)(2,1)S(1)}, bf16[848,128]{1,0:T(8,128)(2,1)S(1)}, u32[]{:S(2)}, u32[]{:S(2)}) %collective-permute-start.10) | collective-permute-done | bytes 217120 | tf_op jit(solution)/shard_map/ppermute | solution.py:891
  37.9 1.8 %collective-permute-start.11 = (bf16[272,128]{1,0:T(8,128)(2,1)S(1)}, bf16[272,128]{1,0:T(8,128)(2,1)S(1)}, u32[]{:S(2)}, u32[]{:S(2)}) collective-permute-start(bf16[272,128]{1,0:T(8,128)(2,1)S(1)} %get-tuple-element.107), channel_id=1, source_target_pairs={{0,2},{1,3},{2,0},{3,1},{4,6},{5,7},{6,4},{7,5},{8,10},{9,11},{10,... | collective-permute-start | bytes 208904 | tf_op jit(solution)/shard_map/ppermute | solution.py:891
  39.7 1.3 %collective-permute-start.12 = (bf16[272,128]{1,0:T(8,128)(2,1)S(1)}, bf16[272,128]{1,0:T(8,128)(2,1)S(1)}, u32[]{:S(2)}, u32[]{:S(2)}) collective-permute-start(bf16[272,128]{1,0:T(8,128)(2,1)S(1)} %get-tuple-element.108), channel_id=1, source_target_pairs={{0,16},{1,17},{2,18},{3,19},{4,20},{5,21},{6,22},{7,23},{8,24},{9,... | collective-permute-start | bytes 208904 | tf_op jit(solution)/shard_map/ppermute | solution.py:891
  41.4 2.1 %shard_map.117 = (bf16[16,64,96]{2,1,0:T(8,128)(2,1)}, f32[8,128]{1,0:T(8,128)S(1)}) custom-call(f32[1600,128]{1,0:T(8,128)S(1)} %get-tuple-element.99.grad0, f32[1024,128]{1,0:T(8,128)S(1)} %get-tuple-element.100.middle, bf16[784,128]{1,0:T(8,128)(2,1)S(1)} %get-tuple-element.64.refs_2_.taps0, f32[80,128]{1,0:T(8,128)S(1)} %get-tuple-element.104.after.small), custom_call_target="tpu_custom_call" | custom-call | flops 3000000000 | bytes 262144 | tf_op jit(solution)/shard_map/pallas_call | solution.py:754
  43.6 1.1 %collective-permute-done.12.refs_1_ = bf16[272,128]{1,0:T(8,128)(2,1)S(1)} collective-permute-done((bf16[272,128]{1,0:T(8,128)(2,1)S(1)}, bf16[272,128]{1,0:T(8,128)(2,1)S(1)}, u32[]{:S(2)}, u32[]{:S(2)}) %collective-permute-start.12) | collective-permute-done | bytes 69664 | tf_op jit(solution)/shard_map/ppermute | solution.py:891
  44.6 1.5 %collective-permute-done.13.refs_2_ = bf16[272,128]{1,0:T(8,128)(2,1)S(1)} collective-permute-done((bf16[272,128]{1,0:T(8,128)(2,1)S(1)}, bf16[272,128]{1,0:T(8,128)(2,1)S(1)}, u32[]{:S(2)}, u32[]{:S(2)}) %collective-permute-start.13) | collective-permute-done | bytes 69664 | tf_op jit(solution)/shard_map/ppermute | solution.py:891
  46.2 2.7 %collective-permute-start.14 = (bf16[128,128]{1,0:T(8,128)(2,1)S(1)}, bf16[128,128]{1,0:T(8,128)(2,1)S(1)}, u32[]{:S(2)}, u32[]{:S(2)}) collective-permute-start(bf16[128,128]{1,0:T(8,128)(2,1)S(1)} %get-tuple-element.113), channel_id=1, source_target_pairs={{0,8},{1,9},{2,10},{3,11},{4,12},{5,13},{6,14},{7,15},{8,0},{9,1},... | collective-permute-start | bytes 98312 | tf_op jit(solution)/shard_map/ppermute | solution.py:891
  49.3 1.4 %collective-permute-start.16 = (bf16[128,128]{1,0:T(8,128)(2,1)S(1)}, bf16[128,128]{1,0:T(8,128)(2,1)S(1)}, u32[]{:S(2)}, u32[]{:S(2)}) collective-permute-start(bf16[128,128]{1,0:T(8,128)(2,1)S(1)} %get-tuple-element.115), channel_id=1, source_target_pairs={{0,12},{1,13},{2,14},{3,15},{4,8},{5,9},{6,10},{7,11},{8,4},{9,5},... | collective-permute-start | bytes 98312 | tf_op jit(solution)/shard_map/ppermute | solution.py:891
  51.2 1.7 %collective-permute-done.15.refs_1_ = bf16[128,128]{1,0:T(8,128)(2,1)S(1)} collective-permute-done((bf16[128,128]{1,0:T(8,128)(2,1)S(1)}, bf16[128,128]{1,0:T(8,128)(2,1)S(1)}, u32[]{:S(2)}, u32[]{:S(2)}) %collective-permute-start.15) | collective-permute-done | bytes 32800 | tf_op jit(solution)/shard_map/ppermute | solution.py:891
  52.9 2.1 %collective-permute-done.16.refs_2_ = bf16[128,128]{1,0:T(8,128)(2,1)S(1)} collective-permute-done((bf16[128,128]{1,0:T(8,128)(2,1)S(1)}, bf16[128,128]{1,0:T(8,128)(2,1)S(1)}, u32[]{:S(2)}, u32[]{:S(2)}) %collective-permute-start.16) | collective-permute-done | bytes 32800 | tf_op jit(solution)/shard_map/ppermute | solution.py:891
  (33 shorter events, 3.4 us)
Async XLA Ops:
  0.6 1.0 %copy-start = (bf16[16,64,96]{2,1,0:T(8,128)(2,1)S(1)}, bf16[16,64,96]{2,1,0:T(8,128)(2,1)}, u32[]{:S(2)}) copy-start(bf16[16,64,96]{2,1,0:T(8,128)(2,1)} %image_in.1) | copy-start | bytes 589828
  1.6 9.3 %collective-permute-start.2 = (bf16[6,64,96]{2,1,0:T(8,128)(2,1)S(1)}, bf16[6,64,96]{2,1,0:T(8,128)(2,1)S(1)}, u32[]{:S(2)}, u32[]{:S(2)}) collective-permute-start(bf16[6,64,96]{2,1,0:T(8,128)(2,1)S(1)} %get-tuple-element.71.refs_0_), channel_id=1, source_target_pairs={{0,16},{1,17},{2,18},{3,19},{4,20},{5,21},{6,22},{7,23},{8,24},{9,... | collective-permute-start | bytes 221192 | tf_op jit(solution)/shard_map/ppermute | solution.py:55
  4.7 3.3 %copy-start.2 = (bf16[2,96,384]{2,1,0:T(8,128)(2,1)S(1)}, bf16[2,96,384]{2,1,0:T(8,128)(2,1)}, u32[]{:S(2)}) copy-start(bf16[2,96,384]{2,1,0:T(8,128)(2,1)} %up_in.1) | copy-start | bytes 442372
  4.7 3.3 %copy-start.3 = (bf16[2,384,96]{1,2,0:T(8,128)(2,1)S(1)}, bf16[2,384,96]{1,2,0:T(8,128)(2,1)}, u32[]{:S(2)}) copy-start(bf16[2,384,96]{1,2,0:T(8,128)(2,1)} %param.10) | copy-start | bytes 442372
  4.7 3.3 %copy-start.4 = (f32[2,7,7,96]{3,0,2,1:T(2,128)S(1)}, f32[2,7,7,96]{3,0,2,1:T(2,128)}, u32[]{:S(2)}) copy-start(f32[2,7,7,96]{3,0,2,1:T(2,128)} %param.7) | copy-start | bytes 112900
  4.7 3.3 %copy-start.5 = (f32[2,96]{1,0:T(2,128)S(1)}, f32[2,96]{1,0:T(2,128)}, u32[]{:S(2)}) copy-start(f32[2,96]{1,0:T(2,128)} %gains_in.1) | copy-start | bytes 2308
  4.7 4.0 %collective-permute-start.3 = (bf16[6,8,96]{2,1,0:T(8,128)(2,1)S(1)}, bf16[6,8,96]{2,1,0:T(8,128)(2,1)S(1)}, u32[]{:S(2)}, u32[]{:S(2)}) collective-permute-start(bf16[6,8,96]{2,1,0:T(8,128)(2,1)S(1)} %get-tuple-element.74), channel_id=1, source_target_pairs={{0,17},{1,16},{2,19},{3,18},{4,21},{5,20},{6,23},{7,22},{8,25},{9,... | collective-permute-start | bytes 27656 | tf_op jit(solution)/shard_map/ppermute | solution.py:55
  4.8 4.0 %collective-permute-start.4 = (bf16[6,8,96]{2,1,0:T(8,128)(2,1)S(1)}, bf16[6,8,96]{2,1,0:T(8,128)(2,1)S(1)}, u32[]{:S(2)}, u32[]{:S(2)}) collective-permute-start(bf16[6,8,96]{2,1,0:T(8,128)(2,1)S(1)} %get-tuple-element.75), channel_id=1, source_target_pairs={{0,16},{1,18},{2,17},{3,20},{4,19},{5,22},{6,21},{7,24},{8,23},{9,... | collective-permute-start | bytes 27656 | tf_op jit(solution)/shard_map/ppermute | solution.py:55
  6.0 2.8 %collective-permute-start = (bf16[16,8,96]{2,1,0:T(8,128)(2,1)S(1)}, bf16[16,8,96]{2,1,0:T(8,128)(2,1)S(1)}, u32[]{:S(2)}, u32[]{:S(2)}) collective-permute-start(bf16[16,8,96]{2,1,0:T(8,128)(2,1)S(1)} %get-tuple-element.72), channel_id=1, source_target_pairs={{0,1},{1,0},{2,3},{3,2},{4,5},{5,4},{6,7},{7,6},{8,9},{9,8},{10,11... | collective-permute-start | bytes 73736 | tf_op jit(solution)/shard_map/ppermute | solution.py:55
  7.0 3.9 %collective-permute-start.1 = (bf16[16,8,96]{2,1,0:T(8,128)(2,1)S(1)}, bf16[16,8,96]{2,1,0:T(8,128)(2,1)S(1)}, u32[]{:S(2)}, u32[]{:S(2)}) collective-permute-start(bf16[16,8,96]{2,1,0:T(8,128)(2,1)S(1)} %get-tuple-element.73), channel_id=1, source_target_pairs={{0,16},{1,2},{2,1},{3,4},{4,3},{5,6},{6,5},{7,8},{8,7},{9,10},{10,... | collective-permute-start | bytes 73736 | tf_op jit(solution)/shard_map/ppermute | solution.py:55
  8.0 3.0 %copy-start.1 = (bf16[16,64,96]{2,1,0:T(8,128)(2,1)S(1)}, bf16[16,64,96]{2,1,0:T(8,128)(2,1)}, u32[]{:S(2)}) copy-start(bf16[16,64,96]{2,1,0:T(8,128)(2,1)} %refs_1_.3) | copy-start | bytes 589828
  21.7 8.1 %collective-permute-start.7 = (bf16[9,64,96]{2,1,0:T(8,128)(2,1)S(1)}, bf16[9,64,96]{2,1,0:T(8,128)(2,1)S(1)}, u32[]{:S(2)}, u32[]{:S(2)}) collective-permute-start(bf16[9,64,96]{2,1,0:T(8,128)(2,1)S(1)} %get-tuple-element.94.refs_0_), channel_id=1, source_target_pairs={{0,16},{1,17},{2,18},{3,19},{4,20},{5,21},{6,22},{7,23},{8,24},{9,... | collective-permute-start | bytes 331784 | tf_op jit(solution)/shard_map/ppermute | solution.py:55
  22.7 6.2 %collective-permute-start.8 = (bf16[9,8,96]{2,1,0:T(8,128)(2,1)S(1)}, bf16[9,8,96]{2,1,0:T(8,128)(2,1)S(1)}, u32[]{:S(2)}, u32[]{:S(2)}) collective-permute-start(bf16[9,8,96]{2,1,0:T(8,128)(2,1)S(1)} %get-tuple-element.97), channel_id=1, source_target_pairs={{0,17},{1,16},{2,19},{3,18},{4,21},{5,20},{6,23},{7,22},{8,25},{9,... | collective-permute-start | bytes 41480 | tf_op jit(solution)/shard_map/ppermute | solution.py:55
  22.8 6.1 %collective-permute-start.9 = (bf16[9,8,96]{2,1,0:T(8,128)(2,1)S(1)}, bf16[9,8,96]{2,1,0:T(8,128)(2,1)S(1)}, u32[]{:S(2)}, u32[]{:S(2)}) collective-permute-start(bf16[9,8,96]{2,1,0:T(8,128)(2,1)S(1)} %get-tuple-element.98), channel_id=1, source_target_pairs={{0,16},{1,18},{2,17},{3,20},{4,19},{5,22},{6,21},{7,24},{8,23},{9,... | collective-permute-start | bytes 41480 | tf_op jit(solution)/shard_map/ppermute | solution.py:55
  24.0 5.0 %collective-permute-start.5 = (bf16[32,8,96]{2,1,0:T(8,128)(2,1)S(1)}, bf16[32,8,96]{2,1,0:T(8,128)(2,1)S(1)}, u32[]{:S(2)}, u32[]{:S(2)}) collective-permute-start(bf16[32,8,96]{2,1,0:T(8,128)(2,1)S(1)} %get-tuple-element.95), channel_id=1, source_target_pairs={{0,1},{1,0},{2,3},{3,2},{4,5},{5,4},{6,7},{7,6},{8,9},{9,8},{10,11... | collective-permute-start | bytes 147464 | tf_op jit(solution)/shard_map/ppermute | solution.py:55
  25.5 4.3 %collective-permute-start.6 = (bf16[32,8,96]{2,1,0:T(8,128)(2,1)S(1)}, bf16[32,8,96]{2,1,0:T(8,128)(2,1)S(1)}, u32[]{:S(2)}, u32[]{:S(2)}) collective-permute-start(bf16[32,8,96]{2,1,0:T(8,128)(2,1)S(1)} %get-tuple-element.96), channel_id=1, source_target_pairs={{0,16},{1,2},{2,1},{3,4},{4,3},{5,6},{6,5},{7,8},{8,7},{9,10},{10,... | collective-permute-start | bytes 147464 | tf_op jit(solution)/shard_map/ppermute | solution.py:55
  36.3 1.5 %collective-permute-start.10 = (bf16[848,128]{1,0:T(8,128)(2,1)S(1)}, bf16[848,128]{1,0:T(8,128)(2,1)S(1)}, u32[]{:S(2)}, u32[]{:S(2)}) collective-permute-start(bf16[848,128]{1,0:T(8,128)(2,1)S(1)} %get-tuple-element.103), channel_id=1, source_target_pairs={{0,1},{1,0},{2,3},{3,2},{4,5},{5,4},{6,7},{7,6},{8,9},{9,8},{10,11... | collective-permute-start | bytes 651272 | tf_op jit(solution)/shard_map/ppermute | solution.py:891
  37.9 5.7 %collective-permute-start.11 = (bf16[272,128]{1,0:T(8,128)(2,1)S(1)}, bf16[272,128]{1,0:T(8,128)(2,1)S(1)}, u32[]{:S(2)}, u32[]{:S(2)}) collective-permute-start(bf16[272,128]{1,0:T(8,128)(2,1)S(1)} %get-tuple-element.107), channel_id=1, source_target_pairs={{0,2},{1,3},{2,0},{3,1},{4,6},{5,7},{6,4},{7,5},{8,10},{9,11},{10,... | collective-permute-start | bytes 208904 | tf_op jit(solution)/shard_map/ppermute | solution.py:891
  39.7 4.9 %collective-permute-start.12 = (bf16[272,128]{1,0:T(8,128)(2,1)S(1)}, bf16[272,128]{1,0:T(8,128)(2,1)S(1)}, u32[]{:S(2)}, u32[]{:S(2)}) collective-permute-start(bf16[272,128]{1,0:T(8,128)(2,1)S(1)} %get-tuple-element.108), channel_id=1, source_target_pairs={{0,16},{1,17},{2,18},{3,19},{4,20},{5,21},{6,22},{7,23},{8,24},{9,... | collective-permute-start | bytes 208904 | tf_op jit(solution)/shard_map/ppermute | solution.py:891
  41.0 5.2 %collective-permute-start.13 = (bf16[272,128]{1,0:T(8,128)(2,1)S(1)}, bf16[272,128]{1,0:T(8,128)(2,1)S(1)}, u32[]{:S(2)}, u32[]{:S(2)}) collective-permute-start(bf16[272,128]{1,0:T(8,128)(2,1)S(1)} %get-tuple-element.109), channel_id=1, source_target_pairs={{0,18},{1,19},{2,16},{3,17},{4,22},{5,23},{6,20},{7,21},{8,26},{9,... | collective-permute-start | bytes 208904 | tf_op jit(solution)/shard_map/ppermute | solution.py:891
  46.2 5.0 %collective-permute-start.14 = (bf16[128,128]{1,0:T(8,128)(2,1)S(1)}, bf16[128,128]{1,0:T(8,128)(2,1)S(1)}, u32[]{:S(2)}, u32[]{:S(2)}) collective-permute-start(bf16[128,128]{1,0:T(8,128)(2,1)S(1)} %get-tuple-element.113), channel_id=1, source_target_pairs={{0,8},{1,9},{2,10},{3,11},{4,12},{5,13},{6,14},{7,15},{8,0},{9,1},... | collective-permute-start | bytes 98312 | tf_op jit(solution)/shard_map/ppermute | solution.py:891
  48.9 4.0 %collective-permute-start.15 = (bf16[128,128]{1,0:T(8,128)(2,1)S(1)}, bf16[128,128]{1,0:T(8,128)(2,1)S(1)}, u32[]{:S(2)}, u32[]{:S(2)}) collective-permute-start(bf16[128,128]{1,0:T(8,128)(2,1)S(1)} %get-tuple-element.114), channel_id=1, source_target_pairs={{0,4},{1,5},{2,6},{3,7},{4,0},{5,1},{6,2},{7,3},{8,12},{9,13},{10,... | collective-permute-start | bytes 98312 | tf_op jit(solution)/shard_map/ppermute | solution.py:891
  49.3 5.7 %collective-permute-start.16 = (bf16[128,128]{1,0:T(8,128)(2,1)S(1)}, bf16[128,128]{1,0:T(8,128)(2,1)S(1)}, u32[]{:S(2)}, u32[]{:S(2)}) collective-permute-start(bf16[128,128]{1,0:T(8,128)(2,1)S(1)} %get-tuple-element.115), channel_id=1, source_target_pairs={{0,12},{1,13},{2,14},{3,15},{4,8},{5,9},{6,10},{7,11},{8,4},{9,5},... | collective-permute-start | bytes 98312 | tf_op jit(solution)/shard_map/ppermute | solution.py:891

commit v10 on v9

--- a/solution.py
+++ b/solution.py
@@ -226,33 +226,53 @@
     return jnp.concatenate([top, bottom], axis=0)
 
 
-def lane_total(x):
+def by_blocks(function, *arrays, size=16):
+    count = arrays[0].shape[0]
+    results = [function(*(x[i : i + size] for x in arrays)) for i in range(0, count, size)]
+    return tuple(jnp.concatenate(parts, axis=0) for parts in zip(*results))
+
+
+def in_channels(shape, channels):
+    return lax.broadcasted_iota(jnp.int32, shape, 1) < channels
+
+
+def high_low(x):
     high = x.astype(bf16)
-    low = (x - high.astype(f32)).astype(bf16)
-    both = jnp.concatenate([high, low], axis=1)
-    return dot(both, jnp.ones((2 * LANES, LANES), bf16))
-
-
-def paired_dot(x, y, weights):
-    total = dot(jnp.concatenate([x.astype(bf16), y.astype(bf16)], axis=1), weights)
-    half = weights.shape[1] // 2
-    return (total[:, :half], total[:, half:])
-
-
-def layer_norm(parts, channels, ones):
-    lane = lax.broadcasted_iota(jnp.int32, parts[0].shape, 1)
-    centred = [jnp.where(lane < channels, x - lane_total(x) * (1.0 / channels), 0.0) for x in parts]
-    variances = paired_dot(centred[0] * centred[0], centred[1] * centred[1], ones)
-    inverses = [lax.rsqrt(v * (1.0 / channels) + epsilon) for v in variances]
-    return ([c * i for c, i in zip(centred, inverses)], inverses)
+    return (jnp.concatenate([high, (x - high.astype(f32)).astype(bf16)], axis=1),)
+
+
+def side_by_side(x, y):
+    return jnp.concatenate([x, y], axis=1)
+
+
+def layer_norm(parts, gain, channels, ones):
+    def centre(x, total):
+        centred = jnp.where(in_channels(x.shape, channels), x - total * (1.0 / channels), 0.0)
+        return (centred, (centred * centred).astype(bf16))
+
+    def finish(centred, total):
+        inverse = lax.rsqrt(total * (1.0 / channels) + epsilon)
+        unit = centred * inverse
+        return (unit, inverse, (unit * gain).astype(bf16))
+
+    totals = [dot(by_blocks(high_low, x)[0], jnp.ones((2 * LANES, LANES), bf16)) for x in parts]
+    centred, squares = zip(*(by_blocks(centre, x, total) for x, total in zip(parts, totals)))
+    variances = dot(side_by_side(*squares), ones)
+    return [by_blocks(finish, c, variances[:, k * LANES : (k + 1) * LANES]) for k, c in enumerate(centred)]
 
 
 def norm_backward(normed_grad, unit, inverse, gain, channels, ones):
-    m = normed_grad * gain
-    mean, along = paired_dot(m, m * unit, ones)
-    lane = lax.broadcasted_iota(jnp.int32, m.shape, 1)
-    centred = m - (mean + unit * along) * (1.0 / channels)
-    return jnp.where(lane < channels, inverse * centred, 0.0)
+    def products(normed_grad, unit):
+        m = normed_grad * gain
+        return (side_by_side(m.astype(bf16), (m * unit).astype(bf16)),)
+
+    def finish(normed_grad, unit, inverse, sums):
+        along = sums[:, :LANES] + unit * sums[:, LANES:]
+        grad = inverse * (normed_grad * gain - along * (1.0 / channels))
+        return (round16(jnp.where(in_channels(grad.shape, channels), grad, 0.0)),)
+
+    sums = dot(by_blocks(products, normed_grad, unit)[0], ones)
+    return by_blocks(finish, normed_grad, unit, inverse, sums)[0]
 
 
 def gelu_parts(v):
@@ -386,20 +406,26 @@
     half = dims.ext_pad // 2
     for start, n in pieces(half, dims.piece):
         spans = [(start, n), (half + start, n)]
-        units, inverses = layer_norm([conv[at : at + n, :] for at, n in spans], channels, ones)
-        pres = paired_dot(units[0] * gain, units[1] * gain, forward0[...])
+        parts = layer_norm([conv[at : at + n, :] for at, n in spans], gain, channels, ones)
+        pres = dot(side_by_side(parts[0][2], parts[1][2]), forward0[...])
+        count = pres.shape[1] // 2
         hiddens = []
-        for (at, n), unit, inverse, pre in zip(spans, units, inverses, pres):
+        for k, ((at, n), (unit, inverse, _)) in enumerate(zip(spans, parts)):
             unit0[at : at + n, :] = unit.astype(bf16)
             inv0[at : at + n, :] = inverse
-            value, slope = gelu_parts(pre)
-            hiddens.append(value.astype(bf16))
-            hidden0[at : at + n, :] = hiddens[-1]
-            slope0[at : at + n, :] = slope.astype(bf16)
-        branches = paired_dot(hiddens[0], hiddens[1], back0[...])
-        for (at, n), branch in zip(spans, branches):
+
+            def activate(pre):
+                value, slope = gelu_parts(pre)
+                return (value.astype(bf16), slope.astype(bf16))
+
+            hidden, slope = by_blocks(activate, pres[:, k * count : (k + 1) * count])
+            hidden0[at : at + n, :] = hidden
+            slope0[at : at + n, :] = slope
+            hiddens.append(hidden)
+        branches = dot(side_by_side(*hiddens), back0[...])
+        for k, (at, n) in enumerate(spans):
             px = pl.ds(frame + at, n)
-            x1[px, :] = round16(x1[px, :] + branch)
+            x1[px, :] = round16(x1[px, :] + branches[:, k * LANES : (k + 1) * LANES])
     clear_outside(place, x1, dims)
 
     def conv1(g, carry):
@@ -417,25 +443,31 @@
     for k in range(rows // lines):
         px = slice(k * step, (k + 1) * step)
         middle = k * step + step // 2
-        units, inverses = layer_norm([conv[k * step : middle, :], conv[middle : (k + 1) * step, :]], channels, ones)
-        unit, inverse = (jnp.concatenate(units, axis=0), jnp.concatenate(inverses, axis=0))
-        normed = (unit * gain1).astype(bf16)
+        parts = layer_norm(
+            [conv[k * step : middle, :], conv[middle : (k + 1) * step, :]], gain1, channels, ones
+        )
+        unit, inverse, normed = (jnp.concatenate(pair, axis=0) for pair in zip(*parts))
         normed1[px, :] = normed
         upstream = pad_lanes(cot[k * lines : (k + 1) * lines].reshape(step, channels))
-        pre, hidden_grad = paired_dot(normed, upstream, forward1[...])
-        value, slope = gelu_parts(pre)
-        hidden = value.astype(bf16)
+        both = dot(side_by_side(normed, upstream), forward1[...])
+
+        def activate(pre, hidden_grad):
+            value, slope = gelu_parts(pre)
+            return (value.astype(bf16), (hidden_grad * slope).astype(bf16))
+
+        count = both.shape[1] // 2
+        hidden, pre_grad = by_blocks(activate, both[:, :count], both[:, count:])
         hidden1[px, :] = hidden
-        pre_grad = (hidden_grad * slope).astype(bf16)
         pre_grad1[px, :] = pre_grad
-        branch, normed_grad = paired_dot(hidden, pre_grad, back1[...])
+        both = dot(side_by_side(hidden, pre_grad), back1[...])
+        branch, normed_grad = (both[:, :LANES], both[:, LANES:])
         for i in range(lines):
             start = (k * lines + i + h) * ext_cols + 4
             line = x1[start : start + cols, :] + branch[i * cols : (i + 1) * cols]
             output[k * lines + i] = line[:, :channels].astype(bf16)
         product = normed_grad * unit
         gain_sum[...] += jnp.sum(product.reshape(step // 8, 8, LANES), axis=0)
-        grad1[px, :] = round16(norm_backward(normed_grad, unit, inverse, gain1, channels, ones))
+        grad1[px, :] = norm_backward(normed_grad, unit, inverse, gain1, channels, ones)
 
     takes = [(flat_take(grad1, cols, channels), 2 * h, rows, cols), (image_take(cot), h, rows, cols)]
     write_strips(place, outs, takes, band_combos(dims.row_count))
@@ -541,11 +573,18 @@
     for start, n in pieces(half_px, dims.piece):
         spans = [(start, n), (half_px + start, n)]
         flows = [upstream[at : at + n, :].astype(bf16) for at, n in spans]
-        hidden_grads = paired_dot(flows[0], flows[1], grad_in0[...])
+        hidden_grads = dot(side_by_side(*flows), grad_in0[...])
+        count = hidden_grads.shape[1] // 2
+
+        def slope_times(grad, slope):
+            return ((grad * slope.astype(f32)).astype(bf16),)
+
         pre_grads = [
-            (grad * slope0[at : at + n, :].astype(f32)).astype(bf16) for grad, (at, n) in zip(hidden_grads, spans)
+            by_blocks(slope_times, hidden_grads[:, k * count : (k + 1) * count], slope0[at : at + n, :])[0]
+            for k, (at, n) in enumerate(spans)
         ]
-        normed_grads = paired_dot(pre_grads[0], pre_grads[1], grad_out0[...])
+        both = dot(side_by_side(*pre_grads), grad_out0[...])
+        normed_grads = (both[:, :LANES], both[:, LANES:])
         for (at, n), flow, pre_grad, normed_grad in zip(spans, flows, pre_grads, normed_grads):
             mine = own[at : at + n, :]
             unit = unit0[at : at + n, :].astype(f32)
@@ -555,7 +594,7 @@
             product = normed_grad * unit * mine
             gain_sum[...] += jnp.sum(product.reshape(n // 8, 8, LANES), axis=0)
             grad = norm_backward(normed_grad, unit, inv0[at : at + n, :], gain, channels, ones)
-            grad0[pl.ds(frame + at, n), :] = round16(grad)
+            grad0[pl.ds(frame + at, n), :] = grad
     clear_outside(place, grad0, dims)
     kernel_sums(
         x0, h * wide + SIDE - h, wide, grad0, h * ext_cols + margin, ext_cols, rows, cols, size, sums

time: 55.9 us -> 55.9 us (level)
  no operation moved by 1% of the time
where the time goes in v10:
time: 55.9 us; the launch traced here: 55.7 us
  Pallas kernels  23.3 us (42%)
  starting transfers between devices  19.3 us (35%)
  waiting for transfers between devices  11.4 us (20%)
  local copies, waits for them, and re-layouts  0.96 us (2%)
  between operations  0.76 us (1%)
    pallas_call x11, Pallas kernels, run(): pl.pallas_call(kernel, out_shape=shapes, in_specs=[far] * in_hbm + [space...  23.3 us
    ppermute x10, starting transfers between devices, exchange(): lax.ppermute(strip, ('row', 'col'), swap_pairs(row_count, col_count, rs,...  11.1 us
    ppermute x7, waiting for transfers between devices, per_device(): lax.ppermute(x, axes, swap_by(d, group, mask))  8.33 us
    ppermute x7, starting transfers between devices, per_device(): lax.ppermute(x, axes, swap_by(d, group, mask))  8.14 us
    ppermute x10, waiting for transfers between devices, exchange(): lax.ppermute(strip, ('row', 'col'), swap_pairs(row_count, col_count, rs,...  3.05 us
  transfers between devices with their start and end apart: 17, of which 8 were waited for; matrix products, arithmetic and copies ran while one was open for 0% of the time, Pallas kernels for 9%

profile of v10, /device:TPU:0, one launch (start us, length us, event | category | flops | bytes accessed | tf_op | source)
XLA Modules:
  0.0 55.7 jit_solution(16709525093360466281)
XLA Ops:
  0.6 0.9 %copy-done = bf16[16,64,96]{2,1,0:T(8,128)(2,1)S(1)} copy-done((bf16[16,64,96]{2,1,0:T(8,128)(2,1)S(1)}, bf16[16,64,96]{2,1,0:T(8,128)(2,1)}, u32[]{:S(2)}) %copy-start) | copy-done | bytes 196632
  1.6 3.0 %collective-permute-start.2 = (bf16[6,64,96]{2,1,0:T(8,128)(2,1)S(1)}, bf16[6,64,96]{2,1,0:T(8,128)(2,1)S(1)}, u32[]{:S(2)}, u32[]{:S(2)}) collective-permute-start(bf16[6,64,96]{2,1,0:T(8,128)(2,1)S(1)} %get-tuple-element.71.refs_0_), channel_id=1, source_target_pairs={{0,16},{1,17},{2,18},{3,19},{4,20},{5,21},{6,22},{7,23},{8,24},{9,... | collective-permute-start | bytes 221192 | tf_op jit(solution)/shard_map/ppermute | solution.py:55
  4.8 1.2 %collective-permute-start.4 = (bf16[6,8,96]{2,1,0:T(8,128)(2,1)S(1)}, bf16[6,8,96]{2,1,0:T(8,128)(2,1)S(1)}, u32[]{:S(2)}, u32[]{:S(2)}) collective-permute-start(bf16[6,8,96]{2,1,0:T(8,128)(2,1)S(1)} %get-tuple-element.75), channel_id=1, source_target_pairs={{0,16},{1,18},{2,17},{3,20},{4,19},{5,22},{6,21},{7,24},{8,23},{9,... | collective-permute-start | bytes 27656 | tf_op jit(solution)/shard_map/ppermute | solution.py:55
  6.0 1.1 %collective-permute-start = (bf16[16,8,96]{2,1,0:T(8,128)(2,1)S(1)}, bf16[16,8,96]{2,1,0:T(8,128)(2,1)S(1)}, u32[]{:S(2)}, u32[]{:S(2)}) collective-permute-start(bf16[16,8,96]{2,1,0:T(8,128)(2,1)S(1)} %get-tuple-element.72), channel_id=1, source_target_pairs={{0,1},{1,0},{2,3},{3,2},{4,5},{5,4},{6,7},{7,6},{8,9},{9,8},{10,11... | collective-permute-start | bytes 73736 | tf_op jit(solution)/shard_map/ppermute | solution.py:55
  7.0 0.9 %collective-permute-start.1 = (bf16[16,8,96]{2,1,0:T(8,128)(2,1)S(1)}, bf16[16,8,96]{2,1,0:T(8,128)(2,1)S(1)}, u32[]{:S(2)}, u32[]{:S(2)}) collective-permute-start(bf16[16,8,96]{2,1,0:T(8,128)(2,1)S(1)} %get-tuple-element.73), channel_id=1, source_target_pairs={{0,16},{1,2},{2,1},{3,4},{4,3},{5,6},{6,5},{7,8},{8,7},{9,10},{10,... | collective-permute-start | bytes 73736 | tf_op jit(solution)/shard_map/ppermute | solution.py:55
  8.8 2.2 %collective-permute-done.1.refs_10_ = bf16[16,8,96]{2,1,0:T(8,128)(2,1)S(1)} collective-permute-done((bf16[16,8,96]{2,1,0:T(8,128)(2,1)S(1)}, bf16[16,8,96]{2,1,0:T(8,128)(2,1)S(1)}, u32[]{:S(2)}, u32[]{:S(2)}) %collective-permute-start.1) | collective-permute-done | bytes 24608 | tf_op jit(solution)/shard_map/ppermute | solution.py:55
  10.9 10.7 %shard_map.112 = (bf16[16,64,96]{2,1,0:T(8,128)(2,1)S(1)}, f32[2240,128]{1,0:T(8,128)S(1)}, f32[1600,128]{1,0:T(8,128)S(1)}, bf16[1376,128]{1,0:T(8,128)(2,1)S(1...) custom-call(bf16[16,64,96]{2,1,0:T(8,128)(2,1)S(1)} %get-tuple-eleme, ...), custom_call_target="tpu_custom_call" | custom-call | flops 15000000512 | bytes 262144 | tf_op jit(solution)/shard_map/pallas_call | solution.py:793
  21.7 1.0 %collective-permute-start.7 = (bf16[9,64,96]{2,1,0:T(8,128)(2,1)S(1)}, bf16[9,64,96]{2,1,0:T(8,128)(2,1)S(1)}, u32[]{:S(2)}, u32[]{:S(2)}) collective-permute-start(bf16[9,64,96]{2,1,0:T(8,128)(2,1)S(1)} %get-tuple-element.94.refs_0_), channel_id=1, source_target_pairs={{0,16},{1,17},{2,18},{3,19},{4,20},{5,21},{6,22},{7,23},{8,24},{9,... | collective-permute-start | bytes 331784 | tf_op jit(solution)/shard_map/ppermute | solution.py:55
  22.8 1.2 %collective-permute-start.9 = (bf16[9,8,96]{2,1,0:T(8,128)(2,1)S(1)}, bf16[9,8,96]{2,1,0:T(8,128)(2,1)S(1)}, u32[]{:S(2)}, u32[]{:S(2)}) collective-permute-start(bf16[9,8,96]{2,1,0:T(8,128)(2,1)S(1)} %get-tuple-element.98), channel_id=1, source_target_pairs={{0,16},{1,18},{2,17},{3,20},{4,19},{5,22},{6,21},{7,24},{8,23},{9,... | collective-permute-start | bytes 41480 | tf_op jit(solution)/shard_map/ppermute | solution.py:55
  23.9 1.6 %collective-permute-start.5 = (bf16[32,8,96]{2,1,0:T(8,128)(2,1)S(1)}, bf16[32,8,96]{2,1,0:T(8,128)(2,1)S(1)}, u32[]{:S(2)}, u32[]{:S(2)}) collective-permute-start(bf16[32,8,96]{2,1,0:T(8,128)(2,1)S(1)} %get-tuple-element.95), channel_id=1, source_target_pairs={{0,1},{1,0},{2,3},{3,2},{4,5},{5,4},{6,7},{7,6},{8,9},{9,8},{10,11... | collective-permute-start | bytes 147464 | tf_op jit(solution)/shard_map/ppermute | solution.py:55
  25.5 1.1 %collective-permute-start.6 = (bf16[32,8,96]{2,1,0:T(8,128)(2,1)S(1)}, bf16[32,8,96]{2,1,0:T(8,128)(2,1)S(1)}, u32[]{:S(2)}, u32[]{:S(2)}) collective-permute-start(bf16[32,8,96]{2,1,0:T(8,128)(2,1)S(1)} %get-tuple-element.96), channel_id=1, source_target_pairs={{0,16},{1,2},{2,1},{3,4},{4,3},{5,6},{6,5},{7,8},{8,7},{9,10},{10,... | collective-permute-start | bytes 147464 | tf_op jit(solution)/shard_map/ppermute | solution.py:55
  26.6 2.3 %shard_map.113 = (f32[56,128]{1,0:T(8,128)S(1)}, f32[384,128]{1,0:T(8,128)S(1)}, f32[384,128]{1,0:T(8,128)S(1)}, bf16[16,64,96]{2,1,0:T(8,128)(2,1)}) custom-call(f32[1600,128]{1,0:T(8,128)S(1)} %get-tuple-element.76.x1, f32[1024,128]{1,0:T(8,128)S(1)} %get-tuple-element.77.grad1.refs_0_, bf16[1024,128]{1,0:T(8,128)(2,1)S(1)} %get-tuple-element.78.normed1, ...), custom_call_target="tpu_custom_call" | custom-call | flops 3000000000 | bytes 262144 | tf_op jit(solution)/shard_map/pallas_call | solution.py:793
  28.9 0.8 %collective-permute-done.6.refs_15_ = bf16[32,8,96]{2,1,0:T(8,128)(2,1)S(1)} collective-permute-done((bf16[32,8,96]{2,1,0:T(8,128)(2,1)S(1)}, bf16[32,8,96]{2,1,0:T(8,128)(2,1)S(1)}, u32[]{:S(2)}, u32[]{:S(2)}) %collective-permute-start.6) | collective-permute-done | bytes 49184 | tf_op jit(solution)/shard_map/ppermute | solution.py:55
  29.8 6.5 %shard_map.115 = (f32[1600,128]{1,0:T(8,128)S(1)}, f32[1024,128]{1,0:T(8,128)S(1)}, f32[768,128]{1,0:T(8,128)S(1)}, f32[80,128]{1,0:T(8,128)S(1)}, bf16[848,128]{1,0:T(8,128)(2,1)S(1)}) custom-call(f32[1024,128]{1,0:T(8,128)S(1)} %get-tuple-element.77.grad1.refs_0_, bf16[16,64,96]{2,1,0:T(8,128)(2,1)S(1)} %copy-done.1, ...), custom_call_target="tpu_custom_call" | custom-call | flops 12000000000 | bytes 262144 | tf_op jit(solution)/shard_map/pallas_call | solution.py:793
  36.4 1.4 %collective-permute-done.10.refs_0_ = bf16[848,128]{1,0:T(8,128)(2,1)S(1)} collective-permute-done((bf16[848,128]{1,0:T(8,128)(2,1)S(1)}, bf16[848,128]{1,0:T(8,128)(2,1)S(1)}, u32[]{:S(2)}, u32[]{:S(2)}) %collective-permute-start.10) | collective-permute-done | bytes 217120 | tf_op jit(solution)/shard_map/ppermute | solution.py:930
  37.9 1.8 %collective-permute-start.11 = (bf16[272,128]{1,0:T(8,128)(2,1)S(1)}, bf16[272,128]{1,0:T(8,128)(2,1)S(1)}, u32[]{:S(2)}, u32[]{:S(2)}) collective-permute-start(bf16[272,128]{1,0:T(8,128)(2,1)S(1)} %get-tuple-element.107), channel_id=1, source_target_pairs={{0,2},{1,3},{2,0},{3,1},{4,6},{5,7},{6,4},{7,5},{8,10},{9,11},{10,... | collective-permute-start | bytes 208904 | tf_op jit(solution)/shard_map/ppermute | solution.py:930
  39.7 1.2 %collective-permute-start.12 = (bf16[272,128]{1,0:T(8,128)(2,1)S(1)}, bf16[272,128]{1,0:T(8,128)(2,1)S(1)}, u32[]{:S(2)}, u32[]{:S(2)}) collective-permute-start(bf16[272,128]{1,0:T(8,128)(2,1)S(1)} %get-tuple-element.108), channel_id=1, source_target_pairs={{0,16},{1,17},{2,18},{3,19},{4,20},{5,21},{6,22},{7,23},{8,24},{9,... | collective-permute-start | bytes 208904 | tf_op jit(solution)/shard_map/ppermute | solution.py:930
  41.4 2.1 %shard_map.117 = (bf16[16,64,96]{2,1,0:T(8,128)(2,1)}, f32[8,128]{1,0:T(8,128)S(1)}) custom-call(f32[1600,128]{1,0:T(8,128)S(1)} %get-tuple-element.99.grad0, f32[1024,128]{1,0:T(8,128)S(1)} %get-tuple-element.100.middle, bf16[784,128]{1,0:T(8,128)(2,1)S(1)} %get-tuple-element.64.refs_2_.taps0, f32[80,128]{1,0:T(8,128)S(1)} %get-tuple-element.104.after.small), custom_call_target="tpu_custom_call" | custom-call | flops 3000000000 | bytes 262144 | tf_op jit(solution)/shard_map/pallas_call | solution.py:793
  43.6 1.1 %collective-permute-done.12.refs_1_ = bf16[272,128]{1,0:T(8,128)(2,1)S(1)} collective-permute-done((bf16[272,128]{1,0:T(8,128)(2,1)S(1)}, bf16[272,128]{1,0:T(8,128)(2,1)S(1)}, u32[]{:S(2)}, u32[]{:S(2)}) %collective-permute-start.12) | collective-permute-done | bytes 69664 | tf_op jit(solution)/shard_map/ppermute | solution.py:930
  44.6 1.5 %collective-permute-done.13.refs_2_ = bf16[272,128]{1,0:T(8,128)(2,1)S(1)} collective-permute-done((bf16[272,128]{1,0:T(8,128)(2,1)S(1)}, bf16[272,128]{1,0:T(8,128)(2,1)S(1)}, u32[]{:S(2)}, u32[]{:S(2)}) %collective-permute-start.13) | collective-permute-done | bytes 69664 | tf_op jit(solution)/shard_map/ppermute | solution.py:930
  46.2 2.7 %collective-permute-start.14 = (bf16[128,128]{1,0:T(8,128)(2,1)S(1)}, bf16[128,128]{1,0:T(8,128)(2,1)S(1)}, u32[]{:S(2)}, u32[]{:S(2)}) collective-permute-start(bf16[128,128]{1,0:T(8,128)(2,1)S(1)} %get-tuple-element.113), channel_id=1, source_target_pairs={{0,8},{1,9},{2,10},{3,11},{4,12},{5,13},{6,14},{7,15},{8,0},{9,1},... | collective-permute-start | bytes 98312 | tf_op jit(solution)/shard_map/ppermute | solution.py:930
  49.3 1.4 %collective-permute-start.16 = (bf16[128,128]{1,0:T(8,128)(2,1)S(1)}, bf16[128,128]{1,0:T(8,128)(2,1)S(1)}, u32[]{:S(2)}, u32[]{:S(2)}) collective-permute-start(bf16[128,128]{1,0:T(8,128)(2,1)S(1)} %get-tuple-element.115), channel_id=1, source_target_pairs={{0,12},{1,13},{2,14},{3,15},{4,8},{5,9},{6,10},{7,11},{8,4},{9,5},... | collective-permute-start | bytes 98312 | tf_op jit(solution)/shard_map/ppermute | solution.py:930
  51.2 1.7 %collective-permute-done.15.refs_1_ = bf16[128,128]{1,0:T(8,128)(2,1)S(1)} collective-permute-done((bf16[128,128]{1,0:T(8,128)(2,1)S(1)}, bf16[128,128]{1,0:T(8,128)(2,1)S(1)}, u32[]{:S(2)}, u32[]{:S(2)}) %collective-permute-start.15) | collective-permute-done | bytes 32800 | tf_op jit(solution)/shard_map/ppermute | solution.py:930
  52.9 2.1 %collective-permute-done.16.refs_2_ = bf16[128,128]{1,0:T(8,128)(2,1)S(1)} collective-permute-done((bf16[128,128]{1,0:T(8,128)(2,1)S(1)}, bf16[128,128]{1,0:T(8,128)(2,1)S(1)}, u32[]{:S(2)}, u32[]{:S(2)}) %collective-permute-start.16) | collective-permute-done | bytes 32800 | tf_op jit(solution)/shard_map/ppermute | solution.py:930
  (33 shorter events, 3.5 us)
Async XLA Ops:
  0.6 1.0 %copy-start = (bf16[16,64,96]{2,1,0:T(8,128)(2,1)S(1)}, bf16[16,64,96]{2,1,0:T(8,128)(2,1)}, u32[]{:S(2)}) copy-start(bf16[16,64,96]{2,1,0:T(8,128)(2,1)} %image_in.1) | copy-start | bytes 589828
  1.6 9.3 %collective-permute-start.2 = (bf16[6,64,96]{2,1,0:T(8,128)(2,1)S(1)}, bf16[6,64,96]{2,1,0:T(8,128)(2,1)S(1)}, u32[]{:S(2)}, u32[]{:S(2)}) collective-permute-start(bf16[6,64,96]{2,1,0:T(8,128)(2,1)S(1)} %get-tuple-element.71.refs_0_), channel_id=1, source_target_pairs={{0,16},{1,17},{2,18},{3,19},{4,20},{5,21},{6,22},{7,23},{8,24},{9,... | collective-permute-start | bytes 221192 | tf_op jit(solution)/shard_map/ppermute | solution.py:55
  4.7 3.3 %copy-start.2 = (bf16[2,96,384]{2,1,0:T(8,128)(2,1)S(1)}, bf16[2,96,384]{2,1,0:T(8,128)(2,1)}, u32[]{:S(2)}) copy-start(bf16[2,96,384]{2,1,0:T(8,128)(2,1)} %up_in.1) | copy-start | bytes 442372
  4.7 3.3 %copy-start.3 = (bf16[2,384,96]{1,2,0:T(8,128)(2,1)S(1)}, bf16[2,384,96]{1,2,0:T(8,128)(2,1)}, u32[]{:S(2)}) copy-start(bf16[2,384,96]{1,2,0:T(8,128)(2,1)} %param.10) | copy-start | bytes 442372
  4.7 3.3 %copy-start.4 = (f32[2,7,7,96]{3,0,2,1:T(2,128)S(1)}, f32[2,7,7,96]{3,0,2,1:T(2,128)}, u32[]{:S(2)}) copy-start(f32[2,7,7,96]{3,0,2,1:T(2,128)} %param.7) | copy-start | bytes 112900
  4.7 3.3 %copy-start.5 = (f32[2,96]{1,0:T(2,128)S(1)}, f32[2,96]{1,0:T(2,128)}, u32[]{:S(2)}) copy-start(f32[2,96]{1,0:T(2,128)} %gains_in.1) | copy-start | bytes 2308
  4.7 4.0 %collective-permute-start.3 = (bf16[6,8,96]{2,1,0:T(8,128)(2,1)S(1)}, bf16[6,8,96]{2,1,0:T(8,128)(2,1)S(1)}, u32[]{:S(2)}, u32[]{:S(2)}) collective-permute-start(bf16[6,8,96]{2,1,0:T(8,128)(2,1)S(1)} %get-tuple-element.74), channel_id=1, source_target_pairs={{0,17},{1,16},{2,19},{3,18},{4,21},{5,20},{6,23},{7,22},{8,25},{9,... | collective-permute-start | bytes 27656 | tf_op jit(solution)/shard_map/ppermute | solution.py:55
  4.8 4.0 %collective-permute-start.4 = (bf16[6,8,96]{2,1,0:T(8,128)(2,1)S(1)}, bf16[6,8,96]{2,1,0:T(8,128)(2,1)S(1)}, u32[]{:S(2)}, u32[]{:S(2)}) collective-permute-start(bf16[6,8,96]{2,1,0:T(8,128)(2,1)S(1)} %get-tuple-element.75), channel_id=1, source_target_pairs={{0,16},{1,18},{2,17},{3,20},{4,19},{5,22},{6,21},{7,24},{8,23},{9,... | collective-permute-start | bytes 27656 | tf_op jit(solution)/shard_map/ppermute | solution.py:55
  6.0 2.8 %collective-permute-start = (bf16[16,8,96]{2,1,0:T(8,128)(2,1)S(1)}, bf16[16,8,96]{2,1,0:T(8,128)(2,1)S(1)}, u32[]{:S(2)}, u32[]{:S(2)}) collective-permute-start(bf16[16,8,96]{2,1,0:T(8,128)(2,1)S(1)} %get-tuple-element.72), channel_id=1, source_target_pairs={{0,1},{1,0},{2,3},{3,2},{4,5},{5,4},{6,7},{7,6},{8,9},{9,8},{10,11... | collective-permute-start | bytes 73736 | tf_op jit(solution)/shard_map/ppermute | solution.py:55
  7.0 3.9 %collective-permute-start.1 = (bf16[16,8,96]{2,1,0:T(8,128)(2,1)S(1)}, bf16[16,8,96]{2,1,0:T(8,128)(2,1)S(1)}, u32[]{:S(2)}, u32[]{:S(2)}) collective-permute-start(bf16[16,8,96]{2,1,0:T(8,128)(2,1)S(1)} %get-tuple-element.73), channel_id=1, source_target_pairs={{0,16},{1,2},{2,1},{3,4},{4,3},{5,6},{6,5},{7,8},{8,7},{9,10},{10,... | collective-permute-start | bytes 73736 | tf_op jit(solution)/shard_map/ppermute | solution.py:55
  8.0 3.0 %copy-start.1 = (bf16[16,64,96]{2,1,0:T(8,128)(2,1)S(1)}, bf16[16,64,96]{2,1,0:T(8,128)(2,1)}, u32[]{:S(2)}) copy-start(bf16[16,64,96]{2,1,0:T(8,128)(2,1)} %refs_1_.3) | copy-start | bytes 589828
  21.7 8.1 %collective-permute-start.7 = (bf16[9,64,96]{2,1,0:T(8,128)(2,1)S(1)}, bf16[9,64,96]{2,1,0:T(8,128)(2,1)S(1)}, u32[]{:S(2)}, u32[]{:S(2)}) collective-permute-start(bf16[9,64,96]{2,1,0:T(8,128)(2,1)S(1)} %get-tuple-element.94.refs_0_), channel_id=1, source_target_pairs={{0,16},{1,17},{2,18},{3,19},{4,20},{5,21},{6,22},{7,23},{8,24},{9,... | collective-permute-start | bytes 331784 | tf_op jit(solution)/shard_map/ppermute | solution.py:55
  22.7 6.2 %collective-permute-start.8 = (bf16[9,8,96]{2,1,0:T(8,128)(2,1)S(1)}, bf16[9,8,96]{2,1,0:T(8,128)(2,1)S(1)}, u32[]{:S(2)}, u32[]{:S(2)}) collective-permute-start(bf16[9,8,96]{2,1,0:T(8,128)(2,1)S(1)} %get-tuple-element.97), channel_id=1, source_target_pairs={{0,17},{1,16},{2,19},{3,18},{4,21},{5,20},{6,23},{7,22},{8,25},{9,... | collective-permute-start | bytes 41480 | tf_op jit(solution)/shard_map/ppermute | solution.py:55
  22.8 6.1 %collective-permute-start.9 = (bf16[9,8,96]{2,1,0:T(8,128)(2,1)S(1)}, bf16[9,8,96]{2,1,0:T(8,128)(2,1)S(1)}, u32[]{:S(2)}, u32[]{:S(2)}) collective-permute-start(bf16[9,8,96]{2,1,0:T(8,128)(2,1)S(1)} %get-tuple-element.98), channel_id=1, source_target_pairs={{0,16},{1,18},{2,17},{3,20},{4,19},{5,22},{6,21},{7,24},{8,23},{9,... | collective-permute-start | bytes 41480 | tf_op jit(solution)/shard_map/ppermute | solution.py:55
  23.9 5.0 %collective-permute-start.5 = (bf16[32,8,96]{2,1,0:T(8,128)(2,1)S(1)}, bf16[32,8,96]{2,1,0:T(8,128)(2,1)S(1)}, u32[]{:S(2)}, u32[]{:S(2)}) collective-permute-start(bf16[32,8,96]{2,1,0:T(8,128)(2,1)S(1)} %get-tuple-element.95), channel_id=1, source_target_pairs={{0,1},{1,0},{2,3},{3,2},{4,5},{5,4},{6,7},{7,6},{8,9},{9,8},{10,11... | collective-permute-start | bytes 147464 | tf_op jit(solution)/shard_map/ppermute | solution.py:55
  25.5 4.3 %collective-permute-start.6 = (bf16[32,8,96]{2,1,0:T(8,128)(2,1)S(1)}, bf16[32,8,96]{2,1,0:T(8,128)(2,1)S(1)}, u32[]{:S(2)}, u32[]{:S(2)}) collective-permute-start(bf16[32,8,96]{2,1,0:T(8,128)(2,1)S(1)} %get-tuple-element.96), channel_id=1, source_target_pairs={{0,16},{1,2},{2,1},{3,4},{4,3},{5,6},{6,5},{7,8},{8,7},{9,10},{10,... | collective-permute-start | bytes 147464 | tf_op jit(solution)/shard_map/ppermute | solution.py:55
  36.3 1.5 %collective-permute-start.10 = (bf16[848,128]{1,0:T(8,128)(2,1)S(1)}, bf16[848,128]{1,0:T(8,128)(2,1)S(1)}, u32[]{:S(2)}, u32[]{:S(2)}) collective-permute-start(bf16[848,128]{1,0:T(8,128)(2,1)S(1)} %get-tuple-element.103), channel_id=1, source_target_pairs={{0,1},{1,0},{2,3},{3,2},{4,5},{5,4},{6,7},{7,6},{8,9},{9,8},{10,11... | collective-permute-start | bytes 651272 | tf_op jit(solution)/shard_map/ppermute | solution.py:930
  37.9 5.7 %collective-permute-start.11 = (bf16[272,128]{1,0:T(8,128)(2,1)S(1)}, bf16[272,128]{1,0:T(8,128)(2,1)S(1)}, u32[]{:S(2)}, u32[]{:S(2)}) collective-permute-start(bf16[272,128]{1,0:T(8,128)(2,1)S(1)} %get-tuple-element.107), channel_id=1, source_target_pairs={{0,2},{1,3},{2,0},{3,1},{4,6},{5,7},{6,4},{7,5},{8,10},{9,11},{10,... | collective-permute-start | bytes 208904 | tf_op jit(solution)/shard_map/ppermute | solution.py:930
  39.7 4.9 %collective-permute-start.12 = (bf16[272,128]{1,0:T(8,128)(2,1)S(1)}, bf16[272,128]{1,0:T(8,128)(2,1)S(1)}, u32[]{:S(2)}, u32[]{:S(2)}) collective-permute-start(bf16[272,128]{1,0:T(8,128)(2,1)S(1)} %get-tuple-element.108), channel_id=1, source_target_pairs={{0,16},{1,17},{2,18},{3,19},{4,20},{5,21},{6,22},{7,23},{8,24},{9,... | collective-permute-start | bytes 208904 | tf_op jit(solution)/shard_map/ppermute | solution.py:930
  40.9 5.2 %collective-permute-start.13 = (bf16[272,128]{1,0:T(8,128)(2,1)S(1)}, bf16[272,128]{1,0:T(8,128)(2,1)S(1)}, u32[]{:S(2)}, u32[]{:S(2)}) collective-permute-start(bf16[272,128]{1,0:T(8,128)(2,1)S(1)} %get-tuple-element.109), channel_id=1, source_target_pairs={{0,18},{1,19},{2,16},{3,17},{4,22},{5,23},{6,20},{7,21},{8,26},{9,... | collective-permute-start | bytes 208904 | tf_op jit(solution)/shard_map/ppermute | solution.py:930
  46.2 5.0 %collective-permute-start.14 = (bf16[128,128]{1,0:T(8,128)(2,1)S(1)}, bf16[128,128]{1,0:T(8,128)(2,1)S(1)}, u32[]{:S(2)}, u32[]{:S(2)}) collective-permute-start(bf16[128,128]{1,0:T(8,128)(2,1)S(1)} %get-tuple-element.113), channel_id=1, source_target_pairs={{0,8},{1,9},{2,10},{3,11},{4,12},{5,13},{6,14},{7,15},{8,0},{9,1},... | collective-permute-start | bytes 98312 | tf_op jit(solution)/shard_map/ppermute | solution.py:930
  48.9 4.0 %collective-permute-start.15 = (bf16[128,128]{1,0:T(8,128)(2,1)S(1)}, bf16[128,128]{1,0:T(8,128)(2,1)S(1)}, u32[]{:S(2)}, u32[]{:S(2)}) collective-permute-start(bf16[128,128]{1,0:T(8,128)(2,1)S(1)} %get-tuple-element.114), channel_id=1, source_target_pairs={{0,4},{1,5},{2,6},{3,7},{4,0},{5,1},{6,2},{7,3},{8,12},{9,13},{10,... | collective-permute-start | bytes 98312 | tf_op jit(solution)/shard_map/ppermute | solution.py:930
  49.3 5.7 %collective-permute-start.16 = (bf16[128,128]{1,0:T(8,128)(2,1)S(1)}, bf16[128,128]{1,0:T(8,128)(2,1)S(1)}, u32[]{:S(2)}, u32[]{:S(2)}) collective-permute-start(bf16[128,128]{1,0:T(8,128)(2,1)S(1)} %get-tuple-element.115), channel_id=1, source_target_pairs={{0,12},{1,13},{2,14},{3,15},{4,8},{5,9},{6,10},{7,11},{8,4},{9,5},... | collective-permute-start | bytes 98312 | tf_op jit(solution)/shard_map/ppermute | solution.py:930

commit v11 on v10

--- a/solution.py
+++ b/solution.py
@@ -226,6 +226,12 @@
     return jnp.concatenate([top, bottom], axis=0)
 
 
+def together(steps):
+    steps = list(steps)
+    while steps:
+        steps = [step for step in steps if next(step, steps) is not steps]
+
+
 def by_blocks(function, *arrays, size=16):
     count = arrays[0].shape[0]
     results = [function(*(x[i : i + size] for x in arrays)) for i in range(0, count, size)]
@@ -256,8 +262,10 @@
         return (unit, inverse, (unit * gain).astype(bf16))
 
     totals = [dot(by_blocks(high_low, x)[0], jnp.ones((2 * LANES, LANES), bf16)) for x in parts]
+    yield
     centred, squares = zip(*(by_blocks(centre, x, total) for x, total in zip(parts, totals)))
     variances = dot(side_by_side(*squares), ones)
+    yield
     return [by_blocks(finish, c, variances[:, k * LANES : (k + 1) * LANES]) for k, c in enumerate(centred)]
 
 
@@ -272,6 +280,7 @@
         return (round16(jnp.where(in_channels(grad.shape, channels), grad, 0.0)),)
 
     sums = dot(by_blocks(products, normed_grad, unit)[0], ones)
+    yield
     return by_blocks(finish, normed_grad, unit, inverse, sums)[0]
 
 
@@ -404,10 +413,12 @@
     gain = pad_lanes(gains[0:1, :])
     ones = diagonal(jnp.ones((LANES, LANES), bf16), jnp.ones((LANES, LANES), bf16))
     half = dims.ext_pad // 2
-    for start, n in pieces(half, dims.piece):
+
+    def mix0(start, n):
         spans = [(start, n), (half + start, n)]
-        parts = layer_norm([conv[at : at + n, :] for at, n in spans], gain, channels, ones)
+        parts = yield from layer_norm([conv[at : at + n, :] for at, n in spans], gain, channels, ones)
         pres = dot(side_by_side(parts[0][2], parts[1][2]), forward0[...])
+        yield
         count = pres.shape[1] // 2
         hiddens = []
         for k, ((at, n), (unit, inverse, _)) in enumerate(zip(spans, parts)):
@@ -423,9 +434,11 @@
             slope0[at : at + n, :] = slope
             hiddens.append(hidden)
         branches = dot(side_by_side(*hiddens), back0[...])
+        yield
         for k, (at, n) in enumerate(spans):
             px = pl.ds(frame + at, n)
             x1[px, :] = round16(x1[px, :] + branches[:, k * LANES : (k + 1) * LANES])
+    together([mix0(start, n) for start, n in pieces(half, dims.piece)])
     clear_outside(place, x1, dims)
 
     def conv1(g, carry):
@@ -440,16 +453,18 @@
     gain_sum[...] = jnp.zeros(gain_sum.shape, f32)
     lines = dims.line_step
     step = lines * cols
-    for k in range(rows // lines):
+
+    def mix1(k):
         px = slice(k * step, (k + 1) * step)
         middle = k * step + step // 2
-        parts = layer_norm(
+        parts = yield from layer_norm(
             [conv[k * step : middle, :], conv[middle : (k + 1) * step, :]], gain1, channels, ones
         )
         unit, inverse, normed = (jnp.concatenate(pair, axis=0) for pair in zip(*parts))
         normed1[px, :] = normed
         upstream = pad_lanes(cot[k * lines : (k + 1) * lines].reshape(step, channels))
         both = dot(side_by_side(normed, upstream), forward1[...])
+        yield
 
         def activate(pre, hidden_grad):
             value, slope = gelu_parts(pre)
@@ -460,6 +475,7 @@
         hidden1[px, :] = hidden
         pre_grad1[px, :] = pre_grad
         both = dot(side_by_side(hidden, pre_grad), back1[...])
+        yield
         branch, normed_grad = (both[:, :LANES], both[:, LANES:])
         for i in range(lines):
             start = (k * lines + i + h) * ext_cols + 4
@@ -467,7 +483,9 @@
             output[k * lines + i] = line[:, :channels].astype(bf16)
         product = normed_grad * unit
         gain_sum[...] += jnp.sum(product.reshape(step // 8, 8, LANES), axis=0)
-        grad1[px, :] = norm_backward(normed_grad, unit, inverse, gain1, channels, ones)
+        grad1[px, :] = yield from norm_backward(normed_grad, unit, inverse, gain1, channels, ones)
+
+    together([mix1(k) for k in range(rows // lines)])
 
     takes = [(flat_take(grad1, cols, channels), 2 * h, rows, cols), (image_take(cot), h, rows, cols)]
     write_strips(place, outs, takes, band_combos(dims.row_count))
@@ -570,10 +588,12 @@
     gain_sum[...] = jnp.zeros(gain_sum.shape, f32)
     ones = diagonal(jnp.ones((LANES, LANES), bf16), jnp.ones((LANES, LANES), bf16))
     half_px = dims.ext_pad // 2
-    for start, n in pieces(half_px, dims.piece):
+
+    def mix0(start, n):
         spans = [(start, n), (half_px + start, n)]
         flows = [upstream[at : at + n, :].astype(bf16) for at, n in spans]
         hidden_grads = dot(side_by_side(*flows), grad_in0[...])
+        yield
         count = hidden_grads.shape[1] // 2
 
         def slope_times(grad, slope):
@@ -584,6 +604,7 @@
             for k, (at, n) in enumerate(spans)
         ]
         both = dot(side_by_side(*pre_grads), grad_out0[...])
+        yield
         normed_grads = (both[:, :LANES], both[:, LANES:])
         for (at, n), flow, pre_grad, normed_grad in zip(spans, flows, pre_grads, normed_grads):
             mine = own[at : at + n, :]
@@ -593,8 +614,10 @@
             pre_grad0[at : at + n, :] = pre_grad
             product = normed_grad * unit * mine
             gain_sum[...] += jnp.sum(product.reshape(n // 8, 8, LANES), axis=0)
-            grad = norm_backward(normed_grad, unit, inv0[at : at + n, :], gain, channels, ones)
+            grad = yield from norm_backward(normed_grad, unit, inv0[at : at + n, :], gain, channels, ones)
             grad0[pl.ds(frame + at, n), :] = grad
+
+    together([mix0(start, n) for start, n in pieces(half_px, dims.piece)])
     clear_outside(place, grad0, dims)
     kernel_sums(
         x0, h * wide + SIDE - h, wide, grad0, h * ext_cols + margin, ext_cols, rows, cols, size, sums

time: 55.9 us -> 53 us (0.948)
  Pallas kernels: 23.3 us -> 20.5 us
    pallas_call x11, Pallas kernels: 23.3 us -> 20.5 us  [run(): pl.pallas_call(kernel, out_shape=shapes, in_specs=[far] * in_hbm + [space...]
  transfers between devices with their start and end apart: 17 -> 17, of which waited for: 8 -> 8; matrix products, arithmetic and copies ran while one was open for 0% -> 0% of each run, Pallas kernels for 9% -> 10%
where the time goes in v11:
time: 53 us; the launch traced here: 52.8 us
  Pallas kernels  20.5 us (39%)
  starting transfers between devices  19.3 us (36%)
  waiting for transfers between devices  11.4 us (22%)
  local copies, waits for them, and re-layouts  0.96 us (2%)
  between operations  0.76 us (1%)
    pallas_call x11, Pallas kernels, run(): pl.pallas_call(kernel, out_shape=shapes, in_specs=[far] * in_hbm + [space...  20.5 us
    ppermute x10, starting transfers between devices, exchange(): lax.ppermute(strip, ('row', 'col'), swap_pairs(row_count, col_count, rs,...  11.1 us
    ppermute x7, waiting for transfers between devices, per_device(): lax.ppermute(x, axes, swap_by(d, group, mask))  8.33 us
    ppermute x7, starting transfers between devices, per_device(): lax.ppermute(x, axes, swap_by(d, group, mask))  8.14 us
    ppermute x10, waiting for transfers between devices, exchange(): lax.ppermute(strip, ('row', 'col'), swap_pairs(row_count, col_count, rs,...  3.04 us
  transfers between devices with their start and end apart: 17, of which 8 were waited for; matrix products, arithmetic and copies ran while one was open for 0% of the time, Pallas kernels for 10%

profile of v11, /device:TPU:0, one launch (start us, length us, event | category | flops | bytes accessed | tf_op | source)
XLA Modules:
  0.0 52.8 jit_solution(9270632589560591478)
XLA Ops:
  0.6 0.9 %copy-done = bf16[16,64,96]{2,1,0:T(8,128)(2,1)S(1)} copy-done((bf16[16,64,96]{2,1,0:T(8,128)(2,1)S(1)}, bf16[16,64,96]{2,1,0:T(8,128)(2,1)}, u32[]{:S(2)}) %copy-start) | copy-done | bytes 196632
  1.6 3.0 %collective-permute-start.2 = (bf16[6,64,96]{2,1,0:T(8,128)(2,1)S(1)}, bf16[6,64,96]{2,1,0:T(8,128)(2,1)S(1)}, u32[]{:S(2)}, u32[]{:S(2)}) collective-permute-start(bf16[6,64,96]{2,1,0:T(8,128)(2,1)S(1)} %get-tuple-element.71.refs_0_), channel_id=1, source_target_pairs={{0,16},{1,17},{2,18},{3,19},{4,20},{5,21},{6,22},{7,23},{8,24},{9,... | collective-permute-start | bytes 221192 | tf_op jit(solution)/shard_map/ppermute | solution.py:55
  4.8 1.2 %collective-permute-start.4 = (bf16[6,8,96]{2,1,0:T(8,128)(2,1)S(1)}, bf16[6,8,96]{2,1,0:T(8,128)(2,1)S(1)}, u32[]{:S(2)}, u32[]{:S(2)}) collective-permute-start(bf16[6,8,96]{2,1,0:T(8,128)(2,1)S(1)} %get-tuple-element.75), channel_id=1, source_target_pairs={{0,16},{1,18},{2,17},{3,20},{4,19},{5,22},{6,21},{7,24},{8,23},{9,... | collective-permute-start | bytes 27656 | tf_op jit(solution)/shard_map/ppermute | solution.py:55
  6.0 1.1 %collective-permute-start = (bf16[16,8,96]{2,1,0:T(8,128)(2,1)S(1)}, bf16[16,8,96]{2,1,0:T(8,128)(2,1)S(1)}, u32[]{:S(2)}, u32[]{:S(2)}) collective-permute-start(bf16[16,8,96]{2,1,0:T(8,128)(2,1)S(1)} %get-tuple-element.72), channel_id=1, source_target_pairs={{0,1},{1,0},{2,3},{3,2},{4,5},{5,4},{6,7},{7,6},{8,9},{9,8},{10,11... | collective-permute-start | bytes 73736 | tf_op jit(solution)/shard_map/ppermute | solution.py:55
  7.0 0.9 %collective-permute-start.1 = (bf16[16,8,96]{2,1,0:T(8,128)(2,1)S(1)}, bf16[16,8,96]{2,1,0:T(8,128)(2,1)S(1)}, u32[]{:S(2)}, u32[]{:S(2)}) collective-permute-start(bf16[16,8,96]{2,1,0:T(8,128)(2,1)S(1)} %get-tuple-element.73), channel_id=1, source_target_pairs={{0,16},{1,2},{2,1},{3,4},{4,3},{5,6},{6,5},{7,8},{8,7},{9,10},{10,... | collective-permute-start | bytes 73736 | tf_op jit(solution)/shard_map/ppermute | solution.py:55
  8.8 2.2 %collective-permute-done.1.refs_10_ = bf16[16,8,96]{2,1,0:T(8,128)(2,1)S(1)} collective-permute-done((bf16[16,8,96]{2,1,0:T(8,128)(2,1)S(1)}, bf16[16,8,96]{2,1,0:T(8,128)(2,1)S(1)}, u32[]{:S(2)}, u32[]{:S(2)}) %collective-permute-start.1) | collective-permute-done | bytes 24608 | tf_op jit(solution)/shard_map/ppermute | solution.py:55
  10.9 8.6 %shard_map.112 = (bf16[16,64,96]{2,1,0:T(8,128)(2,1)S(1)}, f32[2240,128]{1,0:T(8,128)S(1)}, f32[1600,128]{1,0:T(8,128)S(1)}, bf16[1376,128]{1,0:T(8,128)(2,1)S(1...) custom-call(bf16[16,64,96]{2,1,0:T(8,128)(2,1)S(1)} %get-tuple-eleme, ...), custom_call_target="tpu_custom_call" | custom-call | flops 15000000512 | bytes 262144 | tf_op jit(solution)/shard_map/pallas_call | solution.py:816
  19.6 1.0 %collective-permute-start.7 = (bf16[9,64,96]{2,1,0:T(8,128)(2,1)S(1)}, bf16[9,64,96]{2,1,0:T(8,128)(2,1)S(1)}, u32[]{:S(2)}, u32[]{:S(2)}) collective-permute-start(bf16[9,64,96]{2,1,0:T(8,128)(2,1)S(1)} %get-tuple-element.94.refs_0_), channel_id=1, source_target_pairs={{0,16},{1,17},{2,18},{3,19},{4,20},{5,21},{6,22},{7,23},{8,24},{9,... | collective-permute-start | bytes 331784 | tf_op jit(solution)/shard_map/ppermute | solution.py:55
  20.7 1.2 %collective-permute-start.9 = (bf16[9,8,96]{2,1,0:T(8,128)(2,1)S(1)}, bf16[9,8,96]{2,1,0:T(8,128)(2,1)S(1)}, u32[]{:S(2)}, u32[]{:S(2)}) collective-permute-start(bf16[9,8,96]{2,1,0:T(8,128)(2,1)S(1)} %get-tuple-element.98), channel_id=1, source_target_pairs={{0,16},{1,18},{2,17},{3,20},{4,19},{5,22},{6,21},{7,24},{8,23},{9,... | collective-permute-start | bytes 41480 | tf_op jit(solution)/shard_map/ppermute | solution.py:55
  21.9 1.6 %collective-permute-start.5 = (bf16[32,8,96]{2,1,0:T(8,128)(2,1)S(1)}, bf16[32,8,96]{2,1,0:T(8,128)(2,1)S(1)}, u32[]{:S(2)}, u32[]{:S(2)}) collective-permute-start(bf16[32,8,96]{2,1,0:T(8,128)(2,1)S(1)} %get-tuple-element.95), channel_id=1, source_target_pairs={{0,1},{1,0},{2,3},{3,2},{4,5},{5,4},{6,7},{7,6},{8,9},{9,8},{10,11... | collective-permute-start | bytes 147464 | tf_op jit(solution)/shard_map/ppermute | solution.py:55
  23.4 1.1 %collective-permute-start.6 = (bf16[32,8,96]{2,1,0:T(8,128)(2,1)S(1)}, bf16[32,8,96]{2,1,0:T(8,128)(2,1)S(1)}, u32[]{:S(2)}, u32[]{:S(2)}) collective-permute-start(bf16[32,8,96]{2,1,0:T(8,128)(2,1)S(1)} %get-tuple-element.96), channel_id=1, source_target_pairs={{0,16},{1,2},{2,1},{3,4},{4,3},{5,6},{6,5},{7,8},{8,7},{9,10},{10,... | collective-permute-start | bytes 147464 | tf_op jit(solution)/shard_map/ppermute | solution.py:55
  24.5 2.3 %shard_map.113 = (f32[56,128]{1,0:T(8,128)S(1)}, f32[384,128]{1,0:T(8,128)S(1)}, f32[384,128]{1,0:T(8,128)S(1)}, bf16[16,64,96]{2,1,0:T(8,128)(2,1)}) custom-call(f32[1600,128]{1,0:T(8,128)S(1)} %get-tuple-element.76.x1, f32[1024,128]{1,0:T(8,128)S(1)} %get-tuple-element.77.grad1.refs_0_, bf16[1024,128]{1,0:T(8,128)(2,1)S(1)} %get-tuple-element.78.normed1, ...), custom_call_target="tpu_custom_call" | custom-call | flops 3000000000 | bytes 262144 | tf_op jit(solution)/shard_map/pallas_call | solution.py:816
  26.9 0.8 %collective-permute-done.6.refs_15_ = bf16[32,8,96]{2,1,0:T(8,128)(2,1)S(1)} collective-permute-done((bf16[32,8,96]{2,1,0:T(8,128)(2,1)S(1)}, bf16[32,8,96]{2,1,0:T(8,128)(2,1)S(1)}, u32[]{:S(2)}, u32[]{:S(2)}) %collective-permute-start.6) | collective-permute-done | bytes 49184 | tf_op jit(solution)/shard_map/ppermute | solution.py:55
  27.7 5.7 %shard_map.115 = (f32[1600,128]{1,0:T(8,128)S(1)}, f32[1024,128]{1,0:T(8,128)S(1)}, f32[768,128]{1,0:T(8,128)S(1)}, f32[80,128]{1,0:T(8,128)S(1)}, bf16[848,128]{1,0:T(8,128)(2,1)S(1)}) custom-call(f32[1024,128]{1,0:T(8,128)S(1)} %get-tuple-element.77.grad1.refs_0_, bf16[16,64,96]{2,1,0:T(8,128)(2,1)S(1)} %copy-done.1, ...), custom_call_target="tpu_custom_call" | custom-call | flops 12000000000 | bytes 262144 | tf_op jit(solution)/shard_map/pallas_call | solution.py:816
  33.5 1.4 %collective-permute-done.10.refs_0_ = bf16[848,128]{1,0:T(8,128)(2,1)S(1)} collective-permute-done((bf16[848,128]{1,0:T(8,128)(2,1)S(1)}, bf16[848,128]{1,0:T(8,128)(2,1)S(1)}, u32[]{:S(2)}, u32[]{:S(2)}) %collective-permute-start.10) | collective-permute-done | bytes 217120 | tf_op jit(solution)/shard_map/ppermute | solution.py:953
  35.0 1.8 %collective-permute-start.11 = (bf16[272,128]{1,0:T(8,128)(2,1)S(1)}, bf16[272,128]{1,0:T(8,128)(2,1)S(1)}, u32[]{:S(2)}, u32[]{:S(2)}) collective-permute-start(bf16[272,128]{1,0:T(8,128)(2,1)S(1)} %get-tuple-element.107), channel_id=1, source_target_pairs={{0,2},{1,3},{2,0},{3,1},{4,6},{5,7},{6,4},{7,5},{8,10},{9,11},{10,... | collective-permute-start | bytes 208904 | tf_op jit(solution)/shard_map/ppermute | solution.py:953
  36.8 1.2 %collective-permute-start.12 = (bf16[272,128]{1,0:T(8,128)(2,1)S(1)}, bf16[272,128]{1,0:T(8,128)(2,1)S(1)}, u32[]{:S(2)}, u32[]{:S(2)}) collective-permute-start(bf16[272,128]{1,0:T(8,128)(2,1)S(1)} %get-tuple-element.108), channel_id=1, source_target_pairs={{0,16},{1,17},{2,18},{3,19},{4,20},{5,21},{6,22},{7,23},{8,24},{9,... | collective-permute-start | bytes 208904 | tf_op jit(solution)/shard_map/ppermute | solution.py:953
  38.5 2.1 %shard_map.117 = (bf16[16,64,96]{2,1,0:T(8,128)(2,1)}, f32[8,128]{1,0:T(8,128)S(1)}) custom-call(f32[1600,128]{1,0:T(8,128)S(1)} %get-tuple-element.99.grad0, f32[1024,128]{1,0:T(8,128)S(1)} %get-tuple-element.100.middle, bf16[784,128]{1,0:T(8,128)(2,1)S(1)} %get-tuple-element.64.refs_2_.taps0, f32[80,128]{1,0:T(8,128)S(1)} %get-tuple-element.104.after.small), custom_call_target="tpu_custom_call" | custom-call | flops 3000000000 | bytes 262144 | tf_op jit(solution)/shard_map/pallas_call | solution.py:816
  40.7 1.1 %collective-permute-done.12.refs_1_ = bf16[272,128]{1,0:T(8,128)(2,1)S(1)} collective-permute-done((bf16[272,128]{1,0:T(8,128)(2,1)S(1)}, bf16[272,128]{1,0:T(8,128)(2,1)S(1)}, u32[]{:S(2)}, u32[]{:S(2)}) %collective-permute-start.12) | collective-permute-done | bytes 69664 | tf_op jit(solution)/shard_map/ppermute | solution.py:953
  41.7 1.5 %collective-permute-done.13.refs_2_ = bf16[272,128]{1,0:T(8,128)(2,1)S(1)} collective-permute-done((bf16[272,128]{1,0:T(8,128)(2,1)S(1)}, bf16[272,128]{1,0:T(8,128)(2,1)S(1)}, u32[]{:S(2)}, u32[]{:S(2)}) %collective-permute-start.13) | collective-permute-done | bytes 69664 | tf_op jit(solution)/shard_map/ppermute | solution.py:953
  43.3 2.7 %collective-permute-start.14 = (bf16[128,128]{1,0:T(8,128)(2,1)S(1)}, bf16[128,128]{1,0:T(8,128)(2,1)S(1)}, u32[]{:S(2)}, u32[]{:S(2)}) collective-permute-start(bf16[128,128]{1,0:T(8,128)(2,1)S(1)} %get-tuple-element.113), channel_id=1, source_target_pairs={{0,8},{1,9},{2,10},{3,11},{4,12},{5,13},{6,14},{7,15},{8,0},{9,1},... | collective-permute-start | bytes 98312 | tf_op jit(solution)/shard_map/ppermute | solution.py:953
  46.4 1.4 %collective-permute-start.16 = (bf16[128,128]{1,0:T(8,128)(2,1)S(1)}, bf16[128,128]{1,0:T(8,128)(2,1)S(1)}, u32[]{:S(2)}, u32[]{:S(2)}) collective-permute-start(bf16[128,128]{1,0:T(8,128)(2,1)S(1)} %get-tuple-element.115), channel_id=1, source_target_pairs={{0,12},{1,13},{2,14},{3,15},{4,8},{5,9},{6,10},{7,11},{8,4},{9,5},... | collective-permute-start | bytes 98312 | tf_op jit(solution)/shard_map/ppermute | solution.py:953
  48.3 1.7 %collective-permute-done.15.refs_1_ = bf16[128,128]{1,0:T(8,128)(2,1)S(1)} collective-permute-done((bf16[128,128]{1,0:T(8,128)(2,1)S(1)}, bf16[128,128]{1,0:T(8,128)(2,1)S(1)}, u32[]{:S(2)}, u32[]{:S(2)}) %collective-permute-start.15) | collective-permute-done | bytes 32800 | tf_op jit(solution)/shard_map/ppermute | solution.py:953
  50.0 2.1 %collective-permute-done.16.refs_2_ = bf16[128,128]{1,0:T(8,128)(2,1)S(1)} collective-permute-done((bf16[128,128]{1,0:T(8,128)(2,1)S(1)}, bf16[128,128]{1,0:T(8,128)(2,1)S(1)}, u32[]{:S(2)}, u32[]{:S(2)}) %collective-permute-start.16) | collective-permute-done | bytes 32800 | tf_op jit(solution)/shard_map/ppermute | solution.py:953
  (33 shorter events, 3.5 us)
Async XLA Ops:
  0.6 1.0 %copy-start = (bf16[16,64,96]{2,1,0:T(8,128)(2,1)S(1)}, bf16[16,64,96]{2,1,0:T(8,128)(2,1)}, u32[]{:S(2)}) copy-start(bf16[16,64,96]{2,1,0:T(8,128)(2,1)} %image_in.1) | copy-start | bytes 589828
  1.6 9.3 %collective-permute-start.2 = (bf16[6,64,96]{2,1,0:T(8,128)(2,1)S(1)}, bf16[6,64,96]{2,1,0:T(8,128)(2,1)S(1)}, u32[]{:S(2)}, u32[]{:S(2)}) collective-permute-start(bf16[6,64,96]{2,1,0:T(8,128)(2,1)S(1)} %get-tuple-element.71.refs_0_), channel_id=1, source_target_pairs={{0,16},{1,17},{2,18},{3,19},{4,20},{5,21},{6,22},{7,23},{8,24},{9,... | collective-permute-start | bytes 221192 | tf_op jit(solution)/shard_map/ppermute | solution.py:55
  4.7 3.3 %copy-start.2 = (bf16[2,96,384]{2,1,0:T(8,128)(2,1)S(1)}, bf16[2,96,384]{2,1,0:T(8,128)(2,1)}, u32[]{:S(2)}) copy-start(bf16[2,96,384]{2,1,0:T(8,128)(2,1)} %up_in.1) | copy-start | bytes 442372
  4.7 3.3 %copy-start.3 = (bf16[2,384,96]{1,2,0:T(8,128)(2,1)S(1)}, bf16[2,384,96]{1,2,0:T(8,128)(2,1)}, u32[]{:S(2)}) copy-start(bf16[2,384,96]{1,2,0:T(8,128)(2,1)} %param.10) | copy-start | bytes 442372
  4.7 3.3 %copy-start.4 = (f32[2,7,7,96]{3,0,2,1:T(2,128)S(1)}, f32[2,7,7,96]{3,0,2,1:T(2,128)}, u32[]{:S(2)}) copy-start(f32[2,7,7,96]{3,0,2,1:T(2,128)} %param.7) | copy-start | bytes 112900
  4.7 3.3 %copy-start.5 = (f32[2,96]{1,0:T(2,128)S(1)}, f32[2,96]{1,0:T(2,128)}, u32[]{:S(2)}) copy-start(f32[2,96]{1,0:T(2,128)} %gains_in.1) | copy-start | bytes 2308
  4.7 4.0 %collective-permute-start.3 = (bf16[6,8,96]{2,1,0:T(8,128)(2,1)S(1)}, bf16[6,8,96]{2,1,0:T(8,128)(2,1)S(1)}, u32[]{:S(2)}, u32[]{:S(2)}) collective-permute-start(bf16[6,8,96]{2,1,0:T(8,128)(2,1)S(1)} %get-tuple-element.74), channel_id=1, source_target_pairs={{0,17},{1,16},{2,19},{3,18},{4,21},{5,20},{6,23},{7,22},{8,25},{9,... | collective-permute-start | bytes 27656 | tf_op jit(solution)/shard_map/ppermute | solution.py:55
  4.8 4.0 %collective-permute-start.4 = (bf16[6,8,96]{2,1,0:T(8,128)(2,1)S(1)}, bf16[6,8,96]{2,1,0:T(8,128)(2,1)S(1)}, u32[]{:S(2)}, u32[]{:S(2)}) collective-permute-start(bf16[6,8,96]{2,1,0:T(8,128)(2,1)S(1)} %get-tuple-element.75), channel_id=1, source_target_pairs={{0,16},{1,18},{2,17},{3,20},{4,19},{5,22},{6,21},{7,24},{8,23},{9,... | collective-permute-start | bytes 27656 | tf_op jit(solution)/shard_map/ppermute | solution.py:55
  6.0 2.8 %collective-permute-start = (bf16[16,8,96]{2,1,0:T(8,128)(2,1)S(1)}, bf16[16,8,96]{2,1,0:T(8,128)(2,1)S(1)}, u32[]{:S(2)}, u32[]{:S(2)}) collective-permute-start(bf16[16,8,96]{2,1,0:T(8,128)(2,1)S(1)} %get-tuple-element.72), channel_id=1, source_target_pairs={{0,1},{1,0},{2,3},{3,2},{4,5},{5,4},{6,7},{7,6},{8,9},{9,8},{10,11... | collective-permute-start | bytes 73736 | tf_op jit(solution)/shard_map/ppermute | solution.py:55
  7.0 3.9 %collective-permute-start.1 = (bf16[16,8,96]{2,1,0:T(8,128)(2,1)S(1)}, bf16[16,8,96]{2,1,0:T(8,128)(2,1)S(1)}, u32[]{:S(2)}, u32[]{:S(2)}) collective-permute-start(bf16[16,8,96]{2,1,0:T(8,128)(2,1)S(1)} %get-tuple-element.73), channel_id=1, source_target_pairs={{0,16},{1,2},{2,1},{3,4},{4,3},{5,6},{6,5},{7,8},{8,7},{9,10},{10,... | collective-permute-start | bytes 73736 | tf_op jit(solution)/shard_map/ppermute | solution.py:55
  8.0 3.0 %copy-start.1 = (bf16[16,64,96]{2,1,0:T(8,128)(2,1)S(1)}, bf16[16,64,96]{2,1,0:T(8,128)(2,1)}, u32[]{:S(2)}) copy-start(bf16[16,64,96]{2,1,0:T(8,128)(2,1)} %refs_1_.3) | copy-start | bytes 589828
  19.6 8.1 %collective-permute-start.7 = (bf16[9,64,96]{2,1,0:T(8,128)(2,1)S(1)}, bf16[9,64,96]{2,1,0:T(8,128)(2,1)S(1)}, u32[]{:S(2)}, u32[]{:S(2)}) collective-permute-start(bf16[9,64,96]{2,1,0:T(8,128)(2,1)S(1)} %get-tuple-element.94.refs_0_), channel_id=1, source_target_pairs={{0,16},{1,17},{2,18},{3,19},{4,20},{5,21},{6,22},{7,23},{8,24},{9,... | collective-permute-start | bytes 331784 | tf_op jit(solution)/shard_map/ppermute | solution.py:55
  20.6 6.2 %collective-permute-start.8 = (bf16[9,8,96]{2,1,0:T(8,128)(2,1)S(1)}, bf16[9,8,96]{2,1,0:T(8,128)(2,1)S(1)}, u32[]{:S(2)}, u32[]{:S(2)}) collective-permute-start(bf16[9,8,96]{2,1,0:T(8,128)(2,1)S(1)} %get-tuple-element.97), channel_id=1, source_target_pairs={{0,17},{1,16},{2,19},{3,18},{4,21},{5,20},{6,23},{7,22},{8,25},{9,... | collective-permute-start | bytes 41480 | tf_op jit(solution)/shard_map/ppermute | solution.py:55
  20.7 6.1 %collective-permute-start.9 = (bf16[9,8,96]{2,1,0:T(8,128)(2,1)S(1)}, bf16[9,8,96]{2,1,0:T(8,128)(2,1)S(1)}, u32[]{:S(2)}, u32[]{:S(2)}) collective-permute-start(bf16[9,8,96]{2,1,0:T(8,128)(2,1)S(1)} %get-tuple-element.98), channel_id=1, source_target_pairs={{0,16},{1,18},{2,17},{3,20},{4,19},{5,22},{6,21},{7,24},{8,23},{9,... | collective-permute-start | bytes 41480 | tf_op jit(solution)/shard_map/ppermute | solution.py:55
  21.9 5.0 %collective-permute-start.5 = (bf16[32,8,96]{2,1,0:T(8,128)(2,1)S(1)}, bf16[32,8,96]{2,1,0:T(8,128)(2,1)S(1)}, u32[]{:S(2)}, u32[]{:S(2)}) collective-permute-start(bf16[32,8,96]{2,1,0:T(8,128)(2,1)S(1)} %get-tuple-element.95), channel_id=1, source_target_pairs={{0,1},{1,0},{2,3},{3,2},{4,5},{5,4},{6,7},{7,6},{8,9},{9,8},{10,11... | collective-permute-start | bytes 147464 | tf_op jit(solution)/shard_map/ppermute | solution.py:55
  23.4 4.3 %collective-permute-start.6 = (bf16[32,8,96]{2,1,0:T(8,128)(2,1)S(1)}, bf16[32,8,96]{2,1,0:T(8,128)(2,1)S(1)}, u32[]{:S(2)}, u32[]{:S(2)}) collective-permute-start(bf16[32,8,96]{2,1,0:T(8,128)(2,1)S(1)} %get-tuple-element.96), channel_id=1, source_target_pairs={{0,16},{1,2},{2,1},{3,4},{4,3},{5,6},{6,5},{7,8},{8,7},{9,10},{10,... | collective-permute-start | bytes 147464 | tf_op jit(solution)/shard_map/ppermute | solution.py:55
  33.4 1.5 %collective-permute-start.10 = (bf16[848,128]{1,0:T(8,128)(2,1)S(1)}, bf16[848,128]{1,0:T(8,128)(2,1)S(1)}, u32[]{:S(2)}, u32[]{:S(2)}) collective-permute-start(bf16[848,128]{1,0:T(8,128)(2,1)S(1)} %get-tuple-element.103), channel_id=1, source_target_pairs={{0,1},{1,0},{2,3},{3,2},{4,5},{5,4},{6,7},{7,6},{8,9},{9,8},{10,11... | collective-permute-start | bytes 651272 | tf_op jit(solution)/shard_map/ppermute | solution.py:953
  35.0 5.7 %collective-permute-start.11 = (bf16[272,128]{1,0:T(8,128)(2,1)S(1)}, bf16[272,128]{1,0:T(8,128)(2,1)S(1)}, u32[]{:S(2)}, u32[]{:S(2)}) collective-permute-start(bf16[272,128]{1,0:T(8,128)(2,1)S(1)} %get-tuple-element.107), channel_id=1, source_target_pairs={{0,2},{1,3},{2,0},{3,1},{4,6},{5,7},{6,4},{7,5},{8,10},{9,11},{10,... | collective-permute-start | bytes 208904 | tf_op jit(solution)/shard_map/ppermute | solution.py:953
  36.8 4.9 %collective-permute-start.12 = (bf16[272,128]{1,0:T(8,128)(2,1)S(1)}, bf16[272,128]{1,0:T(8,128)(2,1)S(1)}, u32[]{:S(2)}, u32[]{:S(2)}) collective-permute-start(bf16[272,128]{1,0:T(8,128)(2,1)S(1)} %get-tuple-element.108), channel_id=1, source_target_pairs={{0,16},{1,17},{2,18},{3,19},{4,20},{5,21},{6,22},{7,23},{8,24},{9,... | collective-permute-start | bytes 208904 | tf_op jit(solution)/shard_map/ppermute | solution.py:953
  38.0 5.2 %collective-permute-start.13 = (bf16[272,128]{1,0:T(8,128)(2,1)S(1)}, bf16[272,128]{1,0:T(8,128)(2,1)S(1)}, u32[]{:S(2)}, u32[]{:S(2)}) collective-permute-start(bf16[272,128]{1,0:T(8,128)(2,1)S(1)} %get-tuple-element.109), channel_id=1, source_target_pairs={{0,18},{1,19},{2,16},{3,17},{4,22},{5,23},{6,20},{7,21},{8,26},{9,... | collective-permute-start | bytes 208904 | tf_op jit(solution)/shard_map/ppermute | solution.py:953
  43.3 5.0 %collective-permute-start.14 = (bf16[128,128]{1,0:T(8,128)(2,1)S(1)}, bf16[128,128]{1,0:T(8,128)(2,1)S(1)}, u32[]{:S(2)}, u32[]{:S(2)}) collective-permute-start(bf16[128,128]{1,0:T(8,128)(2,1)S(1)} %get-tuple-element.113), channel_id=1, source_target_pairs={{0,8},{1,9},{2,10},{3,11},{4,12},{5,13},{6,14},{7,15},{8,0},{9,1},... | collective-permute-start | bytes 98312 | tf_op jit(solution)/shard_map/ppermute | solution.py:953
  46.0 4.0 %collective-permute-start.15 = (bf16[128,128]{1,0:T(8,128)(2,1)S(1)}, bf16[128,128]{1,0:T(8,128)(2,1)S(1)}, u32[]{:S(2)}, u32[]{:S(2)}) collective-permute-start(bf16[128,128]{1,0:T(8,128)(2,1)S(1)} %get-tuple-element.114), channel_id=1, source_target_pairs={{0,4},{1,5},{2,6},{3,7},{4,0},{5,1},{6,2},{7,3},{8,12},{9,13},{10,... | collective-permute-start | bytes 98312 | tf_op jit(solution)/shard_map/ppermute | solution.py:953
  46.4 5.7 %collective-permute-start.16 = (bf16[128,128]{1,0:T(8,128)(2,1)S(1)}, bf16[128,128]{1,0:T(8,128)(2,1)S(1)}, u32[]{:S(2)}, u32[]{:S(2)}) collective-permute-start(bf16[128,128]{1,0:T(8,128)(2,1)S(1)} %get-tuple-element.115), channel_id=1, source_target_pairs={{0,12},{1,13},{2,14},{3,15},{4,8},{5,9},{6,10},{7,11},{8,4},{9,5},... | collective-permute-start | bytes 98312 | tf_op jit(solution)/shard_map/ppermute | solution.py:953

commit v12 on v11

--- a/solution.py
+++ b/solution.py
@@ -182,17 +182,25 @@
 
 def conv_group(src, base, stride, rows_out, taps, size, flipped=False):
     total = [None] * rows_out
-    for b in range(size):
-        order = [a * size + b for a in range(size)]
-        if flipped:
-            order = [size * size - 1 - t for t in order]
-        weights = [taps[t * 16 : t * 16 + 16, :] for t in order]
-        window = []
+    for first in range(0, size, 2):
+        columns = range(first, min(first + 2, size))
+        weights = []
+        for b in columns:
+            order = [a * size + b for a in range(size)]
+            if flipped:
+                order = [size * size - 1 - t for t in order]
+            weights.append([taps[t * 16 : t * 16 + 16, :] for t in order])
+        windows = [[] for _ in columns]
         for i in range(rows_out + size - 1):
-            window.append(src[pl.ds(base + i * stride + b, 16), :].astype(bf16))
+            for window, b in zip(windows, columns):
+                window.append(src[pl.ds(base + i * stride + b, 16), :].astype(bf16))
             r = i - size + 1
             if r >= 0:
-                term = tree_sum([window[r + a] * weights[a] for a in range(size)]).astype(f32)
+                sums = [
+                    tree_sum([window[r + a] * weight[a] for a in range(size)])
+                    for window, weight in zip(windows, weights)
+                ]
+                term = tree_sum(sums).astype(f32)
                 total[r] = term if total[r] is None else total[r] + term
     return total
 
@@ -203,9 +211,7 @@
 
 def kernel_sums(src, src_base, src_stride, grad, grad_base, grad_stride, rows, cols, size, sums):
     sums[...] = jnp.zeros(sums.shape, f32)
-
-    def group(g, carry):
-        at = pl.multiple_of(g * 16, 16)
+    for at in range(0, cols, 16):
         grads = [grad[pl.ds(grad_base + i * grad_stride + at, 16), :].astype(bf16) for i in range(rows)]
         for b in range(size):
             lines = [
@@ -215,9 +221,14 @@
                 term = tree_sum([lines[r + a] * grads[r] for r in range(rows)]).astype(f32)
                 t = (a * size + b) * 8
                 sums[t : t + 8, :] += term[0:8] + term[8:16]
-        return carry
-
-    lax.fori_loop(0, cols // 16, group, 0)
+            yield
+
+
+def weight_sum(left, right, total, size):
+    for start, n in pieces(left.shape[0], size):
+        term = dot_leading(left[start : start + n, :], right[start : start + n, :])
+        yield
+        total[...] = term if start == 0 else total[...] + term
 
 
 def diagonal(first, second):
@@ -519,7 +530,7 @@
     dims, x1, grad1, normed1, pre_grad1, hidden1, cot, gain_part, final, taps_sum, up_sum, down_sum, output, sums
 ):
     output[...] = final[...]
-    kernel_sums(x1, 1, dims.ext_cols, grad1, 0, dims.cols, dims.rows, dims.cols, dims.size, sums)
+    together([kernel_sums(x1, 1, dims.ext_cols, grad1, 0, dims.cols, dims.rows, dims.cols, dims.size, sums)])
     store_sums(dims, sums, gain_part[...], taps_sum)
     upstream = pad_lanes(cot[...].reshape(dims.rows * dims.cols, dims.channels))
     up_sum[...] = dot_leading(normed1[...], pre_grad1[...]).T
@@ -540,7 +551,7 @@
     (taps_sum1, up_sum1, down_sum1) = refs[11:14]
     strips = refs[14 : 14 + count]
     (grad0, middle, keep, small_keep, send) = refs[14 + count : 19 + count]
-    (wide_grad, cot_frame, upstream, own, sums, normed0, flow0, pre_grad0, gain_sum, small, tall, slabs) = refs[19 + count :]
+    (wide_grad, cot_frame, upstream, own, sums, normed0, flow0, pre_grad0, up_acc, down_acc, gain_sum, small, tall, slabs) = refs[19 + count :]
     place = Place(dims.row_count, dims.col_count)
     rows, cols, channels, h, size = (dims.rows, dims.cols, dims.channels, dims.h, dims.size)
     ext_rows, ext_cols, wide = (dims.ext_rows, dims.ext_cols, dims.wide)
@@ -619,8 +630,13 @@
 
     together([mix0(start, n) for start, n in pieces(half_px, dims.piece)])
     clear_outside(place, grad0, dims)
-    kernel_sums(
-        x0, h * wide + SIDE - h, wide, grad0, h * ext_cols + margin, ext_cols, rows, cols, size, sums
+    at_x0, at_grad0 = (h * wide + SIDE - h, h * ext_cols + margin)
+    together(
+        [
+            weight_sum(normed0, pre_grad0, up_acc, 2 * dims.piece),
+            kernel_sums(x0, at_x0, wide, grad0, at_grad0, ext_cols, rows, cols, size, sums),
+            weight_sum(flow0, hidden0, down_acc, 2 * dims.piece),
+        ]
     )
     store_sums(dims, sums, gain_sum[...], small)
 
@@ -631,8 +647,8 @@
 
     layer_rows, part, half = (dims.layer_rows, dims.part, dims.half)
     units = hidden0.shape[1]
-    up0 = dot_leading(normed0[...], pre_grad0[...]).T * dims.factor
-    down0 = dot_leading(flow0[...], hidden0[...]).T * dims.factor
+    up0 = up_acc[...].T * dims.factor
+    down0 = down_acc[...].T * dims.factor
     up1 = up_sum1[...] * dims.factor
     down1 = down_sum1[...] * dims.factor
     lane = lax.broadcasted_iota(jnp.int32, (units, LANES), 1)
@@ -925,6 +941,8 @@
             ((ext, LANES), bf16),
             ((ext, LANES), bf16),
             ((ext, units), bf16),
+            ((LANES, units), f32),
+            ((LANES, units), f32),
             ((8, LANES), f32),
             ((sums_rows, LANES), f32),
             ((2 * (units + 8), LANES), f32),
@@ -950,7 +968,9 @@
     axes = ("row", "col")
     sends = [send]
     for stage, group in enumerate(d.groups):
-        gots = [lax.ppermute(x, axes, swap_by(d, group, mask)) for mask, x in enumerate(sends, 1)]
+        order = sorted(range(1, len(sends) + 1), key=lambda mask: (3, 1, 2).index(mask))
+        gots = {mask: lax.ppermute(sends[mask - 1], axes, swap_by(d, group, mask)) for mask in order}
+        gots = [gots[mask] for mask in sorted(gots)]
         ready = []
         if stage == 1:
             gradient, *ready = run(

time: 53 us -> 53.2 us (level)
  no operation moved by 1% of the time
where the time goes in v12:
time: 53.2 us; the launch traced here: 53.1 us
  Pallas kernels  20.7 us (39%)
  starting transfers between devices  19.3 us (36%)
  waiting for transfers between devices  11.4 us (21%)
  local copies, waits for them, and re-layouts  0.96 us (2%)
  between operations  0.76 us (1%)
    pallas_call x11, Pallas kernels, run(): pl.pallas_call(kernel, out_shape=shapes, in_specs=[far] * in_hbm + [space...  20.7 us
    ppermute x10, starting transfers between devices, exchange(): lax.ppermute(strip, ('row', 'col'), swap_pairs(row_count, col_count, rs,...  11.1 us
    ppermute x7, waiting for transfers between devices, per_device(): lax.ppermute(sends[mask - 1], axes, swap_by(d, group, mask))  8.33 us
    ppermute x7, starting transfers between devices, per_device(): lax.ppermute(sends[mask - 1], axes, swap_by(d, group, mask))  8.17 us
    ppermute x10, waiting for transfers between devices, exchange(): lax.ppermute(strip, ('row', 'col'), swap_pairs(row_count, col_count, rs,...  3.05 us
  transfers between devices with their start and end apart: 17, of which 8 were waited for; matrix products, arithmetic and copies ran while one was open for 0% of the time, Pallas kernels for 10%

profile of v12, /device:TPU:0, one launch (start us, length us, event | category | flops | bytes accessed | tf_op | source)
XLA Modules:
  0.0 53.1 jit_solution(4153844076707523258)
XLA Ops:
  0.6 0.9 %copy-done = bf16[16,64,96]{2,1,0:T(8,128)(2,1)S(1)} copy-done((bf16[16,64,96]{2,1,0:T(8,128)(2,1)S(1)}, bf16[16,64,96]{2,1,0:T(8,128)(2,1)}, u32[]{:S(2)}) %copy-start) | copy-done | bytes 196632
  1.6 3.0 %collective-permute-start.2 = (bf16[6,64,96]{2,1,0:T(8,128)(2,1)S(1)}, bf16[6,64,96]{2,1,0:T(8,128)(2,1)S(1)}, u32[]{:S(2)}, u32[]{:S(2)}) collective-permute-start(bf16[6,64,96]{2,1,0:T(8,128)(2,1)S(1)} %get-tuple-element.71.refs_0_), channel_id=1, source_target_pairs={{0,16},{1,17},{2,18},{3,19},{4,20},{5,21},{6,22},{7,23},{8,24},{9,... | collective-permute-start | bytes 221192 | tf_op jit(solution)/shard_map/ppermute | solution.py:55
  4.8 1.2 %collective-permute-start.4 = (bf16[6,8,96]{2,1,0:T(8,128)(2,1)S(1)}, bf16[6,8,96]{2,1,0:T(8,128)(2,1)S(1)}, u32[]{:S(2)}, u32[]{:S(2)}) collective-permute-start(bf16[6,8,96]{2,1,0:T(8,128)(2,1)S(1)} %get-tuple-element.75), channel_id=1, source_target_pairs={{0,16},{1,18},{2,17},{3,20},{4,19},{5,22},{6,21},{7,24},{8,23},{9,... | collective-permute-start | bytes 27656 | tf_op jit(solution)/shard_map/ppermute | solution.py:55
  6.0 1.1 %collective-permute-start = (bf16[16,8,96]{2,1,0:T(8,128)(2,1)S(1)}, bf16[16,8,96]{2,1,0:T(8,128)(2,1)S(1)}, u32[]{:S(2)}, u32[]{:S(2)}) collective-permute-start(bf16[16,8,96]{2,1,0:T(8,128)(2,1)S(1)} %get-tuple-element.72), channel_id=1, source_target_pairs={{0,1},{1,0},{2,3},{3,2},{4,5},{5,4},{6,7},{7,6},{8,9},{9,8},{10,11... | collective-permute-start | bytes 73736 | tf_op jit(solution)/shard_map/ppermute | solution.py:55
  7.0 0.9 %collective-permute-start.1 = (bf16[16,8,96]{2,1,0:T(8,128)(2,1)S(1)}, bf16[16,8,96]{2,1,0:T(8,128)(2,1)S(1)}, u32[]{:S(2)}, u32[]{:S(2)}) collective-permute-start(bf16[16,8,96]{2,1,0:T(8,128)(2,1)S(1)} %get-tuple-element.73), channel_id=1, source_target_pairs={{0,16},{1,2},{2,1},{3,4},{4,3},{5,6},{6,5},{7,8},{8,7},{9,10},{10,... | collective-permute-start | bytes 73736 | tf_op jit(solution)/shard_map/ppermute | solution.py:55
  8.8 2.2 %collective-permute-done.1.refs_10_ = bf16[16,8,96]{2,1,0:T(8,128)(2,1)S(1)} collective-permute-done((bf16[16,8,96]{2,1,0:T(8,128)(2,1)S(1)}, bf16[16,8,96]{2,1,0:T(8,128)(2,1)S(1)}, u32[]{:S(2)}, u32[]{:S(2)}) %collective-permute-start.1) | collective-permute-done | bytes 24608 | tf_op jit(solution)/shard_map/ppermute | solution.py:55
  10.9 8.5 %shard_map.112 = (bf16[16,64,96]{2,1,0:T(8,128)(2,1)S(1)}, f32[2240,128]{1,0:T(8,128)S(1)}, f32[1600,128]{1,0:T(8,128)S(1)}, bf16[1376,128]{1,0:T(8,128)(2,1)S(1...) custom-call(bf16[16,64,96]{2,1,0:T(8,128)(2,1)S(1)} %get-tuple-eleme, ...), custom_call_target="tpu_custom_call" | custom-call | flops 15000000512 | bytes 262144 | tf_op jit(solution)/shard_map/pallas_call | solution.py:832
  19.4 1.0 %collective-permute-start.7 = (bf16[9,64,96]{2,1,0:T(8,128)(2,1)S(1)}, bf16[9,64,96]{2,1,0:T(8,128)(2,1)S(1)}, u32[]{:S(2)}, u32[]{:S(2)}) collective-permute-start(bf16[9,64,96]{2,1,0:T(8,128)(2,1)S(1)} %get-tuple-element.94.refs_0_), channel_id=1, source_target_pairs={{0,16},{1,17},{2,18},{3,19},{4,20},{5,21},{6,22},{7,23},{8,24},{9,... | collective-permute-start | bytes 331784 | tf_op jit(solution)/shard_map/ppermute | solution.py:55
  20.6 1.2 %collective-permute-start.9 = (bf16[9,8,96]{2,1,0:T(8,128)(2,1)S(1)}, bf16[9,8,96]{2,1,0:T(8,128)(2,1)S(1)}, u32[]{:S(2)}, u32[]{:S(2)}) collective-permute-start(bf16[9,8,96]{2,1,0:T(8,128)(2,1)S(1)} %get-tuple-element.98), channel_id=1, source_target_pairs={{0,16},{1,18},{2,17},{3,20},{4,19},{5,22},{6,21},{7,24},{8,23},{9,... | collective-permute-start | bytes 41480 | tf_op jit(solution)/shard_map/ppermute | solution.py:55
  21.7 1.6 %collective-permute-start.5 = (bf16[32,8,96]{2,1,0:T(8,128)(2,1)S(1)}, bf16[32,8,96]{2,1,0:T(8,128)(2,1)S(1)}, u32[]{:S(2)}, u32[]{:S(2)}) collective-permute-start(bf16[32,8,96]{2,1,0:T(8,128)(2,1)S(1)} %get-tuple-element.95), channel_id=1, source_target_pairs={{0,1},{1,0},{2,3},{3,2},{4,5},{5,4},{6,7},{7,6},{8,9},{9,8},{10,11... | collective-permute-start | bytes 147464 | tf_op jit(solution)/shard_map/ppermute | solution.py:55
  23.3 1.1 %collective-permute-start.6 = (bf16[32,8,96]{2,1,0:T(8,128)(2,1)S(1)}, bf16[32,8,96]{2,1,0:T(8,128)(2,1)S(1)}, u32[]{:S(2)}, u32[]{:S(2)}) collective-permute-start(bf16[32,8,96]{2,1,0:T(8,128)(2,1)S(1)} %get-tuple-element.96), channel_id=1, source_target_pairs={{0,16},{1,2},{2,1},{3,4},{4,3},{5,6},{6,5},{7,8},{8,7},{9,10},{10,... | collective-permute-start | bytes 147464 | tf_op jit(solution)/shard_map/ppermute | solution.py:55
  24.4 2.3 %shard_map.113 = (f32[56,128]{1,0:T(8,128)S(1)}, f32[384,128]{1,0:T(8,128)S(1)}, f32[384,128]{1,0:T(8,128)S(1)}, bf16[16,64,96]{2,1,0:T(8,128)(2,1)}) custom-call(f32[1600,128]{1,0:T(8,128)S(1)} %get-tuple-element.76.x1, f32[1024,128]{1,0:T(8,128)S(1)} %get-tuple-element.77.grad1.refs_0_, bf16[1024,128]{1,0:T(8,128)(2,1)S(1)} %get-tuple-element.78.normed1, ...), custom_call_target="tpu_custom_call" | custom-call | flops 3000000000 | bytes 262144 | tf_op jit(solution)/shard_map/pallas_call | solution.py:832
  26.7 0.8 %collective-permute-done.6.refs_15_ = bf16[32,8,96]{2,1,0:T(8,128)(2,1)S(1)} collective-permute-done((bf16[32,8,96]{2,1,0:T(8,128)(2,1)S(1)}, bf16[32,8,96]{2,1,0:T(8,128)(2,1)S(1)}, u32[]{:S(2)}, u32[]{:S(2)}) %collective-permute-start.6) | collective-permute-done | bytes 49184 | tf_op jit(solution)/shard_map/ppermute | solution.py:55
  27.5 6.0 %shard_map.115 = (f32[1600,128]{1,0:T(8,128)S(1)}, f32[1024,128]{1,0:T(8,128)S(1)}, f32[768,128]{1,0:T(8,128)S(1)}, f32[80,128]{1,0:T(8,128)S(1)}, bf16[848,128]{1,0:T(8,128)(2,1)S(1)}) custom-call(f32[1024,128]{1,0:T(8,128)S(1)} %get-tuple-element.77.grad1.refs_0_, bf16[16,64,96]{2,1,0:T(8,128)(2,1)S(1)} %copy-done.1, ...), custom_call_target="tpu_custom_call" | custom-call | flops 12000000000 | bytes 262144 | tf_op jit(solution)/shard_map/pallas_call | solution.py:832
  33.8 1.4 %collective-permute-done.10.refs_0_ = bf16[848,128]{1,0:T(8,128)(2,1)S(1)} collective-permute-done((bf16[848,128]{1,0:T(8,128)(2,1)S(1)}, bf16[848,128]{1,0:T(8,128)(2,1)S(1)}, u32[]{:S(2)}, u32[]{:S(2)}) %collective-permute-start.10) | collective-permute-done | bytes 217120 | tf_op jit(solution)/shard_map/ppermute | solution.py:972
  35.2 1.9 %collective-permute-start.11 = (bf16[272,128]{1,0:T(8,128)(2,1)S(1)}, bf16[272,128]{1,0:T(8,128)(2,1)S(1)}, u32[]{:S(2)}, u32[]{:S(2)}) collective-permute-start(bf16[272,128]{1,0:T(8,128)(2,1)S(1)} %get-tuple-element.107), channel_id=1, source_target_pairs={{0,2},{1,3},{2,0},{3,1},{4,6},{5,7},{6,4},{7,5},{8,10},{9,11},{10,... | collective-permute-start | bytes 208904 | tf_op jit(solution)/shard_map/ppermute | solution.py:972
  37.1 1.2 %collective-permute-start.12 = (bf16[272,128]{1,0:T(8,128)(2,1)S(1)}, bf16[272,128]{1,0:T(8,128)(2,1)S(1)}, u32[]{:S(2)}, u32[]{:S(2)}) collective-permute-start(bf16[272,128]{1,0:T(8,128)(2,1)S(1)} %get-tuple-element.108), channel_id=1, source_target_pairs={{0,16},{1,17},{2,18},{3,19},{4,20},{5,21},{6,22},{7,23},{8,24},{9,... | collective-permute-start | bytes 208904 | tf_op jit(solution)/shard_map/ppermute | solution.py:972
  38.8 2.1 %shard_map.117 = (bf16[16,64,96]{2,1,0:T(8,128)(2,1)}, f32[8,128]{1,0:T(8,128)S(1)}) custom-call(f32[1600,128]{1,0:T(8,128)S(1)} %get-tuple-element.99.grad0, f32[1024,128]{1,0:T(8,128)S(1)} %get-tuple-element.100.middle, bf16[784,128]{1,0:T(8,128)(2,1)S(1)} %get-tuple-element.64.refs_2_.taps0, f32[80,128]{1,0:T(8,128)S(1)} %get-tuple-element.104.after.small), custom_call_target="tpu_custom_call" | custom-call | flops 3000000000 | bytes 262144 | tf_op jit(solution)/shard_map/pallas_call | solution.py:832
  40.9 1.1 %collective-permute-done.12.refs_1_ = bf16[272,128]{1,0:T(8,128)(2,1)S(1)} collective-permute-done((bf16[272,128]{1,0:T(8,128)(2,1)S(1)}, bf16[272,128]{1,0:T(8,128)(2,1)S(1)}, u32[]{:S(2)}, u32[]{:S(2)}) %collective-permute-start.12) | collective-permute-done | bytes 69664 | tf_op jit(solution)/shard_map/ppermute | solution.py:972
  42.0 1.5 %collective-permute-done.13.refs_2_ = bf16[272,128]{1,0:T(8,128)(2,1)S(1)} collective-permute-done((bf16[272,128]{1,0:T(8,128)(2,1)S(1)}, bf16[272,128]{1,0:T(8,128)(2,1)S(1)}, u32[]{:S(2)}, u32[]{:S(2)}) %collective-permute-start.13) | collective-permute-done | bytes 69664 | tf_op jit(solution)/shard_map/ppermute | solution.py:972
  43.6 2.7 %collective-permute-start.14 = (bf16[128,128]{1,0:T(8,128)(2,1)S(1)}, bf16[128,128]{1,0:T(8,128)(2,1)S(1)}, u32[]{:S(2)}, u32[]{:S(2)}) collective-permute-start(bf16[128,128]{1,0:T(8,128)(2,1)S(1)} %get-tuple-element.113), channel_id=1, source_target_pairs={{0,8},{1,9},{2,10},{3,11},{4,12},{5,13},{6,14},{7,15},{8,0},{9,1},... | collective-permute-start | bytes 98312 | tf_op jit(solution)/shard_map/ppermute | solution.py:972
  46.6 1.4 %collective-permute-start.16 = (bf16[128,128]{1,0:T(8,128)(2,1)S(1)}, bf16[128,128]{1,0:T(8,128)(2,1)S(1)}, u32[]{:S(2)}, u32[]{:S(2)}) collective-permute-start(bf16[128,128]{1,0:T(8,128)(2,1)S(1)} %get-tuple-element.115), channel_id=1, source_target_pairs={{0,12},{1,13},{2,14},{3,15},{4,8},{5,9},{6,10},{7,11},{8,4},{9,5},... | collective-permute-start | bytes 98312 | tf_op jit(solution)/shard_map/ppermute | solution.py:972
  48.5 1.7 %collective-permute-done.15.refs_1_ = bf16[128,128]{1,0:T(8,128)(2,1)S(1)} collective-permute-done((bf16[128,128]{1,0:T(8,128)(2,1)S(1)}, bf16[128,128]{1,0:T(8,128)(2,1)S(1)}, u32[]{:S(2)}, u32[]{:S(2)}) %collective-permute-start.15) | collective-permute-done | bytes 32800 | tf_op jit(solution)/shard_map/ppermute | solution.py:972
  50.2 2.1 %collective-permute-done.16.refs_2_ = bf16[128,128]{1,0:T(8,128)(2,1)S(1)} collective-permute-done((bf16[128,128]{1,0:T(8,128)(2,1)S(1)}, bf16[128,128]{1,0:T(8,128)(2,1)S(1)}, u32[]{:S(2)}, u32[]{:S(2)}) %collective-permute-start.16) | collective-permute-done | bytes 32800 | tf_op jit(solution)/shard_map/ppermute | solution.py:972
  (33 shorter events, 3.5 us)
Async XLA Ops:
  0.6 1.0 %copy-start = (bf16[16,64,96]{2,1,0:T(8,128)(2,1)S(1)}, bf16[16,64,96]{2,1,0:T(8,128)(2,1)}, u32[]{:S(2)}) copy-start(bf16[16,64,96]{2,1,0:T(8,128)(2,1)} %image_in.1) | copy-start | bytes 589828
  1.6 9.3 %collective-permute-start.2 = (bf16[6,64,96]{2,1,0:T(8,128)(2,1)S(1)}, bf16[6,64,96]{2,1,0:T(8,128)(2,1)S(1)}, u32[]{:S(2)}, u32[]{:S(2)}) collective-permute-start(bf16[6,64,96]{2,1,0:T(8,128)(2,1)S(1)} %get-tuple-element.71.refs_0_), channel_id=1, source_target_pairs={{0,16},{1,17},{2,18},{3,19},{4,20},{5,21},{6,22},{7,23},{8,24},{9,... | collective-permute-start | bytes 221192 | tf_op jit(solution)/shard_map/ppermute | solution.py:55
  4.7 3.3 %copy-start.2 = (bf16[2,96,384]{2,1,0:T(8,128)(2,1)S(1)}, bf16[2,96,384]{2,1,0:T(8,128)(2,1)}, u32[]{:S(2)}) copy-start(bf16[2,96,384]{2,1,0:T(8,128)(2,1)} %up_in.1) | copy-start | bytes 442372
  4.7 3.3 %copy-start.3 = (bf16[2,384,96]{1,2,0:T(8,128)(2,1)S(1)}, bf16[2,384,96]{1,2,0:T(8,128)(2,1)}, u32[]{:S(2)}) copy-start(bf16[2,384,96]{1,2,0:T(8,128)(2,1)} %param.10) | copy-start | bytes 442372
  4.7 3.3 %copy-start.4 = (f32[2,7,7,96]{3,0,2,1:T(2,128)S(1)}, f32[2,7,7,96]{3,0,2,1:T(2,128)}, u32[]{:S(2)}) copy-start(f32[2,7,7,96]{3,0,2,1:T(2,128)} %param.7) | copy-start | bytes 112900
  4.7 3.3 %copy-start.5 = (f32[2,96]{1,0:T(2,128)S(1)}, f32[2,96]{1,0:T(2,128)}, u32[]{:S(2)}) copy-start(f32[2,96]{1,0:T(2,128)} %gains_in.1) | copy-start | bytes 2308
  4.7 4.0 %collective-permute-start.3 = (bf16[6,8,96]{2,1,0:T(8,128)(2,1)S(1)}, bf16[6,8,96]{2,1,0:T(8,128)(2,1)S(1)}, u32[]{:S(2)}, u32[]{:S(2)}) collective-permute-start(bf16[6,8,96]{2,1,0:T(8,128)(2,1)S(1)} %get-tuple-element.74), channel_id=1, source_target_pairs={{0,17},{1,16},{2,19},{3,18},{4,21},{5,20},{6,23},{7,22},{8,25},{9,... | collective-permute-start | bytes 27656 | tf_op jit(solution)/shard_map/ppermute | solution.py:55
  4.8 4.0 %collective-permute-start.4 = (bf16[6,8,96]{2,1,0:T(8,128)(2,1)S(1)}, bf16[6,8,96]{2,1,0:T(8,128)(2,1)S(1)}, u32[]{:S(2)}, u32[]{:S(2)}) collective-permute-start(bf16[6,8,96]{2,1,0:T(8,128)(2,1)S(1)} %get-tuple-element.75), channel_id=1, source_target_pairs={{0,16},{1,18},{2,17},{3,20},{4,19},{5,22},{6,21},{7,24},{8,23},{9,... | collective-permute-start | bytes 27656 | tf_op jit(solution)/shard_map/ppermute | solution.py:55
  6.0 2.8 %collective-permute-start = (bf16[16,8,96]{2,1,0:T(8,128)(2,1)S(1)}, bf16[16,8,96]{2,1,0:T(8,128)(2,1)S(1)}, u32[]{:S(2)}, u32[]{:S(2)}) collective-permute-start(bf16[16,8,96]{2,1,0:T(8,128)(2,1)S(1)} %get-tuple-element.72), channel_id=1, source_target_pairs={{0,1},{1,0},{2,3},{3,2},{4,5},{5,4},{6,7},{7,6},{8,9},{9,8},{10,11... | collective-permute-start | bytes 73736 | tf_op jit(solution)/shard_map/ppermute | solution.py:55
  7.0 3.9 %collective-permute-start.1 = (bf16[16,8,96]{2,1,0:T(8,128)(2,1)S(1)}, bf16[16,8,96]{2,1,0:T(8,128)(2,1)S(1)}, u32[]{:S(2)}, u32[]{:S(2)}) collective-permute-start(bf16[16,8,96]{2,1,0:T(8,128)(2,1)S(1)} %get-tuple-element.73), channel_id=1, source_target_pairs={{0,16},{1,2},{2,1},{3,4},{4,3},{5,6},{6,5},{7,8},{8,7},{9,10},{10,... | collective-permute-start | bytes 73736 | tf_op jit(solution)/shard_map/ppermute | solution.py:55
  8.0 3.0 %copy-start.1 = (bf16[16,64,96]{2,1,0:T(8,128)(2,1)S(1)}, bf16[16,64,96]{2,1,0:T(8,128)(2,1)}, u32[]{:S(2)}) copy-start(bf16[16,64,96]{2,1,0:T(8,128)(2,1)} %refs_1_.3) | copy-start | bytes 589828
  19.4 8.1 %collective-permute-start.7 = (bf16[9,64,96]{2,1,0:T(8,128)(2,1)S(1)}, bf16[9,64,96]{2,1,0:T(8,128)(2,1)S(1)}, u32[]{:S(2)}, u32[]{:S(2)}) collective-permute-start(bf16[9,64,96]{2,1,0:T(8,128)(2,1)S(1)} %get-tuple-element.94.refs_0_), channel_id=1, source_target_pairs={{0,16},{1,17},{2,18},{3,19},{4,20},{5,21},{6,22},{7,23},{8,24},{9,... | collective-permute-start | bytes 331784 | tf_op jit(solution)/shard_map/ppermute | solution.py:55
  20.5 6.2 %collective-permute-start.8 = (bf16[9,8,96]{2,1,0:T(8,128)(2,1)S(1)}, bf16[9,8,96]{2,1,0:T(8,128)(2,1)S(1)}, u32[]{:S(2)}, u32[]{:S(2)}) collective-permute-start(bf16[9,8,96]{2,1,0:T(8,128)(2,1)S(1)} %get-tuple-element.97), channel_id=1, source_target_pairs={{0,17},{1,16},{2,19},{3,18},{4,21},{5,20},{6,23},{7,22},{8,25},{9,... | collective-permute-start | bytes 41480 | tf_op jit(solution)/shard_map/ppermute | solution.py:55
  20.6 6.1 %collective-permute-start.9 = (bf16[9,8,96]{2,1,0:T(8,128)(2,1)S(1)}, bf16[9,8,96]{2,1,0:T(8,128)(2,1)S(1)}, u32[]{:S(2)}, u32[]{:S(2)}) collective-permute-start(bf16[9,8,96]{2,1,0:T(8,128)(2,1)S(1)} %get-tuple-element.98), channel_id=1, source_target_pairs={{0,16},{1,18},{2,17},{3,20},{4,19},{5,22},{6,21},{7,24},{8,23},{9,... | collective-permute-start | bytes 41480 | tf_op jit(solution)/shard_map/ppermute | solution.py:55
  21.7 5.0 %collective-permute-start.5 = (bf16[32,8,96]{2,1,0:T(8,128)(2,1)S(1)}, bf16[32,8,96]{2,1,0:T(8,128)(2,1)S(1)}, u32[]{:S(2)}, u32[]{:S(2)}) collective-permute-start(bf16[32,8,96]{2,1,0:T(8,128)(2,1)S(1)} %get-tuple-element.95), channel_id=1, source_target_pairs={{0,1},{1,0},{2,3},{3,2},{4,5},{5,4},{6,7},{7,6},{8,9},{9,8},{10,11... | collective-permute-start | bytes 147464 | tf_op jit(solution)/shard_map/ppermute | solution.py:55
  23.3 4.3 %collective-permute-start.6 = (bf16[32,8,96]{2,1,0:T(8,128)(2,1)S(1)}, bf16[32,8,96]{2,1,0:T(8,128)(2,1)S(1)}, u32[]{:S(2)}, u32[]{:S(2)}) collective-permute-start(bf16[32,8,96]{2,1,0:T(8,128)(2,1)S(1)} %get-tuple-element.96), channel_id=1, source_target_pairs={{0,16},{1,2},{2,1},{3,4},{4,3},{5,6},{6,5},{7,8},{8,7},{9,10},{10,... | collective-permute-start | bytes 147464 | tf_op jit(solution)/shard_map/ppermute | solution.py:55
  33.6 1.5 %collective-permute-start.10 = (bf16[848,128]{1,0:T(8,128)(2,1)S(1)}, bf16[848,128]{1,0:T(8,128)(2,1)S(1)}, u32[]{:S(2)}, u32[]{:S(2)}) collective-permute-start(bf16[848,128]{1,0:T(8,128)(2,1)S(1)} %get-tuple-element.103), channel_id=1, source_target_pairs={{0,1},{1,0},{2,3},{3,2},{4,5},{5,4},{6,7},{7,6},{8,9},{9,8},{10,11... | collective-permute-start | bytes 651272 | tf_op jit(solution)/shard_map/ppermute | solution.py:972
  35.2 5.7 %collective-permute-start.11 = (bf16[272,128]{1,0:T(8,128)(2,1)S(1)}, bf16[272,128]{1,0:T(8,128)(2,1)S(1)}, u32[]{:S(2)}, u32[]{:S(2)}) collective-permute-start(bf16[272,128]{1,0:T(8,128)(2,1)S(1)} %get-tuple-element.107), channel_id=1, source_target_pairs={{0,2},{1,3},{2,0},{3,1},{4,6},{5,7},{6,4},{7,5},{8,10},{9,11},{10,... | collective-permute-start | bytes 208904 | tf_op jit(solution)/shard_map/ppermute | solution.py:972
  37.1 4.9 %collective-permute-start.12 = (bf16[272,128]{1,0:T(8,128)(2,1)S(1)}, bf16[272,128]{1,0:T(8,128)(2,1)S(1)}, u32[]{:S(2)}, u32[]{:S(2)}) collective-permute-start(bf16[272,128]{1,0:T(8,128)(2,1)S(1)} %get-tuple-element.108), channel_id=1, source_target_pairs={{0,16},{1,17},{2,18},{3,19},{4,20},{5,21},{6,22},{7,23},{8,24},{9,... | collective-permute-start | bytes 208904 | tf_op jit(solution)/shard_map/ppermute | solution.py:972
  38.3 5.2 %collective-permute-start.13 = (bf16[272,128]{1,0:T(8,128)(2,1)S(1)}, bf16[272,128]{1,0:T(8,128)(2,1)S(1)}, u32[]{:S(2)}, u32[]{:S(2)}) collective-permute-start(bf16[272,128]{1,0:T(8,128)(2,1)S(1)} %get-tuple-element.109), channel_id=1, source_target_pairs={{0,18},{1,19},{2,16},{3,17},{4,22},{5,23},{6,20},{7,21},{8,26},{9,... | collective-permute-start | bytes 208904 | tf_op jit(solution)/shard_map/ppermute | solution.py:972
  43.6 4.9 %collective-permute-start.14 = (bf16[128,128]{1,0:T(8,128)(2,1)S(1)}, bf16[128,128]{1,0:T(8,128)(2,1)S(1)}, u32[]{:S(2)}, u32[]{:S(2)}) collective-permute-start(bf16[128,128]{1,0:T(8,128)(2,1)S(1)} %get-tuple-element.113), channel_id=1, source_target_pairs={{0,8},{1,9},{2,10},{3,11},{4,12},{5,13},{6,14},{7,15},{8,0},{9,1},... | collective-permute-start | bytes 98312 | tf_op jit(solution)/shard_map/ppermute | solution.py:972
  46.2 4.0 %collective-permute-start.15 = (bf16[128,128]{1,0:T(8,128)(2,1)S(1)}, bf16[128,128]{1,0:T(8,128)(2,1)S(1)}, u32[]{:S(2)}, u32[]{:S(2)}) collective-permute-start(bf16[128,128]{1,0:T(8,128)(2,1)S(1)} %get-tuple-element.114), channel_id=1, source_target_pairs={{0,4},{1,5},{2,6},{3,7},{4,0},{5,1},{6,2},{7,3},{8,12},{9,13},{10,... | collective-permute-start | bytes 98312 | tf_op jit(solution)/shard_map/ppermute | solution.py:972
  46.6 5.7 %collective-permute-start.16 = (bf16[128,128]{1,0:T(8,128)(2,1)S(1)}, bf16[128,128]{1,0:T(8,128)(2,1)S(1)}, u32[]{:S(2)}, u32[]{:S(2)}) collective-permute-start(bf16[128,128]{1,0:T(8,128)(2,1)S(1)} %get-tuple-element.115), channel_id=1, source_target_pairs={{0,12},{1,13},{2,14},{3,15},{4,8},{5,9},{6,10},{7,11},{8,4},{9,5},... | collective-permute-start | bytes 98312 | tf_op jit(solution)/shard_map/ppermute | solution.py:972

commit v13 on v11

--- a/solution.py
+++ b/solution.py
@@ -182,17 +182,25 @@
 
 def conv_group(src, base, stride, rows_out, taps, size, flipped=False):
     total = [None] * rows_out
-    for b in range(size):
-        order = [a * size + b for a in range(size)]
-        if flipped:
-            order = [size * size - 1 - t for t in order]
-        weights = [taps[t * 16 : t * 16 + 16, :] for t in order]
-        window = []
+    for first in range(0, size, 2):
+        columns = range(first, min(first + 2, size))
+        weights = []
+        for b in columns:
+            order = [a * size + b for a in range(size)]
+            if flipped:
+                order = [size * size - 1 - t for t in order]
+            weights.append([taps[t * 16 : t * 16 + 16, :] for t in order])
+        windows = [[] for _ in columns]
         for i in range(rows_out + size - 1):
-            window.append(src[pl.ds(base + i * stride + b, 16), :].astype(bf16))
+            for window, b in zip(windows, columns):
+                window.append(src[pl.ds(base + i * stride + b, 16), :].astype(bf16))
             r = i - size + 1
             if r >= 0:
-                term = tree_sum([window[r + a] * weights[a] for a in range(size)]).astype(f32)
+                sums = [
+                    tree_sum([window[r + a] * weight[a] for a in range(size)])
+                    for window, weight in zip(windows, weights)
+                ]
+                term = tree_sum(sums).astype(f32)
                 total[r] = term if total[r] is None else total[r] + term
     return total
 
@@ -310,8 +318,8 @@
     return jnp.concatenate([x, jnp.zeros((rows, LANES - channels), x.dtype)], axis=1)
 
 
-def pieces(total, size):
-    return [(start, min(size, total - start)) for start in range(0, total, size)]
+def span(at, n, by=16):
+    return pl.ds(pl.multiple_of(at, by), n)
 
 
 def round16(x):
@@ -414,31 +422,36 @@
     ones = diagonal(jnp.ones((LANES, LANES), bf16), jnp.ones((LANES, LANES), bf16))
     half = dims.ext_pad // 2
 
-    def mix0(start, n):
-        spans = [(start, n), (half + start, n)]
-        parts = yield from layer_norm([conv[at : at + n, :] for at, n in spans], gain, channels, ones)
+    def mix0(start):
+        n = dims.piece
+        starts = (start, half + start)
+        parts = yield from layer_norm([conv[span(at, n), :] for at in starts], gain, channels, ones)
         pres = dot(side_by_side(parts[0][2], parts[1][2]), forward0[...])
         yield
         count = pres.shape[1] // 2
         hiddens = []
-        for k, ((at, n), (unit, inverse, _)) in enumerate(zip(spans, parts)):
-            unit0[at : at + n, :] = unit.astype(bf16)
-            inv0[at : at + n, :] = inverse
+        for k, (at, (unit, inverse, _)) in enumerate(zip(starts, parts)):
+            unit0[span(at, n), :] = unit.astype(bf16)
+            inv0[span(at, n), :] = inverse
 
             def activate(pre):
                 value, slope = gelu_parts(pre)
                 return (value.astype(bf16), slope.astype(bf16))
 
             hidden, slope = by_blocks(activate, pres[:, k * count : (k + 1) * count])
-            hidden0[at : at + n, :] = hidden
-            slope0[at : at + n, :] = slope
+            hidden0[span(at, n), :] = hidden
+            slope0[span(at, n), :] = slope
             hiddens.append(hidden)
         branches = dot(side_by_side(*hiddens), back0[...])
         yield
-        for k, (at, n) in enumerate(spans):
-            px = pl.ds(frame + at, n)
+        for k, at in enumerate(starts):
+            px = pl.ds(frame + pl.multiple_of(at, 16), n)
             x1[px, :] = round16(x1[px, :] + branches[:, k * LANES : (k + 1) * LANES])
-    together([mix0(start, n) for start, n in pieces(half, dims.piece)])
+    def two_pieces(i, carry):
+        together([mix0((2 * i + j) * dims.piece) for j in range(2)])
+        return carry
+
+    lax.fori_loop(0, half // (2 * dims.piece), two_pieces, 0)
     clear_outside(place, x1, dims)
 
     def conv1(g, carry):
@@ -455,14 +468,14 @@
     step = lines * cols
 
     def mix1(k):
-        px = slice(k * step, (k + 1) * step)
-        middle = k * step + step // 2
+        px = span(k * step, step)
+        half = step // 2
         parts = yield from layer_norm(
-            [conv[k * step : middle, :], conv[middle : (k + 1) * step, :]], gain1, channels, ones
+            [conv[span(k * step, half), :], conv[span(k * step + half, half), :]], gain1, channels, ones
         )
         unit, inverse, normed = (jnp.concatenate(pair, axis=0) for pair in zip(*parts))
         normed1[px, :] = normed
-        upstream = pad_lanes(cot[k * lines : (k + 1) * lines].reshape(step, channels))
+        upstream = pad_lanes(cot[pl.ds(k * lines, lines)].reshape(step, channels))
         both = dot(side_by_side(normed, upstream), forward1[...])
         yield
 
@@ -479,13 +492,17 @@
         branch, normed_grad = (both[:, :LANES], both[:, LANES:])
         for i in range(lines):
             start = (k * lines + i + h) * ext_cols + 4
-            line = x1[start : start + cols, :] + branch[i * cols : (i + 1) * cols]
+            line = x1[pl.ds(start, cols), :] + branch[i * cols : (i + 1) * cols]
             output[k * lines + i] = line[:, :channels].astype(bf16)
         product = normed_grad * unit
         gain_sum[...] += jnp.sum(product.reshape(step // 8, 8, LANES), axis=0)
         grad1[px, :] = yield from norm_backward(normed_grad, unit, inverse, gain1, channels, ones)
 
-    together([mix1(k) for k in range(rows // lines)])
+    def two_chunks(i, carry):
+        together([mix1(2 * i + j) for j in range(2)])
+        return carry
+
+    lax.fori_loop(0, rows // (2 * lines), two_chunks, 0)
 
     takes = [(flat_take(grad1, cols, channels), 2 * h, rows, cols), (image_take(cot), h, rows, cols)]
     write_strips(place, outs, takes, band_combos(dims.row_count))
@@ -589,9 +606,10 @@
     ones = diagonal(jnp.ones((LANES, LANES), bf16), jnp.ones((LANES, LANES), bf16))
     half_px = dims.ext_pad // 2
 
-    def mix0(start, n):
-        spans = [(start, n), (half_px + start, n)]
-        flows = [upstream[at : at + n, :].astype(bf16) for at, n in spans]
+    def mix0(start):
+        n = dims.piece
+        starts = (start, half_px + start)
+        flows = [upstream[span(at, n), :].astype(bf16) for at in starts]
         hidden_grads = dot(side_by_side(*flows), grad_in0[...])
         yield
         count = hidden_grads.shape[1] // 2
@@ -600,24 +618,29 @@
             return ((grad * slope.astype(f32)).astype(bf16),)
 
         pre_grads = [
-            by_blocks(slope_times, hidden_grads[:, k * count : (k + 1) * count], slope0[at : at + n, :])[0]
-            for k, (at, n) in enumerate(spans)
+            by_blocks(slope_times, hidden_grads[:, k * count : (k + 1) * count], slope0[span(at, n), :])[0]
+            for k, at in enumerate(starts)
         ]
         both = dot(side_by_side(*pre_grads), grad_out0[...])
         yield
         normed_grads = (both[:, :LANES], both[:, LANES:])
-        for (at, n), flow, pre_grad, normed_grad in zip(spans, flows, pre_grads, normed_grads):
-            mine = own[at : at + n, :]
-            unit = unit0[at : at + n, :].astype(f32)
-            normed0[at : at + n, :] = (unit * gain * mine).astype(bf16)
-            flow0[at : at + n, :] = flow * mine.astype(bf16)
-            pre_grad0[at : at + n, :] = pre_grad
+        for at, flow, pre_grad, normed_grad in zip(starts, flows, pre_grads, normed_grads):
+            px = span(at, n)
+            mine = own[px, :]
+            unit = unit0[px, :].astype(f32)
+            normed0[px, :] = (unit * gain * mine).astype(bf16)
+            flow0[px, :] = flow * mine.astype(bf16)
+            pre_grad0[px, :] = pre_grad
             product = normed_grad * unit * mine
             gain_sum[...] += jnp.sum(product.reshape(n // 8, 8, LANES), axis=0)
-            grad = yield from norm_backward(normed_grad, unit, inv0[at : at + n, :], gain, channels, ones)
-            grad0[pl.ds(frame + at, n), :] = grad
-
-    together([mix0(start, n) for start, n in pieces(half_px, dims.piece)])
+            grad = yield from norm_backward(normed_grad, unit, inv0[px, :], gain, channels, ones)
+            grad0[pl.ds(frame + pl.multiple_of(at, 16), n), :] = grad
+
+    def two_pieces(i, carry):
+        together([mix0((2 * i + j) * dims.piece) for j in range(2)])
+        return carry
+
+    lax.fori_loop(0, half_px // (2 * dims.piece), two_pieces, 0)
     clear_outside(place, grad0, dims)
     kernel_sums(
         x0, h * wide + SIDE - h, wide, grad0, h * ext_cols + margin, ext_cols, rows, cols, size, sums
@@ -778,8 +801,8 @@
     d.h = d.size // 2
     d.ext_rows, d.ext_cols = (d.rows + (d.h if d.row_count == 2 else 2 * d.h), d.cols + 8)
     d.wide = d.cols + 2 * SIDE
-    d.ext_pad = -(-d.ext_rows * d.ext_cols // 32) * 32
-    d.piece = 176
+    total = d.ext_rows * d.ext_cols
+    d.ext_pad, d.piece = min((-(-total // (4 * p)) * 4 * p, p) for p in range(96, 209, 16))
     d.line_step = 4
     d.half = d.channels // d.row_count
     d.part = up_weights.shape[2] // d.col_count
@@ -830,7 +853,7 @@
     rows, cols, channels = image.shape
     units = up_weights.shape[2]
     tile, ext, wide = (rows * cols, d.ext_pad, (rows + 4 * d.h) * d.wide)
-    frame = (rows + 2 * d.h) * d.ext_cols + 16
+    frame = (rows + 2 * d.h) * d.ext_cols + 16 + ext - d.ext_rows * d.ext_cols
     taps = ((d.size * d.size * 16, LANES), bf16)
     tap_sums = ((d.size * d.size * 8, LANES), f32)
     sums_rows = ceil8(d.size * d.size + 1)

time: 53 us -> 54 us (1.019)
  Pallas kernels: 20.5 us -> 21.5 us
    pallas_call x11, Pallas kernels: 20.5 us -> 21.5 us  [run(): pl.pallas_call(kernel, out_shape=shapes, in_specs=[far] * in_hbm + [space...]
where the time goes in v13:
time: 54 us; the launch traced here: 53.9 us
  Pallas kernels  21.5 us (40%)
  starting transfers between devices  19.3 us (36%)
  waiting for transfers between devices  11.4 us (21%)
  local copies, waits for them, and re-layouts  0.96 us (2%)
  between operations  0.76 us (1%)
    pallas_call x11, Pallas kernels, run(): pl.pallas_call(kernel, out_shape=shapes, in_specs=[far] * in_hbm + [space...  21.5 us
    ppermute x10, starting transfers between devices, exchange(): lax.ppermute(strip, ('row', 'col'), swap_pairs(row_count, col_count, rs,...  11.1 us
    ppermute x7, waiting for transfers between devices, per_device(): lax.ppermute(x, axes, swap_by(d, group, mask))  8.34 us
    ppermute x7, starting transfers between devices, per_device(): lax.ppermute(x, axes, swap_by(d, group, mask))  8.14 us
    ppermute x10, waiting for transfers between devices, exchange(): lax.ppermute(strip, ('row', 'col'), swap_pairs(row_count, col_count, rs,...  3.05 us
  transfers between devices with their start and end apart: 17, of which 8 were waited for; matrix products, arithmetic and copies ran while one was open for 0% of the time, Pallas kernels for 10%

profile of v13, /device:TPU:0, one launch (start us, length us, event | category | flops | bytes accessed | tf_op | source)
XLA Modules:
  0.0 53.9 jit_solution(7608932951213394506)
XLA Ops:
  0.6 0.9 %copy-done = bf16[16,64,96]{2,1,0:T(8,128)(2,1)S(1)} copy-done((bf16[16,64,96]{2,1,0:T(8,128)(2,1)S(1)}, bf16[16,64,96]{2,1,0:T(8,128)(2,1)}, u32[]{:S(2)}) %copy-start) | copy-done | bytes 196632
  1.6 3.0 %collective-permute-start.2 = (bf16[6,64,96]{2,1,0:T(8,128)(2,1)S(1)}, bf16[6,64,96]{2,1,0:T(8,128)(2,1)S(1)}, u32[]{:S(2)}, u32[]{:S(2)}) collective-permute-start(bf16[6,64,96]{2,1,0:T(8,128)(2,1)S(1)} %get-tuple-element.71.refs_0_), channel_id=1, source_target_pairs={{0,16},{1,17},{2,18},{3,19},{4,20},{5,21},{6,22},{7,23},{8,24},{9,... | collective-permute-start | bytes 221192 | tf_op jit(solution)/shard_map/ppermute | solution.py:55
  4.8 1.2 %collective-permute-start.4 = (bf16[6,8,96]{2,1,0:T(8,128)(2,1)S(1)}, bf16[6,8,96]{2,1,0:T(8,128)(2,1)S(1)}, u32[]{:S(2)}, u32[]{:S(2)}) collective-permute-start(bf16[6,8,96]{2,1,0:T(8,128)(2,1)S(1)} %get-tuple-element.75), channel_id=1, source_target_pairs={{0,16},{1,18},{2,17},{3,20},{4,19},{5,22},{6,21},{7,24},{8,23},{9,... | collective-permute-start | bytes 27656 | tf_op jit(solution)/shard_map/ppermute | solution.py:55
  6.0 1.1 %collective-permute-start = (bf16[16,8,96]{2,1,0:T(8,128)(2,1)S(1)}, bf16[16,8,96]{2,1,0:T(8,128)(2,1)S(1)}, u32[]{:S(2)}, u32[]{:S(2)}) collective-permute-start(bf16[16,8,96]{2,1,0:T(8,128)(2,1)S(1)} %get-tuple-element.72), channel_id=1, source_target_pairs={{0,1},{1,0},{2,3},{3,2},{4,5},{5,4},{6,7},{7,6},{8,9},{9,8},{10,11... | collective-permute-start | bytes 73736 | tf_op jit(solution)/shard_map/ppermute | solution.py:55
  7.0 0.9 %collective-permute-start.1 = (bf16[16,8,96]{2,1,0:T(8,128)(2,1)S(1)}, bf16[16,8,96]{2,1,0:T(8,128)(2,1)S(1)}, u32[]{:S(2)}, u32[]{:S(2)}) collective-permute-start(bf16[16,8,96]{2,1,0:T(8,128)(2,1)S(1)} %get-tuple-element.73), channel_id=1, source_target_pairs={{0,16},{1,2},{2,1},{3,4},{4,3},{5,6},{6,5},{7,8},{8,7},{9,10},{10,... | collective-permute-start | bytes 73736 | tf_op jit(solution)/shard_map/ppermute | solution.py:55
  8.8 2.2 %collective-permute-done.1.refs_10_ = bf16[16,8,96]{2,1,0:T(8,128)(2,1)S(1)} collective-permute-done((bf16[16,8,96]{2,1,0:T(8,128)(2,1)S(1)}, bf16[16,8,96]{2,1,0:T(8,128)(2,1)S(1)}, u32[]{:S(2)}, u32[]{:S(2)}) %collective-permute-start.1) | collective-permute-done | bytes 24608 | tf_op jit(solution)/shard_map/ppermute | solution.py:55
  10.9 9.4 %shard_map.112 = (bf16[16,64,96]{2,1,0:T(8,128)(2,1)S(1)}, f32[2240,128]{1,0:T(8,128)S(1)}, f32[1640,128]{1,0:T(8,128)S(1)}, bf16[1408,128]{1,0:T(8,128)(2,1)S(1...) custom-call(bf16[16,64,96]{2,1,0:T(8,128)(2,1)S(1)} %get-tuple-eleme, ...), custom_call_target="tpu_custom_call" | custom-call | flops 15000000512 | bytes 262144 | tf_op jit(solution)/shard_map/pallas_call | solution.py:839
  20.3 1.0 %collective-permute-start.7 = (bf16[9,64,96]{2,1,0:T(8,128)(2,1)S(1)}, bf16[9,64,96]{2,1,0:T(8,128)(2,1)S(1)}, u32[]{:S(2)}, u32[]{:S(2)}) collective-permute-start(bf16[9,64,96]{2,1,0:T(8,128)(2,1)S(1)} %get-tuple-element.94.refs_0_), channel_id=1, source_target_pairs={{0,16},{1,17},{2,18},{3,19},{4,20},{5,21},{6,22},{7,23},{8,24},{9,... | collective-permute-start | bytes 331784 | tf_op jit(solution)/shard_map/ppermute | solution.py:55
  21.5 1.1 %collective-permute-start.9 = (bf16[9,8,96]{2,1,0:T(8,128)(2,1)S(1)}, bf16[9,8,96]{2,1,0:T(8,128)(2,1)S(1)}, u32[]{:S(2)}, u32[]{:S(2)}) collective-permute-start(bf16[9,8,96]{2,1,0:T(8,128)(2,1)S(1)} %get-tuple-element.98), channel_id=1, source_target_pairs={{0,16},{1,18},{2,17},{3,20},{4,19},{5,22},{6,21},{7,24},{8,23},{9,... | collective-permute-start | bytes 41480 | tf_op jit(solution)/shard_map/ppermute | solution.py:55
  22.6 1.6 %collective-permute-start.5 = (bf16[32,8,96]{2,1,0:T(8,128)(2,1)S(1)}, bf16[32,8,96]{2,1,0:T(8,128)(2,1)S(1)}, u32[]{:S(2)}, u32[]{:S(2)}) collective-permute-start(bf16[32,8,96]{2,1,0:T(8,128)(2,1)S(1)} %get-tuple-element.95), channel_id=1, source_target_pairs={{0,1},{1,0},{2,3},{3,2},{4,5},{5,4},{6,7},{7,6},{8,9},{9,8},{10,11... | collective-permute-start | bytes 147464 | tf_op jit(solution)/shard_map/ppermute | solution.py:55
  24.2 1.1 %collective-permute-start.6 = (bf16[32,8,96]{2,1,0:T(8,128)(2,1)S(1)}, bf16[32,8,96]{2,1,0:T(8,128)(2,1)S(1)}, u32[]{:S(2)}, u32[]{:S(2)}) collective-permute-start(bf16[32,8,96]{2,1,0:T(8,128)(2,1)S(1)} %get-tuple-element.96), channel_id=1, source_target_pairs={{0,16},{1,2},{2,1},{3,4},{4,3},{5,6},{6,5},{7,8},{8,7},{9,10},{10,... | collective-permute-start | bytes 147464 | tf_op jit(solution)/shard_map/ppermute | solution.py:55
  25.3 2.3 %shard_map.113 = (f32[56,128]{1,0:T(8,128)S(1)}, f32[384,128]{1,0:T(8,128)S(1)}, f32[384,128]{1,0:T(8,128)S(1)}, bf16[16,64,96]{2,1,0:T(8,128)(2,1)}) custom-call(f32[1640,128]{1,0:T(8,128)S(1)} %get-tuple-element.76.x1, f32[1024,128]{1,0:T(8,128)S(1)} %get-tuple-element.77.grad1.refs_0_, bf16[1024,128]{1,0:T(8,128)(2,1)S(1)} %get-tuple-element.78.normed1, ...), custom_call_target="tpu_custom_call" | custom-call | flops 3000000000 | bytes 262144 | tf_op jit(solution)/shard_map/pallas_call | solution.py:839
  27.6 0.8 %collective-permute-done.6.refs_15_ = bf16[32,8,96]{2,1,0:T(8,128)(2,1)S(1)} collective-permute-done((bf16[32,8,96]{2,1,0:T(8,128)(2,1)S(1)}, bf16[32,8,96]{2,1,0:T(8,128)(2,1)S(1)}, u32[]{:S(2)}, u32[]{:S(2)}) %collective-permute-start.6) | collective-permute-done | bytes 49184 | tf_op jit(solution)/shard_map/ppermute | solution.py:55
  28.4 6.0 %shard_map.115 = (f32[1640,128]{1,0:T(8,128)S(1)}, f32[1024,128]{1,0:T(8,128)S(1)}, f32[768,128]{1,0:T(8,128)S(1)}, f32[80,128]{1,0:T(8,128)S(1)}, bf16[848,128]{1,0:T(8,128)(2,1)S(1)}) custom-call(f32[1024,128]{1,0:T(8,128)S(1)} %get-tuple-element.77.grad1.refs_0_, bf16[16,64,96]{2,1,0:T(8,128)(2,1)S(1)} %copy-done.1, ...), custom_call_target="tpu_custom_call" | custom-call | flops 12000000000 | bytes 262144 | tf_op jit(solution)/shard_map/pallas_call | solution.py:839
  34.6 1.4 %collective-permute-done.10.refs_0_ = bf16[848,128]{1,0:T(8,128)(2,1)S(1)} collective-permute-done((bf16[848,128]{1,0:T(8,128)(2,1)S(1)}, bf16[848,128]{1,0:T(8,128)(2,1)S(1)}, u32[]{:S(2)}, u32[]{:S(2)}) %collective-permute-start.10) | collective-permute-done | bytes 217120 | tf_op jit(solution)/shard_map/ppermute | solution.py:976
  36.0 1.8 %collective-permute-start.11 = (bf16[272,128]{1,0:T(8,128)(2,1)S(1)}, bf16[272,128]{1,0:T(8,128)(2,1)S(1)}, u32[]{:S(2)}, u32[]{:S(2)}) collective-permute-start(bf16[272,128]{1,0:T(8,128)(2,1)S(1)} %get-tuple-element.107), channel_id=1, source_target_pairs={{0,2},{1,3},{2,0},{3,1},{4,6},{5,7},{6,4},{7,5},{8,10},{9,11},{10,... | collective-permute-start | bytes 208904 | tf_op jit(solution)/shard_map/ppermute | solution.py:976
  37.9 1.2 %collective-permute-start.12 = (bf16[272,128]{1,0:T(8,128)(2,1)S(1)}, bf16[272,128]{1,0:T(8,128)(2,1)S(1)}, u32[]{:S(2)}, u32[]{:S(2)}) collective-permute-start(bf16[272,128]{1,0:T(8,128)(2,1)S(1)} %get-tuple-element.108), channel_id=1, source_target_pairs={{0,16},{1,17},{2,18},{3,19},{4,20},{5,21},{6,22},{7,23},{8,24},{9,... | collective-permute-start | bytes 208904 | tf_op jit(solution)/shard_map/ppermute | solution.py:976
  39.6 2.1 %shard_map.117 = (bf16[16,64,96]{2,1,0:T(8,128)(2,1)}, f32[8,128]{1,0:T(8,128)S(1)}) custom-call(f32[1640,128]{1,0:T(8,128)S(1)} %get-tuple-element.99.grad0, f32[1024,128]{1,0:T(8,128)S(1)} %get-tuple-element.100.middle, bf16[784,128]{1,0:T(8,128)(2,1)S(1)} %get-tuple-element.64.refs_2_.taps0, f32[80,128]{1,0:T(8,128)S(1)} %get-tuple-element.104.after.small), custom_call_target="tpu_custom_call" | custom-call | flops 3000000000 | bytes 262144 | tf_op jit(solution)/shard_map/pallas_call | solution.py:839
  41.7 1.1 %collective-permute-done.12.refs_1_ = bf16[272,128]{1,0:T(8,128)(2,1)S(1)} collective-permute-done((bf16[272,128]{1,0:T(8,128)(2,1)S(1)}, bf16[272,128]{1,0:T(8,128)(2,1)S(1)}, u32[]{:S(2)}, u32[]{:S(2)}) %collective-permute-start.12) | collective-permute-done | bytes 69664 | tf_op jit(solution)/shard_map/ppermute | solution.py:976
  42.8 1.5 %collective-permute-done.13.refs_2_ = bf16[272,128]{1,0:T(8,128)(2,1)S(1)} collective-permute-done((bf16[272,128]{1,0:T(8,128)(2,1)S(1)}, bf16[272,128]{1,0:T(8,128)(2,1)S(1)}, u32[]{:S(2)}, u32[]{:S(2)}) %collective-permute-start.13) | collective-permute-done | bytes 69664 | tf_op jit(solution)/shard_map/ppermute | solution.py:976
  44.4 2.7 %collective-permute-start.14 = (bf16[128,128]{1,0:T(8,128)(2,1)S(1)}, bf16[128,128]{1,0:T(8,128)(2,1)S(1)}, u32[]{:S(2)}, u32[]{:S(2)}) collective-permute-start(bf16[128,128]{1,0:T(8,128)(2,1)S(1)} %get-tuple-element.113), channel_id=1, source_target_pairs={{0,8},{1,9},{2,10},{3,11},{4,12},{5,13},{6,14},{7,15},{8,0},{9,1},... | collective-permute-start | bytes 98312 | tf_op jit(solution)/shard_map/ppermute | solution.py:976
  47.4 1.4 %collective-permute-start.16 = (bf16[128,128]{1,0:T(8,128)(2,1)S(1)}, bf16[128,128]{1,0:T(8,128)(2,1)S(1)}, u32[]{:S(2)}, u32[]{:S(2)}) collective-permute-start(bf16[128,128]{1,0:T(8,128)(2,1)S(1)} %get-tuple-element.115), channel_id=1, source_target_pairs={{0,12},{1,13},{2,14},{3,15},{4,8},{5,9},{6,10},{7,11},{8,4},{9,5},... | collective-permute-start | bytes 98312 | tf_op jit(solution)/shard_map/ppermute | solution.py:976
  49.3 1.7 %collective-permute-done.15.refs_1_ = bf16[128,128]{1,0:T(8,128)(2,1)S(1)} collective-permute-done((bf16[128,128]{1,0:T(8,128)(2,1)S(1)}, bf16[128,128]{1,0:T(8,128)(2,1)S(1)}, u32[]{:S(2)}, u32[]{:S(2)}) %collective-permute-start.15) | collective-permute-done | bytes 32800 | tf_op jit(solution)/shard_map/ppermute | solution.py:976
  51.0 2.1 %collective-permute-done.16.refs_2_ = bf16[128,128]{1,0:T(8,128)(2,1)S(1)} collective-permute-done((bf16[128,128]{1,0:T(8,128)(2,1)S(1)}, bf16[128,128]{1,0:T(8,128)(2,1)S(1)}, u32[]{:S(2)}, u32[]{:S(2)}) %collective-permute-start.16) | collective-permute-done | bytes 32800 | tf_op jit(solution)/shard_map/ppermute | solution.py:976
  (33 shorter events, 3.5 us)
Async XLA Ops:
  0.6 1.0 %copy-start = (bf16[16,64,96]{2,1,0:T(8,128)(2,1)S(1)}, bf16[16,64,96]{2,1,0:T(8,128)(2,1)}, u32[]{:S(2)}) copy-start(bf16[16,64,96]{2,1,0:T(8,128)(2,1)} %image_in.1) | copy-start | bytes 589828
  1.6 9.3 %collective-permute-start.2 = (bf16[6,64,96]{2,1,0:T(8,128)(2,1)S(1)}, bf16[6,64,96]{2,1,0:T(8,128)(2,1)S(1)}, u32[]{:S(2)}, u32[]{:S(2)}) collective-permute-start(bf16[6,64,96]{2,1,0:T(8,128)(2,1)S(1)} %get-tuple-element.71.refs_0_), channel_id=1, source_target_pairs={{0,16},{1,17},{2,18},{3,19},{4,20},{5,21},{6,22},{7,23},{8,24},{9,... | collective-permute-start | bytes 221192 | tf_op jit(solution)/shard_map/ppermute | solution.py:55
  4.7 3.3 %copy-start.2 = (bf16[2,96,384]{2,1,0:T(8,128)(2,1)S(1)}, bf16[2,96,384]{2,1,0:T(8,128)(2,1)}, u32[]{:S(2)}) copy-start(bf16[2,96,384]{2,1,0:T(8,128)(2,1)} %up_in.1) | copy-start | bytes 442372
  4.7 3.3 %copy-start.3 = (bf16[2,384,96]{1,2,0:T(8,128)(2,1)S(1)}, bf16[2,384,96]{1,2,0:T(8,128)(2,1)}, u32[]{:S(2)}) copy-start(bf16[2,384,96]{1,2,0:T(8,128)(2,1)} %param.10) | copy-start | bytes 442372
  4.7 3.3 %copy-start.4 = (f32[2,7,7,96]{3,0,2,1:T(2,128)S(1)}, f32[2,7,7,96]{3,0,2,1:T(2,128)}, u32[]{:S(2)}) copy-start(f32[2,7,7,96]{3,0,2,1:T(2,128)} %param.7) | copy-start | bytes 112900
  4.7 3.3 %copy-start.5 = (f32[2,96]{1,0:T(2,128)S(1)}, f32[2,96]{1,0:T(2,128)}, u32[]{:S(2)}) copy-start(f32[2,96]{1,0:T(2,128)} %gains_in.1) | copy-start | bytes 2308
  4.7 4.0 %collective-permute-start.3 = (bf16[6,8,96]{2,1,0:T(8,128)(2,1)S(1)}, bf16[6,8,96]{2,1,0:T(8,128)(2,1)S(1)}, u32[]{:S(2)}, u32[]{:S(2)}) collective-permute-start(bf16[6,8,96]{2,1,0:T(8,128)(2,1)S(1)} %get-tuple-element.74), channel_id=1, source_target_pairs={{0,17},{1,16},{2,19},{3,18},{4,21},{5,20},{6,23},{7,22},{8,25},{9,... | collective-permute-start | bytes 27656 | tf_op jit(solution)/shard_map/ppermute | solution.py:55
  4.8 4.0 %collective-permute-start.4 = (bf16[6,8,96]{2,1,0:T(8,128)(2,1)S(1)}, bf16[6,8,96]{2,1,0:T(8,128)(2,1)S(1)}, u32[]{:S(2)}, u32[]{:S(2)}) collective-permute-start(bf16[6,8,96]{2,1,0:T(8,128)(2,1)S(1)} %get-tuple-element.75), channel_id=1, source_target_pairs={{0,16},{1,18},{2,17},{3,20},{4,19},{5,22},{6,21},{7,24},{8,23},{9,... | collective-permute-start | bytes 27656 | tf_op jit(solution)/shard_map/ppermute | solution.py:55
  6.0 2.8 %collective-permute-start = (bf16[16,8,96]{2,1,0:T(8,128)(2,1)S(1)}, bf16[16,8,96]{2,1,0:T(8,128)(2,1)S(1)}, u32[]{:S(2)}, u32[]{:S(2)}) collective-permute-start(bf16[16,8,96]{2,1,0:T(8,128)(2,1)S(1)} %get-tuple-element.72), channel_id=1, source_target_pairs={{0,1},{1,0},{2,3},{3,2},{4,5},{5,4},{6,7},{7,6},{8,9},{9,8},{10,11... | collective-permute-start | bytes 73736 | tf_op jit(solution)/shard_map/ppermute | solution.py:55
  7.0 3.9 %collective-permute-start.1 = (bf16[16,8,96]{2,1,0:T(8,128)(2,1)S(1)}, bf16[16,8,96]{2,1,0:T(8,128)(2,1)S(1)}, u32[]{:S(2)}, u32[]{:S(2)}) collective-permute-start(bf16[16,8,96]{2,1,0:T(8,128)(2,1)S(1)} %get-tuple-element.73), channel_id=1, source_target_pairs={{0,16},{1,2},{2,1},{3,4},{4,3},{5,6},{6,5},{7,8},{8,7},{9,10},{10,... | collective-permute-start | bytes 73736 | tf_op jit(solution)/shard_map/ppermute | solution.py:55
  8.0 3.0 %copy-start.1 = (bf16[16,64,96]{2,1,0:T(8,128)(2,1)S(1)}, bf16[16,64,96]{2,1,0:T(8,128)(2,1)}, u32[]{:S(2)}) copy-start(bf16[16,64,96]{2,1,0:T(8,128)(2,1)} %refs_1_.3) | copy-start | bytes 589828
  20.3 8.1 %collective-permute-start.7 = (bf16[9,64,96]{2,1,0:T(8,128)(2,1)S(1)}, bf16[9,64,96]{2,1,0:T(8,128)(2,1)S(1)}, u32[]{:S(2)}, u32[]{:S(2)}) collective-permute-start(bf16[9,64,96]{2,1,0:T(8,128)(2,1)S(1)} %get-tuple-element.94.refs_0_), channel_id=1, source_target_pairs={{0,16},{1,17},{2,18},{3,19},{4,20},{5,21},{6,22},{7,23},{8,24},{9,... | collective-permute-start | bytes 331784 | tf_op jit(solution)/shard_map/ppermute | solution.py:55
  21.4 6.2 %collective-permute-start.8 = (bf16[9,8,96]{2,1,0:T(8,128)(2,1)S(1)}, bf16[9,8,96]{2,1,0:T(8,128)(2,1)S(1)}, u32[]{:S(2)}, u32[]{:S(2)}) collective-permute-start(bf16[9,8,96]{2,1,0:T(8,128)(2,1)S(1)} %get-tuple-element.97), channel_id=1, source_target_pairs={{0,17},{1,16},{2,19},{3,18},{4,21},{5,20},{6,23},{7,22},{8,25},{9,... | collective-permute-start | bytes 41480 | tf_op jit(solution)/shard_map/ppermute | solution.py:55
  21.5 6.1 %collective-permute-start.9 = (bf16[9,8,96]{2,1,0:T(8,128)(2,1)S(1)}, bf16[9,8,96]{2,1,0:T(8,128)(2,1)S(1)}, u32[]{:S(2)}, u32[]{:S(2)}) collective-permute-start(bf16[9,8,96]{2,1,0:T(8,128)(2,1)S(1)} %get-tuple-element.98), channel_id=1, source_target_pairs={{0,16},{1,18},{2,17},{3,20},{4,19},{5,22},{6,21},{7,24},{8,23},{9,... | collective-permute-start | bytes 41480 | tf_op jit(solution)/shard_map/ppermute | solution.py:55
  22.6 5.0 %collective-permute-start.5 = (bf16[32,8,96]{2,1,0:T(8,128)(2,1)S(1)}, bf16[32,8,96]{2,1,0:T(8,128)(2,1)S(1)}, u32[]{:S(2)}, u32[]{:S(2)}) collective-permute-start(bf16[32,8,96]{2,1,0:T(8,128)(2,1)S(1)} %get-tuple-element.95), channel_id=1, source_target_pairs={{0,1},{1,0},{2,3},{3,2},{4,5},{5,4},{6,7},{7,6},{8,9},{9,8},{10,11... | collective-permute-start | bytes 147464 | tf_op jit(solution)/shard_map/ppermute | solution.py:55
  24.2 4.3 %collective-permute-start.6 = (bf16[32,8,96]{2,1,0:T(8,128)(2,1)S(1)}, bf16[32,8,96]{2,1,0:T(8,128)(2,1)S(1)}, u32[]{:S(2)}, u32[]{:S(2)}) collective-permute-start(bf16[32,8,96]{2,1,0:T(8,128)(2,1)S(1)} %get-tuple-element.96), channel_id=1, source_target_pairs={{0,16},{1,2},{2,1},{3,4},{4,3},{5,6},{6,5},{7,8},{8,7},{9,10},{10,... | collective-permute-start | bytes 147464 | tf_op jit(solution)/shard_map/ppermute | solution.py:55
  34.4 1.5 %collective-permute-start.10 = (bf16[848,128]{1,0:T(8,128)(2,1)S(1)}, bf16[848,128]{1,0:T(8,128)(2,1)S(1)}, u32[]{:S(2)}, u32[]{:S(2)}) collective-permute-start(bf16[848,128]{1,0:T(8,128)(2,1)S(1)} %get-tuple-element.103), channel_id=1, source_target_pairs={{0,1},{1,0},{2,3},{3,2},{4,5},{5,4},{6,7},{7,6},{8,9},{9,8},{10,11... | collective-permute-start | bytes 651272 | tf_op jit(solution)/shard_map/ppermute | solution.py:976
  36.0 5.7 %collective-permute-start.11 = (bf16[272,128]{1,0:T(8,128)(2,1)S(1)}, bf16[272,128]{1,0:T(8,128)(2,1)S(1)}, u32[]{:S(2)}, u32[]{:S(2)}) collective-permute-start(bf16[272,128]{1,0:T(8,128)(2,1)S(1)} %get-tuple-element.107), channel_id=1, source_target_pairs={{0,2},{1,3},{2,0},{3,1},{4,6},{5,7},{6,4},{7,5},{8,10},{9,11},{10,... | collective-permute-start | bytes 208904 | tf_op jit(solution)/shard_map/ppermute | solution.py:976
  37.9 4.9 %collective-permute-start.12 = (bf16[272,128]{1,0:T(8,128)(2,1)S(1)}, bf16[272,128]{1,0:T(8,128)(2,1)S(1)}, u32[]{:S(2)}, u32[]{:S(2)}) collective-permute-start(bf16[272,128]{1,0:T(8,128)(2,1)S(1)} %get-tuple-element.108), channel_id=1, source_target_pairs={{0,16},{1,17},{2,18},{3,19},{4,20},{5,21},{6,22},{7,23},{8,24},{9,... | collective-permute-start | bytes 208904 | tf_op jit(solution)/shard_map/ppermute | solution.py:976
  39.1 5.2 %collective-permute-start.13 = (bf16[272,128]{1,0:T(8,128)(2,1)S(1)}, bf16[272,128]{1,0:T(8,128)(2,1)S(1)}, u32[]{:S(2)}, u32[]{:S(2)}) collective-permute-start(bf16[272,128]{1,0:T(8,128)(2,1)S(1)} %get-tuple-element.109), channel_id=1, source_target_pairs={{0,18},{1,19},{2,16},{3,17},{4,22},{5,23},{6,20},{7,21},{8,26},{9,... | collective-permute-start | bytes 208904 | tf_op jit(solution)/shard_map/ppermute | solution.py:976
  44.4 5.0 %collective-permute-start.14 = (bf16[128,128]{1,0:T(8,128)(2,1)S(1)}, bf16[128,128]{1,0:T(8,128)(2,1)S(1)}, u32[]{:S(2)}, u32[]{:S(2)}) collective-permute-start(bf16[128,128]{1,0:T(8,128)(2,1)S(1)} %get-tuple-element.113), channel_id=1, source_target_pairs={{0,8},{1,9},{2,10},{3,11},{4,12},{5,13},{6,14},{7,15},{8,0},{9,1},... | collective-permute-start | bytes 98312 | tf_op jit(solution)/shard_map/ppermute | solution.py:976
  47.0 4.0 %collective-permute-start.15 = (bf16[128,128]{1,0:T(8,128)(2,1)S(1)}, bf16[128,128]{1,0:T(8,128)(2,1)S(1)}, u32[]{:S(2)}, u32[]{:S(2)}) collective-permute-start(bf16[128,128]{1,0:T(8,128)(2,1)S(1)} %get-tuple-element.114), channel_id=1, source_target_pairs={{0,4},{1,5},{2,6},{3,7},{4,0},{5,1},{6,2},{7,3},{8,12},{9,13},{10,... | collective-permute-start | bytes 98312 | tf_op jit(solution)/shard_map/ppermute | solution.py:976
  47.4 5.7 %collective-permute-start.16 = (bf16[128,128]{1,0:T(8,128)(2,1)S(1)}, bf16[128,128]{1,0:T(8,128)(2,1)S(1)}, u32[]{:S(2)}, u32[]{:S(2)}) collective-permute-start(bf16[128,128]{1,0:T(8,128)(2,1)S(1)} %get-tuple-element.115), channel_id=1, source_target_pairs={{0,12},{1,13},{2,14},{3,15},{4,8},{5,9},{6,10},{7,11},{8,4},{9,5},... | collective-permute-start | bytes 98312 | tf_op jit(solution)/shard_map/ppermute | solution.py:976

commit v14 on v11

--- a/solution.py
+++ b/solution.py
@@ -182,17 +182,25 @@
 
 def conv_group(src, base, stride, rows_out, taps, size, flipped=False):
     total = [None] * rows_out
-    for b in range(size):
-        order = [a * size + b for a in range(size)]
-        if flipped:
-            order = [size * size - 1 - t for t in order]
-        weights = [taps[t * 16 : t * 16 + 16, :] for t in order]
-        window = []
+    for first in range(0, size, 2):
+        columns = range(first, min(first + 2, size))
+        weights = []
+        for b in columns:
+            order = [a * size + b for a in range(size)]
+            if flipped:
+                order = [size * size - 1 - t for t in order]
+            weights.append([taps[t * 16 : t * 16 + 16, :] for t in order])
+        windows = [[] for _ in columns]
         for i in range(rows_out + size - 1):
-            window.append(src[pl.ds(base + i * stride + b, 16), :].astype(bf16))
+            for window, b in zip(windows, columns):
+                window.append(src[pl.ds(base + i * stride + b, 16), :].astype(bf16))
             r = i - size + 1
             if r >= 0:
-                term = tree_sum([window[r + a] * weights[a] for a in range(size)]).astype(f32)
+                sums = [
+                    tree_sum([window[r + a] * weight[a] for a in range(size)])
+                    for window, weight in zip(windows, weights)
+                ]
+                term = tree_sum(sums).astype(f32)
                 total[r] = term if total[r] is None else total[r] + term
     return total
 
@@ -359,8 +367,8 @@
     write_strips(place, outs, takes, other_combos(dims.row_count))
 
 
-def weights_kernel(up_in, down_t_in, kernels_in, gains_in, *refs):
-    forward0, back0, forward1, back1, grad_in0, grad_out0, taps0, taps1, gains, up_w, down_w, kernels, sems = refs
+def weights_kernel(dims, up_in, down_t_in, kernels_in, gains_in, *refs):
+    forward0, back0, forward1, back1, grad_in0, grad_out0, taps0, taps1, gains, own, up_w, down_w, kernels, sems = refs
     fetch((up_in, down_t_in, kernels_in, gains_in), (up_w, down_w, kernels, gains), sems)
     spread_taps(kernels, 0, taps0)
     spread_taps(kernels, 1, taps1)
@@ -379,6 +387,20 @@
     back1[...] = diagonal(down1, up_t1)
     grad_in0[...] = diagonal(down_t0, down_t0)
     grad_out0[...] = diagonal(up_t0, up_t0)
+    own_pixels(dims, own)
+
+
+def own_pixels(dims, own):
+    skip = dims.skipped_rows(Place(dims.row_count, dims.col_count))
+    ext_rows, ext_cols, h = (dims.ext_rows, dims.ext_cols, dims.h)
+    col = lax.broadcasted_iota(jnp.int32, (ext_cols, LANES), 0) - (ext_cols - dims.cols) // 2
+    inside = jnp.where(jnp.logical_and(col >= 0, col < dims.cols), 1.0, 0.0)
+    for r in range(ext_rows):
+        mine = jnp.logical_and(r + skip >= h, r + skip < h + dims.rows)
+        own[r * ext_cols : (r + 1) * ext_cols, :] = jnp.where(mine, inside, 0.0)
+    used = ext_rows * ext_cols
+    if dims.ext_pad > used:
+        own[used:, :] = jnp.zeros((dims.ext_pad - used, LANES), f32)
 
 
 def first_kernel(dims, *refs):
@@ -516,14 +538,27 @@
 
 
 def sums_kernel(
-    dims, x1, grad1, normed1, pre_grad1, hidden1, cot, gain_part, final, taps_sum, up_sum, down_sum, output, sums
+    dims, x1, grad1, normed1, pre_grad1, hidden1, cot, gain_part, final, taps_sum, joined, output, sums
 ):
     output[...] = final[...]
     kernel_sums(x1, 1, dims.ext_cols, grad1, 0, dims.cols, dims.rows, dims.cols, dims.size, sums)
     store_sums(dims, sums, gain_part[...], taps_sum)
     upstream = pad_lanes(cot[...].reshape(dims.rows * dims.cols, dims.channels))
-    up_sum[...] = dot_leading(normed1[...], pre_grad1[...]).T
-    down_sum[...] = dot_leading(upstream, hidden1[...]).T
+    up = dot_leading(normed1[...], pre_grad1[...]).T * dims.factor
+    down = dot_leading(upstream, hidden1[...]).T * dims.factor
+    join_sums(dims, up, down, joined)
+
+
+def join_sums(dims, up, down, target):
+    units, half = (up.shape[0], dims.half)
+    lane = lax.broadcasted_iota(jnp.int32, (units, LANES), 1)
+    for r in range(dims.row_count):
+        first = pltpu.roll(up, LANES - r * half, 1) if r else up
+        shift = (half - r * half) % LANES
+        second = pltpu.roll(down, shift, 1) if shift else down
+        both = jnp.where(lane < half, first, jnp.where(lane < 2 * half, second, 0.0))
+        target[r * units : (r + 1) * units, :] = both
+    target[dims.row_count * units :, :] = jnp.zeros((8, LANES), f32)
 
 
 def store_sums(dims, sums, gain_part, target):
@@ -537,10 +572,10 @@
 def third_kernel(dims, *refs):
     count = len(combos(dims.row_count))
     (grad1, cot, taps1, gains, grad_in0, grad_out0, x0, unit0, inv0, hidden0, slope0) = refs[:11]
-    (taps_sum1, up_sum1, down_sum1) = refs[11:14]
+    (own, taps_sum1, joined1) = refs[11:14]
     strips = refs[14 : 14 + count]
-    (grad0, middle, keep, small_keep, send) = refs[14 + count : 19 + count]
-    (wide_grad, cot_frame, upstream, own, sums, normed0, flow0, pre_grad0, gain_sum, small, tall, slabs) = refs[19 + count :]
+    (grad0, upstream, keep, small_keep, send) = refs[14 + count : 19 + count]
+    (wide_grad, cot_frame, sums, normed0, flow0, pre_grad0, gain_sum, small, tall, slabs) = refs[19 + count :]
     place = Place(dims.row_count, dims.col_count)
     rows, cols, channels, h, size = (dims.rows, dims.cols, dims.channels, dims.h, dims.size)
     ext_rows, ext_cols, wide = (dims.ext_rows, dims.ext_cols, dims.wide)
@@ -563,27 +598,18 @@
     used = ext_rows * ext_cols
     if dims.ext_pad > used:
         upstream[used:, :] = jnp.zeros((dims.ext_pad - used, LANES), f32)
-        own[used:, :] = jnp.zeros((dims.ext_pad - used, LANES), f32)
     grad0[...] = jnp.zeros(grad0.shape, f32)
     frame = pl.multiple_of(skip * ext_cols, 8)
 
     def conv1(g, carry):
         at = group_start(g, ext_cols)
         total = conv_group(wide_grad, pl.multiple_of(skip * wide, 8) + at + 1, wide, ext_rows, taps1, size, True)
-        col = lax.broadcasted_iota(jnp.int32, (16, LANES), 0) + (at - margin)
-        inside = jnp.where(jnp.logical_and(col >= 0, col < cols), 1.0, 0.0)
         for r in range(ext_rows):
             px = pl.ds(r * ext_cols + at, 16)
             upstream[px, :] = cot_frame[pl.ds(frame + r * ext_cols + at, 16), :] + total[r]
-            mine = jnp.logical_and(r + skip >= h, r + skip < h + rows)
-            own[px, :] = jnp.where(mine, inside, 0.0)
         return carry
 
     lax.fori_loop(0, -(-ext_cols // 16), conv1, 0)
-    for i in range(rows):
-        line = upstream[pl.ds((i + h - skip) * ext_cols + margin, cols), :]
-        middle[i * cols : (i + 1) * cols, :] = round16(line)
-
     gain = pad_lanes(gains[0:1, :])
     gain_sum[...] = jnp.zeros(gain_sum.shape, f32)
     ones = diagonal(jnp.ones((LANES, LANES), bf16), jnp.ones((LANES, LANES), bf16))
@@ -629,29 +655,20 @@
     merged = fold_rows(merged, dims.small_rows, channels).astype(bf16)
     small_keep[...] = merged.astype(f32)
 
-    layer_rows, part, half = (dims.layer_rows, dims.part, dims.half)
+    layer_rows, part = (dims.layer_rows, dims.part)
     units = hidden0.shape[1]
     up0 = dot_leading(normed0[...], pre_grad0[...]).T * dims.factor
     down0 = dot_leading(flow0[...], hidden0[...]).T * dims.factor
-    up1 = up_sum1[...] * dims.factor
-    down1 = down_sum1[...] * dims.factor
-    lane = lax.broadcasted_iota(jnp.int32, (units, LANES), 1)
+    join_sums(dims, up0, down0, tall)
     slab_rows = 2 * layer_rows
     for r in range(dims.row_count):
-        for layer, (u, d) in enumerate(((up0, down0), (up1, down1))):
-            first = pltpu.roll(u, LANES - r * half, 1) if r else u
-            shift = (half - r * half) % LANES
-            second = pltpu.roll(d, shift, 1) if shift else d
-            joined = jnp.where(lane < half, first, jnp.where(lane < 2 * half, second, 0.0))
-            tall[layer * (units + 8) : layer * (units + 8) + units, :] = joined
-
         for c in range(dims.col_count):
             index = 0
             for axis, bit in dims.stages:
                 index = 2 * index + ((r if axis == "row" else c) >> bit & 1)
-            for layer in range(2):
-                to, at = (index * slab_rows + layer * layer_rows, layer * (units + 8) + c * part)
-                slabs[to : to + layer_rows, :] = tall[at : at + layer_rows, :]
+            for layer, source in ((0, tall), (1, joined1)):
+                to, at = (index * slab_rows + layer * layer_rows, r * units + c * part)
+                slabs[to : to + layer_rows, :] = source[at : at + layer_rows, :]
 
     split(dims, 0, slabs, merged, keep, (send,))
 
@@ -747,14 +764,17 @@
                 gain_out[layer : layer + 1, :] = row
 
 
-def image_kernel(dims, grad0, middle, taps0, after, out, ready, work):
+def image_kernel(dims, grad0, upstream, taps0, after, out, ready, work):
     rows, cols, size = (dims.rows, dims.cols, dims.size)
+    skip = dims.skipped_rows(Place(dims.row_count, dims.col_count))
+    margin = (dims.ext_cols - cols) // 2
 
     def conv0(g, carry):
         at = group_start(g, cols)
         total = conv_group(grad0, at + 1, dims.ext_cols, rows, taps0, size, True)
         for r in range(rows):
-            work[pl.ds(r * cols + at, 16), :] = middle[pl.ds(r * cols + at, 16), :] + total[r]
+            line = upstream[pl.ds((r + dims.h - skip) * dims.ext_cols + margin + at, 16), :]
+            work[pl.ds(r * cols + at, 16), :] = round16(line) + total[r]
         return carry
 
     lax.fori_loop(0, -(-cols // 16), conv0, 0)
@@ -846,9 +866,9 @@
     other_strips = run(bind(others_kernel, d), strips_of(others, (2 * d.h,)), [], image, *band_strips)
     strips = exchange(band_strips, other_strips, d.row_count, d.col_count)
     mixing = [((2 * LANES, 2 * units), bf16), ((2 * units, 2 * LANES), bf16)]
-    forward0, back0, forward1, back1, grad_in0, grad_out0, taps0, taps1, gains = run(
-        weights_kernel,
-        mixing * 3 + [taps, taps, (gains.shape, f32)],
+    forward0, back0, forward1, back1, grad_in0, grad_out0, taps0, taps1, gains, own = run(
+        bind(weights_kernel, d),
+        mixing * 3 + [taps, taps, (gains.shape, f32), ((ext, LANES), f32)],
         [((2, channels, units), bf16), ((2, channels, units), bf16), ((d.size, d.size, 2, channels), f32)],
         up_weights,
         jnp.swapaxes(down_weights, 1, 2),
@@ -896,9 +916,10 @@
     )
     strips = exchange(band_strips, other_strips, d.row_count, d.col_count)
 
-    taps_sum1, up_sum1, down_sum1, output = run(
+    joined = ((d.row_count * units + 8, LANES), f32)
+    taps_sum1, joined1, output = run(
         bind(sums_kernel, d),
-        [((sums_rows, LANES), f32), ((units, LANES), f32), ((units, LANES), f32), (image.shape, bf16)],
+        [((sums_rows, LANES), f32), joined, (image.shape, bf16)],
         [tap_sums],
         x1,
         grad1,
@@ -913,21 +934,19 @@
 
     held = d.count // 2 * 2 * d.layer_rows
     small = ((d.small_rows, LANES), f32)
-    grad0, middle, keep, sums, send = run(
+    grad0, upstream, keep, sums, send = run(
         bind(third_kernel, d),
-        [((frame, LANES), f32), ((tile, LANES), f32), ((held, LANES), f32), small, ((held + d.small_rows, LANES), bf16)],
+        [((frame, LANES), f32), ((ext, LANES), f32), ((held, LANES), f32), small, ((held + d.small_rows, LANES), bf16)],
         [
             ((wide, LANES), f32),
             ((frame, LANES), f32),
-            ((ext, LANES), f32),
-            ((ext, LANES), f32),
             tap_sums,
             ((ext, LANES), bf16),
             ((ext, LANES), bf16),
             ((ext, units), bf16),
             ((8, LANES), f32),
             ((sums_rows, LANES), f32),
-            ((2 * (units + 8), LANES), f32),
+            joined,
             ((2 * held, LANES), f32),
         ],
         grad1,
@@ -941,9 +960,9 @@
         inv0,
         hidden0,
         slope0,
+        own,
         taps_sum1,
-        up_sum1,
-        down_sum1,
+        joined1,
         *strips,
         busy_us=12,
     )
@@ -958,7 +977,7 @@
                 [(image.shape, bf16), ((8, LANES), f32)],
                 [((tile, LANES), f32)],
                 grad0,
-                middle,
+                upstream,
                 taps0,
                 sums,
                 busy_us=3,

time: 53 us -> 52.5 us (level)
  no operation moved by 1% of the time
where the time goes in v14:
time: 52.5 us; the launch traced here: 52.4 us
  Pallas kernels  20.1 us (38%)
  starting transfers between devices  19.3 us (37%)
  waiting for transfers between devices  11.2 us (21%)
  local copies, waits for them, and re-layouts  0.96 us (2%)
  between operations  0.76 us (1%)
    pallas_call x11, Pallas kernels, run(): pl.pallas_call(kernel, out_shape=shapes, in_specs=[far] * in_hbm + [space...  20.1 us
    ppermute x10, starting transfers between devices, exchange(): lax.ppermute(strip, ('row', 'col'), swap_pairs(row_count, col_count, rs,...  11.1 us
    ppermute x7, waiting for transfers between devices, per_device(): lax.ppermute(x, axes, swap_by(d, group, mask))  8.31 us
    ppermute x7, starting transfers between devices, per_device(): lax.ppermute(x, axes, swap_by(d, group, mask))  8.18 us
    ppermute x10, waiting for transfers between devices, exchange(): lax.ppermute(strip, ('row', 'col'), swap_pairs(row_count, col_count, rs,...  2.87 us
  transfers between devices with their start and end apart: 17, of which 8 were waited for; matrix products, arithmetic and copies ran while one was open for 0% of the time, Pallas kernels for 10%

profile of v14, /device:TPU:0, one launch (start us, length us, event | category | flops | bytes accessed | tf_op | source)
XLA Modules:
  0.0 52.4 jit_solution(7874329619010239564)
XLA Ops:
  0.6 0.9 %copy-done = bf16[16,64,96]{2,1,0:T(8,128)(2,1)S(1)} copy-done((bf16[16,64,96]{2,1,0:T(8,128)(2,1)S(1)}, bf16[16,64,96]{2,1,0:T(8,128)(2,1)}, u32[]{:S(2)}) %copy-start) | copy-done | bytes 196632
  1.6 3.0 %collective-permute-start.2 = (bf16[6,64,96]{2,1,0:T(8,128)(2,1)S(1)}, bf16[6,64,96]{2,1,0:T(8,128)(2,1)S(1)}, u32[]{:S(2)}, u32[]{:S(2)}) collective-permute-start(bf16[6,64,96]{2,1,0:T(8,128)(2,1)S(1)} %get-tuple-element.71.refs_0_), channel_id=1, source_target_pairs={{0,16},{1,17},{2,18},{3,19},{4,20},{5,21},{6,22},{7,23},{8,24},{9,... | collective-permute-start | bytes 221192 | tf_op jit(solution)/shard_map/ppermute | solution.py:55
  4.8 1.2 %collective-permute-start.4 = (bf16[6,8,96]{2,1,0:T(8,128)(2,1)S(1)}, bf16[6,8,96]{2,1,0:T(8,128)(2,1)S(1)}, u32[]{:S(2)}, u32[]{:S(2)}) collective-permute-start(bf16[6,8,96]{2,1,0:T(8,128)(2,1)S(1)} %get-tuple-element.75), channel_id=1, source_target_pairs={{0,16},{1,18},{2,17},{3,20},{4,19},{5,22},{6,21},{7,24},{8,23},{9,... | collective-permute-start | bytes 27656 | tf_op jit(solution)/shard_map/ppermute | solution.py:55
  6.0 1.1 %collective-permute-start = (bf16[16,8,96]{2,1,0:T(8,128)(2,1)S(1)}, bf16[16,8,96]{2,1,0:T(8,128)(2,1)S(1)}, u32[]{:S(2)}, u32[]{:S(2)}) collective-permute-start(bf16[16,8,96]{2,1,0:T(8,128)(2,1)S(1)} %get-tuple-element.72), channel_id=1, source_target_pairs={{0,1},{1,0},{2,3},{3,2},{4,5},{5,4},{6,7},{7,6},{8,9},{9,8},{10,11... | collective-permute-start | bytes 73736 | tf_op jit(solution)/shard_map/ppermute | solution.py:55
  7.0 0.9 %collective-permute-start.1 = (bf16[16,8,96]{2,1,0:T(8,128)(2,1)S(1)}, bf16[16,8,96]{2,1,0:T(8,128)(2,1)S(1)}, u32[]{:S(2)}, u32[]{:S(2)}) collective-permute-start(bf16[16,8,96]{2,1,0:T(8,128)(2,1)S(1)} %get-tuple-element.73), channel_id=1, source_target_pairs={{0,16},{1,2},{2,1},{3,4},{4,3},{5,6},{6,5},{7,8},{8,7},{9,10},{10,... | collective-permute-start | bytes 73736 | tf_op jit(solution)/shard_map/ppermute | solution.py:55
  8.0 0.8 %shard_map.110 = (bf16[256,768]{1,0:T(8,128)(2,1)S(1)}, bf16[768,256]{1,0:T(8,128)(2,1)S(1)}, bf16[256,768]{1,0:T(8,128)(2,1)S(1)}, bf16[768,256]{1,0:T(8,128)(2...) custom-call(bf16[2,96,384]{2,1,0:T(8,128)(2,1)S(1)} %copy-done.2, ...), custom_call_target="tpu_custom_call" | custom-call | flops 2000000000 | bytes 262144 | tf_op jit(solution)/shard_map/pallas_call | solution.py:836
  8.8 2.1 %collective-permute-done.1.refs_10_ = bf16[16,8,96]{2,1,0:T(8,128)(2,1)S(1)} collective-permute-done((bf16[16,8,96]{2,1,0:T(8,128)(2,1)S(1)}, bf16[16,8,96]{2,1,0:T(8,128)(2,1)S(1)}, u32[]{:S(2)}, u32[]{:S(2)}) %collective-permute-start.1) | collective-permute-done | bytes 24608 | tf_op jit(solution)/shard_map/ppermute | solution.py:55
  10.9 8.4 %shard_map.112 = (bf16[16,64,96]{2,1,0:T(8,128)(2,1)S(1)}, f32[2240,128]{1,0:T(8,128)S(1)}, f32[1600,128]{1,0:T(8,128)S(1)}, bf16[1376,128]{1,0:T(8,128)(2,1)S(1...) custom-call(bf16[16,64,96]{2,1,0:T(8,128)(2,1)S(1)} %get-tuple-eleme, ...), custom_call_target="tpu_custom_call" | custom-call | flops 15000000512 | bytes 262144 | tf_op jit(solution)/shard_map/pallas_call | solution.py:836
  19.3 1.0 %collective-permute-start.7 = (bf16[9,64,96]{2,1,0:T(8,128)(2,1)S(1)}, bf16[9,64,96]{2,1,0:T(8,128)(2,1)S(1)}, u32[]{:S(2)}, u32[]{:S(2)}) collective-permute-start(bf16[9,64,96]{2,1,0:T(8,128)(2,1)S(1)} %get-tuple-element.94.refs_0_), channel_id=1, source_target_pairs={{0,16},{1,17},{2,18},{3,19},{4,20},{5,21},{6,22},{7,23},{8,24},{9,... | collective-permute-start | bytes 331784 | tf_op jit(solution)/shard_map/ppermute | solution.py:55
  20.5 1.2 %collective-permute-start.9 = (bf16[9,8,96]{2,1,0:T(8,128)(2,1)S(1)}, bf16[9,8,96]{2,1,0:T(8,128)(2,1)S(1)}, u32[]{:S(2)}, u32[]{:S(2)}) collective-permute-start(bf16[9,8,96]{2,1,0:T(8,128)(2,1)S(1)} %get-tuple-element.98), channel_id=1, source_target_pairs={{0,16},{1,18},{2,17},{3,20},{4,19},{5,22},{6,21},{7,24},{8,23},{9,... | collective-permute-start | bytes 41480 | tf_op jit(solution)/shard_map/ppermute | solution.py:55
  21.6 1.6 %collective-permute-start.5 = (bf16[32,8,96]{2,1,0:T(8,128)(2,1)S(1)}, bf16[32,8,96]{2,1,0:T(8,128)(2,1)S(1)}, u32[]{:S(2)}, u32[]{:S(2)}) collective-permute-start(bf16[32,8,96]{2,1,0:T(8,128)(2,1)S(1)} %get-tuple-element.95), channel_id=1, source_target_pairs={{0,1},{1,0},{2,3},{3,2},{4,5},{5,4},{6,7},{7,6},{8,9},{9,8},{10,11... | collective-permute-start | bytes 147464 | tf_op jit(solution)/shard_map/ppermute | solution.py:55
  23.2 1.1 %collective-permute-start.6 = (bf16[32,8,96]{2,1,0:T(8,128)(2,1)S(1)}, bf16[32,8,96]{2,1,0:T(8,128)(2,1)S(1)}, u32[]{:S(2)}, u32[]{:S(2)}) collective-permute-start(bf16[32,8,96]{2,1,0:T(8,128)(2,1)S(1)} %get-tuple-element.96), channel_id=1, source_target_pairs={{0,16},{1,2},{2,1},{3,4},{4,3},{5,6},{6,5},{7,8},{8,7},{9,10},{10,... | collective-permute-start | bytes 147464 | tf_op jit(solution)/shard_map/ppermute | solution.py:55
  24.3 2.5 %shard_map.113 = (f32[56,128]{1,0:T(8,128)S(1)}, f32[776,128]{1,0:T(8,128)S(1)}, bf16[16,64,96]{2,1,0:T(8,128)(2,1)}) custom-call(f32[1600,128]{1,0:T(8,128)S(1)} %get-tuple-element.76.x1, f32[1024,128]{1,0:T(8,128)S(1)} %get-tuple-element.77.grad1.refs_0_, bf16[1024,128]{1,0:T(8,128)(2,1)S(1)} %get-tuple-element.78.normed1, ...), custom_call_target="tpu_custom_call" | custom-call | flops 3000000000 | bytes 262144 | tf_op jit(solution)/shard_map/pallas_call | solution.py:836
  27.5 5.4 %shard_map.115 = (f32[1600,128]{1,0:T(8,128)S(1)}, f32[1376,128]{1,0:T(8,128)S(1)}, f32[768,128]{1,0:T(8,128)S(1)}, f32[80,128]{1,0:T(8,128)S(1)}, bf16[848,128]{1,0:T(8,128)(2,1)S(1)}) custom-call(f32[1024,128]{1,0:T(8,128)S(1)} %get-tuple-element.77.grad1.refs_0_, bf16[16,64,96]{2,1,0:T(8,128)(2,1)S(1)} %copy-done.1, ...), custom_call_target="tpu_custom_call" | custom-call | flops 12000000000 | bytes 262144 | tf_op jit(solution)/shard_map/pallas_call | solution.py:836
  33.1 1.4 %collective-permute-done.10.refs_0_ = bf16[848,128]{1,0:T(8,128)(2,1)S(1)} collective-permute-done((bf16[848,128]{1,0:T(8,128)(2,1)S(1)}, bf16[848,128]{1,0:T(8,128)(2,1)S(1)}, u32[]{:S(2)}, u32[]{:S(2)}) %collective-permute-start.10) | collective-permute-done | bytes 217120 | tf_op jit(solution)/shard_map/ppermute | solution.py:972
  34.5 1.8 %collective-permute-start.11 = (bf16[272,128]{1,0:T(8,128)(2,1)S(1)}, bf16[272,128]{1,0:T(8,128)(2,1)S(1)}, u32[]{:S(2)}, u32[]{:S(2)}) collective-permute-start(bf16[272,128]{1,0:T(8,128)(2,1)S(1)} %get-tuple-element.107), channel_id=1, source_target_pairs={{0,2},{1,3},{2,0},{3,1},{4,6},{5,7},{6,4},{7,5},{8,10},{9,11},{10,... | collective-permute-start | bytes 208904 | tf_op jit(solution)/shard_map/ppermute | solution.py:972
  36.3 1.3 %collective-permute-start.12 = (bf16[272,128]{1,0:T(8,128)(2,1)S(1)}, bf16[272,128]{1,0:T(8,128)(2,1)S(1)}, u32[]{:S(2)}, u32[]{:S(2)}) collective-permute-start(bf16[272,128]{1,0:T(8,128)(2,1)S(1)} %get-tuple-element.108), channel_id=1, source_target_pairs={{0,16},{1,17},{2,18},{3,19},{4,20},{5,21},{6,22},{7,23},{8,24},{9,... | collective-permute-start | bytes 208904 | tf_op jit(solution)/shard_map/ppermute | solution.py:972
  38.1 2.1 %shard_map.117 = (bf16[16,64,96]{2,1,0:T(8,128)(2,1)}, f32[8,128]{1,0:T(8,128)S(1)}) custom-call(f32[1600,128]{1,0:T(8,128)S(1)} %get-tuple-element.99.grad0, f32[1376,128]{1,0:T(8,128)S(1)} %get-tuple-element.100.upstream, bf16[784,128]{1,0:T(8,128)(2,1)S(1)} %get-tuple-element.64.refs_2_.taps0, f32[80,128]{1,0:T(8,128)S(1)} %get-tuple-element.104.after.small), custom_call_target="tpu_custom_call" | custom-call | flops 3000000000 | bytes 262144 | tf_op jit(solution)/shard_map/pallas_call | solution.py:836
  40.2 1.1 %collective-permute-done.12.refs_1_ = bf16[272,128]{1,0:T(8,128)(2,1)S(1)} collective-permute-done((bf16[272,128]{1,0:T(8,128)(2,1)S(1)}, bf16[272,128]{1,0:T(8,128)(2,1)S(1)}, u32[]{:S(2)}, u32[]{:S(2)}) %collective-permute-start.12) | collective-permute-done | bytes 69664 | tf_op jit(solution)/shard_map/ppermute | solution.py:972
  41.3 1.5 %collective-permute-done.13.refs_2_ = bf16[272,128]{1,0:T(8,128)(2,1)S(1)} collective-permute-done((bf16[272,128]{1,0:T(8,128)(2,1)S(1)}, bf16[272,128]{1,0:T(8,128)(2,1)S(1)}, u32[]{:S(2)}, u32[]{:S(2)}) %collective-permute-start.13) | collective-permute-done | bytes 69664 | tf_op jit(solution)/shard_map/ppermute | solution.py:972
  42.8 2.7 %collective-permute-start.14 = (bf16[128,128]{1,0:T(8,128)(2,1)S(1)}, bf16[128,128]{1,0:T(8,128)(2,1)S(1)}, u32[]{:S(2)}, u32[]{:S(2)}) collective-permute-start(bf16[128,128]{1,0:T(8,128)(2,1)S(1)} %get-tuple-element.113), channel_id=1, source_target_pairs={{0,8},{1,9},{2,10},{3,11},{4,12},{5,13},{6,14},{7,15},{8,0},{9,1},... | collective-permute-start | bytes 98312 | tf_op jit(solution)/shard_map/ppermute | solution.py:972
  45.9 1.4 %collective-permute-start.16 = (bf16[128,128]{1,0:T(8,128)(2,1)S(1)}, bf16[128,128]{1,0:T(8,128)(2,1)S(1)}, u32[]{:S(2)}, u32[]{:S(2)}) collective-permute-start(bf16[128,128]{1,0:T(8,128)(2,1)S(1)} %get-tuple-element.115), channel_id=1, source_target_pairs={{0,12},{1,13},{2,14},{3,15},{4,8},{5,9},{6,10},{7,11},{8,4},{9,5},... | collective-permute-start | bytes 98312 | tf_op jit(solution)/shard_map/ppermute | solution.py:972
  47.8 1.7 %collective-permute-done.15.refs_1_ = bf16[128,128]{1,0:T(8,128)(2,1)S(1)} collective-permute-done((bf16[128,128]{1,0:T(8,128)(2,1)S(1)}, bf16[128,128]{1,0:T(8,128)(2,1)S(1)}, u32[]{:S(2)}, u32[]{:S(2)}) %collective-permute-start.15) | collective-permute-done | bytes 32800 | tf_op jit(solution)/shard_map/ppermute | solution.py:972
  49.5 2.1 %collective-permute-done.16.refs_2_ = bf16[128,128]{1,0:T(8,128)(2,1)S(1)} collective-permute-done((bf16[128,128]{1,0:T(8,128)(2,1)S(1)}, bf16[128,128]{1,0:T(8,128)(2,1)S(1)}, u32[]{:S(2)}, u32[]{:S(2)}) %collective-permute-start.16) | collective-permute-done | bytes 32800 | tf_op jit(solution)/shard_map/ppermute | solution.py:972
  (33 shorter events, 3.4 us)
Async XLA Ops:
  0.6 1.0 %copy-start = (bf16[16,64,96]{2,1,0:T(8,128)(2,1)S(1)}, bf16[16,64,96]{2,1,0:T(8,128)(2,1)}, u32[]{:S(2)}) copy-start(bf16[16,64,96]{2,1,0:T(8,128)(2,1)} %image_in.1) | copy-start | bytes 589828
  1.6 9.3 %collective-permute-start.2 = (bf16[6,64,96]{2,1,0:T(8,128)(2,1)S(1)}, bf16[6,64,96]{2,1,0:T(8,128)(2,1)S(1)}, u32[]{:S(2)}, u32[]{:S(2)}) collective-permute-start(bf16[6,64,96]{2,1,0:T(8,128)(2,1)S(1)} %get-tuple-element.71.refs_0_), channel_id=1, source_target_pairs={{0,16},{1,17},{2,18},{3,19},{4,20},{5,21},{6,22},{7,23},{8,24},{9,... | collective-permute-start | bytes 221192 | tf_op jit(solution)/shard_map/ppermute | solution.py:55
  4.7 3.3 %copy-start.2 = (bf16[2,96,384]{2,1,0:T(8,128)(2,1)S(1)}, bf16[2,96,384]{2,1,0:T(8,128)(2,1)}, u32[]{:S(2)}) copy-start(bf16[2,96,384]{2,1,0:T(8,128)(2,1)} %up_in.1) | copy-start | bytes 442372
  4.7 3.3 %copy-start.3 = (bf16[2,384,96]{1,2,0:T(8,128)(2,1)S(1)}, bf16[2,384,96]{1,2,0:T(8,128)(2,1)}, u32[]{:S(2)}) copy-start(bf16[2,384,96]{1,2,0:T(8,128)(2,1)} %param.10) | copy-start | bytes 442372
  4.7 3.3 %copy-start.4 = (f32[2,7,7,96]{3,0,2,1:T(2,128)S(1)}, f32[2,7,7,96]{3,0,2,1:T(2,128)}, u32[]{:S(2)}) copy-start(f32[2,7,7,96]{3,0,2,1:T(2,128)} %param.7) | copy-start | bytes 112900
  4.7 3.3 %copy-start.5 = (f32[2,96]{1,0:T(2,128)S(1)}, f32[2,96]{1,0:T(2,128)}, u32[]{:S(2)}) copy-start(f32[2,96]{1,0:T(2,128)} %gains_in.1) | copy-start | bytes 2308
  4.7 4.1 %collective-permute-start.3 = (bf16[6,8,96]{2,1,0:T(8,128)(2,1)S(1)}, bf16[6,8,96]{2,1,0:T(8,128)(2,1)S(1)}, u32[]{:S(2)}, u32[]{:S(2)}) collective-permute-start(bf16[6,8,96]{2,1,0:T(8,128)(2,1)S(1)} %get-tuple-element.74), channel_id=1, source_target_pairs={{0,17},{1,16},{2,19},{3,18},{4,21},{5,20},{6,23},{7,22},{8,25},{9,... | collective-permute-start | bytes 27656 | tf_op jit(solution)/shard_map/ppermute | solution.py:55
  4.8 4.0 %collective-permute-start.4 = (bf16[6,8,96]{2,1,0:T(8,128)(2,1)S(1)}, bf16[6,8,96]{2,1,0:T(8,128)(2,1)S(1)}, u32[]{:S(2)}, u32[]{:S(2)}) collective-permute-start(bf16[6,8,96]{2,1,0:T(8,128)(2,1)S(1)} %get-tuple-element.75), channel_id=1, source_target_pairs={{0,16},{1,18},{2,17},{3,20},{4,19},{5,22},{6,21},{7,24},{8,23},{9,... | collective-permute-start | bytes 27656 | tf_op jit(solution)/shard_map/ppermute | solution.py:55
  6.0 2.8 %collective-permute-start = (bf16[16,8,96]{2,1,0:T(8,128)(2,1)S(1)}, bf16[16,8,96]{2,1,0:T(8,128)(2,1)S(1)}, u32[]{:S(2)}, u32[]{:S(2)}) collective-permute-start(bf16[16,8,96]{2,1,0:T(8,128)(2,1)S(1)} %get-tuple-element.72), channel_id=1, source_target_pairs={{0,1},{1,0},{2,3},{3,2},{4,5},{5,4},{6,7},{7,6},{8,9},{9,8},{10,11... | collective-permute-start | bytes 73736 | tf_op jit(solution)/shard_map/ppermute | solution.py:55
  7.0 3.9 %collective-permute-start.1 = (bf16[16,8,96]{2,1,0:T(8,128)(2,1)S(1)}, bf16[16,8,96]{2,1,0:T(8,128)(2,1)S(1)}, u32[]{:S(2)}, u32[]{:S(2)}) collective-permute-start(bf16[16,8,96]{2,1,0:T(8,128)(2,1)S(1)} %get-tuple-element.73), channel_id=1, source_target_pairs={{0,16},{1,2},{2,1},{3,4},{4,3},{5,6},{6,5},{7,8},{8,7},{9,10},{10,... | collective-permute-start | bytes 73736 | tf_op jit(solution)/shard_map/ppermute | solution.py:55
  8.0 3.0 %copy-start.1 = (bf16[16,64,96]{2,1,0:T(8,128)(2,1)S(1)}, bf16[16,64,96]{2,1,0:T(8,128)(2,1)}, u32[]{:S(2)}) copy-start(bf16[16,64,96]{2,1,0:T(8,128)(2,1)} %refs_1_.3) | copy-start | bytes 589828
  19.3 8.1 %collective-permute-start.7 = (bf16[9,64,96]{2,1,0:T(8,128)(2,1)S(1)}, bf16[9,64,96]{2,1,0:T(8,128)(2,1)S(1)}, u32[]{:S(2)}, u32[]{:S(2)}) collective-permute-start(bf16[9,64,96]{2,1,0:T(8,128)(2,1)S(1)} %get-tuple-element.94.refs_0_), channel_id=1, source_target_pairs={{0,16},{1,17},{2,18},{3,19},{4,20},{5,21},{6,22},{7,23},{8,24},{9,... | collective-permute-start | bytes 331784 | tf_op jit(solution)/shard_map/ppermute | solution.py:55
  20.4 6.4 %collective-permute-start.8 = (bf16[9,8,96]{2,1,0:T(8,128)(2,1)S(1)}, bf16[9,8,96]{2,1,0:T(8,128)(2,1)S(1)}, u32[]{:S(2)}, u32[]{:S(2)}) collective-permute-start(bf16[9,8,96]{2,1,0:T(8,128)(2,1)S(1)} %get-tuple-element.97), channel_id=1, source_target_pairs={{0,17},{1,16},{2,19},{3,18},{4,21},{5,20},{6,23},{7,22},{8,25},{9,... | collective-permute-start | bytes 41480 | tf_op jit(solution)/shard_map/ppermute | solution.py:55
  20.5 6.3 %collective-permute-start.9 = (bf16[9,8,96]{2,1,0:T(8,128)(2,1)S(1)}, bf16[9,8,96]{2,1,0:T(8,128)(2,1)S(1)}, u32[]{:S(2)}, u32[]{:S(2)}) collective-permute-start(bf16[9,8,96]{2,1,0:T(8,128)(2,1)S(1)} %get-tuple-element.98), channel_id=1, source_target_pairs={{0,16},{1,18},{2,17},{3,20},{4,19},{5,22},{6,21},{7,24},{8,23},{9,... | collective-permute-start | bytes 41480 | tf_op jit(solution)/shard_map/ppermute | solution.py:55
  21.6 5.1 %collective-permute-start.5 = (bf16[32,8,96]{2,1,0:T(8,128)(2,1)S(1)}, bf16[32,8,96]{2,1,0:T(8,128)(2,1)S(1)}, u32[]{:S(2)}, u32[]{:S(2)}) collective-permute-start(bf16[32,8,96]{2,1,0:T(8,128)(2,1)S(1)} %get-tuple-element.95), channel_id=1, source_target_pairs={{0,1},{1,0},{2,3},{3,2},{4,5},{5,4},{6,7},{7,6},{8,9},{9,8},{10,11... | collective-permute-start | bytes 147464 | tf_op jit(solution)/shard_map/ppermute | solution.py:55
  23.2 4.3 %collective-permute-start.6 = (bf16[32,8,96]{2,1,0:T(8,128)(2,1)S(1)}, bf16[32,8,96]{2,1,0:T(8,128)(2,1)S(1)}, u32[]{:S(2)}, u32[]{:S(2)}) collective-permute-start(bf16[32,8,96]{2,1,0:T(8,128)(2,1)S(1)} %get-tuple-element.96), channel_id=1, source_target_pairs={{0,16},{1,2},{2,1},{3,4},{4,3},{5,6},{6,5},{7,8},{8,7},{9,10},{10,... | collective-permute-start | bytes 147464 | tf_op jit(solution)/shard_map/ppermute | solution.py:55
  32.9 1.5 %collective-permute-start.10 = (bf16[848,128]{1,0:T(8,128)(2,1)S(1)}, bf16[848,128]{1,0:T(8,128)(2,1)S(1)}, u32[]{:S(2)}, u32[]{:S(2)}) collective-permute-start(bf16[848,128]{1,0:T(8,128)(2,1)S(1)} %get-tuple-element.103), channel_id=1, source_target_pairs={{0,1},{1,0},{2,3},{3,2},{4,5},{5,4},{6,7},{7,6},{8,9},{9,8},{10,11... | collective-permute-start | bytes 651272 | tf_op jit(solution)/shard_map/ppermute | solution.py:972
  34.5 5.7 %collective-permute-start.11 = (bf16[272,128]{1,0:T(8,128)(2,1)S(1)}, bf16[272,128]{1,0:T(8,128)(2,1)S(1)}, u32[]{:S(2)}, u32[]{:S(2)}) collective-permute-start(bf16[272,128]{1,0:T(8,128)(2,1)S(1)} %get-tuple-element.107), channel_id=1, source_target_pairs={{0,2},{1,3},{2,0},{3,1},{4,6},{5,7},{6,4},{7,5},{8,10},{9,11},{10,... | collective-permute-start | bytes 208904 | tf_op jit(solution)/shard_map/ppermute | solution.py:972
  36.3 4.9 %collective-permute-start.12 = (bf16[272,128]{1,0:T(8,128)(2,1)S(1)}, bf16[272,128]{1,0:T(8,128)(2,1)S(1)}, u32[]{:S(2)}, u32[]{:S(2)}) collective-permute-start(bf16[272,128]{1,0:T(8,128)(2,1)S(1)} %get-tuple-element.108), channel_id=1, source_target_pairs={{0,16},{1,17},{2,18},{3,19},{4,20},{5,21},{6,22},{7,23},{8,24},{9,... | collective-permute-start | bytes 208904 | tf_op jit(solution)/shard_map/ppermute | solution.py:972
  37.6 5.2 %collective-permute-start.13 = (bf16[272,128]{1,0:T(8,128)(2,1)S(1)}, bf16[272,128]{1,0:T(8,128)(2,1)S(1)}, u32[]{:S(2)}, u32[]{:S(2)}) collective-permute-start(bf16[272,128]{1,0:T(8,128)(2,1)S(1)} %get-tuple-element.109), channel_id=1, source_target_pairs={{0,18},{1,19},{2,16},{3,17},{4,22},{5,23},{6,20},{7,21},{8,26},{9,... | collective-permute-start | bytes 208904 | tf_op jit(solution)/shard_map/ppermute | solution.py:972
  42.8 5.0 %collective-permute-start.14 = (bf16[128,128]{1,0:T(8,128)(2,1)S(1)}, bf16[128,128]{1,0:T(8,128)(2,1)S(1)}, u32[]{:S(2)}, u32[]{:S(2)}) collective-permute-start(bf16[128,128]{1,0:T(8,128)(2,1)S(1)} %get-tuple-element.113), channel_id=1, source_target_pairs={{0,8},{1,9},{2,10},{3,11},{4,12},{5,13},{6,14},{7,15},{8,0},{9,1},... | collective-permute-start | bytes 98312 | tf_op jit(solution)/shard_map/ppermute | solution.py:972
  45.5 4.0 %collective-permute-start.15 = (bf16[128,128]{1,0:T(8,128)(2,1)S(1)}, bf16[128,128]{1,0:T(8,128)(2,1)S(1)}, u32[]{:S(2)}, u32[]{:S(2)}) collective-permute-start(bf16[128,128]{1,0:T(8,128)(2,1)S(1)} %get-tuple-element.114), channel_id=1, source_target_pairs={{0,4},{1,5},{2,6},{3,7},{4,0},{5,1},{6,2},{7,3},{8,12},{9,13},{10,... | collective-permute-start | bytes 98312 | tf_op jit(solution)/shard_map/ppermute | solution.py:972
  45.9 5.7 %collective-permute-start.16 = (bf16[128,128]{1,0:T(8,128)(2,1)S(1)}, bf16[128,128]{1,0:T(8,128)(2,1)S(1)}, u32[]{:S(2)}, u32[]{:S(2)}) collective-permute-start(bf16[128,128]{1,0:T(8,128)(2,1)S(1)} %get-tuple-element.115), channel_id=1, source_target_pairs={{0,12},{1,13},{2,14},{3,15},{4,8},{5,9},{6,10},{7,11},{8,4},{9,5},... | collective-permute-start | bytes 98312 | tf_op jit(solution)/shard_map/ppermute | solution.py:972

commit v15 on v14

--- a/solution.py
+++ b/solution.py
@@ -643,7 +643,7 @@
             grad = yield from norm_backward(normed_grad, unit, inv0[at : at + n, :], gain, channels, ones)
             grad0[pl.ds(frame + at, n), :] = grad
 
-    together([mix0(start, n) for start, n in pieces(half_px, dims.piece)])
+    together([mix0(start, n) for start, n in pieces(half_px, dims.back_piece)])
     clear_outside(place, grad0, dims)
     kernel_sums(
         x0, h * wide + SIDE - h, wide, grad0, h * ext_cols + margin, ext_cols, rows, cols, size, sums
@@ -800,7 +800,8 @@
     d.wide = d.cols + 2 * SIDE
     d.ext_pad = -(-d.ext_rows * d.ext_cols // 32) * 32
     d.piece = 176
-    d.line_step = 4
+    d.back_piece = 128
+    d.line_step = 2
     d.half = d.channels // d.row_count
     d.part = up_weights.shape[2] // d.col_count
     d.layer_rows = ceil8(d.part)

time: 52.5 us -> 52.7 us (level)
  no operation moved by 1% of the time
where the time goes in v15:
time: 52.7 us; the launch traced here: 52.6 us
  Pallas kernels  20.4 us (39%)
  starting transfers between devices  19.3 us (37%)
  waiting for transfers between devices  11.2 us (21%)
  local copies, waits for them, and re-layouts  0.96 us (2%)
  between operations  0.76 us (1%)
    pallas_call x11, Pallas kernels, run(): pl.pallas_call(kernel, out_shape=shapes, in_specs=[far] * in_hbm + [space...  20.4 us
    ppermute x10, starting transfers between devices, exchange(): lax.ppermute(strip, ('row', 'col'), swap_pairs(row_count, col_count, rs,...  11.1 us
    ppermute x7, waiting for transfers between devices, per_device(): lax.ppermute(x, axes, swap_by(d, group, mask))  8.29 us
    ppermute x7, starting transfers between devices, per_device(): lax.ppermute(x, axes, swap_by(d, group, mask))  8.19 us
    ppermute x10, waiting for transfers between devices, exchange(): lax.ppermute(strip, ('row', 'col'), swap_pairs(row_count, col_count, rs,...  2.86 us
  transfers between devices with their start and end apart: 17, of which 8 were waited for; matrix products, arithmetic and copies ran while one was open for 0% of the time, Pallas kernels for 10%

profile of v15, /device:TPU:0, one launch (start us, length us, event | category | flops | bytes accessed | tf_op | source)
XLA Modules:
  0.0 52.6 jit_solution(15675557693106573851)
XLA Ops:
  0.6 0.9 %copy-done = bf16[16,64,96]{2,1,0:T(8,128)(2,1)S(1)} copy-done((bf16[16,64,96]{2,1,0:T(8,128)(2,1)S(1)}, bf16[16,64,96]{2,1,0:T(8,128)(2,1)}, u32[]{:S(2)}) %copy-start) | copy-done | bytes 196632
  1.6 3.0 %collective-permute-start.2 = (bf16[6,64,96]{2,1,0:T(8,128)(2,1)S(1)}, bf16[6,64,96]{2,1,0:T(8,128)(2,1)S(1)}, u32[]{:S(2)}, u32[]{:S(2)}) collective-permute-start(bf16[6,64,96]{2,1,0:T(8,128)(2,1)S(1)} %get-tuple-element.71.refs_0_), channel_id=1, source_target_pairs={{0,16},{1,17},{2,18},{3,19},{4,20},{5,21},{6,22},{7,23},{8,24},{9,... | collective-permute-start | bytes 221192 | tf_op jit(solution)/shard_map/ppermute | solution.py:55
  4.8 1.2 %collective-permute-start.4 = (bf16[6,8,96]{2,1,0:T(8,128)(2,1)S(1)}, bf16[6,8,96]{2,1,0:T(8,128)(2,1)S(1)}, u32[]{:S(2)}, u32[]{:S(2)}) collective-permute-start(bf16[6,8,96]{2,1,0:T(8,128)(2,1)S(1)} %get-tuple-element.75), channel_id=1, source_target_pairs={{0,16},{1,18},{2,17},{3,20},{4,19},{5,22},{6,21},{7,24},{8,23},{9,... | collective-permute-start | bytes 27656 | tf_op jit(solution)/shard_map/ppermute | solution.py:55
  6.0 1.1 %collective-permute-start = (bf16[16,8,96]{2,1,0:T(8,128)(2,1)S(1)}, bf16[16,8,96]{2,1,0:T(8,128)(2,1)S(1)}, u32[]{:S(2)}, u32[]{:S(2)}) collective-permute-start(bf16[16,8,96]{2,1,0:T(8,128)(2,1)S(1)} %get-tuple-element.72), channel_id=1, source_target_pairs={{0,1},{1,0},{2,3},{3,2},{4,5},{5,4},{6,7},{7,6},{8,9},{9,8},{10,11... | collective-permute-start | bytes 73736 | tf_op jit(solution)/shard_map/ppermute | solution.py:55
  7.0 0.9 %collective-permute-start.1 = (bf16[16,8,96]{2,1,0:T(8,128)(2,1)S(1)}, bf16[16,8,96]{2,1,0:T(8,128)(2,1)S(1)}, u32[]{:S(2)}, u32[]{:S(2)}) collective-permute-start(bf16[16,8,96]{2,1,0:T(8,128)(2,1)S(1)} %get-tuple-element.73), channel_id=1, source_target_pairs={{0,16},{1,2},{2,1},{3,4},{4,3},{5,6},{6,5},{7,8},{8,7},{9,10},{10,... | collective-permute-start | bytes 73736 | tf_op jit(solution)/shard_map/ppermute | solution.py:55
  8.0 0.8 %shard_map.110 = (bf16[256,768]{1,0:T(8,128)(2,1)S(1)}, bf16[768,256]{1,0:T(8,128)(2,1)S(1)}, bf16[256,768]{1,0:T(8,128)(2,1)S(1)}, bf16[768,256]{1,0:T(8,128)(2...) custom-call(bf16[2,96,384]{2,1,0:T(8,128)(2,1)S(1)} %copy-done.2, ...), custom_call_target="tpu_custom_call" | custom-call | flops 2000000000 | bytes 262144 | tf_op jit(solution)/shard_map/pallas_call | solution.py:837
  8.8 2.1 %collective-permute-done.1.refs_10_ = bf16[16,8,96]{2,1,0:T(8,128)(2,1)S(1)} collective-permute-done((bf16[16,8,96]{2,1,0:T(8,128)(2,1)S(1)}, bf16[16,8,96]{2,1,0:T(8,128)(2,1)S(1)}, u32[]{:S(2)}, u32[]{:S(2)}) %collective-permute-start.1) | collective-permute-done | bytes 24608 | tf_op jit(solution)/shard_map/ppermute | solution.py:55
  10.9 8.6 %shard_map.112 = (bf16[16,64,96]{2,1,0:T(8,128)(2,1)S(1)}, f32[2240,128]{1,0:T(8,128)S(1)}, f32[1600,128]{1,0:T(8,128)S(1)}, bf16[1376,128]{1,0:T(8,128)(2,1)S(1...) custom-call(bf16[16,64,96]{2,1,0:T(8,128)(2,1)S(1)} %get-tuple-eleme, ...), custom_call_target="tpu_custom_call" | custom-call | flops 15000000512 | bytes 262144 | tf_op jit(solution)/shard_map/pallas_call | solution.py:837
  19.5 1.0 %collective-permute-start.7 = (bf16[9,64,96]{2,1,0:T(8,128)(2,1)S(1)}, bf16[9,64,96]{2,1,0:T(8,128)(2,1)S(1)}, u32[]{:S(2)}, u32[]{:S(2)}) collective-permute-start(bf16[9,64,96]{2,1,0:T(8,128)(2,1)S(1)} %get-tuple-element.94.refs_0_), channel_id=1, source_target_pairs={{0,16},{1,17},{2,18},{3,19},{4,20},{5,21},{6,22},{7,23},{8,24},{9,... | collective-permute-start | bytes 331784 | tf_op jit(solution)/shard_map/ppermute | solution.py:55
  20.6 1.1 %collective-permute-start.9 = (bf16[9,8,96]{2,1,0:T(8,128)(2,1)S(1)}, bf16[9,8,96]{2,1,0:T(8,128)(2,1)S(1)}, u32[]{:S(2)}, u32[]{:S(2)}) collective-permute-start(bf16[9,8,96]{2,1,0:T(8,128)(2,1)S(1)} %get-tuple-element.98), channel_id=1, source_target_pairs={{0,16},{1,18},{2,17},{3,20},{4,19},{5,22},{6,21},{7,24},{8,23},{9,... | collective-permute-start | bytes 41480 | tf_op jit(solution)/shard_map/ppermute | solution.py:55
  21.8 1.6 %collective-permute-start.5 = (bf16[32,8,96]{2,1,0:T(8,128)(2,1)S(1)}, bf16[32,8,96]{2,1,0:T(8,128)(2,1)S(1)}, u32[]{:S(2)}, u32[]{:S(2)}) collective-permute-start(bf16[32,8,96]{2,1,0:T(8,128)(2,1)S(1)} %get-tuple-element.95), channel_id=1, source_target_pairs={{0,1},{1,0},{2,3},{3,2},{4,5},{5,4},{6,7},{7,6},{8,9},{9,8},{10,11... | collective-permute-start | bytes 147464 | tf_op jit(solution)/shard_map/ppermute | solution.py:55
  23.4 1.1 %collective-permute-start.6 = (bf16[32,8,96]{2,1,0:T(8,128)(2,1)S(1)}, bf16[32,8,96]{2,1,0:T(8,128)(2,1)S(1)}, u32[]{:S(2)}, u32[]{:S(2)}) collective-permute-start(bf16[32,8,96]{2,1,0:T(8,128)(2,1)S(1)} %get-tuple-element.96), channel_id=1, source_target_pairs={{0,16},{1,2},{2,1},{3,4},{4,3},{5,6},{6,5},{7,8},{8,7},{9,10},{10,... | collective-permute-start | bytes 147464 | tf_op jit(solution)/shard_map/ppermute | solution.py:55
  24.5 2.5 %shard_map.113 = (f32[56,128]{1,0:T(8,128)S(1)}, f32[776,128]{1,0:T(8,128)S(1)}, bf16[16,64,96]{2,1,0:T(8,128)(2,1)}) custom-call(f32[1600,128]{1,0:T(8,128)S(1)} %get-tuple-element.76.x1, f32[1024,128]{1,0:T(8,128)S(1)} %get-tuple-element.77.grad1.refs_0_, bf16[1024,128]{1,0:T(8,128)(2,1)S(1)} %get-tuple-element.78.normed1, ...), custom_call_target="tpu_custom_call" | custom-call | flops 3000000000 | bytes 262144 | tf_op jit(solution)/shard_map/pallas_call | solution.py:837
  27.6 5.5 %shard_map.115 = (f32[1600,128]{1,0:T(8,128)S(1)}, f32[1376,128]{1,0:T(8,128)S(1)}, f32[768,128]{1,0:T(8,128)S(1)}, f32[80,128]{1,0:T(8,128)S(1)}, bf16[848,128]{1,0:T(8,128)(2,1)S(1)}) custom-call(f32[1024,128]{1,0:T(8,128)S(1)} %get-tuple-element.77.grad1.refs_0_, bf16[16,64,96]{2,1,0:T(8,128)(2,1)S(1)} %copy-done.1, ...), custom_call_target="tpu_custom_call" | custom-call | flops 12000000000 | bytes 262144 | tf_op jit(solution)/shard_map/pallas_call | solution.py:837
  33.3 1.3 %collective-permute-done.10.refs_0_ = bf16[848,128]{1,0:T(8,128)(2,1)S(1)} collective-permute-done((bf16[848,128]{1,0:T(8,128)(2,1)S(1)}, bf16[848,128]{1,0:T(8,128)(2,1)S(1)}, u32[]{:S(2)}, u32[]{:S(2)}) %collective-permute-start.10) | collective-permute-done | bytes 217120 | tf_op jit(solution)/shard_map/ppermute | solution.py:973
  34.7 1.8 %collective-permute-start.11 = (bf16[272,128]{1,0:T(8,128)(2,1)S(1)}, bf16[272,128]{1,0:T(8,128)(2,1)S(1)}, u32[]{:S(2)}, u32[]{:S(2)}) collective-permute-start(bf16[272,128]{1,0:T(8,128)(2,1)S(1)} %get-tuple-element.107), channel_id=1, source_target_pairs={{0,2},{1,3},{2,0},{3,1},{4,6},{5,7},{6,4},{7,5},{8,10},{9,11},{10,... | collective-permute-start | bytes 208904 | tf_op jit(solution)/shard_map/ppermute | solution.py:973
  36.6 1.2 %collective-permute-start.12 = (bf16[272,128]{1,0:T(8,128)(2,1)S(1)}, bf16[272,128]{1,0:T(8,128)(2,1)S(1)}, u32[]{:S(2)}, u32[]{:S(2)}) collective-permute-start(bf16[272,128]{1,0:T(8,128)(2,1)S(1)} %get-tuple-element.108), channel_id=1, source_target_pairs={{0,16},{1,17},{2,18},{3,19},{4,20},{5,21},{6,22},{7,23},{8,24},{9,... | collective-permute-start | bytes 208904 | tf_op jit(solution)/shard_map/ppermute | solution.py:973
  38.3 2.1 %shard_map.117 = (bf16[16,64,96]{2,1,0:T(8,128)(2,1)}, f32[8,128]{1,0:T(8,128)S(1)}) custom-call(f32[1600,128]{1,0:T(8,128)S(1)} %get-tuple-element.99.grad0, f32[1376,128]{1,0:T(8,128)S(1)} %get-tuple-element.100.upstream, bf16[784,128]{1,0:T(8,128)(2,1)S(1)} %get-tuple-element.64.refs_2_.taps0, f32[80,128]{1,0:T(8,128)S(1)} %get-tuple-element.104.after.small), custom_call_target="tpu_custom_call" | custom-call | flops 3000000000 | bytes 262144 | tf_op jit(solution)/shard_map/pallas_call | solution.py:837
  40.4 1.1 %collective-permute-done.12.refs_1_ = bf16[272,128]{1,0:T(8,128)(2,1)S(1)} collective-permute-done((bf16[272,128]{1,0:T(8,128)(2,1)S(1)}, bf16[272,128]{1,0:T(8,128)(2,1)S(1)}, u32[]{:S(2)}, u32[]{:S(2)}) %collective-permute-start.12) | collective-permute-done | bytes 69664 | tf_op jit(solution)/shard_map/ppermute | solution.py:973
  41.5 1.5 %collective-permute-done.13.refs_2_ = bf16[272,128]{1,0:T(8,128)(2,1)S(1)} collective-permute-done((bf16[272,128]{1,0:T(8,128)(2,1)S(1)}, bf16[272,128]{1,0:T(8,128)(2,1)S(1)}, u32[]{:S(2)}, u32[]{:S(2)}) %collective-permute-start.13) | collective-permute-done | bytes 69664 | tf_op jit(solution)/shard_map/ppermute | solution.py:973
  43.1 2.7 %collective-permute-start.14 = (bf16[128,128]{1,0:T(8,128)(2,1)S(1)}, bf16[128,128]{1,0:T(8,128)(2,1)S(1)}, u32[]{:S(2)}, u32[]{:S(2)}) collective-permute-start(bf16[128,128]{1,0:T(8,128)(2,1)S(1)} %get-tuple-element.113), channel_id=1, source_target_pairs={{0,8},{1,9},{2,10},{3,11},{4,12},{5,13},{6,14},{7,15},{8,0},{9,1},... | collective-permute-start | bytes 98312 | tf_op jit(solution)/shard_map/ppermute | solution.py:973
  46.2 1.4 %collective-permute-start.16 = (bf16[128,128]{1,0:T(8,128)(2,1)S(1)}, bf16[128,128]{1,0:T(8,128)(2,1)S(1)}, u32[]{:S(2)}, u32[]{:S(2)}) collective-permute-start(bf16[128,128]{1,0:T(8,128)(2,1)S(1)} %get-tuple-element.115), channel_id=1, source_target_pairs={{0,12},{1,13},{2,14},{3,15},{4,8},{5,9},{6,10},{7,11},{8,4},{9,5},... | collective-permute-start | bytes 98312 | tf_op jit(solution)/shard_map/ppermute | solution.py:973
  48.0 1.7 %collective-permute-done.15.refs_1_ = bf16[128,128]{1,0:T(8,128)(2,1)S(1)} collective-permute-done((bf16[128,128]{1,0:T(8,128)(2,1)S(1)}, bf16[128,128]{1,0:T(8,128)(2,1)S(1)}, u32[]{:S(2)}, u32[]{:S(2)}) %collective-permute-start.15) | collective-permute-done | bytes 32800 | tf_op jit(solution)/shard_map/ppermute | solution.py:973
  49.7 2.1 %collective-permute-done.16.refs_2_ = bf16[128,128]{1,0:T(8,128)(2,1)S(1)} collective-permute-done((bf16[128,128]{1,0:T(8,128)(2,1)S(1)}, bf16[128,128]{1,0:T(8,128)(2,1)S(1)}, u32[]{:S(2)}, u32[]{:S(2)}) %collective-permute-start.16) | collective-permute-done | bytes 32800 | tf_op jit(solution)/shard_map/ppermute | solution.py:973
  (33 shorter events, 3.5 us)
Async XLA Ops:
  0.6 1.0 %copy-start = (bf16[16,64,96]{2,1,0:T(8,128)(2,1)S(1)}, bf16[16,64,96]{2,1,0:T(8,128)(2,1)}, u32[]{:S(2)}) copy-start(bf16[16,64,96]{2,1,0:T(8,128)(2,1)} %image_in.1) | copy-start | bytes 589828
  1.6 9.3 %collective-permute-start.2 = (bf16[6,64,96]{2,1,0:T(8,128)(2,1)S(1)}, bf16[6,64,96]{2,1,0:T(8,128)(2,1)S(1)}, u32[]{:S(2)}, u32[]{:S(2)}) collective-permute-start(bf16[6,64,96]{2,1,0:T(8,128)(2,1)S(1)} %get-tuple-element.71.refs_0_), channel_id=1, source_target_pairs={{0,16},{1,17},{2,18},{3,19},{4,20},{5,21},{6,22},{7,23},{8,24},{9,... | collective-permute-start | bytes 221192 | tf_op jit(solution)/shard_map/ppermute | solution.py:55
  4.7 3.3 %copy-start.2 = (bf16[2,96,384]{2,1,0:T(8,128)(2,1)S(1)}, bf16[2,96,384]{2,1,0:T(8,128)(2,1)}, u32[]{:S(2)}) copy-start(bf16[2,96,384]{2,1,0:T(8,128)(2,1)} %up_in.1) | copy-start | bytes 442372
  4.7 3.3 %copy-start.3 = (bf16[2,384,96]{1,2,0:T(8,128)(2,1)S(1)}, bf16[2,384,96]{1,2,0:T(8,128)(2,1)}, u32[]{:S(2)}) copy-start(bf16[2,384,96]{1,2,0:T(8,128)(2,1)} %param.10) | copy-start | bytes 442372
  4.7 3.3 %copy-start.4 = (f32[2,7,7,96]{3,0,2,1:T(2,128)S(1)}, f32[2,7,7,96]{3,0,2,1:T(2,128)}, u32[]{:S(2)}) copy-start(f32[2,7,7,96]{3,0,2,1:T(2,128)} %param.7) | copy-start | bytes 112900
  4.7 3.3 %copy-start.5 = (f32[2,96]{1,0:T(2,128)S(1)}, f32[2,96]{1,0:T(2,128)}, u32[]{:S(2)}) copy-start(f32[2,96]{1,0:T(2,128)} %gains_in.1) | copy-start | bytes 2308
  4.7 4.1 %collective-permute-start.3 = (bf16[6,8,96]{2,1,0:T(8,128)(2,1)S(1)}, bf16[6,8,96]{2,1,0:T(8,128)(2,1)S(1)}, u32[]{:S(2)}, u32[]{:S(2)}) collective-permute-start(bf16[6,8,96]{2,1,0:T(8,128)(2,1)S(1)} %get-tuple-element.74), channel_id=1, source_target_pairs={{0,17},{1,16},{2,19},{3,18},{4,21},{5,20},{6,23},{7,22},{8,25},{9,... | collective-permute-start | bytes 27656 | tf_op jit(solution)/shard_map/ppermute | solution.py:55
  4.8 4.0 %collective-permute-start.4 = (bf16[6,8,96]{2,1,0:T(8,128)(2,1)S(1)}, bf16[6,8,96]{2,1,0:T(8,128)(2,1)S(1)}, u32[]{:S(2)}, u32[]{:S(2)}) collective-permute-start(bf16[6,8,96]{2,1,0:T(8,128)(2,1)S(1)} %get-tuple-element.75), channel_id=1, source_target_pairs={{0,16},{1,18},{2,17},{3,20},{4,19},{5,22},{6,21},{7,24},{8,23},{9,... | collective-permute-start | bytes 27656 | tf_op jit(solution)/shard_map/ppermute | solution.py:55
  6.0 2.8 %collective-permute-start = (bf16[16,8,96]{2,1,0:T(8,128)(2,1)S(1)}, bf16[16,8,96]{2,1,0:T(8,128)(2,1)S(1)}, u32[]{:S(2)}, u32[]{:S(2)}) collective-permute-start(bf16[16,8,96]{2,1,0:T(8,128)(2,1)S(1)} %get-tuple-element.72), channel_id=1, source_target_pairs={{0,1},{1,0},{2,3},{3,2},{4,5},{5,4},{6,7},{7,6},{8,9},{9,8},{10,11... | collective-permute-start | bytes 73736 | tf_op jit(solution)/shard_map/ppermute | solution.py:55
  7.0 3.9 %collective-permute-start.1 = (bf16[16,8,96]{2,1,0:T(8,128)(2,1)S(1)}, bf16[16,8,96]{2,1,0:T(8,128)(2,1)S(1)}, u32[]{:S(2)}, u32[]{:S(2)}) collective-permute-start(bf16[16,8,96]{2,1,0:T(8,128)(2,1)S(1)} %get-tuple-element.73), channel_id=1, source_target_pairs={{0,16},{1,2},{2,1},{3,4},{4,3},{5,6},{6,5},{7,8},{8,7},{9,10},{10,... | collective-permute-start | bytes 73736 | tf_op jit(solution)/shard_map/ppermute | solution.py:55
  8.0 3.0 %copy-start.1 = (bf16[16,64,96]{2,1,0:T(8,128)(2,1)S(1)}, bf16[16,64,96]{2,1,0:T(8,128)(2,1)}, u32[]{:S(2)}) copy-start(bf16[16,64,96]{2,1,0:T(8,128)(2,1)} %refs_1_.3) | copy-start | bytes 589828
  19.5 8.1 %collective-permute-start.7 = (bf16[9,64,96]{2,1,0:T(8,128)(2,1)S(1)}, bf16[9,64,96]{2,1,0:T(8,128)(2,1)S(1)}, u32[]{:S(2)}, u32[]{:S(2)}) collective-permute-start(bf16[9,64,96]{2,1,0:T(8,128)(2,1)S(1)} %get-tuple-element.94.refs_0_), channel_id=1, source_target_pairs={{0,16},{1,17},{2,18},{3,19},{4,20},{5,21},{6,22},{7,23},{8,24},{9,... | collective-permute-start | bytes 331784 | tf_op jit(solution)/shard_map/ppermute | solution.py:55
  20.6 6.4 %collective-permute-start.8 = (bf16[9,8,96]{2,1,0:T(8,128)(2,1)S(1)}, bf16[9,8,96]{2,1,0:T(8,128)(2,1)S(1)}, u32[]{:S(2)}, u32[]{:S(2)}) collective-permute-start(bf16[9,8,96]{2,1,0:T(8,128)(2,1)S(1)} %get-tuple-element.97), channel_id=1, source_target_pairs={{0,17},{1,16},{2,19},{3,18},{4,21},{5,20},{6,23},{7,22},{8,25},{9,... | collective-permute-start | bytes 41480 | tf_op jit(solution)/shard_map/ppermute | solution.py:55
  20.6 6.3 %collective-permute-start.9 = (bf16[9,8,96]{2,1,0:T(8,128)(2,1)S(1)}, bf16[9,8,96]{2,1,0:T(8,128)(2,1)S(1)}, u32[]{:S(2)}, u32[]{:S(2)}) collective-permute-start(bf16[9,8,96]{2,1,0:T(8,128)(2,1)S(1)} %get-tuple-element.98), channel_id=1, source_target_pairs={{0,16},{1,18},{2,17},{3,20},{4,19},{5,22},{6,21},{7,24},{8,23},{9,... | collective-permute-start | bytes 41480 | tf_op jit(solution)/shard_map/ppermute | solution.py:55
  21.8 5.1 %collective-permute-start.5 = (bf16[32,8,96]{2,1,0:T(8,128)(2,1)S(1)}, bf16[32,8,96]{2,1,0:T(8,128)(2,1)S(1)}, u32[]{:S(2)}, u32[]{:S(2)}) collective-permute-start(bf16[32,8,96]{2,1,0:T(8,128)(2,1)S(1)} %get-tuple-element.95), channel_id=1, source_target_pairs={{0,1},{1,0},{2,3},{3,2},{4,5},{5,4},{6,7},{7,6},{8,9},{9,8},{10,11... | collective-permute-start | bytes 147464 | tf_op jit(solution)/shard_map/ppermute | solution.py:55
  23.4 4.3 %collective-permute-start.6 = (bf16[32,8,96]{2,1,0:T(8,128)(2,1)S(1)}, bf16[32,8,96]{2,1,0:T(8,128)(2,1)S(1)}, u32[]{:S(2)}, u32[]{:S(2)}) collective-permute-start(bf16[32,8,96]{2,1,0:T(8,128)(2,1)S(1)} %get-tuple-element.96), channel_id=1, source_target_pairs={{0,16},{1,2},{2,1},{3,4},{4,3},{5,6},{6,5},{7,8},{8,7},{9,10},{10,... | collective-permute-start | bytes 147464 | tf_op jit(solution)/shard_map/ppermute | solution.py:55
  33.1 1.5 %collective-permute-start.10 = (bf16[848,128]{1,0:T(8,128)(2,1)S(1)}, bf16[848,128]{1,0:T(8,128)(2,1)S(1)}, u32[]{:S(2)}, u32[]{:S(2)}) collective-permute-start(bf16[848,128]{1,0:T(8,128)(2,1)S(1)} %get-tuple-element.103), channel_id=1, source_target_pairs={{0,1},{1,0},{2,3},{3,2},{4,5},{5,4},{6,7},{7,6},{8,9},{9,8},{10,11... | collective-permute-start | bytes 651272 | tf_op jit(solution)/shard_map/ppermute | solution.py:973
  34.7 5.7 %collective-permute-start.11 = (bf16[272,128]{1,0:T(8,128)(2,1)S(1)}, bf16[272,128]{1,0:T(8,128)(2,1)S(1)}, u32[]{:S(2)}, u32[]{:S(2)}) collective-permute-start(bf16[272,128]{1,0:T(8,128)(2,1)S(1)} %get-tuple-element.107), channel_id=1, source_target_pairs={{0,2},{1,3},{2,0},{3,1},{4,6},{5,7},{6,4},{7,5},{8,10},{9,11},{10,... | collective-permute-start | bytes 208904 | tf_op jit(solution)/shard_map/ppermute | solution.py:973
  36.6 4.9 %collective-permute-start.12 = (bf16[272,128]{1,0:T(8,128)(2,1)S(1)}, bf16[272,128]{1,0:T(8,128)(2,1)S(1)}, u32[]{:S(2)}, u32[]{:S(2)}) collective-permute-start(bf16[272,128]{1,0:T(8,128)(2,1)S(1)} %get-tuple-element.108), channel_id=1, source_target_pairs={{0,16},{1,17},{2,18},{3,19},{4,20},{5,21},{6,22},{7,23},{8,24},{9,... | collective-permute-start | bytes 208904 | tf_op jit(solution)/shard_map/ppermute | solution.py:973
  37.8 5.2 %collective-permute-start.13 = (bf16[272,128]{1,0:T(8,128)(2,1)S(1)}, bf16[272,128]{1,0:T(8,128)(2,1)S(1)}, u32[]{:S(2)}, u32[]{:S(2)}) collective-permute-start(bf16[272,128]{1,0:T(8,128)(2,1)S(1)} %get-tuple-element.109), channel_id=1, source_target_pairs={{0,18},{1,19},{2,16},{3,17},{4,22},{5,23},{6,20},{7,21},{8,26},{9,... | collective-permute-start | bytes 208904 | tf_op jit(solution)/shard_map/ppermute | solution.py:973
  43.1 5.0 %collective-permute-start.14 = (bf16[128,128]{1,0:T(8,128)(2,1)S(1)}, bf16[128,128]{1,0:T(8,128)(2,1)S(1)}, u32[]{:S(2)}, u32[]{:S(2)}) collective-permute-start(bf16[128,128]{1,0:T(8,128)(2,1)S(1)} %get-tuple-element.113), channel_id=1, source_target_pairs={{0,8},{1,9},{2,10},{3,11},{4,12},{5,13},{6,14},{7,15},{8,0},{9,1},... | collective-permute-start | bytes 98312 | tf_op jit(solution)/shard_map/ppermute | solution.py:973
  45.7 4.0 %collective-permute-start.15 = (bf16[128,128]{1,0:T(8,128)(2,1)S(1)}, bf16[128,128]{1,0:T(8,128)(2,1)S(1)}, u32[]{:S(2)}, u32[]{:S(2)}) collective-permute-start(bf16[128,128]{1,0:T(8,128)(2,1)S(1)} %get-tuple-element.114), channel_id=1, source_target_pairs={{0,4},{1,5},{2,6},{3,7},{4,0},{5,1},{6,2},{7,3},{8,12},{9,13},{10,... | collective-permute-start | bytes 98312 | tf_op jit(solution)/shard_map/ppermute | solution.py:973
  46.2 5.7 %collective-permute-start.16 = (bf16[128,128]{1,0:T(8,128)(2,1)S(1)}, bf16[128,128]{1,0:T(8,128)(2,1)S(1)}, u32[]{:S(2)}, u32[]{:S(2)}) collective-permute-start(bf16[128,128]{1,0:T(8,128)(2,1)S(1)} %get-tuple-element.115), channel_id=1, source_target_pairs={{0,12},{1,13},{2,14},{3,15},{4,8},{5,9},{6,10},{7,11},{8,4},{9,5},... | collective-permute-start | bytes 98312 | tf_op jit(solution)/shard_map/ppermute | solution.py:973

commit v16 on v14

--- a/solution.py
+++ b/solution.py
@@ -809,7 +809,7 @@
     d.factor = 1.0 / math.sqrt(d.rows * d.cols * d.count)
     row_bits, col_bits = (d.row_count.bit_length() - 1, d.col_count.bit_length() - 1)
     bits = [("row", b) for b in range(row_bits)] + [("col", b) for b in range(1, col_bits)]
-    d.groups = [[("col", 0)]] + [bits[i : i + 2] for i in range(0, len(bits), 2)]
+    d.groups = [[("col", 0)]] + [bits[i : i + 2][::-1] for i in range(0, len(bits), 2)]
     d.stages = [bit for group in d.groups for bit in group]
     return d
 

time: 52.5 us -> 52.4 us (level)
  transfers between devices with their start and end apart: 17 -> 17, of which waited for: 8 -> 7; matrix products, arithmetic and copies ran while one was open for 0% -> 0% of each run, Pallas kernels for 10% -> 10%
where the time goes in v16:
time: 52.4 us; the launch traced here: 52.2 us
  Pallas kernels  20.1 us (38%)
  starting transfers between devices  19.3 us (37%)
  waiting for transfers between devices  11 us (21%)
  local copies, waits for them, and re-layouts  0.96 us (2%)
  between operations  0.76 us (1%)
    pallas_call x11, Pallas kernels, run(): pl.pallas_call(kernel, out_shape=shapes, in_specs=[far] * in_hbm + [space...  20.1 us
    ppermute x10, starting transfers between devices, exchange(): lax.ppermute(strip, ('row', 'col'), swap_pairs(row_count, col_count, rs,...  11.1 us
    ppermute x7, starting transfers between devices, per_device(): lax.ppermute(x, axes, swap_by(d, group, mask))  8.18 us
    ppermute x7, waiting for transfers between devices, per_device(): lax.ppermute(x, axes, swap_by(d, group, mask))  8.17 us
    ppermute x10, waiting for transfers between devices, exchange(): lax.ppermute(strip, ('row', 'col'), swap_pairs(row_count, col_count, rs,...  2.87 us
  transfers between devices with their start and end apart: 17, of which 7 were waited for; matrix products, arithmetic and copies ran while one was open for 0% of the time, Pallas kernels for 10%

profile of v16, /device:TPU:0, one launch (start us, length us, event | category | flops | bytes accessed | tf_op | source)
XLA Modules:
  0.0 52.2 jit_solution(1237660985578352679)
XLA Ops:
  0.6 0.9 %copy-done = bf16[16,64,96]{2,1,0:T(8,128)(2,1)S(1)} copy-done((bf16[16,64,96]{2,1,0:T(8,128)(2,1)S(1)}, bf16[16,64,96]{2,1,0:T(8,128)(2,1)}, u32[]{:S(2)}) %copy-start) | copy-done | bytes 196632
  1.6 3.0 %collective-permute-start.2 = (bf16[6,64,96]{2,1,0:T(8,128)(2,1)S(1)}, bf16[6,64,96]{2,1,0:T(8,128)(2,1)S(1)}, u32[]{:S(2)}, u32[]{:S(2)}) collective-permute-start(bf16[6,64,96]{2,1,0:T(8,128)(2,1)S(1)} %get-tuple-element.71.refs_0_), channel_id=1, source_target_pairs={{0,16},{1,17},{2,18},{3,19},{4,20},{5,21},{6,22},{7,23},{8,24},{9,... | collective-permute-start | bytes 221192 | tf_op jit(solution)/shard_map/ppermute | solution.py:55
  4.8 1.2 %collective-permute-start.4 = (bf16[6,8,96]{2,1,0:T(8,128)(2,1)S(1)}, bf16[6,8,96]{2,1,0:T(8,128)(2,1)S(1)}, u32[]{:S(2)}, u32[]{:S(2)}) collective-permute-start(bf16[6,8,96]{2,1,0:T(8,128)(2,1)S(1)} %get-tuple-element.75), channel_id=1, source_target_pairs={{0,16},{1,18},{2,17},{3,20},{4,19},{5,22},{6,21},{7,24},{8,23},{9,... | collective-permute-start | bytes 27656 | tf_op jit(solution)/shard_map/ppermute | solution.py:55
  6.0 1.1 %collective-permute-start = (bf16[16,8,96]{2,1,0:T(8,128)(2,1)S(1)}, bf16[16,8,96]{2,1,0:T(8,128)(2,1)S(1)}, u32[]{:S(2)}, u32[]{:S(2)}) collective-permute-start(bf16[16,8,96]{2,1,0:T(8,128)(2,1)S(1)} %get-tuple-element.72), channel_id=1, source_target_pairs={{0,1},{1,0},{2,3},{3,2},{4,5},{5,4},{6,7},{7,6},{8,9},{9,8},{10,11... | collective-permute-start | bytes 73736 | tf_op jit(solution)/shard_map/ppermute | solution.py:55
  7.0 0.9 %collective-permute-start.1 = (bf16[16,8,96]{2,1,0:T(8,128)(2,1)S(1)}, bf16[16,8,96]{2,1,0:T(8,128)(2,1)S(1)}, u32[]{:S(2)}, u32[]{:S(2)}) collective-permute-start(bf16[16,8,96]{2,1,0:T(8,128)(2,1)S(1)} %get-tuple-element.73), channel_id=1, source_target_pairs={{0,16},{1,2},{2,1},{3,4},{4,3},{5,6},{6,5},{7,8},{8,7},{9,10},{10,... | collective-permute-start | bytes 73736 | tf_op jit(solution)/shard_map/ppermute | solution.py:55
  8.0 0.8 %shard_map.110 = (bf16[256,768]{1,0:T(8,128)(2,1)S(1)}, bf16[768,256]{1,0:T(8,128)(2,1)S(1)}, bf16[256,768]{1,0:T(8,128)(2,1)S(1)}, bf16[768,256]{1,0:T(8,128)(2...) custom-call(bf16[2,96,384]{2,1,0:T(8,128)(2,1)S(1)} %copy-done.2, ...), custom_call_target="tpu_custom_call" | custom-call | flops 2000000000 | bytes 262144 | tf_op jit(solution)/shard_map/pallas_call | solution.py:836
  8.8 2.1 %collective-permute-done.1.refs_10_ = bf16[16,8,96]{2,1,0:T(8,128)(2,1)S(1)} collective-permute-done((bf16[16,8,96]{2,1,0:T(8,128)(2,1)S(1)}, bf16[16,8,96]{2,1,0:T(8,128)(2,1)S(1)}, u32[]{:S(2)}, u32[]{:S(2)}) %collective-permute-start.1) | collective-permute-done | bytes 24608 | tf_op jit(solution)/shard_map/ppermute | solution.py:55
  10.9 8.4 %shard_map.112 = (bf16[16,64,96]{2,1,0:T(8,128)(2,1)S(1)}, f32[2240,128]{1,0:T(8,128)S(1)}, f32[1600,128]{1,0:T(8,128)S(1)}, bf16[1376,128]{1,0:T(8,128)(2,1)S(1...) custom-call(bf16[16,64,96]{2,1,0:T(8,128)(2,1)S(1)} %get-tuple-eleme, ...), custom_call_target="tpu_custom_call" | custom-call | flops 15000000512 | bytes 262144 | tf_op jit(solution)/shard_map/pallas_call | solution.py:836
  19.3 1.0 %collective-permute-start.7 = (bf16[9,64,96]{2,1,0:T(8,128)(2,1)S(1)}, bf16[9,64,96]{2,1,0:T(8,128)(2,1)S(1)}, u32[]{:S(2)}, u32[]{:S(2)}) collective-permute-start(bf16[9,64,96]{2,1,0:T(8,128)(2,1)S(1)} %get-tuple-element.94.refs_0_), channel_id=1, source_target_pairs={{0,16},{1,17},{2,18},{3,19},{4,20},{5,21},{6,22},{7,23},{8,24},{9,... | collective-permute-start | bytes 331784 | tf_op jit(solution)/shard_map/ppermute | solution.py:55
  20.5 1.2 %collective-permute-start.9 = (bf16[9,8,96]{2,1,0:T(8,128)(2,1)S(1)}, bf16[9,8,96]{2,1,0:T(8,128)(2,1)S(1)}, u32[]{:S(2)}, u32[]{:S(2)}) collective-permute-start(bf16[9,8,96]{2,1,0:T(8,128)(2,1)S(1)} %get-tuple-element.98), channel_id=1, source_target_pairs={{0,16},{1,18},{2,17},{3,20},{4,19},{5,22},{6,21},{7,24},{8,23},{9,... | collective-permute-start | bytes 41480 | tf_op jit(solution)/shard_map/ppermute | solution.py:55
  21.6 1.6 %collective-permute-start.5 = (bf16[32,8,96]{2,1,0:T(8,128)(2,1)S(1)}, bf16[32,8,96]{2,1,0:T(8,128)(2,1)S(1)}, u32[]{:S(2)}, u32[]{:S(2)}) collective-permute-start(bf16[32,8,96]{2,1,0:T(8,128)(2,1)S(1)} %get-tuple-element.95), channel_id=1, source_target_pairs={{0,1},{1,0},{2,3},{3,2},{4,5},{5,4},{6,7},{7,6},{8,9},{9,8},{10,11... | collective-permute-start | bytes 147464 | tf_op jit(solution)/shard_map/ppermute | solution.py:55
  23.2 1.1 %collective-permute-start.6 = (bf16[32,8,96]{2,1,0:T(8,128)(2,1)S(1)}, bf16[32,8,96]{2,1,0:T(8,128)(2,1)S(1)}, u32[]{:S(2)}, u32[]{:S(2)}) collective-permute-start(bf16[32,8,96]{2,1,0:T(8,128)(2,1)S(1)} %get-tuple-element.96), channel_id=1, source_target_pairs={{0,16},{1,2},{2,1},{3,4},{4,3},{5,6},{6,5},{7,8},{8,7},{9,10},{10,... | collective-permute-start | bytes 147464 | tf_op jit(solution)/shard_map/ppermute | solution.py:55
  24.3 2.5 %shard_map.113 = (f32[56,128]{1,0:T(8,128)S(1)}, f32[776,128]{1,0:T(8,128)S(1)}, bf16[16,64,96]{2,1,0:T(8,128)(2,1)}) custom-call(f32[1600,128]{1,0:T(8,128)S(1)} %get-tuple-element.76.x1, f32[1024,128]{1,0:T(8,128)S(1)} %get-tuple-element.77.grad1.refs_0_, bf16[1024,128]{1,0:T(8,128)(2,1)S(1)} %get-tuple-element.78.normed1, ...), custom_call_target="tpu_custom_call" | custom-call | flops 3000000000 | bytes 262144 | tf_op jit(solution)/shard_map/pallas_call | solution.py:836
  27.5 5.4 %shard_map.115 = (f32[1600,128]{1,0:T(8,128)S(1)}, f32[1376,128]{1,0:T(8,128)S(1)}, f32[768,128]{1,0:T(8,128)S(1)}, f32[80,128]{1,0:T(8,128)S(1)}, bf16[848,128]{1,0:T(8,128)(2,1)S(1)}) custom-call(f32[1024,128]{1,0:T(8,128)S(1)} %get-tuple-element.77.grad1.refs_0_, bf16[16,64,96]{2,1,0:T(8,128)(2,1)S(1)} %copy-done.1, ...), custom_call_target="tpu_custom_call" | custom-call | flops 12000000000 | bytes 262144 | tf_op jit(solution)/shard_map/pallas_call | solution.py:836
  33.1 1.4 %collective-permute-done.10.refs_0_ = bf16[848,128]{1,0:T(8,128)(2,1)S(1)} collective-permute-done((bf16[848,128]{1,0:T(8,128)(2,1)S(1)}, bf16[848,128]{1,0:T(8,128)(2,1)S(1)}, u32[]{:S(2)}, u32[]{:S(2)}) %collective-permute-start.10) | collective-permute-done | bytes 217120 | tf_op jit(solution)/shard_map/ppermute | solution.py:972
  34.5 1.1 %collective-permute-start.11 = (bf16[272,128]{1,0:T(8,128)(2,1)S(1)}, bf16[272,128]{1,0:T(8,128)(2,1)S(1)}, u32[]{:S(2)}, u32[]{:S(2)}) collective-permute-start(bf16[272,128]{1,0:T(8,128)(2,1)S(1)} %get-tuple-element.107), channel_id=1, source_target_pairs={{0,16},{1,17},{2,18},{3,19},{4,20},{5,21},{6,22},{7,23},{8,24},{9,... | collective-permute-start | bytes 208904 | tf_op jit(solution)/shard_map/ppermute | solution.py:972
  35.6 1.9 %collective-permute-start.12 = (bf16[272,128]{1,0:T(8,128)(2,1)S(1)}, bf16[272,128]{1,0:T(8,128)(2,1)S(1)}, u32[]{:S(2)}, u32[]{:S(2)}) collective-permute-start(bf16[272,128]{1,0:T(8,128)(2,1)S(1)} %get-tuple-element.108), channel_id=1, source_target_pairs={{0,2},{1,3},{2,0},{3,1},{4,6},{5,7},{6,4},{7,5},{8,10},{9,11},{10,... | collective-permute-start | bytes 208904 | tf_op jit(solution)/shard_map/ppermute | solution.py:972
  38.1 2.1 %shard_map.117 = (bf16[16,64,96]{2,1,0:T(8,128)(2,1)}, f32[8,128]{1,0:T(8,128)S(1)}) custom-call(f32[1600,128]{1,0:T(8,128)S(1)} %get-tuple-element.99.grad0, f32[1376,128]{1,0:T(8,128)S(1)} %get-tuple-element.100.upstream, bf16[784,128]{1,0:T(8,128)(2,1)S(1)} %get-tuple-element.64.refs_2_.taps0, f32[80,128]{1,0:T(8,128)S(1)} %get-tuple-element.104.after.small), custom_call_target="tpu_custom_call" | custom-call | flops 3000000000 | bytes 262144 | tf_op jit(solution)/shard_map/pallas_call | solution.py:836
  40.9 1.9 %collective-permute-done.13.refs_2_ = bf16[272,128]{1,0:T(8,128)(2,1)S(1)} collective-permute-done((bf16[272,128]{1,0:T(8,128)(2,1)S(1)}, bf16[272,128]{1,0:T(8,128)(2,1)S(1)}, u32[]{:S(2)}, u32[]{:S(2)}) %collective-permute-start.13) | collective-permute-done | bytes 69664 | tf_op jit(solution)/shard_map/ppermute | solution.py:972
  42.8 1.6 %collective-permute-start.14 = (bf16[128,128]{1,0:T(8,128)(2,1)S(1)}, bf16[128,128]{1,0:T(8,128)(2,1)S(1)}, u32[]{:S(2)}, u32[]{:S(2)}) collective-permute-start(bf16[128,128]{1,0:T(8,128)(2,1)S(1)} %get-tuple-element.113), channel_id=1, source_target_pairs={{0,4},{1,5},{2,6},{3,7},{4,0},{5,1},{6,2},{7,3},{8,12},{9,13},{10,... | collective-permute-start | bytes 98312 | tf_op jit(solution)/shard_map/ppermute | solution.py:972
  44.5 1.3 %collective-permute-start.15 = (bf16[128,128]{1,0:T(8,128)(2,1)S(1)}, bf16[128,128]{1,0:T(8,128)(2,1)S(1)}, u32[]{:S(2)}, u32[]{:S(2)}) collective-permute-start(bf16[128,128]{1,0:T(8,128)(2,1)S(1)} %get-tuple-element.114), channel_id=1, source_target_pairs={{0,8},{1,9},{2,10},{3,11},{4,12},{5,13},{6,14},{7,15},{8,0},{9,1},... | collective-permute-start | bytes 98312 | tf_op jit(solution)/shard_map/ppermute | solution.py:972
  45.8 1.5 %collective-permute-start.16 = (bf16[128,128]{1,0:T(8,128)(2,1)S(1)}, bf16[128,128]{1,0:T(8,128)(2,1)S(1)}, u32[]{:S(2)}, u32[]{:S(2)}) collective-permute-start(bf16[128,128]{1,0:T(8,128)(2,1)S(1)} %get-tuple-element.115), channel_id=1, source_target_pairs={{0,12},{1,13},{2,14},{3,15},{4,8},{5,9},{6,10},{7,11},{8,4},{9,5},... | collective-permute-start | bytes 98312 | tf_op jit(solution)/shard_map/ppermute | solution.py:972
  47.3 2.4 %collective-permute-done.15.refs_1_ = bf16[128,128]{1,0:T(8,128)(2,1)S(1)} collective-permute-done((bf16[128,128]{1,0:T(8,128)(2,1)S(1)}, bf16[128,128]{1,0:T(8,128)(2,1)S(1)}, u32[]{:S(2)}, u32[]{:S(2)}) %collective-permute-start.15) | collective-permute-done | bytes 32800 | tf_op jit(solution)/shard_map/ppermute | solution.py:972
  49.6 1.8 %collective-permute-done.16.refs_2_ = bf16[128,128]{1,0:T(8,128)(2,1)S(1)} collective-permute-done((bf16[128,128]{1,0:T(8,128)(2,1)S(1)}, bf16[128,128]{1,0:T(8,128)(2,1)S(1)}, u32[]{:S(2)}, u32[]{:S(2)}) %collective-permute-start.16) | collective-permute-done | bytes 32800 | tf_op jit(solution)/shard_map/ppermute | solution.py:972
  (33 shorter events, 3.3 us)
Async XLA Ops:
  0.6 1.0 %copy-start = (bf16[16,64,96]{2,1,0:T(8,128)(2,1)S(1)}, bf16[16,64,96]{2,1,0:T(8,128)(2,1)}, u32[]{:S(2)}) copy-start(bf16[16,64,96]{2,1,0:T(8,128)(2,1)} %image_in.1) | copy-start | bytes 589828
  1.6 9.3 %collective-permute-start.2 = (bf16[6,64,96]{2,1,0:T(8,128)(2,1)S(1)}, bf16[6,64,96]{2,1,0:T(8,128)(2,1)S(1)}, u32[]{:S(2)}, u32[]{:S(2)}) collective-permute-start(bf16[6,64,96]{2,1,0:T(8,128)(2,1)S(1)} %get-tuple-element.71.refs_0_), channel_id=1, source_target_pairs={{0,16},{1,17},{2,18},{3,19},{4,20},{5,21},{6,22},{7,23},{8,24},{9,... | collective-permute-start | bytes 221192 | tf_op jit(solution)/shard_map/ppermute | solution.py:55
  4.7 3.3 %copy-start.2 = (bf16[2,96,384]{2,1,0:T(8,128)(2,1)S(1)}, bf16[2,96,384]{2,1,0:T(8,128)(2,1)}, u32[]{:S(2)}) copy-start(bf16[2,96,384]{2,1,0:T(8,128)(2,1)} %up_in.1) | copy-start | bytes 442372
  4.7 3.3 %copy-start.3 = (bf16[2,384,96]{1,2,0:T(8,128)(2,1)S(1)}, bf16[2,384,96]{1,2,0:T(8,128)(2,1)}, u32[]{:S(2)}) copy-start(bf16[2,384,96]{1,2,0:T(8,128)(2,1)} %param.10) | copy-start | bytes 442372
  4.7 3.3 %copy-start.4 = (f32[2,7,7,96]{3,0,2,1:T(2,128)S(1)}, f32[2,7,7,96]{3,0,2,1:T(2,128)}, u32[]{:S(2)}) copy-start(f32[2,7,7,96]{3,0,2,1:T(2,128)} %param.7) | copy-start | bytes 112900
  4.7 3.3 %copy-start.5 = (f32[2,96]{1,0:T(2,128)S(1)}, f32[2,96]{1,0:T(2,128)}, u32[]{:S(2)}) copy-start(f32[2,96]{1,0:T(2,128)} %gains_in.1) | copy-start | bytes 2308
  4.7 4.1 %collective-permute-start.3 = (bf16[6,8,96]{2,1,0:T(8,128)(2,1)S(1)}, bf16[6,8,96]{2,1,0:T(8,128)(2,1)S(1)}, u32[]{:S(2)}, u32[]{:S(2)}) collective-permute-start(bf16[6,8,96]{2,1,0:T(8,128)(2,1)S(1)} %get-tuple-element.74), channel_id=1, source_target_pairs={{0,17},{1,16},{2,19},{3,18},{4,21},{5,20},{6,23},{7,22},{8,25},{9,... | collective-permute-start | bytes 27656 | tf_op jit(solution)/shard_map/ppermute | solution.py:55
  4.8 4.0 %collective-permute-start.4 = (bf16[6,8,96]{2,1,0:T(8,128)(2,1)S(1)}, bf16[6,8,96]{2,1,0:T(8,128)(2,1)S(1)}, u32[]{:S(2)}, u32[]{:S(2)}) collective-permute-start(bf16[6,8,96]{2,1,0:T(8,128)(2,1)S(1)} %get-tuple-element.75), channel_id=1, source_target_pairs={{0,16},{1,18},{2,17},{3,20},{4,19},{5,22},{6,21},{7,24},{8,23},{9,... | collective-permute-start | bytes 27656 | tf_op jit(solution)/shard_map/ppermute | solution.py:55
  6.0 2.8 %collective-permute-start = (bf16[16,8,96]{2,1,0:T(8,128)(2,1)S(1)}, bf16[16,8,96]{2,1,0:T(8,128)(2,1)S(1)}, u32[]{:S(2)}, u32[]{:S(2)}) collective-permute-start(bf16[16,8,96]{2,1,0:T(8,128)(2,1)S(1)} %get-tuple-element.72), channel_id=1, source_target_pairs={{0,1},{1,0},{2,3},{3,2},{4,5},{5,4},{6,7},{7,6},{8,9},{9,8},{10,11... | collective-permute-start | bytes 73736 | tf_op jit(solution)/shard_map/ppermute | solution.py:55
  7.0 3.9 %collective-permute-start.1 = (bf16[16,8,96]{2,1,0:T(8,128)(2,1)S(1)}, bf16[16,8,96]{2,1,0:T(8,128)(2,1)S(1)}, u32[]{:S(2)}, u32[]{:S(2)}) collective-permute-start(bf16[16,8,96]{2,1,0:T(8,128)(2,1)S(1)} %get-tuple-element.73), channel_id=1, source_target_pairs={{0,16},{1,2},{2,1},{3,4},{4,3},{5,6},{6,5},{7,8},{8,7},{9,10},{10,... | collective-permute-start | bytes 73736 | tf_op jit(solution)/shard_map/ppermute | solution.py:55
  8.0 3.0 %copy-start.1 = (bf16[16,64,96]{2,1,0:T(8,128)(2,1)S(1)}, bf16[16,64,96]{2,1,0:T(8,128)(2,1)}, u32[]{:S(2)}) copy-start(bf16[16,64,96]{2,1,0:T(8,128)(2,1)} %refs_1_.3) | copy-start | bytes 589828
  19.3 8.1 %collective-permute-start.7 = (bf16[9,64,96]{2,1,0:T(8,128)(2,1)S(1)}, bf16[9,64,96]{2,1,0:T(8,128)(2,1)S(1)}, u32[]{:S(2)}, u32[]{:S(2)}) collective-permute-start(bf16[9,64,96]{2,1,0:T(8,128)(2,1)S(1)} %get-tuple-element.94.refs_0_), channel_id=1, source_target_pairs={{0,16},{1,17},{2,18},{3,19},{4,20},{5,21},{6,22},{7,23},{8,24},{9,... | collective-permute-start | bytes 331784 | tf_op jit(solution)/shard_map/ppermute | solution.py:55
  20.4 6.4 %collective-permute-start.8 = (bf16[9,8,96]{2,1,0:T(8,128)(2,1)S(1)}, bf16[9,8,96]{2,1,0:T(8,128)(2,1)S(1)}, u32[]{:S(2)}, u32[]{:S(2)}) collective-permute-start(bf16[9,8,96]{2,1,0:T(8,128)(2,1)S(1)} %get-tuple-element.97), channel_id=1, source_target_pairs={{0,17},{1,16},{2,19},{3,18},{4,21},{5,20},{6,23},{7,22},{8,25},{9,... | collective-permute-start | bytes 41480 | tf_op jit(solution)/shard_map/ppermute | solution.py:55
  20.5 6.3 %collective-permute-start.9 = (bf16[9,8,96]{2,1,0:T(8,128)(2,1)S(1)}, bf16[9,8,96]{2,1,0:T(8,128)(2,1)S(1)}, u32[]{:S(2)}, u32[]{:S(2)}) collective-permute-start(bf16[9,8,96]{2,1,0:T(8,128)(2,1)S(1)} %get-tuple-element.98), channel_id=1, source_target_pairs={{0,16},{1,18},{2,17},{3,20},{4,19},{5,22},{6,21},{7,24},{8,23},{9,... | collective-permute-start | bytes 41480 | tf_op jit(solution)/shard_map/ppermute | solution.py:55
  21.6 5.1 %collective-permute-start.5 = (bf16[32,8,96]{2,1,0:T(8,128)(2,1)S(1)}, bf16[32,8,96]{2,1,0:T(8,128)(2,1)S(1)}, u32[]{:S(2)}, u32[]{:S(2)}) collective-permute-start(bf16[32,8,96]{2,1,0:T(8,128)(2,1)S(1)} %get-tuple-element.95), channel_id=1, source_target_pairs={{0,1},{1,0},{2,3},{3,2},{4,5},{5,4},{6,7},{7,6},{8,9},{9,8},{10,11... | collective-permute-start | bytes 147464 | tf_op jit(solution)/shard_map/ppermute | solution.py:55
  23.2 4.3 %collective-permute-start.6 = (bf16[32,8,96]{2,1,0:T(8,128)(2,1)S(1)}, bf16[32,8,96]{2,1,0:T(8,128)(2,1)S(1)}, u32[]{:S(2)}, u32[]{:S(2)}) collective-permute-start(bf16[32,8,96]{2,1,0:T(8,128)(2,1)S(1)} %get-tuple-element.96), channel_id=1, source_target_pairs={{0,16},{1,2},{2,1},{3,4},{4,3},{5,6},{6,5},{7,8},{8,7},{9,10},{10,... | collective-permute-start | bytes 147464 | tf_op jit(solution)/shard_map/ppermute | solution.py:55
  32.9 1.5 %collective-permute-start.10 = (bf16[848,128]{1,0:T(8,128)(2,1)S(1)}, bf16[848,128]{1,0:T(8,128)(2,1)S(1)}, u32[]{:S(2)}, u32[]{:S(2)}) collective-permute-start(bf16[848,128]{1,0:T(8,128)(2,1)S(1)} %get-tuple-element.103), channel_id=1, source_target_pairs={{0,1},{1,0},{2,3},{3,2},{4,5},{5,4},{6,7},{7,6},{8,9},{9,8},{10,11... | collective-permute-start | bytes 651272 | tf_op jit(solution)/shard_map/ppermute | solution.py:972
  34.5 5.7 %collective-permute-start.11 = (bf16[272,128]{1,0:T(8,128)(2,1)S(1)}, bf16[272,128]{1,0:T(8,128)(2,1)S(1)}, u32[]{:S(2)}, u32[]{:S(2)}) collective-permute-start(bf16[272,128]{1,0:T(8,128)(2,1)S(1)} %get-tuple-element.107), channel_id=1, source_target_pairs={{0,16},{1,17},{2,18},{3,19},{4,20},{5,21},{6,22},{7,23},{8,24},{9,... | collective-permute-start | bytes 208904 | tf_op jit(solution)/shard_map/ppermute | solution.py:972
  35.6 5.3 %collective-permute-start.12 = (bf16[272,128]{1,0:T(8,128)(2,1)S(1)}, bf16[272,128]{1,0:T(8,128)(2,1)S(1)}, u32[]{:S(2)}, u32[]{:S(2)}) collective-permute-start(bf16[272,128]{1,0:T(8,128)(2,1)S(1)} %get-tuple-element.108), channel_id=1, source_target_pairs={{0,2},{1,3},{2,0},{3,1},{4,6},{5,7},{6,4},{7,5},{8,10},{9,11},{10,... | collective-permute-start | bytes 208904 | tf_op jit(solution)/shard_map/ppermute | solution.py:972
  37.6 5.2 %collective-permute-start.13 = (bf16[272,128]{1,0:T(8,128)(2,1)S(1)}, bf16[272,128]{1,0:T(8,128)(2,1)S(1)}, u32[]{:S(2)}, u32[]{:S(2)}) collective-permute-start(bf16[272,128]{1,0:T(8,128)(2,1)S(1)} %get-tuple-element.109), channel_id=1, source_target_pairs={{0,18},{1,19},{2,16},{3,17},{4,22},{5,23},{6,20},{7,21},{8,26},{9,... | collective-permute-start | bytes 208904 | tf_op jit(solution)/shard_map/ppermute | solution.py:972
  42.8 4.5 %collective-permute-start.14 = (bf16[128,128]{1,0:T(8,128)(2,1)S(1)}, bf16[128,128]{1,0:T(8,128)(2,1)S(1)}, u32[]{:S(2)}, u32[]{:S(2)}) collective-permute-start(bf16[128,128]{1,0:T(8,128)(2,1)S(1)} %get-tuple-element.113), channel_id=1, source_target_pairs={{0,4},{1,5},{2,6},{3,7},{4,0},{5,1},{6,2},{7,3},{8,12},{9,13},{10,... | collective-permute-start | bytes 98312 | tf_op jit(solution)/shard_map/ppermute | solution.py:972
  44.5 5.2 %collective-permute-start.15 = (bf16[128,128]{1,0:T(8,128)(2,1)S(1)}, bf16[128,128]{1,0:T(8,128)(2,1)S(1)}, u32[]{:S(2)}, u32[]{:S(2)}) collective-permute-start(bf16[128,128]{1,0:T(8,128)(2,1)S(1)} %get-tuple-element.114), channel_id=1, source_target_pairs={{0,8},{1,9},{2,10},{3,11},{4,12},{5,13},{6,14},{7,15},{8,0},{9,1},... | collective-permute-start | bytes 98312 | tf_op jit(solution)/shard_map/ppermute | solution.py:972
  45.8 5.7 %collective-permute-start.16 = (bf16[128,128]{1,0:T(8,128)(2,1)S(1)}, bf16[128,128]{1,0:T(8,128)(2,1)S(1)}, u32[]{:S(2)}, u32[]{:S(2)}) collective-permute-start(bf16[128,128]{1,0:T(8,128)(2,1)S(1)} %get-tuple-element.115), channel_id=1, source_target_pairs={{0,12},{1,13},{2,14},{3,15},{4,8},{5,9},{6,10},{7,11},{8,4},{9,5},... | collective-permute-start | bytes 98312 | tf_op jit(solution)/shard_map/ppermute | solution.py:972

commit v17 on v16

--- a/solution.py
+++ b/solution.py
@@ -154,14 +154,13 @@
 
 def assemble(place, target, own, read, radius, rows, cols, channels):
     width = cols + 2 * SIDE
-    target[...] = jnp.zeros(target.shape, f32)
     for vertical, start, count in (("above", 0, radius), (None, radius, rows), ("below", radius + rows, radius)):
         for i in range(count):
             base = (start + i) * width
             middle = own(i) if vertical is None else read(vertical, None, i)
-            target[base + SIDE : base + SIDE + cols, 0:channels] = middle
-            target[base : base + SIDE, 0:channels] = read(vertical, "left", i)
-            target[base + SIDE + cols : base + width, 0:channels] = read(vertical, "right", i)
+            target[base + SIDE : base + SIDE + cols, :] = pad_lanes(middle)
+            target[base : base + SIDE, :] = pad_lanes(read(vertical, "left", i))
+            target[base + SIDE + cols : base + width, :] = pad_lanes(read(vertical, "right", i))
 
 
 def spread_taps(kernel_ref, layer, target):

time: 52.4 us -> 52.3 us (level)
  no operation moved by 1% of the time
where the time goes in v17:
time: 52.3 us; the launch traced here: 52.1 us
  Pallas kernels  20 us (38%)
  starting transfers between devices  19.3 us (37%)
  waiting for transfers between devices  11 us (21%)
  local copies, waits for them, and re-layouts  0.96 us (2%)
  between operations  0.76 us (1%)
    pallas_call x11, Pallas kernels, run(): pl.pallas_call(kernel, out_shape=shapes, in_specs=[far] * in_hbm + [space...  20 us
    ppermute x10, starting transfers between devices, exchange(): lax.ppermute(strip, ('row', 'col'), swap_pairs(row_count, col_count, rs,...  11.1 us
    ppermute x7, starting transfers between devices, per_device(): lax.ppermute(x, axes, swap_by(d, group, mask))  8.19 us
    ppermute x7, waiting for transfers between devices, per_device(): lax.ppermute(x, axes, swap_by(d, group, mask))  8.17 us
    ppermute x10, waiting for transfers between devices, exchange(): lax.ppermute(strip, ('row', 'col'), swap_pairs(row_count, col_count, rs,...  2.87 us
  transfers between devices with their start and end apart: 17, of which 7 were waited for; matrix products, arithmetic and copies ran while one was open for 0% of the time, Pallas kernels for 10%

profile of v17, /device:TPU:0, one launch (start us, length us, event | category | flops | bytes accessed | tf_op | source)
XLA Modules:
  0.0 52.1 jit_solution(4050394593060539661)
XLA Ops:
  0.6 0.9 %copy-done = bf16[16,64,96]{2,1,0:T(8,128)(2,1)S(1)} copy-done((bf16[16,64,96]{2,1,0:T(8,128)(2,1)S(1)}, bf16[16,64,96]{2,1,0:T(8,128)(2,1)}, u32[]{:S(2)}) %copy-start) | copy-done | bytes 196632
  1.6 3.0 %collective-permute-start.2 = (bf16[6,64,96]{2,1,0:T(8,128)(2,1)S(1)}, bf16[6,64,96]{2,1,0:T(8,128)(2,1)S(1)}, u32[]{:S(2)}, u32[]{:S(2)}) collective-permute-start(bf16[6,64,96]{2,1,0:T(8,128)(2,1)S(1)} %get-tuple-element.71.refs_0_), channel_id=1, source_target_pairs={{0,16},{1,17},{2,18},{3,19},{4,20},{5,21},{6,22},{7,23},{8,24},{9,... | collective-permute-start | bytes 221192 | tf_op jit(solution)/shard_map/ppermute | solution.py:55
  4.8 1.2 %collective-permute-start.4 = (bf16[6,8,96]{2,1,0:T(8,128)(2,1)S(1)}, bf16[6,8,96]{2,1,0:T(8,128)(2,1)S(1)}, u32[]{:S(2)}, u32[]{:S(2)}) collective-permute-start(bf16[6,8,96]{2,1,0:T(8,128)(2,1)S(1)} %get-tuple-element.75), channel_id=1, source_target_pairs={{0,16},{1,18},{2,17},{3,20},{4,19},{5,22},{6,21},{7,24},{8,23},{9,... | collective-permute-start | bytes 27656 | tf_op jit(solution)/shard_map/ppermute | solution.py:55
  6.0 1.1 %collective-permute-start = (bf16[16,8,96]{2,1,0:T(8,128)(2,1)S(1)}, bf16[16,8,96]{2,1,0:T(8,128)(2,1)S(1)}, u32[]{:S(2)}, u32[]{:S(2)}) collective-permute-start(bf16[16,8,96]{2,1,0:T(8,128)(2,1)S(1)} %get-tuple-element.72), channel_id=1, source_target_pairs={{0,1},{1,0},{2,3},{3,2},{4,5},{5,4},{6,7},{7,6},{8,9},{9,8},{10,11... | collective-permute-start | bytes 73736 | tf_op jit(solution)/shard_map/ppermute | solution.py:55
  7.0 0.9 %collective-permute-start.1 = (bf16[16,8,96]{2,1,0:T(8,128)(2,1)S(1)}, bf16[16,8,96]{2,1,0:T(8,128)(2,1)S(1)}, u32[]{:S(2)}, u32[]{:S(2)}) collective-permute-start(bf16[16,8,96]{2,1,0:T(8,128)(2,1)S(1)} %get-tuple-element.73), channel_id=1, source_target_pairs={{0,16},{1,2},{2,1},{3,4},{4,3},{5,6},{6,5},{7,8},{8,7},{9,10},{10,... | collective-permute-start | bytes 73736 | tf_op jit(solution)/shard_map/ppermute | solution.py:55
  8.0 0.8 %shard_map.110 = (bf16[256,768]{1,0:T(8,128)(2,1)S(1)}, bf16[768,256]{1,0:T(8,128)(2,1)S(1)}, bf16[256,768]{1,0:T(8,128)(2,1)S(1)}, bf16[768,256]{1,0:T(8,128)(2...) custom-call(bf16[2,96,384]{2,1,0:T(8,128)(2,1)S(1)} %copy-done.2, ...), custom_call_target="tpu_custom_call" | custom-call | flops 2000000000 | bytes 262144 | tf_op jit(solution)/shard_map/pallas_call | solution.py:835
  8.8 2.1 %collective-permute-done.1.refs_10_ = bf16[16,8,96]{2,1,0:T(8,128)(2,1)S(1)} collective-permute-done((bf16[16,8,96]{2,1,0:T(8,128)(2,1)S(1)}, bf16[16,8,96]{2,1,0:T(8,128)(2,1)S(1)}, u32[]{:S(2)}, u32[]{:S(2)}) %collective-permute-start.1) | collective-permute-done | bytes 24608 | tf_op jit(solution)/shard_map/ppermute | solution.py:55
  10.9 8.4 %shard_map.112 = (bf16[16,64,96]{2,1,0:T(8,128)(2,1)S(1)}, f32[2240,128]{1,0:T(8,128)S(1)}, f32[1600,128]{1,0:T(8,128)S(1)}, bf16[1376,128]{1,0:T(8,128)(2,1)S(1...) custom-call(bf16[16,64,96]{2,1,0:T(8,128)(2,1)S(1)} %get-tuple-eleme, ...), custom_call_target="tpu_custom_call" | custom-call | flops 15000000512 | bytes 262144 | tf_op jit(solution)/shard_map/pallas_call | solution.py:835
  19.3 1.0 %collective-permute-start.7 = (bf16[9,64,96]{2,1,0:T(8,128)(2,1)S(1)}, bf16[9,64,96]{2,1,0:T(8,128)(2,1)S(1)}, u32[]{:S(2)}, u32[]{:S(2)}) collective-permute-start(bf16[9,64,96]{2,1,0:T(8,128)(2,1)S(1)} %get-tuple-element.94.refs_0_), channel_id=1, source_target_pairs={{0,16},{1,17},{2,18},{3,19},{4,20},{5,21},{6,22},{7,23},{8,24},{9,... | collective-permute-start | bytes 331784 | tf_op jit(solution)/shard_map/ppermute | solution.py:55
  20.4 1.2 %collective-permute-start.9 = (bf16[9,8,96]{2,1,0:T(8,128)(2,1)S(1)}, bf16[9,8,96]{2,1,0:T(8,128)(2,1)S(1)}, u32[]{:S(2)}, u32[]{:S(2)}) collective-permute-start(bf16[9,8,96]{2,1,0:T(8,128)(2,1)S(1)} %get-tuple-element.98), channel_id=1, source_target_pairs={{0,16},{1,18},{2,17},{3,20},{4,19},{5,22},{6,21},{7,24},{8,23},{9,... | collective-permute-start | bytes 41480 | tf_op jit(solution)/shard_map/ppermute | solution.py:55
  21.6 1.6 %collective-permute-start.5 = (bf16[32,8,96]{2,1,0:T(8,128)(2,1)S(1)}, bf16[32,8,96]{2,1,0:T(8,128)(2,1)S(1)}, u32[]{:S(2)}, u32[]{:S(2)}) collective-permute-start(bf16[32,8,96]{2,1,0:T(8,128)(2,1)S(1)} %get-tuple-element.95), channel_id=1, source_target_pairs={{0,1},{1,0},{2,3},{3,2},{4,5},{5,4},{6,7},{7,6},{8,9},{9,8},{10,11... | collective-permute-start | bytes 147464 | tf_op jit(solution)/shard_map/ppermute | solution.py:55
  23.2 1.1 %collective-permute-start.6 = (bf16[32,8,96]{2,1,0:T(8,128)(2,1)S(1)}, bf16[32,8,96]{2,1,0:T(8,128)(2,1)S(1)}, u32[]{:S(2)}, u32[]{:S(2)}) collective-permute-start(bf16[32,8,96]{2,1,0:T(8,128)(2,1)S(1)} %get-tuple-element.96), channel_id=1, source_target_pairs={{0,16},{1,2},{2,1},{3,4},{4,3},{5,6},{6,5},{7,8},{8,7},{9,10},{10,... | collective-permute-start | bytes 147464 | tf_op jit(solution)/shard_map/ppermute | solution.py:55
  24.3 2.5 %shard_map.113 = (f32[56,128]{1,0:T(8,128)S(1)}, f32[776,128]{1,0:T(8,128)S(1)}, bf16[16,64,96]{2,1,0:T(8,128)(2,1)}) custom-call(f32[1600,128]{1,0:T(8,128)S(1)} %get-tuple-element.76.x1, f32[1024,128]{1,0:T(8,128)S(1)} %get-tuple-element.77.grad1.refs_0_, bf16[1024,128]{1,0:T(8,128)(2,1)S(1)} %get-tuple-element.78.normed1, ...), custom_call_target="tpu_custom_call" | custom-call | flops 3000000000 | bytes 262144 | tf_op jit(solution)/shard_map/pallas_call | solution.py:835
  27.4 5.3 %shard_map.115 = (f32[1600,128]{1,0:T(8,128)S(1)}, f32[1376,128]{1,0:T(8,128)S(1)}, f32[768,128]{1,0:T(8,128)S(1)}, f32[80,128]{1,0:T(8,128)S(1)}, bf16[848,128]{1,0:T(8,128)(2,1)S(1)}) custom-call(f32[1024,128]{1,0:T(8,128)S(1)} %get-tuple-element.77.grad1.refs_0_, bf16[16,64,96]{2,1,0:T(8,128)(2,1)S(1)} %copy-done.1, ...), custom_call_target="tpu_custom_call" | custom-call | flops 12000000000 | bytes 262144 | tf_op jit(solution)/shard_map/pallas_call | solution.py:835
  33.0 1.4 %collective-permute-done.10.refs_0_ = bf16[848,128]{1,0:T(8,128)(2,1)S(1)} collective-permute-done((bf16[848,128]{1,0:T(8,128)(2,1)S(1)}, bf16[848,128]{1,0:T(8,128)(2,1)S(1)}, u32[]{:S(2)}, u32[]{:S(2)}) %collective-permute-start.10) | collective-permute-done | bytes 217120 | tf_op jit(solution)/shard_map/ppermute | solution.py:971
  34.4 1.1 %collective-permute-start.11 = (bf16[272,128]{1,0:T(8,128)(2,1)S(1)}, bf16[272,128]{1,0:T(8,128)(2,1)S(1)}, u32[]{:S(2)}, u32[]{:S(2)}) collective-permute-start(bf16[272,128]{1,0:T(8,128)(2,1)S(1)} %get-tuple-element.107), channel_id=1, source_target_pairs={{0,16},{1,17},{2,18},{3,19},{4,20},{5,21},{6,22},{7,23},{8,24},{9,... | collective-permute-start | bytes 208904 | tf_op jit(solution)/shard_map/ppermute | solution.py:971
  35.5 1.9 %collective-permute-start.12 = (bf16[272,128]{1,0:T(8,128)(2,1)S(1)}, bf16[272,128]{1,0:T(8,128)(2,1)S(1)}, u32[]{:S(2)}, u32[]{:S(2)}) collective-permute-start(bf16[272,128]{1,0:T(8,128)(2,1)S(1)} %get-tuple-element.108), channel_id=1, source_target_pairs={{0,2},{1,3},{2,0},{3,1},{4,6},{5,7},{6,4},{7,5},{8,10},{9,11},{10,... | collective-permute-start | bytes 208904 | tf_op jit(solution)/shard_map/ppermute | solution.py:971
  37.9 2.1 %shard_map.117 = (bf16[16,64,96]{2,1,0:T(8,128)(2,1)}, f32[8,128]{1,0:T(8,128)S(1)}) custom-call(f32[1600,128]{1,0:T(8,128)S(1)} %get-tuple-element.99.grad0, f32[1376,128]{1,0:T(8,128)S(1)} %get-tuple-element.100.upstream, bf16[784,128]{1,0:T(8,128)(2,1)S(1)} %get-tuple-element.64.refs_2_.taps0, f32[80,128]{1,0:T(8,128)S(1)} %get-tuple-element.104.after.small), custom_call_target="tpu_custom_call" | custom-call | flops 3000000000 | bytes 262144 | tf_op jit(solution)/shard_map/pallas_call | solution.py:835
  40.8 1.9 %collective-permute-done.13.refs_2_ = bf16[272,128]{1,0:T(8,128)(2,1)S(1)} collective-permute-done((bf16[272,128]{1,0:T(8,128)(2,1)S(1)}, bf16[272,128]{1,0:T(8,128)(2,1)S(1)}, u32[]{:S(2)}, u32[]{:S(2)}) %collective-permute-start.13) | collective-permute-done | bytes 69664 | tf_op jit(solution)/shard_map/ppermute | solution.py:971
  42.7 1.6 %collective-permute-start.14 = (bf16[128,128]{1,0:T(8,128)(2,1)S(1)}, bf16[128,128]{1,0:T(8,128)(2,1)S(1)}, u32[]{:S(2)}, u32[]{:S(2)}) collective-permute-start(bf16[128,128]{1,0:T(8,128)(2,1)S(1)} %get-tuple-element.113), channel_id=1, source_target_pairs={{0,4},{1,5},{2,6},{3,7},{4,0},{5,1},{6,2},{7,3},{8,12},{9,13},{10,... | collective-permute-start | bytes 98312 | tf_op jit(solution)/shard_map/ppermute | solution.py:971
  44.4 1.3 %collective-permute-start.15 = (bf16[128,128]{1,0:T(8,128)(2,1)S(1)}, bf16[128,128]{1,0:T(8,128)(2,1)S(1)}, u32[]{:S(2)}, u32[]{:S(2)}) collective-permute-start(bf16[128,128]{1,0:T(8,128)(2,1)S(1)} %get-tuple-element.114), channel_id=1, source_target_pairs={{0,8},{1,9},{2,10},{3,11},{4,12},{5,13},{6,14},{7,15},{8,0},{9,1},... | collective-permute-start | bytes 98312 | tf_op jit(solution)/shard_map/ppermute | solution.py:971
  45.7 1.5 %collective-permute-start.16 = (bf16[128,128]{1,0:T(8,128)(2,1)S(1)}, bf16[128,128]{1,0:T(8,128)(2,1)S(1)}, u32[]{:S(2)}, u32[]{:S(2)}) collective-permute-start(bf16[128,128]{1,0:T(8,128)(2,1)S(1)} %get-tuple-element.115), channel_id=1, source_target_pairs={{0,12},{1,13},{2,14},{3,15},{4,8},{5,9},{6,10},{7,11},{8,4},{9,5},... | collective-permute-start | bytes 98312 | tf_op jit(solution)/shard_map/ppermute | solution.py:971
  47.2 2.4 %collective-permute-done.15.refs_1_ = bf16[128,128]{1,0:T(8,128)(2,1)S(1)} collective-permute-done((bf16[128,128]{1,0:T(8,128)(2,1)S(1)}, bf16[128,128]{1,0:T(8,128)(2,1)S(1)}, u32[]{:S(2)}, u32[]{:S(2)}) %collective-permute-start.15) | collective-permute-done | bytes 32800 | tf_op jit(solution)/shard_map/ppermute | solution.py:971
  49.5 1.9 %collective-permute-done.16.refs_2_ = bf16[128,128]{1,0:T(8,128)(2,1)S(1)} collective-permute-done((bf16[128,128]{1,0:T(8,128)(2,1)S(1)}, bf16[128,128]{1,0:T(8,128)(2,1)S(1)}, u32[]{:S(2)}, u32[]{:S(2)}) %collective-permute-start.16) | collective-permute-done | bytes 32800 | tf_op jit(solution)/shard_map/ppermute | solution.py:971
  (33 shorter events, 3.3 us)
Async XLA Ops:
  0.6 1.0 %copy-start = (bf16[16,64,96]{2,1,0:T(8,128)(2,1)S(1)}, bf16[16,64,96]{2,1,0:T(8,128)(2,1)}, u32[]{:S(2)}) copy-start(bf16[16,64,96]{2,1,0:T(8,128)(2,1)} %image_in.1) | copy-start | bytes 589828
  1.6 9.3 %collective-permute-start.2 = (bf16[6,64,96]{2,1,0:T(8,128)(2,1)S(1)}, bf16[6,64,96]{2,1,0:T(8,128)(2,1)S(1)}, u32[]{:S(2)}, u32[]{:S(2)}) collective-permute-start(bf16[6,64,96]{2,1,0:T(8,128)(2,1)S(1)} %get-tuple-element.71.refs_0_), channel_id=1, source_target_pairs={{0,16},{1,17},{2,18},{3,19},{4,20},{5,21},{6,22},{7,23},{8,24},{9,... | collective-permute-start | bytes 221192 | tf_op jit(solution)/shard_map/ppermute | solution.py:55
  4.7 3.3 %copy-start.2 = (bf16[2,96,384]{2,1,0:T(8,128)(2,1)S(1)}, bf16[2,96,384]{2,1,0:T(8,128)(2,1)}, u32[]{:S(2)}) copy-start(bf16[2,96,384]{2,1,0:T(8,128)(2,1)} %up_in.1) | copy-start | bytes 442372
  4.7 3.3 %copy-start.3 = (bf16[2,384,96]{1,2,0:T(8,128)(2,1)S(1)}, bf16[2,384,96]{1,2,0:T(8,128)(2,1)}, u32[]{:S(2)}) copy-start(bf16[2,384,96]{1,2,0:T(8,128)(2,1)} %param.10) | copy-start | bytes 442372
  4.7 3.3 %copy-start.4 = (f32[2,7,7,96]{3,0,2,1:T(2,128)S(1)}, f32[2,7,7,96]{3,0,2,1:T(2,128)}, u32[]{:S(2)}) copy-start(f32[2,7,7,96]{3,0,2,1:T(2,128)} %param.7) | copy-start | bytes 112900
  4.7 3.3 %copy-start.5 = (f32[2,96]{1,0:T(2,128)S(1)}, f32[2,96]{1,0:T(2,128)}, u32[]{:S(2)}) copy-start(f32[2,96]{1,0:T(2,128)} %gains_in.1) | copy-start | bytes 2308
  4.7 4.1 %collective-permute-start.3 = (bf16[6,8,96]{2,1,0:T(8,128)(2,1)S(1)}, bf16[6,8,96]{2,1,0:T(8,128)(2,1)S(1)}, u32[]{:S(2)}, u32[]{:S(2)}) collective-permute-start(bf16[6,8,96]{2,1,0:T(8,128)(2,1)S(1)} %get-tuple-element.74), channel_id=1, source_target_pairs={{0,17},{1,16},{2,19},{3,18},{4,21},{5,20},{6,23},{7,22},{8,25},{9,... | collective-permute-start | bytes 27656 | tf_op jit(solution)/shard_map/ppermute | solution.py:55
  4.8 4.0 %collective-permute-start.4 = (bf16[6,8,96]{2,1,0:T(8,128)(2,1)S(1)}, bf16[6,8,96]{2,1,0:T(8,128)(2,1)S(1)}, u32[]{:S(2)}, u32[]{:S(2)}) collective-permute-start(bf16[6,8,96]{2,1,0:T(8,128)(2,1)S(1)} %get-tuple-element.75), channel_id=1, source_target_pairs={{0,16},{1,18},{2,17},{3,20},{4,19},{5,22},{6,21},{7,24},{8,23},{9,... | collective-permute-start | bytes 27656 | tf_op jit(solution)/shard_map/ppermute | solution.py:55
  6.0 2.8 %collective-permute-start = (bf16[16,8,96]{2,1,0:T(8,128)(2,1)S(1)}, bf16[16,8,96]{2,1,0:T(8,128)(2,1)S(1)}, u32[]{:S(2)}, u32[]{:S(2)}) collective-permute-start(bf16[16,8,96]{2,1,0:T(8,128)(2,1)S(1)} %get-tuple-element.72), channel_id=1, source_target_pairs={{0,1},{1,0},{2,3},{3,2},{4,5},{5,4},{6,7},{7,6},{8,9},{9,8},{10,11... | collective-permute-start | bytes 73736 | tf_op jit(solution)/shard_map/ppermute | solution.py:55
  7.0 3.9 %collective-permute-start.1 = (bf16[16,8,96]{2,1,0:T(8,128)(2,1)S(1)}, bf16[16,8,96]{2,1,0:T(8,128)(2,1)S(1)}, u32[]{:S(2)}, u32[]{:S(2)}) collective-permute-start(bf16[16,8,96]{2,1,0:T(8,128)(2,1)S(1)} %get-tuple-element.73), channel_id=1, source_target_pairs={{0,16},{1,2},{2,1},{3,4},{4,3},{5,6},{6,5},{7,8},{8,7},{9,10},{10,... | collective-permute-start | bytes 73736 | tf_op jit(solution)/shard_map/ppermute | solution.py:55
  8.0 3.0 %copy-start.1 = (bf16[16,64,96]{2,1,0:T(8,128)(2,1)S(1)}, bf16[16,64,96]{2,1,0:T(8,128)(2,1)}, u32[]{:S(2)}) copy-start(bf16[16,64,96]{2,1,0:T(8,128)(2,1)} %refs_1_.3) | copy-start | bytes 589828
  19.3 8.1 %collective-permute-start.7 = (bf16[9,64,96]{2,1,0:T(8,128)(2,1)S(1)}, bf16[9,64,96]{2,1,0:T(8,128)(2,1)S(1)}, u32[]{:S(2)}, u32[]{:S(2)}) collective-permute-start(bf16[9,64,96]{2,1,0:T(8,128)(2,1)S(1)} %get-tuple-element.94.refs_0_), channel_id=1, source_target_pairs={{0,16},{1,17},{2,18},{3,19},{4,20},{5,21},{6,22},{7,23},{8,24},{9,... | collective-permute-start | bytes 331784 | tf_op jit(solution)/shard_map/ppermute | solution.py:55
  20.4 6.4 %collective-permute-start.8 = (bf16[9,8,96]{2,1,0:T(8,128)(2,1)S(1)}, bf16[9,8,96]{2,1,0:T(8,128)(2,1)S(1)}, u32[]{:S(2)}, u32[]{:S(2)}) collective-permute-start(bf16[9,8,96]{2,1,0:T(8,128)(2,1)S(1)} %get-tuple-element.97), channel_id=1, source_target_pairs={{0,17},{1,16},{2,19},{3,18},{4,21},{5,20},{6,23},{7,22},{8,25},{9,... | collective-permute-start | bytes 41480 | tf_op jit(solution)/shard_map/ppermute | solution.py:55
  20.4 6.3 %collective-permute-start.9 = (bf16[9,8,96]{2,1,0:T(8,128)(2,1)S(1)}, bf16[9,8,96]{2,1,0:T(8,128)(2,1)S(1)}, u32[]{:S(2)}, u32[]{:S(2)}) collective-permute-start(bf16[9,8,96]{2,1,0:T(8,128)(2,1)S(1)} %get-tuple-element.98), channel_id=1, source_target_pairs={{0,16},{1,18},{2,17},{3,20},{4,19},{5,22},{6,21},{7,24},{8,23},{9,... | collective-permute-start | bytes 41480 | tf_op jit(solution)/shard_map/ppermute | solution.py:55
  21.6 5.1 %collective-permute-start.5 = (bf16[32,8,96]{2,1,0:T(8,128)(2,1)S(1)}, bf16[32,8,96]{2,1,0:T(8,128)(2,1)S(1)}, u32[]{:S(2)}, u32[]{:S(2)}) collective-permute-start(bf16[32,8,96]{2,1,0:T(8,128)(2,1)S(1)} %get-tuple-element.95), channel_id=1, source_target_pairs={{0,1},{1,0},{2,3},{3,2},{4,5},{5,4},{6,7},{7,6},{8,9},{9,8},{10,11... | collective-permute-start | bytes 147464 | tf_op jit(solution)/shard_map/ppermute | solution.py:55
  23.2 4.3 %collective-permute-start.6 = (bf16[32,8,96]{2,1,0:T(8,128)(2,1)S(1)}, bf16[32,8,96]{2,1,0:T(8,128)(2,1)S(1)}, u32[]{:S(2)}, u32[]{:S(2)}) collective-permute-start(bf16[32,8,96]{2,1,0:T(8,128)(2,1)S(1)} %get-tuple-element.96), channel_id=1, source_target_pairs={{0,16},{1,2},{2,1},{3,4},{4,3},{5,6},{6,5},{7,8},{8,7},{9,10},{10,... | collective-permute-start | bytes 147464 | tf_op jit(solution)/shard_map/ppermute | solution.py:55
  32.8 1.5 %collective-permute-start.10 = (bf16[848,128]{1,0:T(8,128)(2,1)S(1)}, bf16[848,128]{1,0:T(8,128)(2,1)S(1)}, u32[]{:S(2)}, u32[]{:S(2)}) collective-permute-start(bf16[848,128]{1,0:T(8,128)(2,1)S(1)} %get-tuple-element.103), channel_id=1, source_target_pairs={{0,1},{1,0},{2,3},{3,2},{4,5},{5,4},{6,7},{7,6},{8,9},{9,8},{10,11... | collective-permute-start | bytes 651272 | tf_op jit(solution)/shard_map/ppermute | solution.py:971
  34.4 5.7 %collective-permute-start.11 = (bf16[272,128]{1,0:T(8,128)(2,1)S(1)}, bf16[272,128]{1,0:T(8,128)(2,1)S(1)}, u32[]{:S(2)}, u32[]{:S(2)}) collective-permute-start(bf16[272,128]{1,0:T(8,128)(2,1)S(1)} %get-tuple-element.107), channel_id=1, source_target_pairs={{0,16},{1,17},{2,18},{3,19},{4,20},{5,21},{6,22},{7,23},{8,24},{9,... | collective-permute-start | bytes 208904 | tf_op jit(solution)/shard_map/ppermute | solution.py:971
  35.5 5.3 %collective-permute-start.12 = (bf16[272,128]{1,0:T(8,128)(2,1)S(1)}, bf16[272,128]{1,0:T(8,128)(2,1)S(1)}, u32[]{:S(2)}, u32[]{:S(2)}) collective-permute-start(bf16[272,128]{1,0:T(8,128)(2,1)S(1)} %get-tuple-element.108), channel_id=1, source_target_pairs={{0,2},{1,3},{2,0},{3,1},{4,6},{5,7},{6,4},{7,5},{8,10},{9,11},{10,... | collective-permute-start | bytes 208904 | tf_op jit(solution)/shard_map/ppermute | solution.py:971
  37.5 5.2 %collective-permute-start.13 = (bf16[272,128]{1,0:T(8,128)(2,1)S(1)}, bf16[272,128]{1,0:T(8,128)(2,1)S(1)}, u32[]{:S(2)}, u32[]{:S(2)}) collective-permute-start(bf16[272,128]{1,0:T(8,128)(2,1)S(1)} %get-tuple-element.109), channel_id=1, source_target_pairs={{0,18},{1,19},{2,16},{3,17},{4,22},{5,23},{6,20},{7,21},{8,26},{9,... | collective-permute-start | bytes 208904 | tf_op jit(solution)/shard_map/ppermute | solution.py:971
  42.7 4.5 %collective-permute-start.14 = (bf16[128,128]{1,0:T(8,128)(2,1)S(1)}, bf16[128,128]{1,0:T(8,128)(2,1)S(1)}, u32[]{:S(2)}, u32[]{:S(2)}) collective-permute-start(bf16[128,128]{1,0:T(8,128)(2,1)S(1)} %get-tuple-element.113), channel_id=1, source_target_pairs={{0,4},{1,5},{2,6},{3,7},{4,0},{5,1},{6,2},{7,3},{8,12},{9,13},{10,... | collective-permute-start | bytes 98312 | tf_op jit(solution)/shard_map/ppermute | solution.py:971
  44.4 5.2 %collective-permute-start.15 = (bf16[128,128]{1,0:T(8,128)(2,1)S(1)}, bf16[128,128]{1,0:T(8,128)(2,1)S(1)}, u32[]{:S(2)}, u32[]{:S(2)}) collective-permute-start(bf16[128,128]{1,0:T(8,128)(2,1)S(1)} %get-tuple-element.114), channel_id=1, source_target_pairs={{0,8},{1,9},{2,10},{3,11},{4,12},{5,13},{6,14},{7,15},{8,0},{9,1},... | collective-permute-start | bytes 98312 | tf_op jit(solution)/shard_map/ppermute | solution.py:971
  45.7 5.7 %collective-permute-start.16 = (bf16[128,128]{1,0:T(8,128)(2,1)S(1)}, bf16[128,128]{1,0:T(8,128)(2,1)S(1)}, u32[]{:S(2)}, u32[]{:S(2)}) collective-permute-start(bf16[128,128]{1,0:T(8,128)(2,1)S(1)} %get-tuple-element.115), channel_id=1, source_target_pairs={{0,12},{1,13},{2,14},{3,15},{4,8},{5,9},{6,10},{7,11},{8,4},{9,5},... | collective-permute-start | bytes 98312 | tf_op jit(solution)/shard_map/ppermute | solution.py:971
